TPU v7x, 512 devices: a whole 4x8x8 slice. The times are simulated.
512 devices in a mesh: gx: 8 (over z), gy: 4 (over y_lo, core), gz: 16 (over x, y_hi).
Axes of the slice: x: 4, y: 8 (y_hi: 4, y_lo: 2; y = y_hi * 2 + y_lo), z: 8, core: 2. Of those that a mesh axis runs over, the one named last changes fastest.
Arguments:
- right_side: float32 [128, 64, 2048], P('gx', 'gy', 'gz'), may hold values from -6 to 6
- iterate: float32 [128, 64, 2048], P('gx', 'gy', 'gz'), may hold values from -3 to 3
- phase_map: int32 [128, 64, 2048], P('gx', 'gy', 'gz'), may hold values from 0 to 3
- phase_coef: float32 [4], replicated, may hold values from 0.5 to 8
Outputs:
- updated: float32 [128, 64, 2048], P('gx', 'gy', 'gz')
All inputs are finite; a program needn't handle non-finite values.
Results may differ from a plain program's by a relative error of at most 0.0001.
Values sent between devices are 32-bit elements; how exact they have to be, the bound alone decides.
No kernel may reach another device: no remote copies, remote signals or barrier semaphores. Data moves between devices by JAX's collectives and lax.ppermute only.
A program may use at most 64 MiB of HBM per device.

v0:
```python
import jax
import jax.numpy as jnp
from jax import lax
from jax.sharding import PartitionSpec as P

PHASES = 4
LEVELS = 5
SWEEPS1 = 3
SWEEPS2 = 3
SWEEPS3 = 4


OMEGA = 2.0 / 3.0
OFFSETS = [
    (step_x, step_y, step_z)
    for step_x in (-1, 0, 1)
    for step_y in (-1, 0, 1)
    for step_z in (-1, 0, 1)
    if (step_x, step_y, step_z) != (0, 0, 0)
]


def extended(block, sides, width):
    for axis, dim in sides:
        count = lax.axis_size(axis)
        forward = [(i, i + 1) for i in range(count - 1)]
        backward = [(target, source) for source, target in forward]
        low = lax.ppermute(
            lax.slice_in_dim(block, block.shape[dim] - width, None, axis=dim), axis, forward
        )
        high = lax.ppermute(lax.slice_in_dim(block, 0, width, axis=dim), axis, backward)
        block = jnp.concatenate([low, block, high], axis=dim)
    return block


def offset_weight(offset):
    return 2.0 ** (1 - (abs(offset[0]) + abs(offset[1]) + abs(offset[2])))


def window(padded, offset):
    ext_x = padded.shape[0] - 2
    ext_y = padded.shape[1] - 2
    ext_z = padded.shape[2] - 2
    return padded[
        1 + offset[0] : 1 + offset[0] + ext_x,
        1 + offset[1] : 1 + offset[1] + ext_y,
        1 + offset[2] : 1 + offset[2] + ext_z,
    ]


def stencil_diag(coef_pad):
    centre = window(coef_pad, (0, 0, 0))
    summed = jnp.zeros(centre.shape, jnp.float32)
    for offset in OFFSETS:
        summed = summed + offset_weight(offset) * 0.5 * (centre + window(coef_pad, offset))
    return summed


def apply_stencil(coef_pad, field_pad):
    centre = window(coef_pad, (0, 0, 0))
    middle = window(field_pad, (0, 0, 0))
    summed = jnp.zeros(centre.shape, jnp.float32)
    for offset in OFFSETS:
        summed = summed + offset_weight(offset) * 0.5 * (centre + window(coef_pad, offset)) * (
            middle - window(field_pad, offset)
        )
    return summed


def coarsen(field):
    ext_x, ext_y, ext_z = field.shape
    return field.reshape(ext_x // 2, 2, ext_y // 2, 2, ext_z // 2, 2).sum(axis=(1, 3, 5))


def refine(field):
    return jnp.repeat(jnp.repeat(jnp.repeat(field, 2, axis=0), 2, axis=1), 2, axis=2)


def lookup(phase_map, phase_coef):
    coefficient = jnp.zeros(phase_map.shape, jnp.float32)
    for phase_index in range(PHASES):
        coefficient = coefficient + jnp.where(
            phase_map == phase_index, phase_coef[phase_index], 0.0
        )
    return coefficient


def level_two_rim(stacked):
    return extended(stacked, (("gx", 1), ("gy", 2), ("gz", 3)), 1)


def block_rim(stacked):
    return extended(stacked, (("gx", 1), ("gy", 2), ("gz", 3)), 1)


def smooth(residual, coefficient, sweeps, rim_fn):
    coef_pad = rim_fn(coefficient[None])[0]
    diagonal = stencil_diag(coef_pad)
    correction = OMEGA * residual / diagonal
    for sweep_index in range(sweeps - 1):
        field_pad = rim_fn(correction[None])[0]
        correction = correction + OMEGA * (residual - apply_stencil(coef_pad, field_pad)) / diagonal
    return correction


def ladder(residual, coefficient):
    level_res = residual
    level_coef = coefficient
    levels_list = []
    for level_index in range(LEVELS - 2):
        levels_list.append((level_res, level_coef))
        if level_index + 1 < LEVELS - 2:
            level_res = 0.5 * coarsen(level_res)
            level_coef = 0.125 * coarsen(level_coef)
    return levels_list


def prolong_sum(corrections):
    summed = corrections[-1]
    for level_index in range(len(corrections) - 2, -1, -1):
        summed = corrections[level_index] + refine(summed)
    return summed


def on_device(right_side, iterate, phase_map, phase_coef):
    coefficient = lookup(phase_map, phase_coef)
    padded = extended(jnp.stack([coefficient, iterate]), (("gx", 1), ("gy", 2), ("gz", 3)), 1)
    coef_pad = padded[0]
    residual = right_side - apply_stencil(coef_pad, padded[1])
    diagonal = stencil_diag(coef_pad)
    fine_corr = OMEGA * residual / diagonal
    for sweep_index in range(SWEEPS1 - 1):
        field_pad = extended(fine_corr[None], (("gx", 1), ("gy", 2), ("gz", 3)), 1)[0]
        fine_corr = fine_corr + OMEGA * (residual - apply_stencil(coef_pad, field_pad)) / diagonal
    res_two = 0.5 * coarsen(residual)
    coef_two = 0.125 * coarsen(coefficient)
    res_three = 0.5 * coarsen(res_two)
    coef_three = 0.125 * coarsen(coef_two)
    coarse_list = ladder(res_three, coef_three)
    corr_two = smooth(res_two, coef_two, SWEEPS2, level_two_rim)
    coarse_corrs = [
        smooth(level_res, level_coef, SWEEPS3, block_rim) for level_res, level_coef in coarse_list
    ]
    coarse_total = prolong_sum(coarse_corrs)
    summed = corr_two + refine(coarse_total)
    summed = fine_corr + refine(summed)
    return iterate + summed


def solution(mesh):
    placed = (P("gx", "gy", "gz"), P("gx", "gy", "gz"), P("gx", "gy", "gz"), P())
    return jax.shard_map(
        on_device, mesh=mesh, in_specs=placed, out_specs=P("gx", "gy", "gz"), check_vma=False
    )
```

profile of v0, /device:TPU:206, one launch (start us, length us, event | category | flops | bytes accessed | tf_op | source)
XLA Modules:
  0.0 542.4 jit_solution(10404263144696644363)
XLA Ops:
  5.0 9.7 %reshape.122 = f32[8,2,8,2,64,2]{5,4,3,2,1,0:T(8,128)} reshape(f32[16,16,128]{2,1,0:T(8,128)S(1)} %select_add_fusion) | data formatting | bytes 262144 | tf_op jit(solution)/shard_map/reshape | solution.py:72
  14.7 4.1 reduce_sum.87
  22.5 5.5 %collective-permute-start.84 = (f32[1,1,1,8]{3,2,1,0:T(1,128)S(1)}, f32[1,1,1,8]{3,2,1,0:T(1,128)S(1)}, u32[]{:S(2)}, u32[]{:S(2)}) collective-permute-start(f32[1,1,1,8]{3,2,1,0:T(1,128)S(1)} %multiply_bitcast_fusion.1), channel_id=1, source_target_pairs={{0,64},{64,128},{128,192},{192,256},{256,320},{320,384},{384,448},... | collective-permute-start | bytes 104 | tf_op jit(solution)/shard_map/ppermute | solution.py:28
  32.6 5.1 collective-permute-start
  39.7 5.1 collective-permute-start.60
  54.5 5.5 %collective-permute-start.89 = (f32[1,3,3,1]{3,2,1,0:T(4,128)S(1)}, f32[1,3,3,1]{3,2,1,0:T(4,128)S(1)}, u32[]{:S(2)}, u32[]{:S(2)}) collective-permute-start(f32[1,3,3,1]{3,2,1,0:T(4,128)S(1)} %get-tuple-element.171), channel_id=1, source_target_pairs={{1,0},{2,1},{3,2},{4,3},{5,4},{6,5},{7,6},{8,7},{9,8},{10,9},{11,1... | collective-permute-start | bytes 116 | tf_op jit(solution)/shard_map/ppermute | solution.py:31
  61.3 5.3 collective-permute-start.88
  72.1 5.1 collective-permute-start.36
  79.3 4.8 collective-permute-start.65
  95.3 5.1 collective-permute-start.18
  117.4 5.0 collective-permute-start.23
  129.6 6.6 %collective-permute-start.5 = (f32[2,18,18,1]{3,0,2,1:T(2,128)S(1)}, f32[2,18,18,1]{3,0,2,1:T(2,128)S(1)}, u32[]{:S(2)}, u32[]{:S(2)}) collective-permute-start(f32[2,18,18,1]{3,0,2,1:T(2,128)S(1)} %get-tuple-element.93), channel_id=1, source_target_pairs={{1,0},{2,1},{3,2},{4,3},{5,4},{6,5},{7,6},{8,7},{9,8},{10,9},{11,1... | collective-permute-start | bytes 7784 | tf_op jit(solution)/shard_map/ppermute | solution.py:31
  138.7 10.5 %collective-permute-done.5 = f32[2,18,18,1]{3,0,2,1:T(2,128)S(1)} collective-permute-done((f32[2,18,18,1]{3,0,2,1:T(2,128)S(1)}, f32[2,18,18,1]{3,0,2,1:T(2,128)S(1)}, u32[]{:S(2)}, u32[]{:S(2)}) %collective-permute-start.5) | collective-permute-done | bytes 2624 | tf_op jit(solution)/shard_map/ppermute | solution.py:31
  149.2 7.2 %collective-permute-done.4 = f32[2,18,18,1]{3,0,2,1:T(2,128)S(1)} collective-permute-done((f32[2,18,18,1]{3,0,2,1:T(2,128)S(1)}, f32[2,18,18,1]{3,0,2,1:T(2,128)S(1)}, u32[]{:S(2)}, u32[]{:S(2)}) %collective-permute-start.4) | collective-permute-done | bytes 2624 | tf_op jit(solution)/shard_map/ppermute | solution.py:28
  160.5 9.7 %reshape.121 = f32[8,2,8,2,64,2]{5,4,3,2,1,0:T(8,128)} reshape(f32[16,16,128]{2,1,0:T(8,128)S(1)} %get-tuple-element.6) | data formatting | bytes 262144 | tf_op jit(solution)/shard_map/reshape | solution.py:72
  170.2 4.1 reduce_sum.86
  183.5 5.1 collective-permute-start.90
  192.3 5.1 collective-permute-start.66
  203.7 5.1 collective-permute-start.42
  219.6 4.8 collective-permute-start.94
  230.9 5.1 collective-permute-start.96
  246.8 4.5 collective-permute-done.101
  251.3 3.9 collective-permute-start.100
  255.3 4.6 collective-permute-done.100
  262.6 4.9 collective-permute-done.103
  279.9 4.8 collective-permute-start.70
  295.7 4.1 collective-permute-done.107
  303.7 4.6 collective-permute-done.106
  308.3 5.1 collective-permute-start.72
  324.4 4.5 collective-permute-start.76
  328.9 5.4 collective-permute-start.24
  340.0 5.1 collective-permute-start.78
  359.0 4.4 collective-permute-start.47
  365.8 6.5 %collective-permute-start.83 = (f32[1,4,4,1]{3,2,1,0:T(4,128)S(1)}, f32[1,4,4,1]{3,2,1,0:T(4,128)S(1)}, u32[]{:S(2)}, u32[]{:S(2)}) collective-permute-start(f32[1,4,4,1]{3,2,1,0:T(4,128)S(1)} %get-tuple-element.157), channel_id=1, source_target_pairs={{1,0},{2,1},{3,2},{4,3},{5,4},{6,5},{7,6},{8,7},{9,8},{10,9},{11,1... | collective-permute-start | bytes 200 | tf_op jit(solution)/shard_map/ppermute | solution.py:31
  380.8 5.4 collective-permute-start.48
  404.0 5.4 collective-permute-start.6
  413.4 5.4 collective-permute-start.54
  429.7 5.3 collective-permute-start.59
  437.2 6.9 %collective-permute-start.29 = (f32[1,10,10,1]{3,0,2,1:T(1,128)S(1)}, f32[1,10,10,1]{3,0,2,1:T(1,128)S(1)}, u32[]{:S(2)}, u32[]{:S(2)}) collective-permute-start(f32[1,10,10,1]{3,0,2,1:T(1,128)S(1)} %get-tuple-element.113), channel_id=1, source_target_pairs={{1,0},{2,1},{3,2},{4,3},{5,4},{6,5},{7,6},{8,7},{9,8},{10,9},{11,1... | collective-permute-start | bytes 1208 | tf_op jit(solution)/shard_map/ppermute | solution.py:31
  446.3 7.8 %collective-permute-done.28 = f32[1,10,10,1]{3,0,2,1:T(1,128)S(1)} collective-permute-done((f32[1,10,10,1]{3,0,2,1:T(1,128)S(1)}, f32[1,10,10,1]{3,0,2,1:T(1,128)S(1)}, u32[]{:S(2)}, u32[]{:S(2)}) %collective-permute-start.28) | collective-permute-done | bytes 432 | tf_op jit(solution)/shard_map/ppermute | solution.py:28
  457.3 5.4 collective-permute-start.30
  481.5 4.8 collective-permute-start.10
  486.4 4.2 collective-permute-done.11
  490.6 4.7 collective-permute-done.10
  500.2 5.1 collective-permute-start.12
  507.5 4.8 collective-permute-start.34
  520.5 4.0 collective-permute-start.17
  531.9 5.3 collective-permute-done.16
  (462 shorter events, 278.4 us)
Async XLA Ops:
  20.6 19.1 %collective-permute-start.85 = (f32[1,1,1,8]{3,2,1,0:T(1,128)S(1)}, f32[1,1,1,8]{3,2,1,0:T(1,128)S(1)}, u32[]{:S(2)}, u32[]{:S(2)}) collective-permute-start(f32[1,1,1,8]{3,2,1,0:T(1,128)S(1)} %multiply_bitcast_fusion.1), channel_id=1, source_target_pairs={{64,0},{128,64},{192,128},{256,192},{320,256},{384,320},{448,384},... | collective-permute-start | bytes 104 | tf_op jit(solution)/shard_map/ppermute | solution.py:31
  22.5 22.4 %collective-permute-start.84 = (f32[1,1,1,8]{3,2,1,0:T(1,128)S(1)}, f32[1,1,1,8]{3,2,1,0:T(1,128)S(1)}, u32[]{:S(2)}, u32[]{:S(2)}) collective-permute-start(f32[1,1,1,8]{3,2,1,0:T(1,128)S(1)} %multiply_bitcast_fusion.1), channel_id=1, source_target_pairs={{0,64},{64,128},{128,192},{192,256},{256,320},{320,384},{384,448},... | collective-permute-start | bytes 104 | tf_op jit(solution)/shard_map/ppermute | solution.py:28
  30.7 84.5 %collective-permute-start.1 = (f32[2,1,16,128]{3,2,1,0:T(8,128)S(1)}, f32[2,1,16,128]{3,2,1,0:T(8,128)S(1)}, u32[]{:S(2)}, u32[]{:S(2)}) collective-permute-start(f32[2,1,16,128]{3,2,1,0:T(8,128)S(1)} %get-tuple-element.97), channel_id=1, source_target_pairs={{64,0},{128,64},{192,128},{256,192},{320,256},{384,320},{448,384},... | collective-permute-start | bytes 49160 | tf_op jit(solution)/shard_map/ppermute | solution.py:31
  32.6 82.6 %collective-permute-start = (f32[2,1,16,128]{3,2,1,0:T(8,128)S(1)}, f32[2,1,16,128]{3,2,1,0:T(8,128)S(1)}, u32[]{:S(2)}, u32[]{:S(2)}) collective-permute-start(f32[2,1,16,128]{3,2,1,0:T(8,128)S(1)} %get-tuple-element.96), channel_id=1, source_target_pairs={{0,64},{64,128},{128,192},{192,256},{256,320},{320,384},{384,448},... | collective-permute-start | bytes 49160 | tf_op jit(solution)/shard_map/ppermute | solution.py:28
  44.9 34.4 %collective-permute-start.37 = (f32[1,1,4,32]{3,2,1,0:T(4,128)S(1)}, f32[1,1,4,32]{3,2,1,0:T(4,128)S(1)}, u32[]{:S(2)}, u32[]{:S(2)}) collective-permute-start(f32[1,1,4,32]{3,2,1,0:T(4,128)S(1)} %get-tuple-element.153), channel_id=1, source_target_pairs={{64,0},{128,64},{192,128},{256,192},{320,256},{384,320},{448,384},... | collective-permute-start | bytes 1544 | tf_op jit(solution)/shard_map/ppermute | solution.py:31
  51.2 20.9 %collective-permute-start.63 = (f32[1,4,1,16]{3,2,1,0:T(1,128)S(1)}, f32[1,4,1,16]{3,2,1,0:T(1,128)S(1)}, u32[]{:S(2)}, u32[]{:S(2)}) collective-permute-start(f32[1,4,1,16]{3,2,1,0:T(1,128)S(1)} %get-tuple-element.179), channel_id=1, source_target_pairs={{16,0},{32,16},{48,32},{17,1},{33,17},{49,33},{18,2},{34,18},{50,3... | collective-permute-start | bytes 776 | tf_op jit(solution)/shard_map/ppermute | solution.py:31
  72.1 12.0 %collective-permute-start.36 = (f32[1,1,4,32]{3,2,1,0:T(4,128)S(1)}, f32[1,1,4,32]{3,2,1,0:T(4,128)S(1)}, u32[]{:S(2)}, u32[]{:S(2)}) collective-permute-start(f32[1,1,4,32]{3,2,1,0:T(4,128)S(1)} %get-tuple-element.152), channel_id=1, source_target_pairs={{0,64},{64,128},{128,192},{192,256},{256,320},{320,384},{384,448},... | collective-permute-start | bytes 1544 | tf_op jit(solution)/shard_map/ppermute | solution.py:28
  77.3 26.2 %collective-permute-start.19 = (f32[1,1,8,64]{3,2,1,0:T(8,128)S(1)}, f32[1,1,8,64]{3,2,1,0:T(8,128)S(1)}, u32[]{:S(2)}, u32[]{:S(2)}) collective-permute-start(f32[1,1,8,64]{3,2,1,0:T(8,128)S(1)} %get-tuple-element.127), channel_id=1, source_target_pairs={{64,0},{128,64},{192,128},{256,192},{320,256},{384,320},{448,384},... | collective-permute-start | bytes 6152 | tf_op jit(solution)/shard_map/ppermute | solution.py:31
  95.3 12.0 %collective-permute-start.18 = (f32[1,1,8,64]{3,2,1,0:T(8,128)S(1)}, f32[1,1,8,64]{3,2,1,0:T(8,128)S(1)}, u32[]{:S(2)}, u32[]{:S(2)}) collective-permute-start(f32[1,1,8,64]{3,2,1,0:T(8,128)S(1)} %get-tuple-element.126), channel_id=1, source_target_pairs={{0,64},{64,128},{128,192},{192,256},{256,320},{320,384},{384,448},... | collective-permute-start | bytes 6152 | tf_op jit(solution)/shard_map/ppermute | solution.py:28
  100.5 9.6 %collective-permute-start.41 = (f32[1,6,6,1]{3,0,2,1:T(1,128)S(1)}, f32[1,6,6,1]{3,0,2,1:T(1,128)S(1)}, u32[]{:S(2)}, u32[]{:S(2)}) collective-permute-start(f32[1,6,6,1]{3,0,2,1:T(1,128)S(1)} %get-tuple-element.137), channel_id=1, source_target_pairs={{1,0},{2,1},{3,2},{4,3},{5,4},{6,5},{7,6},{8,7},{9,8},{10,9},{11,1... | collective-permute-start | bytes 440 | tf_op jit(solution)/shard_map/ppermute | solution.py:31
  115.3 12.5 %collective-permute-start.2 = (f32[2,18,1,128]{3,0,2,1:T(2,128)S(1)}, f32[2,18,1,128]{3,0,2,1:T(2,128)S(1)}, u32[]{:S(2)}, u32[]{:S(2)}) collective-permute-start(f32[2,18,1,128]{3,0,2,1:T(2,128)S(1)} %copy.227), channel_id=1, source_target_pairs={{0,16},{16,32},{32,48},{1,17},{17,33},{33,49},{2,18},{18,34},{34,5... | collective-permute-start | bytes 55304 | tf_op jit(solution)/shard_map/ppermute | solution.py:28
  117.4 21.0 %collective-permute-start.23 = (f32[1,10,10,1]{3,0,2,1:T(1,128)S(1)}, f32[1,10,10,1]{3,0,2,1:T(1,128)S(1)}, u32[]{:S(2)}, u32[]{:S(2)}) collective-permute-start(f32[1,10,10,1]{3,0,2,1:T(1,128)S(1)} %get-tuple-element.115), channel_id=1, source_target_pairs={{1,0},{2,1},{3,2},{4,3},{5,4},{6,5},{7,6},{8,7},{9,8},{10,9},{11,1... | collective-permute-start | bytes 1208 | tf_op jit(solution)/shard_map/ppermute | solution.py:31
  122.4 16.0 %collective-permute-start.22 = (f32[1,10,10,1]{3,0,2,1:T(1,128)S(1)}, f32[1,10,10,1]{3,0,2,1:T(1,128)S(1)}, u32[]{:S(2)}, u32[]{:S(2)}) collective-permute-start(f32[1,10,10,1]{3,0,2,1:T(1,128)S(1)} %get-tuple-element.114), channel_id=1, source_target_pairs={{0,1},{1,2},{2,3},{3,4},{4,5},{5,6},{6,7},{7,8},{8,9},{9,10},{10,1... | collective-permute-start | bytes 1208 | tf_op jit(solution)/shard_map/ppermute | solution.py:28
  129.6 19.6 %collective-permute-start.5 = (f32[2,18,18,1]{3,0,2,1:T(2,128)S(1)}, f32[2,18,18,1]{3,0,2,1:T(2,128)S(1)}, u32[]{:S(2)}, u32[]{:S(2)}) collective-permute-start(f32[2,18,18,1]{3,0,2,1:T(2,128)S(1)} %get-tuple-element.93), channel_id=1, source_target_pairs={{1,0},{2,1},{3,2},{4,3},{5,4},{6,5},{7,6},{8,7},{9,8},{10,9},{11,1... | collective-permute-start | bytes 7784 | tf_op jit(solution)/shard_map/ppermute | solution.py:31
  136.2 20.2 %collective-permute-start.4 = (f32[2,18,18,1]{3,0,2,1:T(2,128)S(1)}, f32[2,18,18,1]{3,0,2,1:T(2,128)S(1)}, u32[]{:S(2)}, u32[]{:S(2)}) collective-permute-start(f32[2,18,18,1]{3,0,2,1:T(2,128)S(1)} %get-tuple-element.92), channel_id=1, source_target_pairs={{0,1},{1,2},{2,3},{3,4},{4,5},{5,6},{6,7},{7,8},{8,9},{9,10},{10,1... | collective-permute-start | bytes 7784 | tf_op jit(solution)/shard_map/ppermute | solution.py:28
  181.6 22.1 %collective-permute-start.91 = (f32[1,1,1,8]{3,2,1,0:T(1,128)S(1)}, f32[1,1,1,8]{3,2,1,0:T(1,128)S(1)}, u32[]{:S(2)}, u32[]{:S(2)}) collective-permute-start(f32[1,1,1,8]{3,2,1,0:T(1,128)S(1)} %get-tuple-element.60), channel_id=1, source_target_pairs={{64,0},{128,64},{192,128},{256,192},{320,256},{384,320},{448,384},... | collective-permute-start | bytes 104 | tf_op jit(solution)/shard_map/ppermute | solution.py:31
  183.5 25.3 %collective-permute-start.90 = (f32[1,1,1,8]{3,2,1,0:T(1,128)S(1)}, f32[1,1,1,8]{3,2,1,0:T(1,128)S(1)}, u32[]{:S(2)}, u32[]{:S(2)}) collective-permute-start(f32[1,1,1,8]{3,2,1,0:T(1,128)S(1)} %get-tuple-element.60), channel_id=1, source_target_pairs={{0,64},{64,128},{128,192},{192,256},{256,320},{320,384},{384,448},... | collective-permute-start | bytes 104 | tf_op jit(solution)/shard_map/ppermute | solution.py:28
  190.4 20.4 %collective-permute-start.67 = (f32[1,1,2,16]{3,2,1,0:T(2,128)S(1)}, f32[1,1,2,16]{3,2,1,0:T(2,128)S(1)}, u32[]{:S(2)}, u32[]{:S(2)}) collective-permute-start(f32[1,1,2,16]{3,2,1,0:T(2,128)S(1)} %get-tuple-element.187), channel_id=1, source_target_pairs={{64,0},{128,64},{192,128},{256,192},{320,256},{384,320},{448,384},... | collective-permute-start | bytes 392 | tf_op jit(solution)/shard_map/ppermute | solution.py:31
  192.3 20.4 %collective-permute-start.66 = (f32[1,1,2,16]{3,2,1,0:T(2,128)S(1)}, f32[1,1,2,16]{3,2,1,0:T(2,128)S(1)}, u32[]{:S(2)}, u32[]{:S(2)}) collective-permute-start(f32[1,1,2,16]{3,2,1,0:T(2,128)S(1)} %get-tuple-element.186), channel_id=1, source_target_pairs={{0,64},{64,128},{128,192},{192,256},{256,320},{320,384},{384,448},... | collective-permute-start | bytes 392 | tf_op jit(solution)/shard_map/ppermute | solution.py:28
  199.6 138.4 %collective-permute-start.43 = (f32[1,1,4,32]{3,2,1,0:T(4,128)}, f32[1,1,4,32]{3,2,1,0:T(4,128)}, u32[]{:S(2)}, u32[]{:S(2)}) collective-permute-start(f32[1,1,4,32]{3,2,1,0:T(4,128)} %get-tuple-element.151), channel_id=1, source_target_pairs={{64,0},{128,64},{192,128},{256,192},{320,256},{384,320},{448,384},... | collective-permute-start | bytes 1544 | tf_op jit(solution)/shard_map/ppermute | solution.py:31
  203.7 136.2 %collective-permute-start.42 = (f32[1,1,4,32]{3,2,1,0:T(4,128)}, f32[1,1,4,32]{3,2,1,0:T(4,128)}, u32[]{:S(2)}, u32[]{:S(2)}) collective-permute-start(f32[1,1,4,32]{3,2,1,0:T(4,128)} %get-tuple-element.150), channel_id=1, source_target_pairs={{0,64},{64,128},{128,192},{192,256},{256,320},{320,384},{384,448},... | collective-permute-start | bytes 1544 | tf_op jit(solution)/shard_map/ppermute | solution.py:28
  208.8 204.5 %collective-permute-start.25 = (f32[1,1,8,64]{3,2,1,0:T(8,128)}, f32[1,1,8,64]{3,2,1,0:T(8,128)}, u32[]{:S(2)}, u32[]{:S(2)}) collective-permute-start(f32[1,1,8,64]{3,2,1,0:T(8,128)} %get-tuple-element.125), channel_id=1, source_target_pairs={{64,0},{128,64},{192,128},{256,192},{320,256},{384,320},{448,384},... | collective-permute-start | bytes 6152 | tf_op jit(solution)/shard_map/ppermute | solution.py:31
  241.7 33.2 %collective-permute-start.69 = (f32[1,4,1,16]{3,2,1,0:T(1,128)S(1)}, f32[1,4,1,16]{3,2,1,0:T(1,128)S(1)}, u32[]{:S(2)}, u32[]{:S(2)}) collective-permute-start(f32[1,4,1,16]{3,2,1,0:T(1,128)S(1)} %get-tuple-element.177), channel_id=1, source_target_pairs={{16,0},{32,16},{48,32},{17,1},{33,17},{49,33},{18,2},{34,18},{50,3... | collective-permute-start | bytes 776 | tf_op jit(solution)/shard_map/ppermute | solution.py:31
  290.6 23.0 %collective-permute-start.73 = (f32[1,1,2,16]{3,2,1,0:T(2,128)S(1)}, f32[1,1,2,16]{3,2,1,0:T(2,128)S(1)}, u32[]{:S(2)}, u32[]{:S(2)}) collective-permute-start(f32[1,1,2,16]{3,2,1,0:T(2,128)S(1)} %get-tuple-element.185), channel_id=1, source_target_pairs={{64,0},{128,64},{192,128},{256,192},{320,256},{384,320},{448,384},... | collective-permute-start | bytes 392 | tf_op jit(solution)/shard_map/ppermute | solution.py:31
  324.4 9.9 %collective-permute-start.76 = (f32[1,4,4,1]{3,2,1,0:T(4,128)S(1)}, f32[1,4,4,1]{3,2,1,0:T(4,128)S(1)}, u32[]{:S(2)}, u32[]{:S(2)}) collective-permute-start(f32[1,4,4,1]{3,2,1,0:T(4,128)S(1)} %get-tuple-element.158), channel_id=1, source_target_pairs={{0,1},{1,2},{2,3},{3,4},{4,5},{5,6},{6,7},{7,8},{8,9},{9,10},{10,1... | collective-permute-start | bytes 200 | tf_op jit(solution)/shard_map/ppermute | solution.py:28
  328.9 89.9 %collective-permute-start.24 = (f32[1,1,8,64]{3,2,1,0:T(8,128)}, f32[1,1,8,64]{3,2,1,0:T(8,128)}, u32[]{:S(2)}, u32[]{:S(2)}) collective-permute-start(f32[1,1,8,64]{3,2,1,0:T(8,128)} %get-tuple-element.124), channel_id=1, source_target_pairs={{0,64},{64,128},{128,192},{192,256},{256,320},{320,384},{384,448},... | collective-permute-start | bytes 6152 | tf_op jit(solution)/shard_map/ppermute | solution.py:28
  334.3 134.2 %collective-permute-start.7 = (f32[1,1,16,128]{3,2,1,0:T(8,128)}, f32[1,1,16,128]{3,2,1,0:T(8,128)}, u32[]{:S(2)}, u32[]{:S(2)}) collective-permute-start(f32[1,1,16,128]{3,2,1,0:T(8,128)} %get-tuple-element.109), channel_id=1, source_target_pairs={{64,0},{128,64},{192,128},{256,192},{320,256},{384,320},{448,384},... | collective-permute-start | bytes 24584 | tf_op jit(solution)/shard_map/ppermute | solution.py:31
  365.8 9.7 %collective-permute-start.83 = (f32[1,4,4,1]{3,2,1,0:T(4,128)S(1)}, f32[1,4,4,1]{3,2,1,0:T(4,128)S(1)}, u32[]{:S(2)}, u32[]{:S(2)}) collective-permute-start(f32[1,4,4,1]{3,2,1,0:T(4,128)S(1)} %get-tuple-element.157), channel_id=1, source_target_pairs={{1,0},{2,1},{3,2},{4,3},{5,4},{6,5},{7,6},{8,7},{9,8},{10,9},{11,1... | collective-permute-start | bytes 200 | tf_op jit(solution)/shard_map/ppermute | solution.py:31
  375.5 10.8 %collective-permute-start.49 = (f32[1,1,4,32]{3,2,1,0:T(4,128)S(1)}, f32[1,1,4,32]{3,2,1,0:T(4,128)S(1)}, u32[]{:S(2)}, u32[]{:S(2)}) collective-permute-start(f32[1,1,4,32]{3,2,1,0:T(4,128)S(1)} %get-tuple-element.149), channel_id=1, source_target_pairs={{64,0},{128,64},{192,128},{256,192},{320,256},{384,320},{448,384},... | collective-permute-start | bytes 1544 | tf_op jit(solution)/shard_map/ppermute | solution.py:31
  404.0 64.5 %collective-permute-start.6 = (f32[1,1,16,128]{3,2,1,0:T(8,128)}, f32[1,1,16,128]{3,2,1,0:T(8,128)}, u32[]{:S(2)}, u32[]{:S(2)}) collective-permute-start(f32[1,1,16,128]{3,2,1,0:T(8,128)} %get-tuple-element.108), channel_id=1, source_target_pairs={{0,64},{64,128},{128,192},{192,256},{256,320},{320,384},{384,448},... | collective-permute-start | bytes 24584 | tf_op jit(solution)/shard_map/ppermute | solution.py:28
  424.4 10.6 %collective-permute-start.27 = (f32[1,10,1,64]{3,2,1,0:T(1,128)S(1)}, f32[1,10,1,64]{3,2,1,0:T(1,128)S(1)}, u32[]{:S(2)}, u32[]{:S(2)}) collective-permute-start(f32[1,10,1,64]{3,2,1,0:T(1,128)S(1)} %get-tuple-element.119), channel_id=1, source_target_pairs={{16,0},{32,16},{48,32},{17,1},{33,17},{49,33},{18,2},{34,18},{50,3... | collective-permute-start | bytes 7688 | tf_op jit(solution)/shard_map/ppermute | solution.py:31
  427.6 9.3 %collective-permute-start.26 = (f32[1,10,1,64]{3,2,1,0:T(1,128)S(1)}, f32[1,10,1,64]{3,2,1,0:T(1,128)S(1)}, u32[]{:S(2)}, u32[]{:S(2)}) collective-permute-start(f32[1,10,1,64]{3,2,1,0:T(1,128)S(1)} %get-tuple-element.118), channel_id=1, source_target_pairs={{0,16},{16,32},{32,48},{1,17},{17,33},{33,49},{2,18},{18,34},{34,5... | collective-permute-start | bytes 7688 | tf_op jit(solution)/shard_map/ppermute | solution.py:28
  429.7 14.5 %collective-permute-start.59 = (f32[1,6,6,1]{3,0,2,1:T(1,128)S(1)}, f32[1,6,6,1]{3,0,2,1:T(1,128)S(1)}, u32[]{:S(2)}, u32[]{:S(2)}) collective-permute-start(f32[1,6,6,1]{3,0,2,1:T(1,128)S(1)} %get-tuple-element.131), channel_id=1, source_target_pairs={{1,0},{2,1},{3,2},{4,3},{5,4},{6,5},{7,6},{8,7},{9,8},{10,9},{11,1... | collective-permute-start | bytes 440 | tf_op jit(solution)/shard_map/ppermute | solution.py:31
  435.0 11.1 %collective-permute-start.58 = (f32[1,6,6,1]{3,0,2,1:T(1,128)S(1)}, f32[1,6,6,1]{3,0,2,1:T(1,128)S(1)}, u32[]{:S(2)}, u32[]{:S(2)}) collective-permute-start(f32[1,6,6,1]{3,0,2,1:T(1,128)S(1)} %get-tuple-element.130), channel_id=1, source_target_pairs={{0,1},{1,2},{2,3},{3,4},{4,5},{5,6},{6,7},{7,8},{8,9},{9,10},{10,1... | collective-permute-start | bytes 440 | tf_op jit(solution)/shard_map/ppermute | solution.py:28
  444.2 9.9 %collective-permute-start.28 = (f32[1,10,10,1]{3,0,2,1:T(1,128)S(1)}, f32[1,10,10,1]{3,0,2,1:T(1,128)S(1)}, u32[]{:S(2)}, u32[]{:S(2)}) collective-permute-start(f32[1,10,10,1]{3,0,2,1:T(1,128)S(1)} %get-tuple-element.112), channel_id=1, source_target_pairs={{0,1},{1,2},{2,3},{3,4},{4,5},{5,6},{6,7},{7,8},{8,9},{9,10},{10,1... | collective-permute-start | bytes 1208 | tf_op jit(solution)/shard_map/ppermute | solution.py:28
  455.4 12.4 %collective-permute-start.31 = (f32[1,1,8,64]{3,2,1,0:T(8,128)}, f32[1,1,8,64]{3,2,1,0:T(8,128)S(1)}, u32[]{:S(2)}, u32[]{:S(2)}) collective-permute-start(f32[1,1,8,64]{3,2,1,0:T(8,128)} %get-tuple-element.123), channel_id=1, source_target_pairs={{64,0},{128,64},{192,128},{256,192},{320,256},{384,320},{448,384},... | collective-permute-start | bytes 6152 | tf_op jit(solution)/shard_map/ppermute | solution.py:31
  457.3 10.4 %collective-permute-start.30 = (f32[1,1,8,64]{3,2,1,0:T(8,128)}, f32[1,1,8,64]{3,2,1,0:T(8,128)S(1)}, u32[]{:S(2)}, u32[]{:S(2)}) collective-permute-start(f32[1,1,8,64]{3,2,1,0:T(8,128)} %get-tuple-element.122), channel_id=1, source_target_pairs={{0,64},{64,128},{128,192},{192,256},{256,320},{320,384},{384,448},... | collective-permute-start | bytes 6152 | tf_op jit(solution)/shard_map/ppermute | solution.py:28
  469.5 9.5 %collective-permute-start.9 = (f32[1,18,1,128]{3,2,1,0:T(1,128)S(1)}, f32[1,18,1,128]{3,2,1,0:T(1,128)S(1)}, u32[]{:S(2)}, u32[]{:S(2)}) collective-permute-start(f32[1,18,1,128]{3,2,1,0:T(1,128)S(1)} %get-tuple-element.105), channel_id=1, source_target_pairs={{16,0},{32,16},{48,32},{17,1},{33,17},{49,33},{18,2},{34,18},{50,3... | collective-permute-start | bytes 27656 | tf_op jit(solution)/shard_map/ppermute | solution.py:31
  473.9 12.4 %collective-permute-start.33 = (f32[1,10,1,64]{3,2,1,0:T(1,128)S(1)}, f32[1,10,1,64]{3,2,1,0:T(1,128)S(1)}, u32[]{:S(2)}, u32[]{:S(2)}) collective-permute-start(f32[1,10,1,64]{3,2,1,0:T(1,128)S(1)} %get-tuple-element.117), channel_id=1, source_target_pairs={{16,0},{32,16},{48,32},{17,1},{33,17},{49,33},{18,2},{34,18},{50,3... | collective-permute-start | bytes 7688 | tf_op jit(solution)/shard_map/ppermute | solution.py:31
  477.0 9.3 %collective-permute-start.32 = (f32[1,10,1,64]{3,2,1,0:T(1,128)S(1)}, f32[1,10,1,64]{3,2,1,0:T(1,128)S(1)}, u32[]{:S(2)}, u32[]{:S(2)}) collective-permute-start(f32[1,10,1,64]{3,2,1,0:T(1,128)S(1)} %get-tuple-element.116), channel_id=1, source_target_pairs={{0,16},{16,32},{32,48},{1,17},{17,33},{33,49},{2,18},{18,34},{34,5... | collective-permute-start | bytes 7688 | tf_op jit(solution)/shard_map/ppermute | solution.py:28
  479.6 11.0 %collective-permute-start.11 = (f32[1,18,18,1]{3,0,2,1:T(1,128)S(1)}, f32[1,18,18,1]{3,0,2,1:T(1,128)S(1)}, u32[]{:S(2)}, u32[]{:S(2)}) collective-permute-start(f32[1,18,18,1]{3,0,2,1:T(1,128)S(1)} %get-tuple-element.101), channel_id=1, source_target_pairs={{1,0},{2,1},{3,2},{4,3},{5,4},{6,5},{7,6},{8,7},{9,8},{10,9},{11,1... | collective-permute-start | bytes 3896 | tf_op jit(solution)/shard_map/ppermute | solution.py:31
  481.5 13.8 %collective-permute-start.10 = (f32[1,18,18,1]{3,0,2,1:T(1,128)S(1)}, f32[1,18,18,1]{3,0,2,1:T(1,128)S(1)}, u32[]{:S(2)}, u32[]{:S(2)}) collective-permute-start(f32[1,18,18,1]{3,0,2,1:T(1,128)S(1)} %get-tuple-element.100), channel_id=1, source_target_pairs={{0,1},{1,2},{2,3},{3,4},{4,5},{5,6},{6,7},{7,8},{8,9},{9,10},{10,1... | collective-permute-start | bytes 3896 | tf_op jit(solution)/shard_map/ppermute | solution.py:28
  498.3 14.0 %collective-permute-start.13 = (f32[1,1,16,128]{3,2,1,0:T(8,128)S(1)}, f32[1,1,16,128]{3,2,1,0:T(8,128)S(1)}, u32[]{:S(2)}, u32[]{:S(2)}) collective-permute-start(f32[1,1,16,128]{3,2,1,0:T(8,128)S(1)} %get-tuple-element.107), channel_id=1, source_target_pairs={{64,0},{128,64},{192,128},{256,192},{320,256},{384,320},{448,384},... | collective-permute-start | bytes 24584 | tf_op jit(solution)/shard_map/ppermute | solution.py:31
  500.2 12.1 %collective-permute-start.12 = (f32[1,1,16,128]{3,2,1,0:T(8,128)S(1)}, f32[1,1,16,128]{3,2,1,0:T(8,128)S(1)}, u32[]{:S(2)}, u32[]{:S(2)}) collective-permute-start(f32[1,1,16,128]{3,2,1,0:T(8,128)S(1)} %get-tuple-element.106), channel_id=1, source_target_pairs={{0,64},{64,128},{128,192},{192,256},{256,320},{320,384},{384,448},... | collective-permute-start | bytes 24584 | tf_op jit(solution)/shard_map/ppermute | solution.py:28
  505.5 11.2 %collective-permute-start.35 = (f32[1,10,10,1]{3,0,2,1:T(1,128)S(1)}, f32[1,10,10,1]{3,0,2,1:T(1,128)S(1)}, u32[]{:S(2)}, u32[]{:S(2)}) collective-permute-start(f32[1,10,10,1]{3,0,2,1:T(1,128)S(1)} %get-tuple-element.111), channel_id=1, source_target_pairs={{1,0},{2,1},{3,2},{4,3},{5,4},{6,5},{7,6},{8,7},{9,8},{10,9},{11,1... | collective-permute-start | bytes 1208 | tf_op jit(solution)/shard_map/ppermute | solution.py:31
  507.5 9.2 %collective-permute-start.34 = (f32[1,10,10,1]{3,0,2,1:T(1,128)S(1)}, f32[1,10,10,1]{3,0,2,1:T(1,128)S(1)}, u32[]{:S(2)}, u32[]{:S(2)}) collective-permute-start(f32[1,10,10,1]{3,0,2,1:T(1,128)S(1)} %get-tuple-element.110), channel_id=1, source_target_pairs={{0,1},{1,2},{2,3},{3,4},{4,5},{5,6},{6,7},{7,8},{8,9},{9,10},{10,1... | collective-permute-start | bytes 1208 | tf_op jit(solution)/shard_map/ppermute | solution.py:28
  520.5 11.4 %collective-permute-start.17 = (f32[1,18,18,1]{3,0,2,1:T(1,128)}, f32[1,18,18,1]{3,0,2,1:T(1,128)}, u32[]{:S(2)}, u32[]{:S(2)}) collective-permute-start(f32[1,18,18,1]{3,0,2,1:T(1,128)} %get-tuple-element.99), channel_id=1, source_target_pairs={{1,0},{2,1},{3,2},{4,3},{5,4},{6,5},{7,6},{8,7},{9,8},{10,9},{11,1... | collective-permute-start | bytes 3896 | tf_op jit(solution)/shard_map/ppermute | solution.py:31
  524.6 12.7 %collective-permute-start.16 = (f32[1,18,18,1]{3,0,2,1:T(1,128)}, f32[1,18,18,1]{3,0,2,1:T(1,128)}, u32[]{:S(2)}, u32[]{:S(2)}) collective-permute-start(f32[1,18,18,1]{3,0,2,1:T(1,128)} %get-tuple-element.98), channel_id=1, source_target_pairs={{0,1},{1,2},{2,3},{3,4},{4,5},{5,6},{6,7},{7,8},{8,9},{9,10},{10,1... | collective-permute-start | bytes 3896 | tf_op jit(solution)/shard_map/ppermute | solution.py:28
  (118 other events, 9733.9 us)
where the time goes:
time: 547 us; the launch traced here: 542 us
  starting transfers between devices  341 us (62%)
  waiting for transfers between devices  106 us (19%)
  other arithmetic  50.7 us (9%)
  local copies, waits for them, and re-layouts  42 us (8%)
    ppermute x54, starting transfers between devices, extended(): lax.ppermute(lax.slice_in_dim(block, block.shape[dim] - width, None, axis...  193 us
    ppermute x54, starting transfers between devices, extended(): lax.ppermute(lax.slice_in_dim(block, 0, width, axis=dim), axis, backward)  148 us
    ppermute x54, waiting for transfers between devices, extended(): lax.ppermute(lax.slice_in_dim(block, block.shape[dim] - width, None, axis...  71.6 us
    ppermute x54, waiting for transfers between devices, extended(): lax.ppermute(lax.slice_in_dim(block, 0, width, axis=dim), axis, backward)  34.2 us
    reshape x2, local copies, waits for them, and re-layouts, coarsen(): field.reshape(ext_x // 2, 2, ext_y // 2, 2, ext_z // 2, 2)  19.5 us
    reduce_sum x10, other arithmetic, coarsen(): field.reshape(ext_x // 2, 2, ext_y // 2, 2, ext_z // 2, 2)  11 us
    concatenate x45, other arithmetic, extended(): block = jnp.concatenate([low, block, high], axis=dim)  11 us
  transfers between devices with their start and end apart: 108, of which 34 were waited for; matrix products, arithmetic and copies ran while one was open for 7% of the time, Pallas kernels for 0%

commit v1 on v0

v1 whole, which is shorter than its diff:
```python
import jax
import jax.numpy as jnp
from jax import lax
from jax.experimental import pallas as pl
from jax.experimental.pallas import tpu as pltpu
from jax.sharding import PartitionSpec as P

HALO = (6, 5, 4)
ROWS = (0, 6, 11, 15)
OMEGA = 2.0 / 3.0
F32 = jnp.float32
BF16 = jnp.bfloat16


def iota(shape, dim):
    return lax.broadcasted_iota(jnp.int32, shape, dim)


def ones_where(cond, scale=1.0):
    return jnp.where(cond, F32(scale), F32(0.0)).astype(BF16)


def split3(x):
    high = x.astype(BF16)
    rest = x - high.astype(F32)
    middle = rest.astype(BF16)
    low = (rest - middle.astype(F32)).astype(BF16)
    return high, middle, low


def select_rows(pattern, x):
    parts = [jnp.dot(pattern, part, preferred_element_type=F32) for part in split3(x)]
    return parts[0] + (parts[1] + parts[2])


def select_lanes(x, pattern):
    parts = [jnp.dot(part, pattern, preferred_element_type=F32) for part in split3(x)]
    return parts[0] + (parts[1] + parts[2])


def band(x, axis):
    x = x + pltpu.roll(x, 1, axis)
    return x + pltpu.roll(x, x.shape[axis] - 1, axis)


def band_yz(x):
    return band(band(x, x.ndim - 1), x.ndim - 2)


def band_x(x):
    up = jnp.concatenate([x[1:], x[:1]], axis=0)
    down = jnp.concatenate([x[-1:], x[:-1]], axis=0)
    return (up + down) + 2.0 * x


def damped_inverse(coef, diagonal):
    inside = coef > 0.0
    return jnp.where(inside, OMEGA / jnp.where(inside, diagonal, 1.0), 0.0)


def relax(corr, inverse, residual, coef, tu_corr, tu_product):
    return corr * (1.0 / 3.0) + inverse * (residual - 2.0 * (coef * corr) + 0.125 * (coef * tu_corr + tu_product))


def smooth_small(residual, coef, sweeps):
    inverse = damped_inverse(coef, 6.0 * coef + 0.125 * band_x(band_yz(coef)))
    corr = inverse * residual
    for _ in range(sweeps - 1):
        corr = relax(corr, inverse, residual, coef, band_x(band_yz(corr)), band_x(band_yz(coef * corr)))
    return corr


def pack_y(table, phase, iterate, right, coef, to_up, to_down):
    p = phase[...]
    k = jnp.zeros(p.shape, F32)
    for index in range(4):
        k = jnp.where(p == index, table[index], k)
    coef[...] = k
    for field, ref in enumerate((coef, iterate, right)):
        h, a, b = HALO[field], ROWS[field], ROWS[field + 1]
        to_up[:, a:b, :] = ref[:, 16 - h : 16, :]
        to_down[:, a:b, :] = ref[:, 0:h, :]
    to_up[:, 15:16, :] = jnp.zeros((16, 1, 128), F32)
    to_down[:, 15:16, :] = jnp.zeros((16, 1, 128), F32)


def pack_x(coef, iterate, right, from_down, from_up, ext, to_up, to_down):
    for field, ref in enumerate((coef, iterate, right)):
        h, a, b = HALO[field], ROWS[field], ROWS[field + 1]
        ext[field, :, 0:16, :] = ref[...]
        ext[field, :, 16 : 16 + h, :] = from_up[:, a:b, :]
        ext[field, :, 16 + h : 32 - h, :] = jnp.zeros((16, 16 - 2 * h, 128), F32)
        ext[field, :, 32 - h : 32, :] = from_down[:, a:b, :]
        to_up[a:b] = ext[field, 16 - h : 16]
        to_down[a:b] = ext[field, 0:h]


def pack_z(ext, from_down, from_up, full, to_up, to_down):
    up = jnp.zeros((16, 896), F32)
    down = jnp.zeros((16, 896), F32)
    row = iota((16, 128), 0)
    lane = iota((16, 128), 1)
    contract = (((1,), (1,)), ((), ()))
    for field in range(3):
        h, a, b = HALO[field], ROWS[field], ROWS[field + 1]
        if h < 6:
            full[field, 0 : 6 - h] = jnp.zeros((6 - h, 32, 128), F32)
            full[field, 22 + h : 28] = jnp.zeros((6 - h, 32, 128), F32)
        full[field, 6 - h : 6] = from_down[a:b]
        full[field, 6:22] = ext[field]
        full[field, 22 : 22 + h] = from_up[a:b]
        mine = (row >= a) & (row < b)
        pick_up = ones_where(mine & (lane == row - a + 128 - h))
        pick_down = ones_where(mine & (lane == row - a))
        for part in split3(full[field].reshape(896, 128)):
            up = up + lax.dot_general(pick_up, part, contract, preferred_element_type=F32)
            down = down + lax.dot_general(pick_down, part, contract, preferred_element_type=F32)
    to_up[...] = up
    to_down[...] = down


def fine_residual(full, from_down, from_up, coef, res, inv, own, to_up, to_down, field, yz_k, yz_v, yz_kv):
    halo = jnp.concatenate([from_up[...], from_down[...]], axis=0).T
    row = iota((32, 128), 0)
    lane = iota((32, 128), 1)
    for index in range(3):
        h, a, b = HALO[index], ROWS[index], ROWS[index + 1]
        upper = (row >= a) & (row < b) & (lane == row - a)
        lower = (row >= 16 + a) & (row < 16 + b) & (lane == row - 16 - a + 128 - h)
        tile = select_lanes(halo, ones_where(upper | lower)).reshape(28, 32, 128)
        target = coef if index == 0 else field.at[index - 1]
        target[:, :, 0:128] = full[index]
        target[:, :, 128:256] = tile

    def bands(x, carry):
        k = coef[x]
        v = field[0, x]
        yz_k[x] = band_yz(k)
        yz_v[x] = band_yz(v)
        yz_kv[x] = band_yz(k * v)
        return carry

    lax.fori_loop(0, 28, bands, 0, unroll=2)
    for x in (0, 1, 26, 27):
        res[x] = jnp.zeros((32, 256), F32)
        inv[x] = jnp.zeros((32, 256), F32)

    def over_x(ref, x):
        return (ref[x - 1] + ref[x + 1]) + 2.0 * ref[x]

    def cells(x, carry):
        k = coef[x]
        v = field[0, x]
        diagonal = 6.0 * k + 0.125 * over_x(yz_k, x)
        applied = v * diagonal + 2.0 * (k * v) - 0.125 * (k * over_x(yz_v, x) + over_x(yz_kv, x))
        res[x] = field[1, x] - applied
        inv[x] = damped_inverse(k, diagonal)
        return carry

    lax.fori_loop(2, 26, cells, 0, unroll=2)

    row = iota((16, 512), 0)
    cell = iota((16, 512), 1)
    block = ones_where((row == (cell >> 7) * 4 + ((cell & 31) >> 2)) & ((cell & 31) < 16))
    both = jnp.concatenate([res[6:22, :, 0:128].reshape(512, 128), coef[6:22, :, 0:128].reshape(512, 128)], axis=1)
    sums = select_rows(block, both)
    source = iota((256, 128), 0)
    lane = iota((256, 128), 1)
    coarse = (source & 127) >> 2
    base = (source >> 7) * 64
    scale = jnp.where(source < 128, F32(0.25), F32(1.0 / 64.0))
    for ref, place in (
        (own, lane == base + 16 + coarse),
        (to_up, (lane == base + coarse - 16) & (coarse >= 16)),
        (to_down, (lane == base + 48 + coarse) & (coarse < 16)),
    ):
        ref[...] = select_lanes(sums, jnp.where(place, scale, 0.0).astype(BF16))


def fine_smooth(coef, res, inv, iterate, base, corr, corr_next, yz_c, yz_kc, pairs, narrow, spread):
    def over_x(ref, x):
        return (ref[x - 1] + ref[x + 1]) + 2.0 * ref[x]

    def first(x, carry):
        c = inv[x] * res[x]
        corr[x] = c
        yz_c[x] = band_yz(c)
        yz_kc[x] = band_yz(coef[x] * c)
        return carry

    lax.fori_loop(4, 24, first, 0, unroll=2)

    def second(x, carry):
        corr_next[x] = relax(corr[x], inv[x], res[x], coef[x], over_x(yz_c, x), over_x(yz_kc, x))
        return carry

    lax.fori_loop(5, 23, second, 0, unroll=2)

    def second_bands(x, carry):
        c = corr_next[x]
        yz_c[x] = band_yz(c)
        yz_kc[x] = band_yz(coef[x] * c)
        return carry

    lax.fori_loop(5, 23, second_bands, 0, unroll=2)

    lane = iota((256, 128), 0)
    halves = ones_where((lane >> 1) == iota((256, 128), 1))

    def coarse(ref, scale):
        def pair(x, carry):
            pairs[pl.ds(pl.multiple_of(32 * x, 32), 32), :] = ref[2 * x] + ref[2 * x + 1]
            return carry

        lax.fori_loop(0, 14, pair, 0, unroll=2)
        narrow[...] = select_lanes(pairs[...], halves)
        summed = narrow[pl.ds(0, 224, stride=2), :] + narrow[pl.ds(1, 224, stride=2), :]
        return (scale * summed).reshape(14, 16, 128)

    corr_two = smooth_small(coarse(res, 0.5), coarse(coef, 0.125), 3)
    doubled = ones_where(iota((128, 128), 0) == (iota((128, 128), 1) >> 1))
    wide = select_lanes(corr_two[3:11].reshape(128, 128), doubled).reshape(8, 16, 128)
    rows = wide[:, 0:8, :].reshape(64, 128)
    spread[pl.ds(0, 64, stride=2), :] = rows
    spread[pl.ds(1, 64, stride=2), :] = rows

    def third(x, carry):
        c = relax(
            corr_next[x, 0:16, 0:128],
            inv[x, 0:16, 0:128],
            res[x, 0:16, 0:128],
            coef[x, 0:16, 0:128],
            (yz_c[x - 1, 0:16, 0:128] + yz_c[x + 1, 0:16, 0:128]) + 2.0 * yz_c[x, 0:16, 0:128],
            (yz_kc[x - 1, 0:16, 0:128] + yz_kc[x + 1, 0:16, 0:128]) + 2.0 * yz_kc[x, 0:16, 0:128],
        )
        block = x - 6
        base[block] = iterate[block] + (c + spread[pl.ds(pl.multiple_of(16 * (block // 2), 16), 16), :])
        return carry

    lax.fori_loop(6, 22, third, 0, unroll=2)


def coarse_levels(place, plane, base, out):
    row = iota((192, 512), 0)
    cell = iota((192, 512), 1)
    cell_x = (cell >> 6) * 4 + ((cell >> 2) & 3)
    cell_y = ((cell >> 4) & 3) * 4 + (cell & 3)
    parts = split3(plane[...])
    windows = []
    for level in range(3):
        at_x = place[0] * (4 >> level) - 4 + (row >> 4)
        at_y = place[1] * (4 >> level) - 4 + (row & 15)
        pattern = ones_where(((cell_x >> level) == at_x) & ((cell_y >> level) == at_y))
        found = [jnp.dot(pattern, part, preferred_element_type=F32) for part in parts]
        windows.append(found[0] + (found[1] + found[2]))
    source = iota((128, 128), 0)
    lane = iota((128, 128), 1)
    residual = jnp.zeros((192, 128), F32)
    coef = jnp.zeros((192, 128), F32)
    for level, start in enumerate((0, 64, 96)):
        parts = split3(windows[level])
        target = start + ((source & 63) >> level)
        to_res = ones_where((source < 64) & (lane == target), 0.5**level)
        to_coef = ones_where((source >= 64) & (lane == target), 0.125**level)
        for part in parts:
            residual = residual + jnp.dot(part, to_res, preferred_element_type=F32)
            coef = coef + jnp.dot(part, to_coef, preferred_element_type=F32)
    corr = smooth_small(residual.reshape(12, 16, 128), coef.reshape(12, 16, 128), 4)
    mine = corr[4:8].reshape(64, 128)
    total = base[...].reshape(256, 128)
    row = iota((256, 64), 0)
    found = iota((256, 64), 1)
    for level, start in enumerate((16, 72, 100)):
        shift = 2 + level
        spread = ones_where(source == start + (lane >> shift))
        at = ((row >> 4) >> shift) * 16 + 4 + ((row & 15) >> shift)
        total = total + select_rows(ones_where(found == at), select_lanes(mine, spread))
    out[...] = total.reshape(16, 16, 128)


VMEM = pl.BlockSpec(memory_space=pltpu.VMEM)
SMEM = pl.BlockSpec(memory_space=pltpu.SMEM)


def call(kernel, outs, ins, scratch=(), scalars=0, flops=1000000):
    specs = [SMEM] * scalars + [VMEM] * (len(ins) - scalars)
    moved = 4 * sum(x.size for x in ins)
    return pl.pallas_call(
        kernel,
        out_shape=[jax.ShapeDtypeStruct(shape, F32) for shape in outs],
        in_specs=specs,
        out_specs=[VMEM] * len(outs),
        scratch_shapes=[pltpu.VMEM(shape, F32) for shape in scratch],
        compiler_params=pltpu.CompilerParams(vmem_limit_bytes=32 * 1024 * 1024),
        cost_estimate=pl.CostEstimate(flops=flops, bytes_accessed=moved, transcendentals=0),
        name=kernel.__name__,
    )(*ins)


def swap(axis, to_up, to_down):
    count = lax.axis_size(axis)
    up = [(i, i + 1) for i in range(count - 1)]
    down = [(i + 1, i) for i in range(count - 1)]
    return lax.ppermute(to_up, axis, up), lax.ppermute(to_down, axis, down)


def on_device(right, iterate, phase, table):
    block = (16, 16, 128)
    coef, to_up, to_down = call(pack_y, [block] * 3, [table, phase, iterate, right], scalars=1)
    from_down, from_up = swap("gy", to_up, to_down)
    ext, to_up, to_down = call(
        pack_x,
        [(3, 16, 32, 128), (15, 32, 128), (15, 32, 128)],
        [coef, iterate, right, from_down, from_up],
    )
    from_down, from_up = swap("gx", to_up, to_down)
    full, to_up, to_down = call(pack_z, [(3, 28, 32, 128), (16, 896), (16, 896)], [ext, from_down, from_up])
    from_down, from_up = swap("gz", to_up, to_down)
    wide = (28, 32, 256)
    coef, res, inv, own, to_up, to_down = call(
        fine_residual,
        [wide, wide, wide, (16, 128), (16, 128), (16, 128)],
        [full, from_down, from_up],
        scratch=[(2, *wide), wide, wide, wide],
        flops=30000000,
    )
    from_down, from_up = swap("gz", to_up, to_down)
    (base,) = call(
        fine_smooth,
        [block],
        [coef, res, inv, iterate],
        scratch=[wide, wide, wide, wide, (448, 256), (448, 128), (128, 128)],
        flops=30000000,
    )
    mine = own + from_down + from_up
    planes = lax.axis_size("gx") * lax.axis_size("gy")
    plane = lax.all_to_all(jnp.broadcast_to(mine[None], (planes, 16, 128)), ("gx", "gy"), 0, 0, tiled=True)
    place = jnp.stack([lax.axis_index("gx"), lax.axis_index("gy")]).astype(jnp.int32)
    (out,) = call(coarse_levels, [block], [place, plane.reshape(planes * 16, 128), base], scalars=1, flops=30000000)
    return out


def solution(mesh):
    placed = (P("gx", "gy", "gz"), P("gx", "gy", "gz"), P("gx", "gy", "gz"), P())
    return jax.shard_map(on_device, mesh=mesh, in_specs=placed, out_specs=P("gx", "gy", "gz"), check_vma=False)
```

time: 547 us -> 85.2 us (0.16)
  the two profiles are of different devices: /device:TPU:206 before, /device:TPU:56 now
where the time goes in v1:
time: 85.2 us; the launch traced here: 84.2 us
  starting transfers between devices  35.7 us (42%)
  waiting for transfers between devices  25.5 us (30%)
  Pallas kernels  16.9 us (20%)
  local copies, waits for them, and re-layouts  5.9 us (7%)
    ppermute x8, starting transfers between devices, swap(): return (lax.ppermute(to_up, axis, up), lax.ppermute(to_down, axis, down))  24.8 us
    ppermute x8, waiting for transfers between devices, swap(): return (lax.ppermute(to_up, axis, up), lax.ppermute(to_down, axis, down))  19.8 us
    pallas_call x6, Pallas kernels, call(): pl.pallas_call(kernel, out_shape=[jax.ShapeDtypeStruct(shape, F32) for sh...  16.9 us
    all_to_all x1, starting transfers between devices, on_device(): lax.all_to_all(jnp.broadcast_to(mine[None], (planes, 16, 128)), ('gx', 'g...  10.9 us
    all_to_all x1, waiting for transfers between devices, on_device(): lax.all_to_all(jnp.broadcast_to(mine[None], (planes, 16, 128)), ('gx', 'g...  5.72 us
    unnamed x14, local copies, waits for them, and re-layouts  5.18 us
  transfers between devices with their start and end apart: 9, of which 8 were waited for; matrix products, arithmetic and copies ran while one was open for 0% of the time, Pallas kernels for 7%

profile of v1, /device:TPU:56, one launch (start us, length us, event | category | flops | bytes accessed | tf_op | source)
XLA Modules:
  0.0 84.2 jit_solution(2422541415789480924)
XLA Ops:
  0.0 0.0 copy-start
  0.0 0.9 %copy-done = f32[16,16,128]{2,1,0:T(8,128)S(1)} copy-done((f32[16,16,128]{2,1,0:T(8,128)S(1)}, f32[16,16,128]{2,1,0:T(8,128)}, u32[]{:S(2)}) %copy-start) | copy-done | bytes 131096
  0.9 0.0 copy-start.3
  0.9 0.9 %copy-done.3 = f32[16,16,128]{2,1,0:T(8,128)S(1)} copy-done((f32[16,16,128]{2,1,0:T(8,128)S(1)}, f32[16,16,128]{2,1,0:T(8,128)}, u32[]{:S(2)}) %copy-start.3) | copy-done | bytes 131096
  1.8 0.0 copy-start.5
  1.8 0.9 %copy-done.5 = s32[16,16,128]{2,1,0:T(8,128)S(1)} copy-done((s32[16,16,128]{2,1,0:T(8,128)S(1)}, s32[16,16,128]{2,1,0:T(8,128)}, u32[]{:S(2)}) %copy-start.5) | copy-done | bytes 131096
  2.7 0.0 copy-start.6
  2.7 0.7 copy-done.6
  3.4 0.6 pack_y.1
  4.0 1.9 %collective-permute-start = (f32[16,16,128]{2,1,0:T(8,128)S(1)}, f32[16,16,128]{2,1,0:T(8,128)S(1)}, u32[]{:S(2)}, u32[]{:S(2)}) collective-permute-start(f32[16,16,128]{2,1,0:T(8,128)S(1)} %get-tuple-element.21), channel_id=1, source_target_pairs={{0,16},{16,32},{32,48},{1,17},{17,33},{33,49},{2,18},{18,34},{34,5... | collective-permute-start | bytes 393224 | tf_op jit(solution)/shard_map/ppermute | solution.py:304
  5.9 3.6 %collective-permute-start.1 = (f32[16,16,128]{2,1,0:T(8,128)S(1)}, f32[16,16,128]{2,1,0:T(8,128)S(1)}, u32[]{:S(2)}, u32[]{:S(2)}) collective-permute-start(f32[16,16,128]{2,1,0:T(8,128)S(1)} %get-tuple-element.22), channel_id=1, source_target_pairs={{16,0},{32,16},{48,32},{17,1},{33,17},{49,33},{18,2},{34,18},{50,3... | collective-permute-start | bytes 393224 | tf_op jit(solution)/shard_map/ppermute | solution.py:304
  9.6 0.7 collective-permute-done.from_down
  10.3 1.8 %collective-permute-done.1.from_up = f32[16,16,128]{2,1,0:T(8,128)S(1)} collective-permute-done((f32[16,16,128]{2,1,0:T(8,128)S(1)}, f32[16,16,128]{2,1,0:T(8,128)S(1)}, u32[]{:S(2)}, u32[]{:S(2)}) %collective-permute-start.1) | collective-permute-done | bytes 131104 | tf_op jit(solution)/shard_map/ppermute | solution.py:304
  12.1 0.0 copy-start.1
  12.1 0.9 %copy-done.1 = f32[16,16,128]{2,1,0:T(8,128)S(1)} copy-done((f32[16,16,128]{2,1,0:T(8,128)S(1)}, f32[16,16,128]{2,1,0:T(8,128)}, u32[]{:S(2)}) %copy-start.1) | copy-done | bytes 131096
  13.0 0.0 copy-start.4
  13.0 0.9 %copy-done.4 = f32[16,16,128]{2,1,0:T(8,128)S(1)} copy-done((f32[16,16,128]{2,1,0:T(8,128)S(1)}, f32[16,16,128]{2,1,0:T(8,128)}, u32[]{:S(2)}) %copy-start.4) | copy-done | bytes 131096
  13.9 0.1 pack_x.1
  14.0 4.3 %collective-permute-start.2 = (f32[15,32,128]{2,1,0:T(8,128)S(1)}, f32[15,32,128]{2,1,0:T(8,128)S(1)}, u32[]{:S(2)}, u32[]{:S(2)}) collective-permute-start(f32[15,32,128]{2,1,0:T(8,128)S(1)} %get-tuple-element.24), channel_id=1, source_target_pairs={{0,64},{64,128},{128,192},{192,256},{256,320},{320,384},{384,448},... | collective-permute-start | bytes 737288 | tf_op jit(solution)/shard_map/ppermute | solution.py:304
  18.3 1.3 %collective-permute-start.3 = (f32[15,32,128]{2,1,0:T(8,128)S(1)}, f32[15,32,128]{2,1,0:T(8,128)S(1)}, u32[]{:S(2)}, u32[]{:S(2)}) collective-permute-start(f32[15,32,128]{2,1,0:T(8,128)S(1)} %get-tuple-element.25), channel_id=1, source_target_pairs={{64,0},{128,64},{192,128},{256,192},{320,256},{384,320},{448,384},... | collective-permute-start | bytes 737288 | tf_op jit(solution)/shard_map/ppermute | solution.py:304
  19.6 2.4 %collective-permute-done.2.from_down = f32[15,32,128]{2,1,0:T(8,128)S(1)} collective-permute-done((f32[15,32,128]{2,1,0:T(8,128)S(1)}, f32[15,32,128]{2,1,0:T(8,128)S(1)}, u32[]{:S(2)}, u32[]{:S(2)}) %collective-permute-start.2) | collective-permute-done | bytes 245792 | tf_op jit(solution)/shard_map/ppermute | solution.py:304
  22.0 4.8 %collective-permute-done.3.from_up = f32[15,32,128]{2,1,0:T(8,128)S(1)} collective-permute-done((f32[15,32,128]{2,1,0:T(8,128)S(1)}, f32[15,32,128]{2,1,0:T(8,128)S(1)}, u32[]{:S(2)}, u32[]{:S(2)}) %collective-permute-start.3) | collective-permute-done | bytes 245792 | tf_op jit(solution)/shard_map/ppermute | solution.py:304
  26.8 1.4 %pack_z.1 = (f32[3,28,32,128]{3,2,1,0:T(8,128)S(1)}, f32[16,896]{1,0:T(8,128)S(1)}, f32[16,896]{1,0:T(8,128)S(1)}) custom-call(f32[3,16,32,128]{3,2,1,0:T(8,128)S(1)} %get-tuple-element.23.ext, f32[15,32,128]{2,1,0:T(8,128)S(1)} %collective-permute-done.2.from_down, f32[15,32,128]{2,1,0:T(8,128)S(1)} %collective-permute-done.3.from_up), custom_call_target="tpu_custom_call" | custom-call | flops 1000000 | bytes 1277952 | tf_op jit(solution)/shard_map/pack_z/pallas_call | solution.py:288
  28.1 0.0 copy-start.2
  28.1 3.8 %collective-permute-start.4 = (f32[16,896]{1,0:T(8,128)S(1)}, f32[16,896]{1,0:T(8,128)S(1)}, u32[]{:S(2)}, u32[]{:S(2)}) collective-permute-start(f32[16,896]{1,0:T(8,128)S(1)} %get-tuple-element.27), channel_id=1, source_target_pairs={{0,1},{1,2},{2,3},{3,4},{4,5},{5,6},{6,7},{7,8},{8,9},{9,10},{10,1... | collective-permute-start | bytes 172040 | tf_op jit(solution)/shard_map/ppermute | solution.py:304
  31.9 3.1 %collective-permute-start.5 = (f32[16,896]{1,0:T(8,128)S(1)}, f32[16,896]{1,0:T(8,128)S(1)}, u32[]{:S(2)}, u32[]{:S(2)}) collective-permute-start(f32[16,896]{1,0:T(8,128)S(1)} %get-tuple-element.28), channel_id=1, source_target_pairs={{1,0},{2,1},{3,2},{4,3},{5,4},{6,5},{7,6},{8,7},{9,8},{10,9},{11,1... | collective-permute-start | bytes 172040 | tf_op jit(solution)/shard_map/ppermute | solution.py:304
  35.0 0.5 collective-permute-done.4.from_down
  35.5 5.5 %collective-permute-done.5.from_up = f32[16,896]{1,0:T(8,128)S(1)} collective-permute-done((f32[16,896]{1,0:T(8,128)S(1)}, f32[16,896]{1,0:T(8,128)S(1)}, u32[]{:S(2)}, u32[]{:S(2)}) %collective-permute-start.5) | collective-permute-done | bytes 57376 | tf_op jit(solution)/shard_map/ppermute | solution.py:304
  41.0 5.1 %fine_residual.1 = (f32[28,32,256]{2,1,0:T(8,128)S(1)}, f32[28,32,256]{2,1,0:T(8,128)S(1)}, f32[28,32,256]{2,1,0:T(8,128)S(1)}, f32[16,128]{1,0:T(8,128)S(1)}, f...) custom-call(f32[3,28,32,128]{3,2,1,0:T(8,128)S(1)} %get-tuple-element.26.full, ...), custom_call_target="tpu_custom_call" | custom-call | flops 30000000 | bytes 1490944 | tf_op jit(solution)/shard_map/fine_residual/pallas_call | solution.py:288
  46.1 2.4 %collective-permute-start.6 = (f32[16,128]{1,0:T(8,128)S(1)}, f32[16,128]{1,0:T(8,128)S(1)}, u32[]{:S(2)}, u32[]{:S(2)}) collective-permute-start(f32[16,128]{1,0:T(8,128)S(1)} %get-tuple-element.30), channel_id=1, source_target_pairs={{0,1},{1,2},{2,3},{3,4},{4,5},{5,6},{6,7},{7,8},{8,9},{9,10},{10,1... | collective-permute-start | bytes 24584 | tf_op jit(solution)/shard_map/ppermute | solution.py:304
  48.5 4.4 %collective-permute-start.7 = (f32[16,128]{1,0:T(8,128)S(1)}, f32[16,128]{1,0:T(8,128)S(1)}, u32[]{:S(2)}, u32[]{:S(2)}) collective-permute-start(f32[16,128]{1,0:T(8,128)S(1)} %get-tuple-element.31), channel_id=1, source_target_pairs={{1,0},{2,1},{3,2},{4,3},{5,4},{6,5},{7,6},{8,7},{9,8},{10,9},{11,1... | collective-permute-start | bytes 24584 | tf_op jit(solution)/shard_map/ppermute | solution.py:304
  52.9 0.0 collective-permute-done.6
  52.9 4.2 %collective-permute-done.7 = f32[16,128]{1,0:T(8,128)S(1)} collective-permute-done((f32[16,128]{1,0:T(8,128)S(1)}, f32[16,128]{1,0:T(8,128)S(1)}, u32[]{:S(2)}, u32[]{:S(2)}) %collective-permute-start.7) | collective-permute-done | bytes 8224 | tf_op jit(solution)/shard_map/ppermute | solution.py:304
  57.1 0.7 broadcast_in_dim.2
  57.8 10.9 %all-to-all-start = ((f32[32,16,128]{2,1,0:T(8,128)}), f32[32,16,128]{2,1,0:T(8,128)S(1)}, u32[]{:S(2)}, u32[]{:S(2)}) async-start(f32[32,16,128]{2,1,0:T(8,128)} %broadcast_in_dim.2), calls=%async_computation | async-start | bytes 524288 | tf_op jit(solution)/shard_map/all_to_all | solution.py:337
  68.8 0.1 pad_add_fusion.place
  68.8 0.0 copy-done.2
  68.8 6.1 %fine_smooth.1.base = f32[16,16,128]{2,1,0:T(8,128)S(1)} custom-call(f32[28,32,256]{2,1,0:T(8,128)S(1)} %get-tuple-element.32.coef, f32[28,32,256]{2,1,0:T(8,128)S(1)} %get-tuple-element.33.res, f32[28,32,256]{2,1,0:T(8,128)S(1)} %get-tuple-element.34.inv, f32[16,16,128]{2,1,0:T(8,128)S(1)} %copy-done.2), custom_call_target="tpu_custom_call" | custom-call | flops 30000000 | bytes 2883584 | tf_op jit(solution)/shard_map/fine_smooth/pallas_call | solution.py:288
  75.0 5.7 %all-to-all-done = f32[32,16,128]{2,1,0:T(8,128)S(1)} async-done(((f32[32,16,128]{2,1,0:T(8,128)}), f32[32,16,128]{2,1,0:T(8,128)S(1)}, u32[]{:S(2)}, u32[]{:S(2)}) %all-to-all-start) | async-done | bytes 262176 | tf_op jit(solution)/shard_map/all_to_all | solution.py:337
  80.7 3.5 %coarse_levels.1 = f32[16,16,128]{2,1,0:T(8,128)} custom-call(s32[2]{0:T(128)S(1)} %pad_add_fusion.place, f32[512,128]{1,0:T(8,128)S(1)} %bitcast.3, f32[16,16,128]{2,1,0:T(8,128)S(1)} %fine_smooth.1.base), custom_call_target="tpu_custom_call" | custom-call | flops 30000000 | bytes 393224 | tf_op jit(solution)/shard_map/coarse_levels/pallas_call | solution.py:288
  (1 shorter events, 0.0 us)
Async XLA Ops:
  0.0 0.9 %copy-start = (f32[16,16,128]{2,1,0:T(8,128)S(1)}, f32[16,16,128]{2,1,0:T(8,128)}, u32[]{:S(2)}) copy-start(f32[16,16,128]{2,1,0:T(8,128)} %iterate.5) | copy-start | bytes 393220
  0.9 0.9 %copy-start.3 = (f32[16,16,128]{2,1,0:T(8,128)S(1)}, f32[16,16,128]{2,1,0:T(8,128)}, u32[]{:S(2)}) copy-start(f32[16,16,128]{2,1,0:T(8,128)} %right.3) | copy-start | bytes 393220
  1.8 0.9 %copy-start.5 = (s32[16,16,128]{2,1,0:T(8,128)S(1)}, s32[16,16,128]{2,1,0:T(8,128)}, u32[]{:S(2)}) copy-start(s32[16,16,128]{2,1,0:T(8,128)} %phase.1) | copy-start | bytes 393220
  2.7 0.7 copy-start.6
  4.0 6.3 %collective-permute-start = (f32[16,16,128]{2,1,0:T(8,128)S(1)}, f32[16,16,128]{2,1,0:T(8,128)S(1)}, u32[]{:S(2)}, u32[]{:S(2)}) collective-permute-start(f32[16,16,128]{2,1,0:T(8,128)S(1)} %get-tuple-element.21), channel_id=1, source_target_pairs={{0,16},{16,32},{32,48},{1,17},{17,33},{33,49},{2,18},{18,34},{34,5... | collective-permute-start | bytes 393224 | tf_op jit(solution)/shard_map/ppermute | solution.py:304
  5.9 6.1 %collective-permute-start.1 = (f32[16,16,128]{2,1,0:T(8,128)S(1)}, f32[16,16,128]{2,1,0:T(8,128)S(1)}, u32[]{:S(2)}, u32[]{:S(2)}) collective-permute-start(f32[16,16,128]{2,1,0:T(8,128)S(1)} %get-tuple-element.22), channel_id=1, source_target_pairs={{16,0},{32,16},{48,32},{17,1},{33,17},{49,33},{18,2},{34,18},{50,3... | collective-permute-start | bytes 393224 | tf_op jit(solution)/shard_map/ppermute | solution.py:304
  12.1 0.9 %copy-start.1 = (f32[16,16,128]{2,1,0:T(8,128)S(1)}, f32[16,16,128]{2,1,0:T(8,128)}, u32[]{:S(2)}) copy-start(f32[16,16,128]{2,1,0:T(8,128)} %iterate.5) | copy-start | bytes 393220
  13.0 0.9 %copy-start.4 = (f32[16,16,128]{2,1,0:T(8,128)S(1)}, f32[16,16,128]{2,1,0:T(8,128)}, u32[]{:S(2)}) copy-start(f32[16,16,128]{2,1,0:T(8,128)} %right.3) | copy-start | bytes 393220
  14.0 8.0 %collective-permute-start.2 = (f32[15,32,128]{2,1,0:T(8,128)S(1)}, f32[15,32,128]{2,1,0:T(8,128)S(1)}, u32[]{:S(2)}, u32[]{:S(2)}) collective-permute-start(f32[15,32,128]{2,1,0:T(8,128)S(1)} %get-tuple-element.24), channel_id=1, source_target_pairs={{0,64},{64,128},{128,192},{192,256},{256,320},{320,384},{384,448},... | collective-permute-start | bytes 737288 | tf_op jit(solution)/shard_map/ppermute | solution.py:304
  18.3 8.4 %collective-permute-start.3 = (f32[15,32,128]{2,1,0:T(8,128)S(1)}, f32[15,32,128]{2,1,0:T(8,128)S(1)}, u32[]{:S(2)}, u32[]{:S(2)}) collective-permute-start(f32[15,32,128]{2,1,0:T(8,128)S(1)} %get-tuple-element.25), channel_id=1, source_target_pairs={{64,0},{128,64},{192,128},{256,192},{320,256},{384,320},{448,384},... | collective-permute-start | bytes 737288 | tf_op jit(solution)/shard_map/ppermute | solution.py:304
  28.1 40.7 %copy-start.2 = (f32[16,16,128]{2,1,0:T(8,128)S(1)}, f32[16,16,128]{2,1,0:T(8,128)}, u32[]{:S(2)}) copy-start(f32[16,16,128]{2,1,0:T(8,128)} %iterate.5) | copy-start | bytes 393220
  28.1 7.4 %collective-permute-start.4 = (f32[16,896]{1,0:T(8,128)S(1)}, f32[16,896]{1,0:T(8,128)S(1)}, u32[]{:S(2)}, u32[]{:S(2)}) collective-permute-start(f32[16,896]{1,0:T(8,128)S(1)} %get-tuple-element.27), channel_id=1, source_target_pairs={{0,1},{1,2},{2,3},{3,4},{4,5},{5,6},{6,7},{7,8},{8,9},{9,10},{10,1... | collective-permute-start | bytes 172040 | tf_op jit(solution)/shard_map/ppermute | solution.py:304
  31.9 9.1 %collective-permute-start.5 = (f32[16,896]{1,0:T(8,128)S(1)}, f32[16,896]{1,0:T(8,128)S(1)}, u32[]{:S(2)}, u32[]{:S(2)}) collective-permute-start(f32[16,896]{1,0:T(8,128)S(1)} %get-tuple-element.28), channel_id=1, source_target_pairs={{1,0},{2,1},{3,2},{4,3},{5,4},{6,5},{7,6},{8,7},{9,8},{10,9},{11,1... | collective-permute-start | bytes 172040 | tf_op jit(solution)/shard_map/ppermute | solution.py:304
  46.1 6.8 %collective-permute-start.6 = (f32[16,128]{1,0:T(8,128)S(1)}, f32[16,128]{1,0:T(8,128)S(1)}, u32[]{:S(2)}, u32[]{:S(2)}) collective-permute-start(f32[16,128]{1,0:T(8,128)S(1)} %get-tuple-element.30), channel_id=1, source_target_pairs={{0,1},{1,2},{2,3},{3,4},{4,5},{5,6},{6,7},{7,8},{8,9},{9,10},{10,1... | collective-permute-start | bytes 24584 | tf_op jit(solution)/shard_map/ppermute | solution.py:304
  48.5 8.6 %collective-permute-start.7 = (f32[16,128]{1,0:T(8,128)S(1)}, f32[16,128]{1,0:T(8,128)S(1)}, u32[]{:S(2)}, u32[]{:S(2)}) collective-permute-start(f32[16,128]{1,0:T(8,128)S(1)} %get-tuple-element.31), channel_id=1, source_target_pairs={{1,0},{2,1},{3,2},{4,3},{5,4},{6,5},{7,6},{8,7},{9,8},{10,9},{11,1... | collective-permute-start | bytes 24584 | tf_op jit(solution)/shard_map/ppermute | solution.py:304
  57.8 22.9 %all-to-all-start = ((f32[32,16,128]{2,1,0:T(8,128)}), f32[32,16,128]{2,1,0:T(8,128)S(1)}, u32[]{:S(2)}, u32[]{:S(2)}) async-start(f32[32,16,128]{2,1,0:T(8,128)} %broadcast_in_dim.2), calls=%async_computation | async-start | bytes 524288 | tf_op jit(solution)/shard_map/all_to_all | solution.py:337

commit v2 on v1

v2 whole, which is shorter than its diff:
```python
import jax
import jax.numpy as jnp
from jax import lax
from jax.experimental import pallas as pl
from jax.experimental.pallas import tpu as pltpu
from jax.sharding import PartitionSpec as P

HALO = (6, 5, 4)
ROWS = (0, 6, 11, 15)
OMEGA = 2.0 / 3.0
F32 = jnp.float32
BF16 = jnp.bfloat16


def iota(shape, dim):
    return lax.broadcasted_iota(jnp.int32, shape, dim)


def ones_where(cond, scale=1.0):
    return jnp.where(cond, F32(scale), F32(0.0)).astype(BF16)


def split3(x):
    high = x.astype(BF16)
    rest = x - high.astype(F32)
    middle = rest.astype(BF16)
    low = (rest - middle.astype(F32)).astype(BF16)
    return high, middle, low


def select_rows(pattern, x):
    parts = [jnp.dot(pattern, part, preferred_element_type=F32) for part in split3(x)]
    return parts[0] + (parts[1] + parts[2])


def select_lanes(x, pattern):
    parts = [jnp.dot(part, pattern, preferred_element_type=F32) for part in split3(x)]
    return parts[0] + (parts[1] + parts[2])


def band(x, axis):
    x = x + pltpu.roll(x, 1, axis)
    return x + pltpu.roll(x, x.shape[axis] - 1, axis)


def band_yz(x):
    return band(band(x, x.ndim - 1), x.ndim - 2)


def band_x(x):
    up = jnp.concatenate([x[1:], x[:1]], axis=0)
    down = jnp.concatenate([x[-1:], x[:-1]], axis=0)
    return (up + down) + 2.0 * x


def damped_inverse(coef, diagonal):
    inside = coef > 0.0
    return jnp.where(inside, OMEGA / jnp.where(inside, diagonal, 1.0), 0.0)


def relax(corr, inverse, residual, coef, tu_corr, tu_product):
    return corr * (1.0 / 3.0) + inverse * (residual - 2.0 * (coef * corr) + 0.125 * (coef * tu_corr + tu_product))


def smooth_small(residual, coef, sweeps):
    inverse = damped_inverse(coef, 6.0 * coef + 0.125 * band_x(band_yz(coef)))
    corr = inverse * residual
    for _ in range(sweeps - 1):
        corr = relax(corr, inverse, residual, coef, band_x(band_yz(corr)), band_x(band_yz(coef * corr)))
    return corr


def lookup(phase, values):
    k = jnp.zeros(phase.shape, F32)
    for index in range(4):
        k = jnp.where(phase == index, values[index], k)
    return k


def send_x(table, phase, iterate, right, to_up, to_down, values, upper, lower, sems):
    copies = [
        pltpu.make_async_copy(table, values, sems.at[0]),
        pltpu.make_async_copy(phase.at[10:16], upper, sems.at[1]),
        pltpu.make_async_copy(phase.at[0:6], lower, sems.at[2]),
        pltpu.make_async_copy(iterate.at[11:16], to_up.at[6:11], sems.at[3]),
        pltpu.make_async_copy(iterate.at[0:5], to_down.at[6:11], sems.at[4]),
        pltpu.make_async_copy(right.at[12:16], to_up.at[11:15], sems.at[5]),
        pltpu.make_async_copy(right.at[0:4], to_down.at[11:15], sems.at[6]),
    ]
    for copy in copies:
        copy.start()
    for copy in copies:
        copy.wait()
    to_up[0:6] = lookup(upper[...], values)
    to_down[0:6] = lookup(lower[...], values)


def keep_fields(table, phase, iterate, right, fields, values, phases, sems):
    copies = [
        pltpu.make_async_copy(table, values, sems.at[0]),
        pltpu.make_async_copy(phase, phases, sems.at[1]),
        pltpu.make_async_copy(iterate, fields.at[1], sems.at[2]),
        pltpu.make_async_copy(right, fields.at[2], sems.at[3]),
    ]
    for copy in copies:
        copy.start()
    for copy in copies:
        copy.wait()
    fields[0] = lookup(phases[...], values)


def pack_y(fields, from_down, from_up, ext, to_up, to_down):
    for field in range(3):
        h, a, b = HALO[field], ROWS[field], ROWS[field + 1]
        if h < 6:
            ext[field, 0 : 6 - h] = jnp.zeros((6 - h, 16, 128), F32)
            ext[field, 22 + h : 28] = jnp.zeros((6 - h, 16, 128), F32)
        ext[field, 6 - h : 6] = from_down[a:b]
        ext[field, 6:22] = fields[field]
        ext[field, 22 : 22 + h] = from_up[a:b]
        to_up[:, a:b, :] = ext[field, :, 16 - h : 16, :]
        to_down[:, a:b, :] = ext[field, :, 0:h, :]
    to_up[:, 15:16, :] = jnp.zeros((28, 1, 128), F32)
    to_down[:, 15:16, :] = jnp.zeros((28, 1, 128), F32)


def pack_z(ext, from_down, from_up, full, to_up, to_down):
    for field in range(3):
        h, a, b = HALO[field], ROWS[field], ROWS[field + 1]
        full[field, :, 0:16, :] = ext[field]
        full[field, :, 16 : 16 + h, :] = from_up[:, a:b, :]
        full[field, :, 16 + h : 32 - h, :] = jnp.zeros((28, 16 - 2 * h, 128), F32)
        full[field, :, 32 - h : 32, :] = from_down[:, a:b, :]
    lane = iota((32, 128), 1)
    for group in range(4):
        up = jnp.zeros((32, 128), F32)
        down = jnp.zeros((32, 128), F32)
        for x in range(8 * group, min(8 * group + 8, 28)):
            first = 16 * (x - 8 * group)
            for field in range(3):
                h, a, b = HALO[field], ROWS[field], ROWS[field + 1]
                cells = full[field, x]
                mine = (lane >= first + a) & (lane < first + b)
                up = jnp.where(mine, pltpu.roll(cells, (first + a + h) % 128, 1), up)
                down = jnp.where(mine, rolled(cells, first + a), down)
        to_up[:, 128 * group : 128 * group + 128] = up
        to_down[:, 128 * group : 128 * group + 128] = down


def rolled(x, shift):
    shift = shift % x.shape[1]
    return pltpu.roll(x, shift, 1) if shift else x


def bands_xy(full, xy, bands):
    def in_y(x, carry):
        k = full[0, x]
        v = full[1, x]
        bands[0, x] = band(k, 0)
        bands[1, x] = band(v, 0)
        bands[2, x] = band(k * v, 0)
        return carry

    lax.fori_loop(0, 28, in_y, 0, unroll=2)

    def in_x(x, carry):
        for field in range(3):
            xy[field, x] = (bands[field, x - 1] + bands[field, x + 1]) + 2.0 * bands[field, x]
        return carry

    lax.fori_loop(1, 27, in_x, 0, unroll=2)
    for field in range(3):
        for x in (0, 27):
            xy[field, x] = jnp.zeros((32, 128), F32)


def own_residual(full, xy, from_down, from_up, own, to_up, to_down, quads):
    def edge(cells, shift):
        k = cells
        v = pltpu.roll(cells, 512 - shift, 1)
        found = []
        for f in (k, v, k * v):
            f = band(f, 0)
            f = f + pltpu.roll(f, 16, 1)
            found.append(f + pltpu.roll(f, 512 - 16, 1))
        return found

    below = edge(from_down[...], 5)
    above = edge(from_up[...], 6)
    lane = iota((16, 128), 1)
    sums = [None, None]
    for x in range(6, 22):
        group, first = 128 * (x // 8), 16 * (x % 8)
        tu = []
        for field in range(3):
            cells = xy[field, x, 0:16, :]
            left = rolled(below[field][0:16, group : group + 128], -first - 5)
            after = rolled(above[field][0:16, group : group + 128], 127 - first)
            left = jnp.where(lane == 0, left, pltpu.roll(cells, 1, 1))
            after = jnp.where(lane == 127, after, pltpu.roll(cells, 127, 1))
            tu.append((left + after) + 2.0 * cells)
        k = full[0, x, 0:16, :]
        v = full[1, x, 0:16, :]
        diagonal = 6.0 * k + 0.125 * tu[0]
        res = full[2, x, 0:16, :] - (v * diagonal + 2.0 * (k * v) - 0.125 * (k * tu[1] + tu[2]))
        for at, f in enumerate((res, k)):
            sums[at] = f if (x - 6) % 4 == 0 else sums[at] + f
        if (x - 6) % 4 == 3:
            for at in range(2):
                f = sums[at] + pltpu.roll(sums[at], 15, 0)
                f = f + pltpu.roll(f, 14, 0)
                start = 64 * at + 16 * ((x - 6) // 4)
                quads[start : start + 16, :] = f
    sums = jnp.concatenate([quads[pl.ds(0, 16, stride=4), :], quads[pl.ds(64, 16, stride=4), :]], axis=1)
    source = iota((256, 128), 0)
    lane = iota((256, 128), 1)
    coarse = (source & 127) >> 2
    base = (source >> 7) * 64
    scale = jnp.where(source < 128, F32(0.25), F32(1.0 / 64.0))
    for ref, place in (
        (own, lane == base + 16 + coarse),
        (to_up, (lane == base + coarse - 16) & (coarse >= 16)),
        (to_down, (lane == base + 48 + coarse) & (coarse < 16)),
    ):
        ref[...] = select_lanes(sums, jnp.where(place, scale, 0.0).astype(BF16))


def fine_level(
    full, xy, from_down, from_up, base, res_two, coef_two, coef, side, res, inv, corr, corr_next, yz_c, yz_kc, pairs, narrow
):
    lane = iota((32, 128), 1)
    for x in range(28):
        group, first = 128 * (x // 8), 16 * (x % 8)
        up = from_up[:, group : group + 128]
        down = from_down[:, group : group + 128]
        tiles = []
        for field in range(3):
            h, a = HALO[field], ROWS[field]
            tile = jnp.where(lane >= 128 - h, rolled(down, 128 - h - first - a), 0.0)
            tiles.append(jnp.where(lane < h, rolled(up, -first - a), tile))
        coef[x, :, 0:128] = full[0, x]
        coef[x, :, 128:256] = tiles[0]
        side[0, x] = tiles[1]
        side[1, x] = tiles[2]
        corr[x, :, 0:128] = band(tiles[0], 0)
        corr[x, :, 128:256] = band(tiles[1], 0)
        corr_next[x, :, 0:128] = band(tiles[0] * tiles[1], 0)

    for x in (0, 1, 26, 27):
        res[x] = jnp.zeros((32, 256), F32)

    def over_x(ref, x):
        return (ref[x - 1] + ref[x + 1]) + 2.0 * ref[x]

    def cells(x, carry):
        sides = over_x(corr, x)
        product = (corr_next[x - 1, :, 0:128] + corr_next[x + 1, :, 0:128]) + 2.0 * corr_next[x, :, 0:128]
        tu_k = band(jnp.concatenate([xy[0, x], sides[:, 0:128]], axis=1), 1)
        tu_v = band(jnp.concatenate([xy[1, x], sides[:, 128:256]], axis=1), 1)
        tu_kv = band(jnp.concatenate([xy[2, x], product], axis=1), 1)
        k = coef[x]
        v = jnp.concatenate([full[1, x], side[0, x]], axis=1)
        diagonal = 6.0 * k + 0.125 * tu_k
        applied = v * diagonal + 2.0 * (k * v) - 0.125 * (k * tu_v + tu_kv)
        res[x] = jnp.concatenate([full[2, x], side[1, x]], axis=1) - applied
        inv[x] = damped_inverse(k, diagonal)
        return carry

    lax.fori_loop(2, 26, cells, 0, unroll=2)

    def first_sweep(x, carry):
        c = inv[x] * res[x]
        corr[x] = c
        yz_c[x] = band_yz(c)
        yz_kc[x] = band_yz(coef[x] * c)
        return carry

    lax.fori_loop(4, 24, first_sweep, 0, unroll=2)

    def second(x, carry):
        corr_next[x] = relax(corr[x], inv[x], res[x], coef[x], over_x(yz_c, x), over_x(yz_kc, x))
        return carry

    lax.fori_loop(5, 23, second, 0, unroll=2)

    def second_bands(x, carry):
        c = corr_next[x]
        yz_c[x] = band_yz(c)
        yz_kc[x] = band_yz(coef[x] * c)
        return carry

    lax.fori_loop(5, 23, second_bands, 0, unroll=2)

    def third(x, carry):
        c = relax(
            corr_next[x, 0:16, 0:128],
            inv[x, 0:16, 0:128],
            res[x, 0:16, 0:128],
            coef[x, 0:16, 0:128],
            (yz_c[x - 1, 0:16, 0:128] + yz_c[x + 1, 0:16, 0:128]) + 2.0 * yz_c[x, 0:16, 0:128],
            (yz_kc[x - 1, 0:16, 0:128] + yz_kc[x + 1, 0:16, 0:128]) + 2.0 * yz_kc[x, 0:16, 0:128],
        )
        base[x - 6] = full[1, x, 0:16, :] + c
        return carry

    lax.fori_loop(6, 22, third, 0, unroll=2)

    halves = ones_where((iota((256, 128), 0) >> 1) == iota((256, 128), 1))
    for ref, scale, out in ((res, 0.5, res_two), (coef, 0.125, coef_two)):

        def pair(x, carry):
            pairs[pl.ds(pl.multiple_of(32 * x, 32), 32), :] = ref[2 * x] + ref[2 * x + 1]
            return carry

        lax.fori_loop(0, 14, pair, 0, unroll=2)
        narrow[...] = select_lanes(pairs[...], halves)
        summed = narrow[pl.ds(0, 224, stride=2), :] + narrow[pl.ds(1, 224, stride=2), :]
        out[...] = (scale * summed).reshape(14, 16, 128)


def second_level(res_two, coef_two, base, out, spread):
    corr_two = smooth_small(res_two[...], coef_two[...], 3)
    doubled = ones_where(iota((128, 128), 0) == (iota((128, 128), 1) >> 1))
    wide = select_lanes(corr_two[3:11].reshape(128, 128), doubled).reshape(8, 16, 128)
    rows = wide[:, 0:8, :].reshape(64, 128)
    spread[pl.ds(0, 64, stride=2), :] = rows
    spread[pl.ds(1, 64, stride=2), :] = rows
    for x in range(16):
        start = 16 * (x // 2)
        out[x] = base[x] + spread[start : start + 16, :]


def coarse_levels(place, plane, base, out):
    row = iota((192, 512), 0)
    cell = iota((192, 512), 1)
    cell_x = (cell >> 6) * 4 + ((cell >> 2) & 3)
    cell_y = ((cell >> 4) & 3) * 4 + (cell & 3)
    parts = split3(plane[...])
    windows = []
    for level in range(3):
        at_x = place[0] * (4 >> level) - 4 + (row >> 4)
        at_y = place[1] * (4 >> level) - 4 + (row & 15)
        pattern = ones_where(((cell_x >> level) == at_x) & ((cell_y >> level) == at_y))
        found = [jnp.dot(pattern, part, preferred_element_type=F32) for part in parts]
        windows.append(found[0] + (found[1] + found[2]))
    source = iota((128, 128), 0)
    lane = iota((128, 128), 1)
    residual = jnp.zeros((192, 128), F32)
    coef = jnp.zeros((192, 128), F32)
    for level, start in enumerate((0, 64, 96)):
        parts = split3(windows[level])
        target = start + ((source & 63) >> level)
        to_res = ones_where((source < 64) & (lane == target), 0.5**level)
        to_coef = ones_where((source >= 64) & (lane == target), 0.125**level)
        for part in parts:
            residual = residual + jnp.dot(part, to_res, preferred_element_type=F32)
            coef = coef + jnp.dot(part, to_coef, preferred_element_type=F32)
    corr = smooth_small(residual.reshape(12, 16, 128), coef.reshape(12, 16, 128), 4)
    mine = corr[4:8].reshape(64, 128)
    total = base[...].reshape(256, 128)
    row = iota((256, 64), 0)
    found = iota((256, 64), 1)
    for level, start in enumerate((16, 72, 100)):
        shift = 2 + level
        spread = ones_where(source == start + (lane >> shift))
        at = ((row >> 4) >> shift) * 16 + 4 + ((row & 15) >> shift)
        total = total + select_rows(ones_where(found == at), select_lanes(mine, spread))
    out[...] = total.reshape(16, 16, 128)


VMEM = pl.BlockSpec(memory_space=pltpu.VMEM)
SMEM = pl.BlockSpec(memory_space=pltpu.SMEM)
HBM = pl.BlockSpec(memory_space=pltpu.HBM)


def call(kernel, outs, ins, scratch=(), first=VMEM, rest=VMEM, flops=1000000, grant=32):
    moved = 4 * sum(x.size for x in ins)
    return pl.pallas_call(
        kernel,
        out_shape=[jax.ShapeDtypeStruct(shape, F32) for shape in outs],
        in_specs=[first] + [rest] * (len(ins) - 1),
        out_specs=[VMEM] * len(outs),
        scratch_shapes=[pltpu.VMEM(shape, F32) if isinstance(shape, tuple) else shape for shape in scratch],
        compiler_params=pltpu.CompilerParams(vmem_limit_bytes=grant * 1024 * 1024),
        cost_estimate=pl.CostEstimate(flops=flops, bytes_accessed=moved, transcendentals=0),
        name=kernel.__name__,
    )(*ins)


def swap(axis, to_up, to_down):
    count = lax.axis_size(axis)
    up = [(i, i + 1) for i in range(count - 1)]
    down = [(i + 1, i) for i in range(count - 1)]
    return lax.ppermute(to_up, axis, up), lax.ppermute(to_down, axis, down)


def on_device(right, iterate, phase, table):
    block = (16, 16, 128)
    inputs = [table, phase, iterate, right]
    values = pltpu.SMEM((4,), F32)
    to_up, to_down = call(
        send_x,
        [(15, 16, 128)] * 2,
        inputs,
        scratch=[values, pltpu.VMEM((6, 16, 128), jnp.int32), pltpu.VMEM((6, 16, 128), jnp.int32), pltpu.SemaphoreType.DMA((7,))],
        first=HBM,
        rest=HBM,
        grant=60,
    )
    from_down, from_up = swap("gx", to_up, to_down)
    (fields,) = call(
        keep_fields,
        [(3, *block)],
        inputs,
        scratch=[values, pltpu.VMEM(block, jnp.int32), pltpu.SemaphoreType.DMA((4,))],
        first=HBM,
        rest=HBM,
    )
    ext, to_up, to_down = call(pack_y, [(3, 28, 16, 128), (28, 16, 128), (28, 16, 128)], [fields, from_down, from_up])
    from_down, from_up = swap("gy", to_up, to_down)
    planes = (3, 28, 32, 128)
    full, to_up, to_down = call(pack_z, [planes, (32, 512), (32, 512)], [ext, from_down, from_up])
    from_down, from_up = swap("gz", to_up, to_down)
    (xy,) = call(bands_xy, [planes], [full], scratch=[planes], flops=30000000)
    z_sides = [from_down, from_up]
    own, to_up, to_down = call(own_residual, [(16, 128)] * 3, [full, xy, *z_sides], scratch=[(128, 128)])
    from_down, from_up = swap("gz", to_up, to_down)
    wide = (28, 32, 256)
    base, res_two, coef_two = call(
        fine_level,
        [block, (14, 16, 128), (14, 16, 128)],
        [full, xy, *z_sides],
        scratch=[wide, (2, 28, 32, 128), wide, wide, wide, wide, wide, wide, (448, 256), (448, 128)],
        flops=60000000,
    )
    own, from_down, from_up, base, res_two, coef_two = lax.optimization_barrier(
        (own, from_down, from_up, base, res_two, coef_two)
    )
    mine = own + from_down + from_up
    chunks = lax.axis_size("gx") * lax.axis_size("gy")
    plane = lax.all_to_all(jnp.broadcast_to(mine[None], (chunks, 16, 128)), ("gx", "gy"), 0, 0, tiled=True)
    (base,) = call(second_level, [block], [res_two, coef_two, base], scratch=[(128, 128)], flops=30000000)
    place = jnp.stack([lax.axis_index("gx"), lax.axis_index("gy")]).astype(jnp.int32)
    (out,) = call(coarse_levels, [block], [place, plane.reshape(chunks * 16, 128), base], first=SMEM, flops=30000000)
    return out


def solution(mesh):
    placed = (P("gx", "gy", "gz"), P("gx", "gy", "gz"), P("gx", "gy", "gz"), P())
    return jax.shard_map(on_device, mesh=mesh, in_specs=placed, out_specs=P("gx", "gy", "gz"), check_vma=False)
```

time: 85.2 us -> 82.2 us (0.965)
  waiting for transfers between devices: 25.5 us -> 22.8 us
  local copies, waits for them, and re-layouts: 5.9 us -> 4.09 us
    ppermute x8, waiting for transfers between devices: 19.8 us -> 11.6 us  [swap(): return (lax.ppermute(to_up, axis, up), lax.ppermute(to_down, axis, down))]
    all_to_all x1, waiting for transfers between devices: 5.72 us -> 11.1 us  [on_device(): lax.all_to_all(jnp.broadcast_to(mine[None], (chunks, 16, 128)), ('gx', 'g...]
    unnamed x14 -> x8, local copies, waits for them, and re-layouts: 5.18 us -> 3.36 us
    pallas_call x6 -> x9, Pallas kernels: 16.9 us -> 17.7 us  [call(): pl.pallas_call(kernel, out_shape=[jax.ShapeDtypeStruct(shape, F32) for sh...]
  transfers between devices with their start and end apart: 9 -> 9, of which waited for: 8 -> 5; matrix products, arithmetic and copies ran while one was open for 0% -> 0% of each run, Pallas kernels for 7% -> 13%
where the time goes in v2:
time: 82.2 us; the launch traced here: 80.6 us
  starting transfers between devices  35.8 us (44%)
  waiting for transfers between devices  22.8 us (28%)
  Pallas kernels  17.7 us (22%)
  local copies, waits for them, and re-layouts  4.09 us (5%)
    ppermute x8, starting transfers between devices, swap(): return (lax.ppermute(to_up, axis, up), lax.ppermute(to_down, axis, down))  24.6 us
    pallas_call x9, Pallas kernels, call(): pl.pallas_call(kernel, out_shape=[jax.ShapeDtypeStruct(shape, F32) for sh...  17.7 us
    ppermute x8, waiting for transfers between devices, swap(): return (lax.ppermute(to_up, axis, up), lax.ppermute(to_down, axis, down))  11.6 us
    all_to_all x1, starting transfers between devices, on_device(): lax.all_to_all(jnp.broadcast_to(mine[None], (chunks, 16, 128)), ('gx', 'g...  11.2 us
    all_to_all x1, waiting for transfers between devices, on_device(): lax.all_to_all(jnp.broadcast_to(mine[None], (chunks, 16, 128)), ('gx', 'g...  11.1 us
    unnamed x8, local copies, waits for them, and re-layouts  3.36 us
  transfers between devices with their start and end apart: 9, of which 5 were waited for; matrix products, arithmetic and copies ran while one was open for 0% of the time, Pallas kernels for 13%

profile of v2, /device:TPU:56, one launch (start us, length us, event | category | flops | bytes accessed | tf_op | source)
XLA Modules:
  0.0 80.6 jit_solution(1475989643854797447)
XLA Ops:
  0.0 1.6 %send_x.1 = (f32[15,16,128]{2,1,0:T(8,128)}, f32[15,16,128]{2,1,0:T(8,128)}) custom-call(f32[4]{0:T(128)} %table.3, s32[16,16,128]{2,1,0:T(8,128)} %phase.3, f32[16,16,128]{2,1,0:T(8,128)} %iterate.3, f32[16,16,128]{2,1,0:T(8,128)} %right.3), custom_call_target="tpu_custom_call" | custom-call | flops 1000000 | bytes 393232 | tf_op jit(solution)/shard_map/send_x/pallas_call | solution.py:378
  1.7 4.3 %collective-permute-start = (f32[15,16,128]{2,1,0:T(8,128)}, f32[15,16,128]{2,1,0:T(8,128)S(1)}, u32[]{:S(2)}, u32[]{:S(2)}) collective-permute-start(f32[15,16,128]{2,1,0:T(8,128)} %get-tuple-element.25), channel_id=1, source_target_pairs={{0,64},{64,128},{128,192},{192,256},{256,320},{320,384},{384,448},... | collective-permute-start | bytes 368648 | tf_op jit(solution)/shard_map/ppermute | solution.py:394
  5.9 1.3 %collective-permute-start.1 = (f32[15,16,128]{2,1,0:T(8,128)}, f32[15,16,128]{2,1,0:T(8,128)S(1)}, u32[]{:S(2)}, u32[]{:S(2)}) collective-permute-start(f32[15,16,128]{2,1,0:T(8,128)} %get-tuple-element.26), channel_id=1, source_target_pairs={{64,0},{128,64},{192,128},{256,192},{320,256},{384,320},{448,384},... | collective-permute-start | bytes 368648 | tf_op jit(solution)/shard_map/ppermute | solution.py:394
  7.2 0.0 copy-start
  7.3 0.9 %copy-done = s32[16,16,128]{2,1,0:T(8,128)S(1)} copy-done((s32[16,16,128]{2,1,0:T(8,128)S(1)}, s32[16,16,128]{2,1,0:T(8,128)}, u32[]{:S(2)}) %copy-start) | copy-done | bytes 131096
  8.2 0.0 copy-start.1
  8.2 0.9 %copy-done.1 = f32[16,16,128]{2,1,0:T(8,128)S(1)} copy-done((f32[16,16,128]{2,1,0:T(8,128)S(1)}, f32[16,16,128]{2,1,0:T(8,128)}, u32[]{:S(2)}) %copy-start.1) | copy-done | bytes 131096
  9.1 0.0 copy-start.2
  9.1 0.9 %copy-done.2 = f32[16,16,128]{2,1,0:T(8,128)S(1)} copy-done((f32[16,16,128]{2,1,0:T(8,128)S(1)}, f32[16,16,128]{2,1,0:T(8,128)}, u32[]{:S(2)}) %copy-start.2) | copy-done | bytes 131096
  10.0 0.0 copy-start.3
  10.0 0.7 copy-done.3
  10.6 0.6 keep_fields.1.fields
  11.2 0.0 collective-permute-done.from_down
  11.3 2.2 %collective-permute-done.1.from_up = f32[15,16,128]{2,1,0:T(8,128)S(1)} collective-permute-done((f32[15,16,128]{2,1,0:T(8,128)}, f32[15,16,128]{2,1,0:T(8,128)S(1)}, u32[]{:S(2)}, u32[]{:S(2)}) %collective-permute-start.1) | collective-permute-done | bytes 122912 | tf_op jit(solution)/shard_map/ppermute | solution.py:394
  13.5 0.1 pack_y.1
  13.6 1.9 %collective-permute-start.2 = (f32[28,16,128]{2,1,0:T(8,128)S(1)}, f32[28,16,128]{2,1,0:T(8,128)S(1)}, u32[]{:S(2)}, u32[]{:S(2)}) collective-permute-start(f32[28,16,128]{2,1,0:T(8,128)S(1)} %get-tuple-element.28), channel_id=1, source_target_pairs={{0,16},{16,32},{32,48},{1,17},{17,33},{33,49},{2,18},{18,34},{34,5... | collective-permute-start | bytes 688136 | tf_op jit(solution)/shard_map/ppermute | solution.py:394
  15.5 3.6 %collective-permute-start.3 = (f32[28,16,128]{2,1,0:T(8,128)S(1)}, f32[28,16,128]{2,1,0:T(8,128)S(1)}, u32[]{:S(2)}, u32[]{:S(2)}) collective-permute-start(f32[28,16,128]{2,1,0:T(8,128)S(1)} %get-tuple-element.29), channel_id=1, source_target_pairs={{16,0},{32,16},{48,32},{17,1},{33,17},{49,33},{18,2},{34,18},{50,3... | collective-permute-start | bytes 688136 | tf_op jit(solution)/shard_map/ppermute | solution.py:394
  19.2 1.8 %collective-permute-done.2.from_down = f32[28,16,128]{2,1,0:T(8,128)S(1)} collective-permute-done((f32[28,16,128]{2,1,0:T(8,128)S(1)}, f32[28,16,128]{2,1,0:T(8,128)S(1)}, u32[]{:S(2)}, u32[]{:S(2)}) %collective-permute-start.2) | collective-permute-done | bytes 229408 | tf_op jit(solution)/shard_map/ppermute | solution.py:394
  20.9 1.8 %collective-permute-done.3.from_up = f32[28,16,128]{2,1,0:T(8,128)S(1)} collective-permute-done((f32[28,16,128]{2,1,0:T(8,128)S(1)}, f32[28,16,128]{2,1,0:T(8,128)S(1)}, u32[]{:S(2)}, u32[]{:S(2)}) %collective-permute-start.3) | collective-permute-done | bytes 229408 | tf_op jit(solution)/shard_map/ppermute | solution.py:394
  22.7 0.8 %pack_z.1 = (f32[3,28,32,128]{3,2,1,0:T(8,128)S(1)}, f32[32,512]{1,0:T(8,128)S(1)}, f32[32,512]{1,0:T(8,128)S(1)}) custom-call(f32[3,28,16,128]{3,2,1,0:T(8,128)S(1)} %get-tuple-element.27.ext, f32[28,16,128]{2,1,0:T(8,128)S(1)} %collective-permute-done.2.from_down, f32[28,16,128]{2,1,0:T(8,128)S(1)} %collective-permute-done.3.from_up), custom_call_target="tpu_custom_call" | custom-call | flops 1000000 | bytes 1146880 | tf_op jit(solution)/shard_map/pack_z/pallas_call | solution.py:378
  23.5 3.6 %collective-permute-start.4 = (f32[32,512]{1,0:T(8,128)S(1)}, f32[32,512]{1,0:T(8,128)S(1)}, u32[]{:S(2)}, u32[]{:S(2)}) collective-permute-start(f32[32,512]{1,0:T(8,128)S(1)} %get-tuple-element.31), channel_id=1, source_target_pairs={{0,1},{1,2},{2,3},{3,4},{4,5},{5,6},{6,7},{7,8},{8,9},{9,10},{10,1... | collective-permute-start | bytes 196616 | tf_op jit(solution)/shard_map/ppermute | solution.py:394
  27.1 3.1 %collective-permute-start.5 = (f32[32,512]{1,0:T(8,128)S(1)}, f32[32,512]{1,0:T(8,128)S(1)}, u32[]{:S(2)}, u32[]{:S(2)}) collective-permute-start(f32[32,512]{1,0:T(8,128)S(1)} %get-tuple-element.32), channel_id=1, source_target_pairs={{1,0},{2,1},{3,2},{4,3},{5,4},{6,5},{7,6},{8,7},{9,8},{10,9},{11,1... | collective-permute-start | bytes 196616 | tf_op jit(solution)/shard_map/ppermute | solution.py:394
  30.3 0.6 bands_xy.1.xy
  30.9 0.0 collective-permute-done.4.from_down
  30.9 5.9 %collective-permute-done.5.from_up = f32[32,512]{1,0:T(8,128)S(1)} collective-permute-done((f32[32,512]{1,0:T(8,128)S(1)}, f32[32,512]{1,0:T(8,128)S(1)}, u32[]{:S(2)}, u32[]{:S(2)}) %collective-permute-start.5) | collective-permute-done | bytes 65568 | tf_op jit(solution)/shard_map/ppermute | solution.py:394
  36.8 0.9 %own_residual.1 = (f32[16,128]{1,0:T(8,128)S(1)}, f32[16,128]{1,0:T(8,128)S(1)}, f32[16,128]{1,0:T(8,128)S(1)}) custom-call(f32[3,28,32,128]{3,2,1,0:T(8,128)S(1)} %get-tuple-element.30.full, f32[3,28,32,128]{3,2,1,0:T(8,128)S(1)} %bands_xy.1.xy, f32[32,512]{1,0:T(8,128)S(1)} %collective-permute-done.4.from_down, f32[32,512]{1,0:T(8,128)S(1)} %collective-permute-done.5.from_up), custom_call_target="tpu_custom_call" | custom-call | flops 1000000 | bytes 2883584 | tf_op jit(solution)/shard_map/own_residual/pallas_call | solution.py:378
  37.7 2.6 %collective-permute-start.6 = (f32[16,128]{1,0:T(8,128)S(1)}, f32[16,128]{1,0:T(8,128)S(1)}, u32[]{:S(2)}, u32[]{:S(2)}) collective-permute-start(f32[16,128]{1,0:T(8,128)S(1)} %get-tuple-element.34), channel_id=1, source_target_pairs={{0,1},{1,2},{2,3},{3,4},{4,5},{5,6},{6,7},{7,8},{8,9},{9,10},{10,1... | collective-permute-start | bytes 24584 | tf_op jit(solution)/shard_map/ppermute | solution.py:394
  40.3 4.1 %collective-permute-start.7 = (f32[16,128]{1,0:T(8,128)S(1)}, f32[16,128]{1,0:T(8,128)S(1)}, u32[]{:S(2)}, u32[]{:S(2)}) collective-permute-start(f32[16,128]{1,0:T(8,128)S(1)} %get-tuple-element.35), channel_id=1, source_target_pairs={{1,0},{2,1},{3,2},{4,3},{5,4},{6,5},{7,6},{8,7},{9,8},{10,9},{11,1... | collective-permute-start | bytes 24584 | tf_op jit(solution)/shard_map/ppermute | solution.py:394
  44.5 8.7 %fine_level.1 = (f32[16,16,128]{2,1,0:T(8,128)S(1)}, f32[14,16,128]{2,1,0:T(8,128)S(1)}, f32[14,16,128]{2,1,0:T(8,128)S(1)}) custom-call(f32[3,28,32,128]{3,2,1,0:T(8,128)S(1)} %get-tuple-element.30.full, f32[3,28,32,128]{3,2,1,0:T(8,128)S(1)} %bands_xy.1.xy, f32[32,512]{1,0:T(8,128)S(1)} %collective-permute-done.4.from_down, ...), custom_call_target="tpu_custom_call" | custom-call | flops 60000000 | bytes 2883584 | tf_op jit(solution)/shard_map/fine_level/pallas_call | solution.py:378
  53.2 0.0 collective-permute-done.6
  53.2 0.0 collective-permute-done.7
  53.2 0.7 broadcast_in_dim.2
  54.0 11.2 %all-to-all-start = ((f32[32,16,128]{2,1,0:T(8,128)}), f32[32,16,128]{2,1,0:T(8,128)S(1)}, u32[]{:S(2)}, u32[]{:S(2)}) async-start(f32[32,16,128]{2,1,0:T(8,128)} %broadcast_in_dim.2), calls=%async_computation | async-start | bytes 524288 | tf_op jit(solution)/shard_map/all_to_all | solution.py:441
  65.2 0.1 pad_add_fusion.place
  65.2 0.8 second_level.1.base
  66.0 11.1 %all-to-all-done = f32[32,16,128]{2,1,0:T(8,128)S(1)} async-done(((f32[32,16,128]{2,1,0:T(8,128)}), f32[32,16,128]{2,1,0:T(8,128)S(1)}, u32[]{:S(2)}, u32[]{:S(2)}) %all-to-all-start) | async-done | bytes 262176 | tf_op jit(solution)/shard_map/all_to_all | solution.py:441
  77.1 3.5 %coarse_levels.1 = f32[16,16,128]{2,1,0:T(8,128)} custom-call(s32[2]{0:T(128)S(1)} %pad_add_fusion.place, f32[512,128]{1,0:T(8,128)S(1)} %bitcast.3, f32[16,16,128]{2,1,0:T(8,128)S(1)} %second_level.1.base), custom_call_target="tpu_custom_call" | custom-call | flops 30000000 | bytes 393224 | tf_op jit(solution)/shard_map/coarse_levels/pallas_call | solution.py:378
  (1 shorter events, 0.0 us)
Async XLA Ops:
  1.7 9.6 %collective-permute-start = (f32[15,16,128]{2,1,0:T(8,128)}, f32[15,16,128]{2,1,0:T(8,128)S(1)}, u32[]{:S(2)}, u32[]{:S(2)}) collective-permute-start(f32[15,16,128]{2,1,0:T(8,128)} %get-tuple-element.25), channel_id=1, source_target_pairs={{0,64},{64,128},{128,192},{192,256},{256,320},{320,384},{384,448},... | collective-permute-start | bytes 368648 | tf_op jit(solution)/shard_map/ppermute | solution.py:394
  5.9 7.5 %collective-permute-start.1 = (f32[15,16,128]{2,1,0:T(8,128)}, f32[15,16,128]{2,1,0:T(8,128)S(1)}, u32[]{:S(2)}, u32[]{:S(2)}) collective-permute-start(f32[15,16,128]{2,1,0:T(8,128)} %get-tuple-element.26), channel_id=1, source_target_pairs={{64,0},{128,64},{192,128},{256,192},{320,256},{384,320},{448,384},... | collective-permute-start | bytes 368648 | tf_op jit(solution)/shard_map/ppermute | solution.py:394
  7.2 0.9 %copy-start = (s32[16,16,128]{2,1,0:T(8,128)S(1)}, s32[16,16,128]{2,1,0:T(8,128)}, u32[]{:S(2)}) copy-start(s32[16,16,128]{2,1,0:T(8,128)} %phase.3) | copy-start | bytes 393220
  8.2 0.9 %copy-start.1 = (f32[16,16,128]{2,1,0:T(8,128)S(1)}, f32[16,16,128]{2,1,0:T(8,128)}, u32[]{:S(2)}) copy-start(f32[16,16,128]{2,1,0:T(8,128)} %iterate.3) | copy-start | bytes 393220
  9.1 0.9 %copy-start.2 = (f32[16,16,128]{2,1,0:T(8,128)S(1)}, f32[16,16,128]{2,1,0:T(8,128)}, u32[]{:S(2)}) copy-start(f32[16,16,128]{2,1,0:T(8,128)} %right.3) | copy-start | bytes 393220
  10.0 0.7 copy-start.3
  13.6 7.3 %collective-permute-start.2 = (f32[28,16,128]{2,1,0:T(8,128)S(1)}, f32[28,16,128]{2,1,0:T(8,128)S(1)}, u32[]{:S(2)}, u32[]{:S(2)}) collective-permute-start(f32[28,16,128]{2,1,0:T(8,128)S(1)} %get-tuple-element.28), channel_id=1, source_target_pairs={{0,16},{16,32},{32,48},{1,17},{17,33},{33,49},{2,18},{18,34},{34,5... | collective-permute-start | bytes 688136 | tf_op jit(solution)/shard_map/ppermute | solution.py:394
  15.5 7.2 %collective-permute-start.3 = (f32[28,16,128]{2,1,0:T(8,128)S(1)}, f32[28,16,128]{2,1,0:T(8,128)S(1)}, u32[]{:S(2)}, u32[]{:S(2)}) collective-permute-start(f32[28,16,128]{2,1,0:T(8,128)S(1)} %get-tuple-element.29), channel_id=1, source_target_pairs={{16,0},{32,16},{48,32},{17,1},{33,17},{49,33},{18,2},{34,18},{50,3... | collective-permute-start | bytes 688136 | tf_op jit(solution)/shard_map/ppermute | solution.py:394
  23.5 7.4 %collective-permute-start.4 = (f32[32,512]{1,0:T(8,128)S(1)}, f32[32,512]{1,0:T(8,128)S(1)}, u32[]{:S(2)}, u32[]{:S(2)}) collective-permute-start(f32[32,512]{1,0:T(8,128)S(1)} %get-tuple-element.31), channel_id=1, source_target_pairs={{0,1},{1,2},{2,3},{3,4},{4,5},{5,6},{6,7},{7,8},{8,9},{9,10},{10,1... | collective-permute-start | bytes 196616 | tf_op jit(solution)/shard_map/ppermute | solution.py:394
  27.1 9.7 %collective-permute-start.5 = (f32[32,512]{1,0:T(8,128)S(1)}, f32[32,512]{1,0:T(8,128)S(1)}, u32[]{:S(2)}, u32[]{:S(2)}) collective-permute-start(f32[32,512]{1,0:T(8,128)S(1)} %get-tuple-element.32), channel_id=1, source_target_pairs={{1,0},{2,1},{3,2},{4,3},{5,4},{6,5},{7,6},{8,7},{9,8},{10,9},{11,1... | collective-permute-start | bytes 196616 | tf_op jit(solution)/shard_map/ppermute | solution.py:394
  37.7 15.5 %collective-permute-start.6 = (f32[16,128]{1,0:T(8,128)S(1)}, f32[16,128]{1,0:T(8,128)S(1)}, u32[]{:S(2)}, u32[]{:S(2)}) collective-permute-start(f32[16,128]{1,0:T(8,128)S(1)} %get-tuple-element.34), channel_id=1, source_target_pairs={{0,1},{1,2},{2,3},{3,4},{4,5},{5,6},{6,7},{7,8},{8,9},{9,10},{10,1... | collective-permute-start | bytes 24584 | tf_op jit(solution)/shard_map/ppermute | solution.py:394
  40.3 12.9 %collective-permute-start.7 = (f32[16,128]{1,0:T(8,128)S(1)}, f32[16,128]{1,0:T(8,128)S(1)}, u32[]{:S(2)}, u32[]{:S(2)}) collective-permute-start(f32[16,128]{1,0:T(8,128)S(1)} %get-tuple-element.35), channel_id=1, source_target_pairs={{1,0},{2,1},{3,2},{4,3},{5,4},{6,5},{7,6},{8,7},{9,8},{10,9},{11,1... | collective-permute-start | bytes 24584 | tf_op jit(solution)/shard_map/ppermute | solution.py:394
  54.0 23.1 %all-to-all-start = ((f32[32,16,128]{2,1,0:T(8,128)}), f32[32,16,128]{2,1,0:T(8,128)S(1)}, u32[]{:S(2)}, u32[]{:S(2)}) async-start(f32[32,16,128]{2,1,0:T(8,128)} %broadcast_in_dim.2), calls=%async_computation | async-start | bytes 524288 | tf_op jit(solution)/shard_map/all_to_all | solution.py:441

commit v3 on v2

--- a/solution.py
+++ b/solution.py
@@ -433,14 +433,12 @@
         scratch=[wide, (2, 28, 32, 128), wide, wide, wide, wide, wide, wide, (448, 256), (448, 128)],
         flops=60000000,
     )
-    own, from_down, from_up, base, res_two, coef_two = lax.optimization_barrier(
-        (own, from_down, from_up, base, res_two, coef_two)
-    )
+    (base,) = call(second_level, [block], [res_two, coef_two, base], scratch=[(128, 128)], flops=30000000)
+    place = jnp.stack([lax.axis_index("gx"), lax.axis_index("gy")]).astype(jnp.int32)
+    own, from_down, from_up, base, place = lax.optimization_barrier((own, from_down, from_up, base, place))
     mine = own + from_down + from_up
     chunks = lax.axis_size("gx") * lax.axis_size("gy")
     plane = lax.all_to_all(jnp.broadcast_to(mine[None], (chunks, 16, 128)), ("gx", "gy"), 0, 0, tiled=True)
-    (base,) = call(second_level, [block], [res_two, coef_two, base], scratch=[(128, 128)], flops=30000000)
-    place = jnp.stack([lax.axis_index("gx"), lax.axis_index("gy")]).astype(jnp.int32)
     (out,) = call(coarse_levels, [block], [place, plane.reshape(chunks * 16, 128), base], first=SMEM, flops=30000000)
     return out
 

time: 82.2 us -> 82 us (level)
  blocking collectives: 0 us -> 22.9 us
  waiting for transfers between devices: 22.8 us -> 11.6 us
  starting transfers between devices: 35.8 us -> 24.6 us
    all_to_all x0 -> x1, blocking collectives: none -> 22.9 us  [on_device(): lax.all_to_all(jnp.broadcast_to(mine[None], (chunks, 16, 128)), ('gx', 'g...]
    all_to_all x1 -> x0, starting transfers between devices: 11.2 us -> none  [on_device(): lax.all_to_all(jnp.broadcast_to(mine[None], (chunks, 16, 128)), ('gx', 'g...]
    all_to_all x1 -> x0, waiting for transfers between devices: 11.1 us -> none  [on_device(): lax.all_to_all(jnp.broadcast_to(mine[None], (chunks, 16, 128)), ('gx', 'g...]
  transfers between devices with their start and end apart: 9 -> 8, of which waited for: 5 -> 4; matrix products, arithmetic and copies ran while one was open for 0% -> 0% of each run, Pallas kernels for 13% -> 13%
where the time goes in v3:
time: 82 us; the launch traced here: 80.4 us
  starting transfers between devices  24.6 us (30%)
  blocking collectives  22.9 us (28%)
  Pallas kernels  17.7 us (22%)
  waiting for transfers between devices  11.6 us (14%)
  local copies, waits for them, and re-layouts  3.38 us (4%)
    ppermute x8, starting transfers between devices, swap(): return (lax.ppermute(to_up, axis, up), lax.ppermute(to_down, axis, down))  24.6 us
    all_to_all x1, blocking collectives, on_device(): lax.all_to_all(jnp.broadcast_to(mine[None], (chunks, 16, 128)), ('gx', 'g...  22.9 us
    pallas_call x9, Pallas kernels, call(): pl.pallas_call(kernel, out_shape=[jax.ShapeDtypeStruct(shape, F32) for sh...  17.7 us
    ppermute x8, waiting for transfers between devices, swap(): return (lax.ppermute(to_up, axis, up), lax.ppermute(to_down, axis, down))  11.6 us
    unnamed x8, local copies, waits for them, and re-layouts  3.36 us
  transfers between devices with their start and end apart: 8, of which 4 were waited for; matrix products, arithmetic and copies ran while one was open for 0% of the time, Pallas kernels for 13%

profile of v3, /device:TPU:56, one launch (start us, length us, event | category | flops | bytes accessed | tf_op | source)
XLA Modules:
  0.0 80.4 jit_solution(1020414717098209062)
XLA Ops:
  0.0 1.6 %send_x.1 = (f32[15,16,128]{2,1,0:T(8,128)}, f32[15,16,128]{2,1,0:T(8,128)}) custom-call(f32[4]{0:T(128)} %table.3, s32[16,16,128]{2,1,0:T(8,128)} %phase.3, f32[16,16,128]{2,1,0:T(8,128)} %iterate.3, f32[16,16,128]{2,1,0:T(8,128)} %right.3), custom_call_target="tpu_custom_call" | custom-call | flops 1000000 | bytes 393232 | tf_op jit(solution)/shard_map/send_x/pallas_call | solution.py:378
  1.6 4.3 %collective-permute-start = (f32[15,16,128]{2,1,0:T(8,128)}, f32[15,16,128]{2,1,0:T(8,128)S(1)}, u32[]{:S(2)}, u32[]{:S(2)}) collective-permute-start(f32[15,16,128]{2,1,0:T(8,128)} %get-tuple-element.24), channel_id=1, source_target_pairs={{0,64},{64,128},{128,192},{192,256},{256,320},{320,384},{384,448},... | collective-permute-start | bytes 368648 | tf_op jit(solution)/shard_map/ppermute | solution.py:394
  5.9 1.3 %collective-permute-start.1 = (f32[15,16,128]{2,1,0:T(8,128)}, f32[15,16,128]{2,1,0:T(8,128)S(1)}, u32[]{:S(2)}, u32[]{:S(2)}) collective-permute-start(f32[15,16,128]{2,1,0:T(8,128)} %get-tuple-element.25), channel_id=1, source_target_pairs={{64,0},{128,64},{192,128},{256,192},{320,256},{384,320},{448,384},... | collective-permute-start | bytes 368648 | tf_op jit(solution)/shard_map/ppermute | solution.py:394
  7.2 0.0 copy-start
  7.2 0.9 %copy-done = s32[16,16,128]{2,1,0:T(8,128)S(1)} copy-done((s32[16,16,128]{2,1,0:T(8,128)S(1)}, s32[16,16,128]{2,1,0:T(8,128)}, u32[]{:S(2)}) %copy-start) | copy-done | bytes 131096
  8.1 0.0 copy-start.1
  8.1 0.9 %copy-done.1 = f32[16,16,128]{2,1,0:T(8,128)S(1)} copy-done((f32[16,16,128]{2,1,0:T(8,128)S(1)}, f32[16,16,128]{2,1,0:T(8,128)}, u32[]{:S(2)}) %copy-start.1) | copy-done | bytes 131096
  9.0 0.0 copy-start.2
  9.0 0.9 %copy-done.2 = f32[16,16,128]{2,1,0:T(8,128)S(1)} copy-done((f32[16,16,128]{2,1,0:T(8,128)S(1)}, f32[16,16,128]{2,1,0:T(8,128)}, u32[]{:S(2)}) %copy-start.2) | copy-done | bytes 131096
  9.9 0.0 copy-start.3
  10.0 0.7 copy-done.3
  10.6 0.6 keep_fields.1.fields
  11.2 0.0 collective-permute-done.from_down
  11.2 2.2 %collective-permute-done.1.from_up = f32[15,16,128]{2,1,0:T(8,128)S(1)} collective-permute-done((f32[15,16,128]{2,1,0:T(8,128)}, f32[15,16,128]{2,1,0:T(8,128)S(1)}, u32[]{:S(2)}, u32[]{:S(2)}) %collective-permute-start.1) | collective-permute-done | bytes 122912 | tf_op jit(solution)/shard_map/ppermute | solution.py:394
  13.5 0.1 pack_y.1
  13.6 1.9 %collective-permute-start.2 = (f32[28,16,128]{2,1,0:T(8,128)S(1)}, f32[28,16,128]{2,1,0:T(8,128)S(1)}, u32[]{:S(2)}, u32[]{:S(2)}) collective-permute-start(f32[28,16,128]{2,1,0:T(8,128)S(1)} %get-tuple-element.27), channel_id=1, source_target_pairs={{0,16},{16,32},{32,48},{1,17},{17,33},{33,49},{2,18},{18,34},{34,5... | collective-permute-start | bytes 688136 | tf_op jit(solution)/shard_map/ppermute | solution.py:394
  15.5 3.6 %collective-permute-start.3 = (f32[28,16,128]{2,1,0:T(8,128)S(1)}, f32[28,16,128]{2,1,0:T(8,128)S(1)}, u32[]{:S(2)}, u32[]{:S(2)}) collective-permute-start(f32[28,16,128]{2,1,0:T(8,128)S(1)} %get-tuple-element.28), channel_id=1, source_target_pairs={{16,0},{32,16},{48,32},{17,1},{33,17},{49,33},{18,2},{34,18},{50,3... | collective-permute-start | bytes 688136 | tf_op jit(solution)/shard_map/ppermute | solution.py:394
  19.2 1.8 %collective-permute-done.2.from_down = f32[28,16,128]{2,1,0:T(8,128)S(1)} collective-permute-done((f32[28,16,128]{2,1,0:T(8,128)S(1)}, f32[28,16,128]{2,1,0:T(8,128)S(1)}, u32[]{:S(2)}, u32[]{:S(2)}) %collective-permute-start.2) | collective-permute-done | bytes 229408 | tf_op jit(solution)/shard_map/ppermute | solution.py:394
  20.9 1.8 %collective-permute-done.3.from_up = f32[28,16,128]{2,1,0:T(8,128)S(1)} collective-permute-done((f32[28,16,128]{2,1,0:T(8,128)S(1)}, f32[28,16,128]{2,1,0:T(8,128)S(1)}, u32[]{:S(2)}, u32[]{:S(2)}) %collective-permute-start.3) | collective-permute-done | bytes 229408 | tf_op jit(solution)/shard_map/ppermute | solution.py:394
  22.7 0.8 %pack_z.1 = (f32[3,28,32,128]{3,2,1,0:T(8,128)S(1)}, f32[32,512]{1,0:T(8,128)S(1)}, f32[32,512]{1,0:T(8,128)S(1)}) custom-call(f32[3,28,16,128]{3,2,1,0:T(8,128)S(1)} %get-tuple-element.26.ext, f32[28,16,128]{2,1,0:T(8,128)S(1)} %collective-permute-done.2.from_down, f32[28,16,128]{2,1,0:T(8,128)S(1)} %collective-permute-done.3.from_up), custom_call_target="tpu_custom_call" | custom-call | flops 1000000 | bytes 1146880 | tf_op jit(solution)/shard_map/pack_z/pallas_call | solution.py:378
  23.5 3.6 %collective-permute-start.4 = (f32[32,512]{1,0:T(8,128)S(1)}, f32[32,512]{1,0:T(8,128)S(1)}, u32[]{:S(2)}, u32[]{:S(2)}) collective-permute-start(f32[32,512]{1,0:T(8,128)S(1)} %get-tuple-element.30), channel_id=1, source_target_pairs={{0,1},{1,2},{2,3},{3,4},{4,5},{5,6},{6,7},{7,8},{8,9},{9,10},{10,1... | collective-permute-start | bytes 196616 | tf_op jit(solution)/shard_map/ppermute | solution.py:394
  27.1 3.1 %collective-permute-start.5 = (f32[32,512]{1,0:T(8,128)S(1)}, f32[32,512]{1,0:T(8,128)S(1)}, u32[]{:S(2)}, u32[]{:S(2)}) collective-permute-start(f32[32,512]{1,0:T(8,128)S(1)} %get-tuple-element.31), channel_id=1, source_target_pairs={{1,0},{2,1},{3,2},{4,3},{5,4},{6,5},{7,6},{8,7},{9,8},{10,9},{11,1... | collective-permute-start | bytes 196616 | tf_op jit(solution)/shard_map/ppermute | solution.py:394
  30.3 0.1 pad_add_fusion.place
  30.3 0.6 bands_xy.1.xy
  30.9 0.0 collective-permute-done.4.from_down
  30.9 5.8 %collective-permute-done.5.from_up = f32[32,512]{1,0:T(8,128)S(1)} collective-permute-done((f32[32,512]{1,0:T(8,128)S(1)}, f32[32,512]{1,0:T(8,128)S(1)}, u32[]{:S(2)}, u32[]{:S(2)}) %collective-permute-start.5) | collective-permute-done | bytes 65568 | tf_op jit(solution)/shard_map/ppermute | solution.py:394
  36.8 0.9 %own_residual.1 = (f32[16,128]{1,0:T(8,128)S(1)}, f32[16,128]{1,0:T(8,128)S(1)}, f32[16,128]{1,0:T(8,128)S(1)}) custom-call(f32[3,28,32,128]{3,2,1,0:T(8,128)S(1)} %get-tuple-element.29.full, f32[3,28,32,128]{3,2,1,0:T(8,128)S(1)} %bands_xy.1.xy, f32[32,512]{1,0:T(8,128)S(1)} %collective-permute-done.4.from_down, f32[32,512]{1,0:T(8,128)S(1)} %collective-permute-done.5.from_up), custom_call_target="tpu_custom_call" | custom-call | flops 1000000 | bytes 2883584 | tf_op jit(solution)/shard_map/own_residual/pallas_call | solution.py:378
  37.7 2.6 %collective-permute-start.6 = (f32[16,128]{1,0:T(8,128)S(1)}, f32[16,128]{1,0:T(8,128)S(1)}, u32[]{:S(2)}, u32[]{:S(2)}) collective-permute-start(f32[16,128]{1,0:T(8,128)S(1)} %get-tuple-element.33), channel_id=1, source_target_pairs={{0,1},{1,2},{2,3},{3,4},{4,5},{5,6},{6,7},{7,8},{8,9},{9,10},{10,1... | collective-permute-start | bytes 24584 | tf_op jit(solution)/shard_map/ppermute | solution.py:394
  40.3 4.1 %collective-permute-start.7 = (f32[16,128]{1,0:T(8,128)S(1)}, f32[16,128]{1,0:T(8,128)S(1)}, u32[]{:S(2)}, u32[]{:S(2)}) collective-permute-start(f32[16,128]{1,0:T(8,128)S(1)} %get-tuple-element.34), channel_id=1, source_target_pairs={{1,0},{2,1},{3,2},{4,3},{5,4},{6,5},{7,6},{8,7},{9,8},{10,9},{11,1... | collective-permute-start | bytes 24584 | tf_op jit(solution)/shard_map/ppermute | solution.py:394
  44.5 8.7 %fine_level.1 = (f32[16,16,128]{2,1,0:T(8,128)S(1)}, f32[14,16,128]{2,1,0:T(8,128)S(1)}, f32[14,16,128]{2,1,0:T(8,128)S(1)}) custom-call(f32[3,28,32,128]{3,2,1,0:T(8,128)S(1)} %get-tuple-element.29.full, f32[3,28,32,128]{3,2,1,0:T(8,128)S(1)} %bands_xy.1.xy, f32[32,512]{1,0:T(8,128)S(1)} %collective-permute-done.4.from_down, ...), custom_call_target="tpu_custom_call" | custom-call | flops 60000000 | bytes 2883584 | tf_op jit(solution)/shard_map/fine_level/pallas_call | solution.py:378
  53.2 0.8 second_level.1.base
  54.0 0.0 collective-permute-done.6
  54.0 0.0 collective-permute-done.7
  54.0 22.9 %all_to_all.5 = f32[32,16,128]{2,1,0:T(8,128)S(1)} all-to-all(f32[32,16,128]{2,1,0:T(8,128)S(1)} %broadcast_in_dim.2), channel_id=1, replica_groups=mesh['gx'=8,'gy'=4,'gz'=16] {'gx','gy'}, dimensions={0} | all-to-all | bytes 524288 | tf_op jit(solution)/shard_map/all_to_all | solution.py:441
  77.0 3.5 %coarse_levels.1 = f32[16,16,128]{2,1,0:T(8,128)} custom-call(s32[2]{0:T(128)S(1)} %pad_add_fusion.place, f32[512,128]{1,0:T(8,128)S(1)} %bitcast.3, f32[16,16,128]{2,1,0:T(8,128)S(1)} %second_level.1.base), custom_call_target="tpu_custom_call" | custom-call | flops 30000000 | bytes 393224 | tf_op jit(solution)/shard_map/coarse_levels/pallas_call | solution.py:378
  (2 shorter events, 0.0 us)
Async XLA Ops:
  1.6 9.6 %collective-permute-start = (f32[15,16,128]{2,1,0:T(8,128)}, f32[15,16,128]{2,1,0:T(8,128)S(1)}, u32[]{:S(2)}, u32[]{:S(2)}) collective-permute-start(f32[15,16,128]{2,1,0:T(8,128)} %get-tuple-element.24), channel_id=1, source_target_pairs={{0,64},{64,128},{128,192},{192,256},{256,320},{320,384},{384,448},... | collective-permute-start | bytes 368648 | tf_op jit(solution)/shard_map/ppermute | solution.py:394
  5.9 7.5 %collective-permute-start.1 = (f32[15,16,128]{2,1,0:T(8,128)}, f32[15,16,128]{2,1,0:T(8,128)S(1)}, u32[]{:S(2)}, u32[]{:S(2)}) collective-permute-start(f32[15,16,128]{2,1,0:T(8,128)} %get-tuple-element.25), channel_id=1, source_target_pairs={{64,0},{128,64},{192,128},{256,192},{320,256},{384,320},{448,384},... | collective-permute-start | bytes 368648 | tf_op jit(solution)/shard_map/ppermute | solution.py:394
  7.2 0.9 %copy-start = (s32[16,16,128]{2,1,0:T(8,128)S(1)}, s32[16,16,128]{2,1,0:T(8,128)}, u32[]{:S(2)}) copy-start(s32[16,16,128]{2,1,0:T(8,128)} %phase.3) | copy-start | bytes 393220
  8.1 0.9 %copy-start.1 = (f32[16,16,128]{2,1,0:T(8,128)S(1)}, f32[16,16,128]{2,1,0:T(8,128)}, u32[]{:S(2)}) copy-start(f32[16,16,128]{2,1,0:T(8,128)} %iterate.3) | copy-start | bytes 393220
  9.0 0.9 %copy-start.2 = (f32[16,16,128]{2,1,0:T(8,128)S(1)}, f32[16,16,128]{2,1,0:T(8,128)}, u32[]{:S(2)}) copy-start(f32[16,16,128]{2,1,0:T(8,128)} %right.3) | copy-start | bytes 393220
  9.9 0.7 copy-start.3
  13.6 7.3 %collective-permute-start.2 = (f32[28,16,128]{2,1,0:T(8,128)S(1)}, f32[28,16,128]{2,1,0:T(8,128)S(1)}, u32[]{:S(2)}, u32[]{:S(2)}) collective-permute-start(f32[28,16,128]{2,1,0:T(8,128)S(1)} %get-tuple-element.27), channel_id=1, source_target_pairs={{0,16},{16,32},{32,48},{1,17},{17,33},{33,49},{2,18},{18,34},{34,5... | collective-permute-start | bytes 688136 | tf_op jit(solution)/shard_map/ppermute | solution.py:394
  15.5 7.2 %collective-permute-start.3 = (f32[28,16,128]{2,1,0:T(8,128)S(1)}, f32[28,16,128]{2,1,0:T(8,128)S(1)}, u32[]{:S(2)}, u32[]{:S(2)}) collective-permute-start(f32[28,16,128]{2,1,0:T(8,128)S(1)} %get-tuple-element.28), channel_id=1, source_target_pairs={{16,0},{32,16},{48,32},{17,1},{33,17},{49,33},{18,2},{34,18},{50,3... | collective-permute-start | bytes 688136 | tf_op jit(solution)/shard_map/ppermute | solution.py:394
  23.5 7.4 %collective-permute-start.4 = (f32[32,512]{1,0:T(8,128)S(1)}, f32[32,512]{1,0:T(8,128)S(1)}, u32[]{:S(2)}, u32[]{:S(2)}) collective-permute-start(f32[32,512]{1,0:T(8,128)S(1)} %get-tuple-element.30), channel_id=1, source_target_pairs={{0,1},{1,2},{2,3},{3,4},{4,5},{5,6},{6,7},{7,8},{8,9},{9,10},{10,1... | collective-permute-start | bytes 196616 | tf_op jit(solution)/shard_map/ppermute | solution.py:394
  27.1 9.7 %collective-permute-start.5 = (f32[32,512]{1,0:T(8,128)S(1)}, f32[32,512]{1,0:T(8,128)S(1)}, u32[]{:S(2)}, u32[]{:S(2)}) collective-permute-start(f32[32,512]{1,0:T(8,128)S(1)} %get-tuple-element.31), channel_id=1, source_target_pairs={{1,0},{2,1},{3,2},{4,3},{5,4},{6,5},{7,6},{8,7},{9,8},{10,9},{11,1... | collective-permute-start | bytes 196616 | tf_op jit(solution)/shard_map/ppermute | solution.py:394
  37.7 16.3 %collective-permute-start.6 = (f32[16,128]{1,0:T(8,128)S(1)}, f32[16,128]{1,0:T(8,128)S(1)}, u32[]{:S(2)}, u32[]{:S(2)}) collective-permute-start(f32[16,128]{1,0:T(8,128)S(1)} %get-tuple-element.33), channel_id=1, source_target_pairs={{0,1},{1,2},{2,3},{3,4},{4,5},{5,6},{6,7},{7,8},{8,9},{9,10},{10,1... | collective-permute-start | bytes 24584 | tf_op jit(solution)/shard_map/ppermute | solution.py:394
  40.3 13.7 %collective-permute-start.7 = (f32[16,128]{1,0:T(8,128)S(1)}, f32[16,128]{1,0:T(8,128)S(1)}, u32[]{:S(2)}, u32[]{:S(2)}) collective-permute-start(f32[16,128]{1,0:T(8,128)S(1)} %get-tuple-element.34), channel_id=1, source_target_pairs={{1,0},{2,1},{3,2},{4,3},{5,4},{6,5},{7,6},{8,7},{9,8},{10,9},{11,1... | collective-permute-start | bytes 24584 | tf_op jit(solution)/shard_map/ppermute | solution.py:394

commit v4 on v3

--- a/solution.py
+++ b/solution.py
@@ -77,25 +77,7 @@
     return k
 
 
-def send_x(table, phase, iterate, right, to_up, to_down, values, upper, lower, sems):
-    copies = [
-        pltpu.make_async_copy(table, values, sems.at[0]),
-        pltpu.make_async_copy(phase.at[10:16], upper, sems.at[1]),
-        pltpu.make_async_copy(phase.at[0:6], lower, sems.at[2]),
-        pltpu.make_async_copy(iterate.at[11:16], to_up.at[6:11], sems.at[3]),
-        pltpu.make_async_copy(iterate.at[0:5], to_down.at[6:11], sems.at[4]),
-        pltpu.make_async_copy(right.at[12:16], to_up.at[11:15], sems.at[5]),
-        pltpu.make_async_copy(right.at[0:4], to_down.at[11:15], sems.at[6]),
-    ]
-    for copy in copies:
-        copy.start()
-    for copy in copies:
-        copy.wait()
-    to_up[0:6] = lookup(upper[...], values)
-    to_down[0:6] = lookup(lower[...], values)
-
-
-def keep_fields(table, phase, iterate, right, fields, values, phases, sems):
+def send_x(table, phase, iterate, right, fields, to_up, to_down, values, phases, sems):
     copies = [
         pltpu.make_async_copy(table, values, sems.at[0]),
         pltpu.make_async_copy(phase, phases, sems.at[1]),
@@ -106,7 +88,15 @@
         copy.start()
     for copy in copies:
         copy.wait()
-    fields[0] = lookup(phases[...], values)
+    p = phases[...]
+    k = jnp.zeros(p.shape, F32)
+    for index in range(4):
+        k = jnp.where(p == index, values[index], k)
+    fields[0] = k
+    for field in range(3):
+        h, a, b = HALO[field], ROWS[field], ROWS[field + 1]
+        to_up[a:b] = fields[field, 16 - h : 16]
+        to_down[a:b] = fields[field, 0:h]
 
 
 def pack_y(fields, from_down, from_up, ext, to_up, to_down):
@@ -152,7 +142,17 @@
     return pltpu.roll(x, shift, 1) if shift else x
 
 
-def bands_xy(full, xy, bands):
+def bands_xy(place, full, xy, patterns, bands):
+    row = iota((192, 512), 0)
+    cell = iota((192, 512), 1)
+    cell_x = (cell >> 6) * 4 + ((cell >> 2) & 3)
+    cell_y = ((cell >> 4) & 3) * 4 + (cell & 3)
+    for level in range(3):
+        at_x = place[0] * (4 >> level) - 4 + (row >> 4)
+        at_y = place[1] * (4 >> level) - 4 + (row & 15)
+        found = ((cell_x >> level) == at_x) & ((cell_y >> level) == at_y)
+        patterns[192 * level : 192 * level + 192, :] = ones_where(found)
+
     def in_y(x, carry):
         k = full[0, x]
         v = full[1, x]
@@ -225,9 +225,7 @@
         ref[...] = select_lanes(sums, jnp.where(place, scale, 0.0).astype(BF16))
 
 
-def fine_level(
-    full, xy, from_down, from_up, base, res_two, coef_two, coef, side, res, inv, corr, corr_next, yz_c, yz_kc, pairs, narrow
-):
+def fine_residual(full, xy, from_down, from_up, coef, res, inv, side, sides_kv, product):
     lane = iota((32, 128), 1)
     for x in range(28):
         group, first = 128 * (x // 8), 16 * (x % 8)
@@ -242,9 +240,9 @@
         coef[x, :, 128:256] = tiles[0]
         side[0, x] = tiles[1]
         side[1, x] = tiles[2]
-        corr[x, :, 0:128] = band(tiles[0], 0)
-        corr[x, :, 128:256] = band(tiles[1], 0)
-        corr_next[x, :, 0:128] = band(tiles[0] * tiles[1], 0)
+        sides_kv[x, :, 0:128] = band(tiles[0], 0)
+        sides_kv[x, :, 128:256] = band(tiles[1], 0)
+        product[x] = band(tiles[0] * tiles[1], 0)
 
     for x in (0, 1, 26, 27):
         res[x] = jnp.zeros((32, 256), F32)
@@ -253,11 +251,10 @@
         return (ref[x - 1] + ref[x + 1]) + 2.0 * ref[x]
 
     def cells(x, carry):
-        sides = over_x(corr, x)
-        product = (corr_next[x - 1, :, 0:128] + corr_next[x + 1, :, 0:128]) + 2.0 * corr_next[x, :, 0:128]
+        sides = over_x(sides_kv, x)
         tu_k = band(jnp.concatenate([xy[0, x], sides[:, 0:128]], axis=1), 1)
         tu_v = band(jnp.concatenate([xy[1, x], sides[:, 128:256]], axis=1), 1)
-        tu_kv = band(jnp.concatenate([xy[2, x], product], axis=1), 1)
+        tu_kv = band(jnp.concatenate([xy[2, x], over_x(product, x)], axis=1), 1)
         k = coef[x]
         v = jnp.concatenate([full[1, x], side[0, x]], axis=1)
         diagonal = 6.0 * k + 0.125 * tu_k
@@ -268,6 +265,11 @@
 
     lax.fori_loop(2, 26, cells, 0, unroll=2)
 
+
+def fine_sweeps(full, coef, res, inv, base, corr, corr_next, yz_c, yz_kc, pairs, narrow, spread):
+    def over_x(ref, x):
+        return (ref[x - 1] + ref[x + 1]) + 2.0 * ref[x]
+
     def first_sweep(x, carry):
         c = inv[x] * res[x]
         corr[x] = c
@@ -290,6 +292,25 @@
         return carry
 
     lax.fori_loop(5, 23, second_bands, 0, unroll=2)
+
+    halves = ones_where((iota((256, 128), 0) >> 1) == iota((256, 128), 1))
+
+    def coarse(ref, scale):
+        def pair(x, carry):
+            pairs[pl.ds(pl.multiple_of(32 * x, 32), 32), :] = ref[2 * x] + ref[2 * x + 1]
+            return carry
+
+        lax.fori_loop(0, 14, pair, 0, unroll=2)
+        narrow[...] = select_lanes(pairs[...], halves)
+        summed = narrow[pl.ds(0, 224, stride=2), :] + narrow[pl.ds(1, 224, stride=2), :]
+        return (scale * summed).reshape(14, 16, 128)
+
+    corr_two = smooth_small(coarse(res, 0.5), coarse(coef, 0.125), 3)
+    doubled = ones_where(iota((128, 128), 0) == (iota((128, 128), 1) >> 1))
+    wide = select_lanes(corr_two[3:11].reshape(128, 128), doubled).reshape(8, 16, 128)
+    rows = wide[:, 0:8, :].reshape(64, 128)
+    spread[pl.ds(0, 64, stride=2), :] = rows
+    spread[pl.ds(1, 64, stride=2), :] = rows
 
     def third(x, carry):
         c = relax(
@@ -300,72 +321,38 @@
             (yz_c[x - 1, 0:16, 0:128] + yz_c[x + 1, 0:16, 0:128]) + 2.0 * yz_c[x, 0:16, 0:128],
             (yz_kc[x - 1, 0:16, 0:128] + yz_kc[x + 1, 0:16, 0:128]) + 2.0 * yz_kc[x, 0:16, 0:128],
         )
-        base[x - 6] = full[1, x, 0:16, :] + c
+        block = x - 6
+        base[block] = full[1, x, 0:16, :] + (c + spread[pl.ds(pl.multiple_of(16 * (block // 2), 16), 16), :])
         return carry
 
     lax.fori_loop(6, 22, third, 0, unroll=2)
 
-    halves = ones_where((iota((256, 128), 0) >> 1) == iota((256, 128), 1))
-    for ref, scale, out in ((res, 0.5, res_two), (coef, 0.125, coef_two)):
-
-        def pair(x, carry):
-            pairs[pl.ds(pl.multiple_of(32 * x, 32), 32), :] = ref[2 * x] + ref[2 * x + 1]
-            return carry
-
-        lax.fori_loop(0, 14, pair, 0, unroll=2)
-        narrow[...] = select_lanes(pairs[...], halves)
-        summed = narrow[pl.ds(0, 224, stride=2), :] + narrow[pl.ds(1, 224, stride=2), :]
-        out[...] = (scale * summed).reshape(14, 16, 128)
-
-
-def second_level(res_two, coef_two, base, out, spread):
-    corr_two = smooth_small(res_two[...], coef_two[...], 3)
-    doubled = ones_where(iota((128, 128), 0) == (iota((128, 128), 1) >> 1))
-    wide = select_lanes(corr_two[3:11].reshape(128, 128), doubled).reshape(8, 16, 128)
-    rows = wide[:, 0:8, :].reshape(64, 128)
-    spread[pl.ds(0, 64, stride=2), :] = rows
-    spread[pl.ds(1, 64, stride=2), :] = rows
-    for x in range(16):
-        start = 16 * (x // 2)
-        out[x] = base[x] + spread[start : start + 16, :]
-
-
-def coarse_levels(place, plane, base, out):
-    row = iota((192, 512), 0)
-    cell = iota((192, 512), 1)
-    cell_x = (cell >> 6) * 4 + ((cell >> 2) & 3)
-    cell_y = ((cell >> 4) & 3) * 4 + (cell & 3)
-    parts = split3(plane[...])
-    windows = []
-    for level in range(3):
-        at_x = place[0] * (4 >> level) - 4 + (row >> 4)
-        at_y = place[1] * (4 >> level) - 4 + (row & 15)
-        pattern = ones_where(((cell_x >> level) == at_x) & ((cell_y >> level) == at_y))
-        found = [jnp.dot(pattern, part, preferred_element_type=F32) for part in parts]
-        windows.append(found[0] + (found[1] + found[2]))
-    source = iota((128, 128), 0)
-    lane = iota((128, 128), 1)
-    residual = jnp.zeros((192, 128), F32)
-    coef = jnp.zeros((192, 128), F32)
-    for level, start in enumerate((0, 64, 96)):
-        parts = split3(windows[level])
-        target = start + ((source & 63) >> level)
-        to_res = ones_where((source < 64) & (lane == target), 0.5**level)
-        to_coef = ones_where((source >= 64) & (lane == target), 0.125**level)
-        for part in parts:
-            residual = residual + jnp.dot(part, to_res, preferred_element_type=F32)
-            coef = coef + jnp.dot(part, to_coef, preferred_element_type=F32)
-    corr = smooth_small(residual.reshape(12, 16, 128), coef.reshape(12, 16, 128), 4)
-    mine = corr[4:8].reshape(64, 128)
-    total = base[...].reshape(256, 128)
-    row = iota((256, 64), 0)
-    found = iota((256, 64), 1)
-    for level, start in enumerate((16, 72, 100)):
-        shift = 2 + level
-        spread = ones_where(source == start + (lane >> shift))
-        at = ((row >> 4) >> shift) * 16 + 4 + ((row & 15) >> shift)
-        total = total + select_rows(ones_where(found == at), select_lanes(mine, spread))
-    out[...] = total.reshape(16, 16, 128)
+
+def coarse_levels(patterns, plane, base, out):
+    found = jnp.dot(patterns[...], jnp.concatenate(split3(plane[...]), axis=1), preferred_element_type=F32)
+    found = found[:, 0:128] + (found[:, 128:256] + found[:, 256:384])
+    windows = jnp.concatenate([found[192 * level : 192 * level + 192, :] for level in range(3)], axis=1)
+    source = iota((384, 256), 0)
+    lane = iota((384, 256), 1)
+    level = source >> 7
+    is_coef = (source >> 6) & 1
+    start = jnp.where(level == 0, 0, jnp.where(level == 1, 64, 96))
+    scale = jnp.where(is_coef == 1, jnp.where(level == 0, 1.0, jnp.where(level == 1, 0.125, 0.125**2)), 1.0)
+    scale = jnp.where(is_coef == 0, jnp.where(level == 0, 1.0, jnp.where(level == 1, 0.5, 0.25)), scale)
+    at = is_coef * 128 + start + ((source & 63) >> level)
+    both = select_lanes(windows, jnp.where(lane == at, scale, 0.0).astype(BF16))
+    corr = smooth_small(both[:, 0:128].reshape(12, 16, 128), both[:, 128:256].reshape(12, 16, 128), 4)
+    source = iota((128, 384), 0)
+    lane = iota((128, 384), 1)
+    level = lane >> 7
+    start = jnp.where(level == 0, 16, jnp.where(level == 1, 72, 100))
+    wide = select_lanes(corr[4:8].reshape(64, 128), ones_where(source == start + ((lane & 127) >> (level + 2))))
+    wide = jnp.concatenate([wide[:, 128 * level : 128 * level + 128] for level in range(3)], axis=0)
+    row = iota((256, 192), 0)
+    found = iota((256, 192), 1)
+    shift = (found >> 6) + 2
+    at = ((row >> 4) >> shift) * 16 + 4 + ((row & 15) >> shift)
+    out[...] = base[...] + select_rows(ones_where((found & 63) == at), wide).reshape(16, 16, 128)
 
 
 VMEM = pl.BlockSpec(memory_space=pltpu.VMEM)
@@ -377,7 +364,7 @@
     moved = 4 * sum(x.size for x in ins)
     return pl.pallas_call(
         kernel,
-        out_shape=[jax.ShapeDtypeStruct(shape, F32) for shape in outs],
+        out_shape=[out if isinstance(out, jax.ShapeDtypeStruct) else jax.ShapeDtypeStruct(out, F32) for out in outs],
         in_specs=[first] + [rest] * (len(ins) - 1),
         out_specs=[VMEM] * len(outs),
         scratch_shapes=[pltpu.VMEM(shape, F32) if isinstance(shape, tuple) else shape for shape in scratch],
@@ -396,50 +383,52 @@
 
 def on_device(right, iterate, phase, table):
     block = (16, 16, 128)
-    inputs = [table, phase, iterate, right]
-    values = pltpu.SMEM((4,), F32)
-    to_up, to_down = call(
+    fields, to_up, to_down = call(
         send_x,
-        [(15, 16, 128)] * 2,
-        inputs,
-        scratch=[values, pltpu.VMEM((6, 16, 128), jnp.int32), pltpu.VMEM((6, 16, 128), jnp.int32), pltpu.SemaphoreType.DMA((7,))],
+        [(3, *block), (15, 16, 128), (15, 16, 128)],
+        [table, phase, iterate, right],
+        scratch=[pltpu.SMEM((4,), F32), pltpu.VMEM(block, jnp.int32), pltpu.SemaphoreType.DMA((4,))],
         first=HBM,
         rest=HBM,
         grant=60,
     )
     from_down, from_up = swap("gx", to_up, to_down)
-    (fields,) = call(
-        keep_fields,
-        [(3, *block)],
-        inputs,
-        scratch=[values, pltpu.VMEM(block, jnp.int32), pltpu.SemaphoreType.DMA((4,))],
-        first=HBM,
-        rest=HBM,
-    )
     ext, to_up, to_down = call(pack_y, [(3, 28, 16, 128), (28, 16, 128), (28, 16, 128)], [fields, from_down, from_up])
     from_down, from_up = swap("gy", to_up, to_down)
     planes = (3, 28, 32, 128)
     full, to_up, to_down = call(pack_z, [planes, (32, 512), (32, 512)], [ext, from_down, from_up])
     from_down, from_up = swap("gz", to_up, to_down)
-    (xy,) = call(bands_xy, [planes], [full], scratch=[planes], flops=30000000)
+    place = jnp.stack([lax.axis_index("gx"), lax.axis_index("gy")]).astype(jnp.int32)
+    xy, patterns = call(
+        bands_xy,
+        [planes, jax.ShapeDtypeStruct((576, 512), BF16)],
+        [place, full],
+        scratch=[planes],
+        first=SMEM,
+        flops=30000000,
+    )
     z_sides = [from_down, from_up]
     own, to_up, to_down = call(own_residual, [(16, 128)] * 3, [full, xy, *z_sides], scratch=[(128, 128)])
     from_down, from_up = swap("gz", to_up, to_down)
-    wide = (28, 32, 256)
-    base, res_two, coef_two = call(
-        fine_level,
-        [block, (14, 16, 128), (14, 16, 128)],
-        [full, xy, *z_sides],
-        scratch=[wide, (2, 28, 32, 128), wide, wide, wide, wide, wide, wide, (448, 256), (448, 128)],
-        flops=60000000,
-    )
-    (base,) = call(second_level, [block], [res_two, coef_two, base], scratch=[(128, 128)], flops=30000000)
-    place = jnp.stack([lax.axis_index("gx"), lax.axis_index("gy")]).astype(jnp.int32)
-    own, from_down, from_up, base, place = lax.optimization_barrier((own, from_down, from_up, base, place))
     mine = own + from_down + from_up
     chunks = lax.axis_size("gx") * lax.axis_size("gy")
     plane = lax.all_to_all(jnp.broadcast_to(mine[None], (chunks, 16, 128)), ("gx", "gy"), 0, 0, tiled=True)
-    (out,) = call(coarse_levels, [block], [place, plane.reshape(chunks * 16, 128), base], first=SMEM, flops=30000000)
+    wide = (28, 32, 256)
+    coef, res, inv = call(
+        fine_residual,
+        [wide] * 3,
+        [full, xy, *z_sides],
+        scratch=[(2, 28, 32, 128), wide, (28, 32, 128)],
+        flops=30000000,
+    )
+    (base,) = call(
+        fine_sweeps,
+        [block],
+        [full, coef, res, inv],
+        scratch=[wide, wide, wide, wide, (448, 256), (448, 128), (128, 128)],
+        flops=60000000,
+    )
+    (out,) = call(coarse_levels, [block], [patterns, plane.reshape(chunks * 16, 128), base], flops=30000000)
     return out
 
 

time: 82 us -> 76.7 us (0.935); the launches traced: 80.4 us -> 76.3 us
  blocking collectives: 22.9 us -> 0 us
  starting transfers between devices: 24.6 us -> 35.4 us
  waiting for transfers between devices: 11.6 us -> 21.7 us
  local copies, waits for them, and re-layouts: 3.38 us -> 1.72 us
    all_to_all x1 -> x0, blocking collectives: 22.9 us -> none  [on_device(): lax.all_to_all(jnp.broadcast_to(mine[None], (chunks, 16, 128)), ('gx', 'g...]
    all_to_all x0 -> x1, starting transfers between devices: none -> 10.8 us  [on_device(): lax.all_to_all(jnp.broadcast_to(mine[None], (chunks, 16, 128)), ('gx', 'g...]
    ppermute x8, waiting for transfers between devices: 11.6 us -> 19.2 us  [swap(): return (lax.ppermute(to_up, axis, up), lax.ppermute(to_down, axis, down))]
    all_to_all x0 -> x1, waiting for transfers between devices: none -> 2.48 us  [on_device(): lax.all_to_all(jnp.broadcast_to(mine[None], (chunks, 16, 128)), ('gx', 'g...]
    unnamed x8 -> x6, local copies, waits for them, and re-layouts: 3.36 us -> 1 us
    pallas_call x9 -> x8, Pallas kernels: 17.7 us -> 17.2 us  [call(): pl.pallas_call(kernel, out_shape=[out if isinstance(out, jax.ShapeDtypeSt...]
  transfers between devices with their start and end apart: 8 -> 9, of which waited for: 4 -> 7; matrix products, arithmetic and copies ran while one was open for 0% -> 0% of each run, Pallas kernels for 13% -> 14%
where the time goes in v4:
time: 76.7 us; the launch traced here: 76.3 us
  starting transfers between devices  35.4 us (46%)
  waiting for transfers between devices  21.7 us (28%)
  Pallas kernels  17.2 us (22%)
  local copies, waits for them, and re-layouts  1.72 us (2%)
    ppermute x8, starting transfers between devices, swap(): return (lax.ppermute(to_up, axis, up), lax.ppermute(to_down, axis, down))  24.6 us
    ppermute x8, waiting for transfers between devices, swap(): return (lax.ppermute(to_up, axis, up), lax.ppermute(to_down, axis, down))  19.2 us
    pallas_call x8, Pallas kernels, call(): pl.pallas_call(kernel, out_shape=[out if isinstance(out, jax.ShapeDtypeSt...  17.2 us
    all_to_all x1, starting transfers between devices, on_device(): lax.all_to_all(jnp.broadcast_to(mine[None], (chunks, 16, 128)), ('gx', 'g...  10.8 us
    all_to_all x1, waiting for transfers between devices, on_device(): lax.all_to_all(jnp.broadcast_to(mine[None], (chunks, 16, 128)), ('gx', 'g...  2.48 us
  transfers between devices with their start and end apart: 9, of which 7 were waited for; matrix products, arithmetic and copies ran while one was open for 0% of the time, Pallas kernels for 14%

profile of v4, /device:TPU:56, one launch (start us, length us, event | category | flops | bytes accessed | tf_op | source)
XLA Modules:
  0.0 76.3 jit_solution(17115806454407435835)
XLA Ops:
  0.0 1.9 %send_x.1 = (f32[3,16,16,128]{3,2,1,0:T(8,128)}, f32[15,16,128]{2,1,0:T(8,128)}, f32[15,16,128]{2,1,0:T(8,128)}) custom-call(f32[4]{0:T(128)} %table.1, s32[16,16,128]{2,1,0:T(8,128)} %phase.1, f32[16,16,128]{2,1,0:T(8,128)} %iterate.1, f32[16,16,128]{2,1,0:T(8,128)} %right.1), custom_call_target="tpu_custom_call" | custom-call | flops 1000000 | bytes 393232 | tf_op jit(solution)/shard_map/send_x/pallas_call | solution.py:365
  1.9 4.3 %collective-permute-start = (f32[15,16,128]{2,1,0:T(8,128)}, f32[15,16,128]{2,1,0:T(8,128)S(1)}, u32[]{:S(2)}, u32[]{:S(2)}) collective-permute-start(f32[15,16,128]{2,1,0:T(8,128)} %get-tuple-element.23), channel_id=1, source_target_pairs={{0,64},{64,128},{128,192},{192,256},{256,320},{320,384},{384,448},... | collective-permute-start | bytes 368648 | tf_op jit(solution)/shard_map/ppermute | solution.py:381
  6.2 1.3 %collective-permute-start.1 = (f32[15,16,128]{2,1,0:T(8,128)}, f32[15,16,128]{2,1,0:T(8,128)S(1)}, u32[]{:S(2)}, u32[]{:S(2)}) collective-permute-start(f32[15,16,128]{2,1,0:T(8,128)} %get-tuple-element.24), channel_id=1, source_target_pairs={{64,0},{128,64},{192,128},{256,192},{320,256},{384,320},{448,384},... | collective-permute-start | bytes 368648 | tf_op jit(solution)/shard_map/ppermute | solution.py:381
  7.5 1.6 %collective-permute-done.from_down = f32[15,16,128]{2,1,0:T(8,128)S(1)} collective-permute-done((f32[15,16,128]{2,1,0:T(8,128)}, f32[15,16,128]{2,1,0:T(8,128)S(1)}, u32[]{:S(2)}, u32[]{:S(2)}) %collective-permute-start) | collective-permute-done | bytes 122912 | tf_op jit(solution)/shard_map/ppermute | solution.py:381
  9.1 4.6 %collective-permute-done.1.from_up = f32[15,16,128]{2,1,0:T(8,128)S(1)} collective-permute-done((f32[15,16,128]{2,1,0:T(8,128)}, f32[15,16,128]{2,1,0:T(8,128)S(1)}, u32[]{:S(2)}, u32[]{:S(2)}) %collective-permute-start.1) | collective-permute-done | bytes 122912 | tf_op jit(solution)/shard_map/ppermute | solution.py:381
  13.7 0.0 copy-start.2
  13.7 1.0 %copy-done.2 = f32[3,16,16,128]{3,2,1,0:T(8,128)S(1)} copy-done((f32[3,16,16,128]{3,2,1,0:T(8,128)S(1)}, f32[3,16,16,128]{3,2,1,0:T(8,128)}, u32[]{:S(2)}) %copy-start.2) | copy-done | bytes 393240
  14.7 0.1 pack_y.1
  14.9 1.9 %collective-permute-start.2 = (f32[28,16,128]{2,1,0:T(8,128)S(1)}, f32[28,16,128]{2,1,0:T(8,128)S(1)}, u32[]{:S(2)}, u32[]{:S(2)}) collective-permute-start(f32[28,16,128]{2,1,0:T(8,128)S(1)} %get-tuple-element.26), channel_id=1, source_target_pairs={{0,16},{16,32},{32,48},{1,17},{17,33},{33,49},{2,18},{18,34},{34,5... | collective-permute-start | bytes 688136 | tf_op jit(solution)/shard_map/ppermute | solution.py:381
  16.8 3.6 %collective-permute-start.3 = (f32[28,16,128]{2,1,0:T(8,128)S(1)}, f32[28,16,128]{2,1,0:T(8,128)S(1)}, u32[]{:S(2)}, u32[]{:S(2)}) collective-permute-start(f32[28,16,128]{2,1,0:T(8,128)S(1)} %get-tuple-element.27), channel_id=1, source_target_pairs={{16,0},{32,16},{48,32},{17,1},{33,17},{49,33},{18,2},{34,18},{50,3... | collective-permute-start | bytes 688136 | tf_op jit(solution)/shard_map/ppermute | solution.py:381
  20.4 1.8 %collective-permute-done.2.from_down = f32[28,16,128]{2,1,0:T(8,128)S(1)} collective-permute-done((f32[28,16,128]{2,1,0:T(8,128)S(1)}, f32[28,16,128]{2,1,0:T(8,128)S(1)}, u32[]{:S(2)}, u32[]{:S(2)}) %collective-permute-start.2) | collective-permute-done | bytes 229408 | tf_op jit(solution)/shard_map/ppermute | solution.py:381
  22.2 1.8 %collective-permute-done.3.from_up = f32[28,16,128]{2,1,0:T(8,128)S(1)} collective-permute-done((f32[28,16,128]{2,1,0:T(8,128)S(1)}, f32[28,16,128]{2,1,0:T(8,128)S(1)}, u32[]{:S(2)}, u32[]{:S(2)}) %collective-permute-start.3) | collective-permute-done | bytes 229408 | tf_op jit(solution)/shard_map/ppermute | solution.py:381
  24.0 0.8 %pack_z.1 = (f32[3,28,32,128]{3,2,1,0:T(8,128)S(1)}, f32[32,512]{1,0:T(8,128)S(1)}, f32[32,512]{1,0:T(8,128)S(1)}) custom-call(f32[3,28,16,128]{3,2,1,0:T(8,128)S(1)} %get-tuple-element.25.ext, f32[28,16,128]{2,1,0:T(8,128)S(1)} %collective-permute-done.2.from_down, f32[28,16,128]{2,1,0:T(8,128)S(1)} %collective-permute-done.3.from_up), custom_call_target="tpu_custom_call" | custom-call | flops 1000000 | bytes 1146880 | tf_op jit(solution)/shard_map/pack_z/pallas_call | solution.py:365
  24.8 3.6 %collective-permute-start.4 = (f32[32,512]{1,0:T(8,128)S(1)}, f32[32,512]{1,0:T(8,128)S(1)}, u32[]{:S(2)}, u32[]{:S(2)}) collective-permute-start(f32[32,512]{1,0:T(8,128)S(1)} %get-tuple-element.31), channel_id=1, source_target_pairs={{0,1},{1,2},{2,3},{3,4},{4,5},{5,6},{6,7},{7,8},{8,9},{9,10},{10,1... | collective-permute-start | bytes 196616 | tf_op jit(solution)/shard_map/ppermute | solution.py:381
  28.4 3.1 %collective-permute-start.5 = (f32[32,512]{1,0:T(8,128)S(1)}, f32[32,512]{1,0:T(8,128)S(1)}, u32[]{:S(2)}, u32[]{:S(2)}) collective-permute-start(f32[32,512]{1,0:T(8,128)S(1)} %get-tuple-element.32), channel_id=1, source_target_pairs={{1,0},{2,1},{3,2},{4,3},{5,4},{6,5},{7,6},{8,7},{9,8},{10,9},{11,1... | collective-permute-start | bytes 196616 | tf_op jit(solution)/shard_map/ppermute | solution.py:381
  31.5 0.1 pad_add_fusion.place
  31.6 1.3 %bands_xy.1 = (f32[3,28,32,128]{3,2,1,0:T(8,128)S(1)}, bf16[576,512]{1,0:T(8,128)(2,1)S(1)}) custom-call(s32[2]{0:T(128)S(1)} %pad_add_fusion.place, f32[3,28,32,128]{3,2,1,0:T(8,128)S(1)} %get-tuple-element.28.full), custom_call_target="tpu_custom_call" | custom-call | flops 30000000 | bytes 1376264 | tf_op jit(solution)/shard_map/bands_xy/pallas_call | solution.py:365
  33.0 0.0 copy-start
  33.0 0.0 collective-permute-done.4.from_down
  33.0 5.1 %collective-permute-done.5.from_up = f32[32,512]{1,0:T(8,128)S(1)} collective-permute-done((f32[32,512]{1,0:T(8,128)S(1)}, f32[32,512]{1,0:T(8,128)S(1)}, u32[]{:S(2)}, u32[]{:S(2)}) %collective-permute-start.5) | collective-permute-done | bytes 65568 | tf_op jit(solution)/shard_map/ppermute | solution.py:381
  38.1 0.9 %own_residual.1 = (f32[16,128]{1,0:T(8,128)S(1)}, f32[16,128]{1,0:T(8,128)S(1)}, f32[16,128]{1,0:T(8,128)S(1)}) custom-call(f32[3,28,32,128]{3,2,1,0:T(8,128)S(1)} %get-tuple-element.28.full, f32[3,28,32,128]{3,2,1,0:T(8,128)S(1)} %get-tuple-element.30.xy, f32[32,512]{1,0:T(8,128)S(1)} %collective-permute-done.4.from_down, ...), custom_call_target="tpu_custom_call" | custom-call | flops 1000000 | bytes 2883584 | tf_op jit(solution)/shard_map/own_residual/pallas_call | solution.py:365
  39.0 0.0 copy-done
  39.0 2.6 %collective-permute-start.6 = (f32[16,128]{1,0:T(8,128)S(1)}, f32[16,128]{1,0:T(8,128)S(1)}, u32[]{:S(2)}, u32[]{:S(2)}) collective-permute-start(f32[16,128]{1,0:T(8,128)S(1)} %get-tuple-element.34), channel_id=1, source_target_pairs={{0,1},{1,2},{2,3},{3,4},{4,5},{5,6},{6,7},{7,8},{8,9},{9,10},{10,1... | collective-permute-start | bytes 24584 | tf_op jit(solution)/shard_map/ppermute | solution.py:381
  41.6 4.1 %collective-permute-start.7 = (f32[16,128]{1,0:T(8,128)S(1)}, f32[16,128]{1,0:T(8,128)S(1)}, u32[]{:S(2)}, u32[]{:S(2)}) collective-permute-start(f32[16,128]{1,0:T(8,128)S(1)} %get-tuple-element.35), channel_id=1, source_target_pairs={{1,0},{2,1},{3,2},{4,3},{5,4},{6,5},{7,6},{8,7},{9,8},{10,9},{11,1... | collective-permute-start | bytes 24584 | tf_op jit(solution)/shard_map/ppermute | solution.py:381
  45.7 0.0 collective-permute-done.6
  45.7 4.4 %collective-permute-done.7 = f32[16,128]{1,0:T(8,128)S(1)} collective-permute-done((f32[16,128]{1,0:T(8,128)S(1)}, f32[16,128]{1,0:T(8,128)S(1)}, u32[]{:S(2)}, u32[]{:S(2)}) %collective-permute-start.7) | collective-permute-done | bytes 8224 | tf_op jit(solution)/shard_map/ppermute | solution.py:381
  50.1 0.7 broadcast_in_dim.2
  50.9 10.8 %all-to-all-start = ((f32[32,16,128]{2,1,0:T(8,128)}), f32[32,16,128]{2,1,0:T(8,128)S(1)}, u32[]{:S(2)}, u32[]{:S(2)}) async-start(f32[32,16,128]{2,1,0:T(8,128)} %broadcast_in_dim.2), calls=%async_computation | async-start | bytes 524288 | tf_op jit(solution)/shard_map/all_to_all | solution.py:415
  61.6 3.3 %fine_residual.1 = (f32[28,32,256]{2,1,0:T(8,128)S(1)}, f32[28,32,256]{2,1,0:T(8,128)S(1)}, f32[28,32,256]{2,1,0:T(8,128)S(1)}) custom-call(f32[3,28,32,128]{3,2,1,0:T(8,128)S(1)} %get-tuple-element.28.full, f32[3,28,32,128]{3,2,1,0:T(8,128)S(1)} %get-tuple-element.30.xy, f32[32,512]{1,0:T(8,128)S(1)} %collective-permute-done.4.from_down, ...), custom_call_target="tpu_custom_call" | custom-call | flops 30000000 | bytes 2883584 | tf_op jit(solution)/shard_map/fine_residual/pallas_call | solution.py:365
  64.9 0.0 copy-start.1
  64.9 6.1 %fine_sweeps.1.base = f32[16,16,128]{2,1,0:T(8,128)S(1)} custom-call(f32[3,28,32,128]{3,2,1,0:T(8,128)S(1)} %get-tuple-element.28.full, f32[28,32,256]{2,1,0:T(8,128)S(1)} %get-tuple-element.36.coef, f32[28,32,256]{2,1,0:T(8,128)S(1)} %get-tuple-element.37.res, f32[28,32,256]{2,1,0:T(8,128)S(1)} %get-tuple-element.38.inv), custom_call_target="tpu_custom_call" | custom-call | flops 60000000 | bytes 4128768 | tf_op jit(solution)/shard_map/fine_sweeps/pallas_call | solution.py:365
  71.1 2.5 %all-to-all-done = f32[32,16,128]{2,1,0:T(8,128)S(1)} async-done(((f32[32,16,128]{2,1,0:T(8,128)}), f32[32,16,128]{2,1,0:T(8,128)S(1)}, u32[]{:S(2)}, u32[]{:S(2)}) %all-to-all-start) | async-done | bytes 262176 | tf_op jit(solution)/shard_map/all_to_all | solution.py:415
  73.6 0.0 copy-done.1
  73.6 2.7 %coarse_levels.1 = f32[16,16,128]{2,1,0:T(8,128)} custom-call(bf16[576,512]{1,0:T(8,128)(2,1)S(1)} %copy-done.1, f32[512,128]{1,0:T(8,128)S(1)} %bitcast.3, f32[16,16,128]{2,1,0:T(8,128)S(1)} %fine_sweeps.1.base), custom_call_target="tpu_custom_call" | custom-call | flops 30000000 | bytes 1572864 | tf_op jit(solution)/shard_map/coarse_levels/pallas_call | solution.py:365
  (1 shorter events, 0.0 us)
Async XLA Ops:
  1.9 7.2 %collective-permute-start = (f32[15,16,128]{2,1,0:T(8,128)}, f32[15,16,128]{2,1,0:T(8,128)S(1)}, u32[]{:S(2)}, u32[]{:S(2)}) collective-permute-start(f32[15,16,128]{2,1,0:T(8,128)} %get-tuple-element.23), channel_id=1, source_target_pairs={{0,64},{64,128},{128,192},{192,256},{256,320},{320,384},{384,448},... | collective-permute-start | bytes 368648 | tf_op jit(solution)/shard_map/ppermute | solution.py:381
  6.2 7.5 %collective-permute-start.1 = (f32[15,16,128]{2,1,0:T(8,128)}, f32[15,16,128]{2,1,0:T(8,128)S(1)}, u32[]{:S(2)}, u32[]{:S(2)}) collective-permute-start(f32[15,16,128]{2,1,0:T(8,128)} %get-tuple-element.24), channel_id=1, source_target_pairs={{64,0},{128,64},{192,128},{256,192},{320,256},{384,320},{448,384},... | collective-permute-start | bytes 368648 | tf_op jit(solution)/shard_map/ppermute | solution.py:381
  13.7 1.0 %copy-start.2 = (f32[3,16,16,128]{3,2,1,0:T(8,128)S(1)}, f32[3,16,16,128]{3,2,1,0:T(8,128)}, u32[]{:S(2)}) copy-start(f32[3,16,16,128]{3,2,1,0:T(8,128)} %get-tuple-element.22.fields) | copy-start | bytes 1179652
  14.9 7.3 %collective-permute-start.2 = (f32[28,16,128]{2,1,0:T(8,128)S(1)}, f32[28,16,128]{2,1,0:T(8,128)S(1)}, u32[]{:S(2)}, u32[]{:S(2)}) collective-permute-start(f32[28,16,128]{2,1,0:T(8,128)S(1)} %get-tuple-element.26), channel_id=1, source_target_pairs={{0,16},{16,32},{32,48},{1,17},{17,33},{33,49},{2,18},{18,34},{34,5... | collective-permute-start | bytes 688136 | tf_op jit(solution)/shard_map/ppermute | solution.py:381
  16.8 7.2 %collective-permute-start.3 = (f32[28,16,128]{2,1,0:T(8,128)S(1)}, f32[28,16,128]{2,1,0:T(8,128)S(1)}, u32[]{:S(2)}, u32[]{:S(2)}) collective-permute-start(f32[28,16,128]{2,1,0:T(8,128)S(1)} %get-tuple-element.27), channel_id=1, source_target_pairs={{16,0},{32,16},{48,32},{17,1},{33,17},{49,33},{18,2},{34,18},{50,3... | collective-permute-start | bytes 688136 | tf_op jit(solution)/shard_map/ppermute | solution.py:381
  24.8 8.2 %collective-permute-start.4 = (f32[32,512]{1,0:T(8,128)S(1)}, f32[32,512]{1,0:T(8,128)S(1)}, u32[]{:S(2)}, u32[]{:S(2)}) collective-permute-start(f32[32,512]{1,0:T(8,128)S(1)} %get-tuple-element.31), channel_id=1, source_target_pairs={{0,1},{1,2},{2,3},{3,4},{4,5},{5,6},{6,7},{7,8},{8,9},{9,10},{10,1... | collective-permute-start | bytes 196616 | tf_op jit(solution)/shard_map/ppermute | solution.py:381
  28.4 9.7 %collective-permute-start.5 = (f32[32,512]{1,0:T(8,128)S(1)}, f32[32,512]{1,0:T(8,128)S(1)}, u32[]{:S(2)}, u32[]{:S(2)}) collective-permute-start(f32[32,512]{1,0:T(8,128)S(1)} %get-tuple-element.32), channel_id=1, source_target_pairs={{1,0},{2,1},{3,2},{4,3},{5,4},{6,5},{7,6},{8,7},{9,8},{10,9},{11,1... | collective-permute-start | bytes 196616 | tf_op jit(solution)/shard_map/ppermute | solution.py:381
  33.0 6.0 %copy-start = (bf16[576,512]{1,0:T(8,128)(2,1)}, bf16[576,512]{1,0:T(8,128)(2,1)S(1)}, u32[]{:S(2)}) copy-start(bf16[576,512]{1,0:T(8,128)(2,1)S(1)} %get-tuple-element.29.patterns) | copy-start | bytes 1769476
  39.0 6.8 %collective-permute-start.6 = (f32[16,128]{1,0:T(8,128)S(1)}, f32[16,128]{1,0:T(8,128)S(1)}, u32[]{:S(2)}, u32[]{:S(2)}) collective-permute-start(f32[16,128]{1,0:T(8,128)S(1)} %get-tuple-element.34), channel_id=1, source_target_pairs={{0,1},{1,2},{2,3},{3,4},{4,5},{5,6},{6,7},{7,8},{8,9},{9,10},{10,1... | collective-permute-start | bytes 24584 | tf_op jit(solution)/shard_map/ppermute | solution.py:381
  41.6 8.6 %collective-permute-start.7 = (f32[16,128]{1,0:T(8,128)S(1)}, f32[16,128]{1,0:T(8,128)S(1)}, u32[]{:S(2)}, u32[]{:S(2)}) collective-permute-start(f32[16,128]{1,0:T(8,128)S(1)} %get-tuple-element.35), channel_id=1, source_target_pairs={{1,0},{2,1},{3,2},{4,3},{5,4},{6,5},{7,6},{8,7},{9,8},{10,9},{11,1... | collective-permute-start | bytes 24584 | tf_op jit(solution)/shard_map/ppermute | solution.py:381
  50.9 22.7 %all-to-all-start = ((f32[32,16,128]{2,1,0:T(8,128)}), f32[32,16,128]{2,1,0:T(8,128)S(1)}, u32[]{:S(2)}, u32[]{:S(2)}) async-start(f32[32,16,128]{2,1,0:T(8,128)} %broadcast_in_dim.2), calls=%async_computation | async-start | bytes 524288 | tf_op jit(solution)/shard_map/all_to_all | solution.py:415
  64.9 8.6 %copy-start.1 = (bf16[576,512]{1,0:T(8,128)(2,1)S(1)}, bf16[576,512]{1,0:T(8,128)(2,1)}, u32[]{:S(2)}) copy-start(bf16[576,512]{1,0:T(8,128)(2,1)} %copy-done) | copy-start | bytes 1769476

commit v5 on v4

--- a/solution.py
+++ b/solution.py
@@ -114,13 +114,53 @@
     to_down[:, 15:16, :] = jnp.zeros((28, 1, 128), F32)
 
 
-def pack_z(ext, from_down, from_up, full, to_up, to_down):
+def add_quads(quads, sums, x):
+    if (x - 6) % 4 == 3:
+        for at, f in enumerate(sums):
+            f = f + pltpu.roll(f, 15, 0)
+            f = f + pltpu.roll(f, 14, 0)
+            for tile in range(f.shape[1] // 128):
+                start = 64 * (at * (f.shape[1] // 128) + tile) + 16 * ((x - 6) // 4)
+                quads[start : start + 16, :] = f[:, 128 * tile : 128 * tile + 128]
+
+
+def read_quads(quads):
+    count = quads.shape[0] // 64
+    return jnp.concatenate([quads[pl.ds(64 * at, 16, stride=4), :] for at in range(count)], axis=1)
+
+
+def pack_z(ext, from_down, from_up, full, to_up, to_down, quads):
     for field in range(3):
         h, a, b = HALO[field], ROWS[field], ROWS[field + 1]
         full[field, :, 0:16, :] = ext[field]
         full[field, :, 16 : 16 + h, :] = from_up[:, a:b, :]
         full[field, :, 16 + h : 32 - h, :] = jnp.zeros((28, 16 - 2 * h, 128), F32)
         full[field, :, 32 - h : 32, :] = from_down[:, a:b, :]
+    in_y = {}
+    sums = [None, None]
+    for x in range(5, 23):
+        k = full[0, x]
+        v = full[1, x]
+        in_y[x] = [band(f, 0)[0:16, :] for f in (k, v, k * v)]
+        x = x - 1
+        if x < 6:
+            continue
+        tu = [band((low + high) + 2.0 * f, 1) for low, f, high in zip(in_y.pop(x - 1), in_y[x], in_y[x + 1])]
+        k = full[0, x, 0:16, :]
+        v = full[1, x, 0:16, :]
+        diagonal = 6.0 * k + 0.125 * tu[0]
+        res = full[2, x, 0:16, :] - (v * diagonal + 2.0 * (k * v) - 0.125 * (k * tu[1] + tu[2]))
+        sums = [f if (x - 6) % 4 == 0 else total + f for total, f in zip(sums, (res, k))]
+        add_quads(quads, sums, x)
+    source = iota((256, 128), 0)
+    lane = iota((256, 128), 1)
+    coarse = (source & 127) >> 2
+    base = 64 + (source >> 7) * 16
+    scale = jnp.where(source < 128, F32(0.25), F32(1.0 / 64.0))
+    upper = (lane == base + coarse - 16) & (coarse >= 16) & (coarse <= 30)
+    lower = (lane == base + coarse) & (coarse >= 1) & (coarse <= 15)
+    place = jnp.concatenate([jnp.where(upper, scale, 0.0), jnp.where(lower, scale, 0.0)], axis=1).astype(BF16)
+    level3 = select_lanes(read_quads(quads), place)
     lane = iota((32, 128), 1)
     for group in range(4):
         up = jnp.zeros((32, 128), F32)
@@ -135,6 +175,8 @@
                 down = jnp.where(mine, rolled(cells, first + a), down)
         to_up[:, 128 * group : 128 * group + 128] = up
         to_down[:, 128 * group : 128 * group + 128] = down
+    to_up[0:16, 384:512] += level3[:, 0:128]
+    to_down[0:16, 384:512] += level3[:, 128:256]
 
 
 def rolled(x, shift):
@@ -174,55 +216,49 @@
             xy[field, x] = jnp.zeros((32, 128), F32)
 
 
-def own_residual(full, xy, from_down, from_up, own, to_up, to_down, quads):
-    def edge(cells, shift):
+def own_residual(full, xy, from_down, from_up, chunks, quads):
+    def edge(cells, shift_v, shift_right):
         k = cells
-        v = pltpu.roll(cells, 512 - shift, 1)
-        found = []
+        v = pltpu.roll(cells, 512 - shift_v, 1)
+        found = [k, v, pltpu.roll(cells, 512 - shift_right, 1)]
         for f in (k, v, k * v):
             f = band(f, 0)
             f = f + pltpu.roll(f, 16, 1)
             found.append(f + pltpu.roll(f, 512 - 16, 1))
-        return found
-
-    below = edge(from_down[...], 5)
-    above = edge(from_up[...], 6)
+        return [f[0:16, :] for f in found]
+
+    below = edge(from_down[...], 5, 9)
+    above = edge(from_up[...], 6, 11)
     lane = iota((16, 128), 1)
     sums = [None, None]
     for x in range(6, 22):
         group, first = 128 * (x // 8), 16 * (x % 8)
-        tu = []
-        for field in range(3):
-            cells = xy[field, x, 0:16, :]
-            left = rolled(below[field][0:16, group : group + 128], -first - 5)
-            after = rolled(above[field][0:16, group : group + 128], 127 - first)
-            left = jnp.where(lane == 0, left, pltpu.roll(cells, 1, 1))
-            after = jnp.where(lane == 127, after, pltpu.roll(cells, 127, 1))
-            tu.append((left + after) + 2.0 * cells)
-        k = full[0, x, 0:16, :]
-        v = full[1, x, 0:16, :]
+        beyond = []
+        for low, high in zip(below, above):
+            tile = jnp.where(lane >= 122, rolled(low[:, group : group + 128], 122 - first), 0.0)
+            beyond.append(jnp.where(lane < 6, rolled(high[:, group : group + 128], -first), tile))
+        k, v, right = [jnp.concatenate([full[at, x, 0:16, :], beyond[at]], axis=1) for at in range(3)]
+        tu = [band(jnp.concatenate([xy[at, x, 0:16, :], beyond[3 + at]], axis=1), 1) for at in range(3)]
         diagonal = 6.0 * k + 0.125 * tu[0]
-        res = full[2, x, 0:16, :] - (v * diagonal + 2.0 * (k * v) - 0.125 * (k * tu[1] + tu[2]))
-        for at, f in enumerate((res, k)):
-            sums[at] = f if (x - 6) % 4 == 0 else sums[at] + f
-        if (x - 6) % 4 == 3:
-            for at in range(2):
-                f = sums[at] + pltpu.roll(sums[at], 15, 0)
-                f = f + pltpu.roll(f, 14, 0)
-                start = 64 * at + 16 * ((x - 6) // 4)
-                quads[start : start + 16, :] = f
-    sums = jnp.concatenate([quads[pl.ds(0, 16, stride=4), :], quads[pl.ds(64, 16, stride=4), :]], axis=1)
-    source = iota((256, 128), 0)
-    lane = iota((256, 128), 1)
-    coarse = (source & 127) >> 2
-    base = (source >> 7) * 64
-    scale = jnp.where(source < 128, F32(0.25), F32(1.0 / 64.0))
-    for ref, place in (
-        (own, lane == base + 16 + coarse),
-        (to_up, (lane == base + coarse - 16) & (coarse >= 16)),
-        (to_down, (lane == base + 48 + coarse) & (coarse < 16)),
-    ):
-        ref[...] = select_lanes(sums, jnp.where(place, scale, 0.0).astype(BF16))
+        res = right - (v * diagonal + 2.0 * (k * v) - 0.125 * (k * tu[1] + tu[2]))
+        sums = [f if (x - 6) % 4 == 0 else total + f for total, f in zip(sums, (res, k))]
+        add_quads(quads, sums, x)
+    source = iota((512, 128), 0)
+    lane = iota((512, 128), 1)
+    cell = source & 255
+    coarse = jnp.where(cell < 132, cell >> 2, -1)
+    used = (cell < 132) | (cell >= 252)
+    scale = jnp.where(source < 256, F32(0.25), F32(1.0 / 64.0))
+    place = jnp.where(used & (lane == (source >> 8) * 64 + 16 + coarse), scale, 0.0).astype(BF16)
+    mine = select_lanes(read_quads(quads), place)
+    lane = iota((16, 128), 1)
+    low = from_down[0:16, 384:512]
+    high = from_up[0:16, 384:512]
+    mine = jnp.where(lane < 15, pltpu.roll(low, 64, 1), mine)
+    mine = jnp.where((lane >= 64) & (lane < 79), pltpu.roll(low, 112, 1), mine)
+    mine = jnp.where((lane >= 49) & (lane < 64), pltpu.roll(high, 112, 1), mine)
+    mine = jnp.where(lane >= 113, pltpu.roll(high, 32, 1), mine)
+    chunks[...] = jnp.broadcast_to(mine[None], chunks.shape)
 
 
 def fine_residual(full, xy, from_down, from_up, coef, res, inv, side, sides_kv, product):
@@ -396,7 +432,9 @@
     ext, to_up, to_down = call(pack_y, [(3, 28, 16, 128), (28, 16, 128), (28, 16, 128)], [fields, from_down, from_up])
     from_down, from_up = swap("gy", to_up, to_down)
     planes = (3, 28, 32, 128)
-    full, to_up, to_down = call(pack_z, [planes, (32, 512), (32, 512)], [ext, from_down, from_up])
+    full, to_up, to_down = call(
+        pack_z, [planes, (32, 512), (32, 512)], [ext, from_down, from_up], scratch=[(128, 128)]
+    )
     from_down, from_up = swap("gz", to_up, to_down)
     place = jnp.stack([lax.axis_index("gx"), lax.axis_index("gy")]).astype(jnp.int32)
     xy, patterns = call(
@@ -408,11 +446,9 @@
         flops=30000000,
     )
     z_sides = [from_down, from_up]
-    own, to_up, to_down = call(own_residual, [(16, 128)] * 3, [full, xy, *z_sides], scratch=[(128, 128)])
-    from_down, from_up = swap("gz", to_up, to_down)
-    mine = own + from_down + from_up
-    chunks = lax.axis_size("gx") * lax.axis_size("gy")
-    plane = lax.all_to_all(jnp.broadcast_to(mine[None], (chunks, 16, 128)), ("gx", "gy"), 0, 0, tiled=True)
+    count = lax.axis_size("gx") * lax.axis_size("gy")
+    (chunks,) = call(own_residual, [(count, 16, 128)], [full, xy, *z_sides], scratch=[(256, 128)])
+    plane = lax.all_to_all(chunks, ("gx", "gy"), 0, 0, tiled=True)
     wide = (28, 32, 256)
     coef, res, inv = call(
         fine_residual,
@@ -428,7 +464,7 @@
         scratch=[wide, wide, wide, wide, (448, 256), (448, 128), (128, 128)],
         flops=60000000,
     )
-    (out,) = call(coarse_levels, [block], [patterns, plane.reshape(chunks * 16, 128), base], flops=30000000)
+    (out,) = call(coarse_levels, [block], [patterns, plane.reshape(count * 16, 128), base], flops=30000000)
     return out
 
 

time: 76.7 us -> 69.8 us (0.910)
  starting transfers between devices: 35.4 us -> 28.6 us
  waiting for transfers between devices: 21.7 us -> 16.5 us
  Pallas kernels: 17.2 us -> 22.3 us
    ppermute x8 -> x6, starting transfers between devices: 24.6 us -> 17.9 us  [swap(): return (lax.ppermute(to_up, axis, up), lax.ppermute(to_down, axis, down))]
    ppermute x8 -> x6, waiting for transfers between devices: 19.2 us -> 14 us  [swap(): return (lax.ppermute(to_up, axis, up), lax.ppermute(to_down, axis, down))]
    pallas_call x8, Pallas kernels: 17.2 us -> 22.3 us  [call(): pl.pallas_call(kernel, out_shape=[out if isinstance(out, jax.ShapeDtypeSt...]
    unnamed x6, local copies, waits for them, and re-layouts: 1 us -> 1.81 us
  transfers between devices with their start and end apart: 9 -> 7, of which waited for: 7 -> 6; matrix products, arithmetic and copies ran while one was open for 0% -> 0% of each run, Pallas kernels for 14% -> 16%
where the time goes in v5:
time: 69.8 us; the launch traced here: 69.5 us
  starting transfers between devices  28.6 us (41%)
  Pallas kernels  22.3 us (32%)
  waiting for transfers between devices  16.5 us (24%)
  local copies, waits for them, and re-layouts  1.81 us (3%)
    pallas_call x8, Pallas kernels, call(): pl.pallas_call(kernel, out_shape=[out if isinstance(out, jax.ShapeDtypeSt...  22.3 us
    ppermute x6, starting transfers between devices, swap(): return (lax.ppermute(to_up, axis, up), lax.ppermute(to_down, axis, down))  17.9 us
    ppermute x6, waiting for transfers between devices, swap(): return (lax.ppermute(to_up, axis, up), lax.ppermute(to_down, axis, down))  14 us
    all_to_all x1, starting transfers between devices, on_device(): plane = lax.all_to_all(chunks, ('gx', 'gy'), 0, 0, tiled=True)  10.8 us
    all_to_all x1, waiting for transfers between devices, on_device(): plane = lax.all_to_all(chunks, ('gx', 'gy'), 0, 0, tiled=True)  2.48 us
    unnamed x6, local copies, waits for them, and re-layouts  1.81 us
  transfers between devices with their start and end apart: 7, of which 6 were waited for; matrix products, arithmetic and copies ran while one was open for 0% of the time, Pallas kernels for 16%

profile of v5, /device:TPU:56, one launch (start us, length us, event | category | flops | bytes accessed | tf_op | source)
XLA Modules:
  0.0 69.5 jit_solution(9951816013943005255)
XLA Ops:
  0.0 1.9 %send_x.1 = (f32[3,16,16,128]{3,2,1,0:T(8,128)}, f32[15,16,128]{2,1,0:T(8,128)}, f32[15,16,128]{2,1,0:T(8,128)}) custom-call(f32[4]{0:T(128)} %table.1, s32[16,16,128]{2,1,0:T(8,128)} %phase.1, f32[16,16,128]{2,1,0:T(8,128)} %iterate.1, f32[16,16,128]{2,1,0:T(8,128)} %right.1), custom_call_target="tpu_custom_call" | custom-call | flops 1000000 | bytes 393232 | tf_op jit(solution)/shard_map/send_x/pallas_call | solution.py:401
  1.9 4.3 %collective-permute-start = (f32[15,16,128]{2,1,0:T(8,128)}, f32[15,16,128]{2,1,0:T(8,128)S(1)}, u32[]{:S(2)}, u32[]{:S(2)}) collective-permute-start(f32[15,16,128]{2,1,0:T(8,128)} %get-tuple-element.20), channel_id=1, source_target_pairs={{0,64},{64,128},{128,192},{192,256},{256,320},{320,384},{384,448},... | collective-permute-start | bytes 368648 | tf_op jit(solution)/shard_map/ppermute | solution.py:417
  6.2 1.3 %collective-permute-start.1 = (f32[15,16,128]{2,1,0:T(8,128)}, f32[15,16,128]{2,1,0:T(8,128)S(1)}, u32[]{:S(2)}, u32[]{:S(2)}) collective-permute-start(f32[15,16,128]{2,1,0:T(8,128)} %get-tuple-element.21), channel_id=1, source_target_pairs={{64,0},{128,64},{192,128},{256,192},{320,256},{384,320},{448,384},... | collective-permute-start | bytes 368648 | tf_op jit(solution)/shard_map/ppermute | solution.py:417
  7.5 1.6 %collective-permute-done.from_down = f32[15,16,128]{2,1,0:T(8,128)S(1)} collective-permute-done((f32[15,16,128]{2,1,0:T(8,128)}, f32[15,16,128]{2,1,0:T(8,128)S(1)}, u32[]{:S(2)}, u32[]{:S(2)}) %collective-permute-start) | collective-permute-done | bytes 122912 | tf_op jit(solution)/shard_map/ppermute | solution.py:417
  9.1 4.6 %collective-permute-done.1.from_up = f32[15,16,128]{2,1,0:T(8,128)S(1)} collective-permute-done((f32[15,16,128]{2,1,0:T(8,128)}, f32[15,16,128]{2,1,0:T(8,128)S(1)}, u32[]{:S(2)}, u32[]{:S(2)}) %collective-permute-start.1) | collective-permute-done | bytes 122912 | tf_op jit(solution)/shard_map/ppermute | solution.py:417
  13.7 0.0 copy-start.2
  13.7 1.0 %copy-done.2 = f32[3,16,16,128]{3,2,1,0:T(8,128)S(1)} copy-done((f32[3,16,16,128]{3,2,1,0:T(8,128)S(1)}, f32[3,16,16,128]{3,2,1,0:T(8,128)}, u32[]{:S(2)}) %copy-start.2) | copy-done | bytes 393240
  14.7 0.1 pack_y.1
  14.9 1.9 %collective-permute-start.2 = (f32[28,16,128]{2,1,0:T(8,128)S(1)}, f32[28,16,128]{2,1,0:T(8,128)S(1)}, u32[]{:S(2)}, u32[]{:S(2)}) collective-permute-start(f32[28,16,128]{2,1,0:T(8,128)S(1)} %get-tuple-element.23), channel_id=1, source_target_pairs={{0,16},{16,32},{32,48},{1,17},{17,33},{33,49},{2,18},{18,34},{34,5... | collective-permute-start | bytes 688136 | tf_op jit(solution)/shard_map/ppermute | solution.py:417
  16.8 3.6 %collective-permute-start.3 = (f32[28,16,128]{2,1,0:T(8,128)S(1)}, f32[28,16,128]{2,1,0:T(8,128)S(1)}, u32[]{:S(2)}, u32[]{:S(2)}) collective-permute-start(f32[28,16,128]{2,1,0:T(8,128)S(1)} %get-tuple-element.24), channel_id=1, source_target_pairs={{16,0},{32,16},{48,32},{17,1},{33,17},{49,33},{18,2},{34,18},{50,3... | collective-permute-start | bytes 688136 | tf_op jit(solution)/shard_map/ppermute | solution.py:417
  20.4 1.8 %collective-permute-done.2.from_down = f32[28,16,128]{2,1,0:T(8,128)S(1)} collective-permute-done((f32[28,16,128]{2,1,0:T(8,128)S(1)}, f32[28,16,128]{2,1,0:T(8,128)S(1)}, u32[]{:S(2)}, u32[]{:S(2)}) %collective-permute-start.2) | collective-permute-done | bytes 229408 | tf_op jit(solution)/shard_map/ppermute | solution.py:417
  22.2 1.8 %collective-permute-done.3.from_up = f32[28,16,128]{2,1,0:T(8,128)S(1)} collective-permute-done((f32[28,16,128]{2,1,0:T(8,128)S(1)}, f32[28,16,128]{2,1,0:T(8,128)S(1)}, u32[]{:S(2)}, u32[]{:S(2)}) %collective-permute-start.3) | collective-permute-done | bytes 229408 | tf_op jit(solution)/shard_map/ppermute | solution.py:417
  24.0 3.0 %pack_z.1 = (f32[3,28,32,128]{3,2,1,0:T(8,128)S(1)}, f32[32,512]{1,0:T(8,128)S(1)}, f32[32,512]{1,0:T(8,128)S(1)}) custom-call(f32[3,28,16,128]{3,2,1,0:T(8,128)S(1)} %get-tuple-element.22.ext, f32[28,16,128]{2,1,0:T(8,128)S(1)} %collective-permute-done.2.from_down, f32[28,16,128]{2,1,0:T(8,128)S(1)} %collective-permute-done.3.from_up), custom_call_target="tpu_custom_call" | custom-call | flops 1000000 | bytes 1146880 | tf_op jit(solution)/shard_map/pack_z/pallas_call | solution.py:401
  26.9 3.6 %collective-permute-start.4 = (f32[32,512]{1,0:T(8,128)S(1)}, f32[32,512]{1,0:T(8,128)S(1)}, u32[]{:S(2)}, u32[]{:S(2)}) collective-permute-start(f32[32,512]{1,0:T(8,128)S(1)} %get-tuple-element.28), channel_id=1, source_target_pairs={{0,1},{1,2},{2,3},{3,4},{4,5},{5,6},{6,7},{7,8},{8,9},{9,10},{10,1... | collective-permute-start | bytes 196616 | tf_op jit(solution)/shard_map/ppermute | solution.py:417
  30.6 3.1 %collective-permute-start.5 = (f32[32,512]{1,0:T(8,128)S(1)}, f32[32,512]{1,0:T(8,128)S(1)}, u32[]{:S(2)}, u32[]{:S(2)}) collective-permute-start(f32[32,512]{1,0:T(8,128)S(1)} %get-tuple-element.29), channel_id=1, source_target_pairs={{1,0},{2,1},{3,2},{4,3},{5,4},{6,5},{7,6},{8,7},{9,8},{10,9},{11,1... | collective-permute-start | bytes 196616 | tf_op jit(solution)/shard_map/ppermute | solution.py:417
  33.7 0.1 pad_add_fusion.place
  33.8 1.3 %bands_xy.1 = (f32[3,28,32,128]{3,2,1,0:T(8,128)S(1)}, bf16[576,512]{1,0:T(8,128)(2,1)S(1)}) custom-call(s32[2]{0:T(128)S(1)} %pad_add_fusion.place, f32[3,28,32,128]{3,2,1,0:T(8,128)S(1)} %get-tuple-element.25.full), custom_call_target="tpu_custom_call" | custom-call | flops 30000000 | bytes 1376264 | tf_op jit(solution)/shard_map/bands_xy/pallas_call | solution.py:401
  35.1 0.0 copy-start
  35.1 0.8 %copy-done = bf16[576,512]{1,0:T(8,128)(2,1)} copy-done((bf16[576,512]{1,0:T(8,128)(2,1)}, bf16[576,512]{1,0:T(8,128)(2,1)S(1)}, u32[]{:S(2)}) %copy-start) | copy-done | bytes 589848
  35.9 0.0 collective-permute-done.4.from_down
  36.0 4.3 %collective-permute-done.5.from_up = f32[32,512]{1,0:T(8,128)S(1)} collective-permute-done((f32[32,512]{1,0:T(8,128)S(1)}, f32[32,512]{1,0:T(8,128)S(1)}, u32[]{:S(2)}, u32[]{:S(2)}) %collective-permute-start.5) | collective-permute-done | bytes 65568 | tf_op jit(solution)/shard_map/ppermute | solution.py:417
  40.2 3.8 %own_residual.1 = f32[32,16,128]{2,1,0:T(8,128)} custom-call(f32[3,28,32,128]{3,2,1,0:T(8,128)S(1)} %get-tuple-element.25.full, f32[3,28,32,128]{3,2,1,0:T(8,128)S(1)} %get-tuple-element.27.xy, f32[32,512]{1,0:T(8,128)S(1)} %collective-permute-done.4.from_down, f32[32,512]{1,0:T(8,128)S(1)} %collective-permute-done.5.from_up), custom_call_target="tpu_custom_call" | custom-call | flops 1000000 | bytes 2883584 | tf_op jit(solution)/shard_map/own_residual/pallas_call | solution.py:401
  44.1 10.8 %all-to-all-start = ((f32[32,16,128]{2,1,0:T(8,128)}), f32[32,16,128]{2,1,0:T(8,128)S(1)}, u32[]{:S(2)}, u32[]{:S(2)}) async-start(f32[32,16,128]{2,1,0:T(8,128)} %own_residual.1), calls=%async_computation | async-start | bytes 524288 | tf_op jit(solution)/shard_map/all_to_all | solution.py:451
  54.8 3.3 %fine_residual.1 = (f32[28,32,256]{2,1,0:T(8,128)S(1)}, f32[28,32,256]{2,1,0:T(8,128)S(1)}, f32[28,32,256]{2,1,0:T(8,128)S(1)}) custom-call(f32[3,28,32,128]{3,2,1,0:T(8,128)S(1)} %get-tuple-element.25.full, f32[3,28,32,128]{3,2,1,0:T(8,128)S(1)} %get-tuple-element.27.xy, f32[32,512]{1,0:T(8,128)S(1)} %collective-permute-done.4.from_down, ...), custom_call_target="tpu_custom_call" | custom-call | flops 30000000 | bytes 2883584 | tf_op jit(solution)/shard_map/fine_residual/pallas_call | solution.py:401
  58.1 0.0 copy-start.1
  58.2 6.1 %fine_sweeps.1.base = f32[16,16,128]{2,1,0:T(8,128)S(1)} custom-call(f32[3,28,32,128]{3,2,1,0:T(8,128)S(1)} %get-tuple-element.25.full, f32[28,32,256]{2,1,0:T(8,128)S(1)} %get-tuple-element.30.coef, f32[28,32,256]{2,1,0:T(8,128)S(1)} %get-tuple-element.31.res, f32[28,32,256]{2,1,0:T(8,128)S(1)} %get-tuple-element.32.inv), custom_call_target="tpu_custom_call" | custom-call | flops 60000000 | bytes 4128768 | tf_op jit(solution)/shard_map/fine_sweeps/pallas_call | solution.py:401
  64.3 2.5 %all-to-all-done = f32[32,16,128]{2,1,0:T(8,128)S(1)} async-done(((f32[32,16,128]{2,1,0:T(8,128)}), f32[32,16,128]{2,1,0:T(8,128)S(1)}, u32[]{:S(2)}, u32[]{:S(2)}) %all-to-all-start) | async-done | bytes 262176 | tf_op jit(solution)/shard_map/all_to_all | solution.py:451
  66.8 0.0 copy-done.1
  66.8 2.7 %coarse_levels.1 = f32[16,16,128]{2,1,0:T(8,128)} custom-call(bf16[576,512]{1,0:T(8,128)(2,1)S(1)} %copy-done.1, f32[512,128]{1,0:T(8,128)S(1)} %bitcast.3, f32[16,16,128]{2,1,0:T(8,128)S(1)} %fine_sweeps.1.base), custom_call_target="tpu_custom_call" | custom-call | flops 30000000 | bytes 1572864 | tf_op jit(solution)/shard_map/coarse_levels/pallas_call | solution.py:401
Async XLA Ops:
  1.9 7.2 %collective-permute-start = (f32[15,16,128]{2,1,0:T(8,128)}, f32[15,16,128]{2,1,0:T(8,128)S(1)}, u32[]{:S(2)}, u32[]{:S(2)}) collective-permute-start(f32[15,16,128]{2,1,0:T(8,128)} %get-tuple-element.20), channel_id=1, source_target_pairs={{0,64},{64,128},{128,192},{192,256},{256,320},{320,384},{384,448},... | collective-permute-start | bytes 368648 | tf_op jit(solution)/shard_map/ppermute | solution.py:417
  6.2 7.5 %collective-permute-start.1 = (f32[15,16,128]{2,1,0:T(8,128)}, f32[15,16,128]{2,1,0:T(8,128)S(1)}, u32[]{:S(2)}, u32[]{:S(2)}) collective-permute-start(f32[15,16,128]{2,1,0:T(8,128)} %get-tuple-element.21), channel_id=1, source_target_pairs={{64,0},{128,64},{192,128},{256,192},{320,256},{384,320},{448,384},... | collective-permute-start | bytes 368648 | tf_op jit(solution)/shard_map/ppermute | solution.py:417
  13.7 1.0 %copy-start.2 = (f32[3,16,16,128]{3,2,1,0:T(8,128)S(1)}, f32[3,16,16,128]{3,2,1,0:T(8,128)}, u32[]{:S(2)}) copy-start(f32[3,16,16,128]{3,2,1,0:T(8,128)} %get-tuple-element.19.fields) | copy-start | bytes 1179652
  14.9 7.3 %collective-permute-start.2 = (f32[28,16,128]{2,1,0:T(8,128)S(1)}, f32[28,16,128]{2,1,0:T(8,128)S(1)}, u32[]{:S(2)}, u32[]{:S(2)}) collective-permute-start(f32[28,16,128]{2,1,0:T(8,128)S(1)} %get-tuple-element.23), channel_id=1, source_target_pairs={{0,16},{16,32},{32,48},{1,17},{17,33},{33,49},{2,18},{18,34},{34,5... | collective-permute-start | bytes 688136 | tf_op jit(solution)/shard_map/ppermute | solution.py:417
  16.8 7.2 %collective-permute-start.3 = (f32[28,16,128]{2,1,0:T(8,128)S(1)}, f32[28,16,128]{2,1,0:T(8,128)S(1)}, u32[]{:S(2)}, u32[]{:S(2)}) collective-permute-start(f32[28,16,128]{2,1,0:T(8,128)S(1)} %get-tuple-element.24), channel_id=1, source_target_pairs={{16,0},{32,16},{48,32},{17,1},{33,17},{49,33},{18,2},{34,18},{50,3... | collective-permute-start | bytes 688136 | tf_op jit(solution)/shard_map/ppermute | solution.py:417
  26.9 9.0 %collective-permute-start.4 = (f32[32,512]{1,0:T(8,128)S(1)}, f32[32,512]{1,0:T(8,128)S(1)}, u32[]{:S(2)}, u32[]{:S(2)}) collective-permute-start(f32[32,512]{1,0:T(8,128)S(1)} %get-tuple-element.28), channel_id=1, source_target_pairs={{0,1},{1,2},{2,3},{3,4},{4,5},{5,6},{6,7},{7,8},{8,9},{9,10},{10,1... | collective-permute-start | bytes 196616 | tf_op jit(solution)/shard_map/ppermute | solution.py:417
  30.6 9.7 %collective-permute-start.5 = (f32[32,512]{1,0:T(8,128)S(1)}, f32[32,512]{1,0:T(8,128)S(1)}, u32[]{:S(2)}, u32[]{:S(2)}) collective-permute-start(f32[32,512]{1,0:T(8,128)S(1)} %get-tuple-element.29), channel_id=1, source_target_pairs={{1,0},{2,1},{3,2},{4,3},{5,4},{6,5},{7,6},{8,7},{9,8},{10,9},{11,1... | collective-permute-start | bytes 196616 | tf_op jit(solution)/shard_map/ppermute | solution.py:417
  35.1 0.8 %copy-start = (bf16[576,512]{1,0:T(8,128)(2,1)}, bf16[576,512]{1,0:T(8,128)(2,1)S(1)}, u32[]{:S(2)}) copy-start(bf16[576,512]{1,0:T(8,128)(2,1)S(1)} %get-tuple-element.26.patterns) | copy-start | bytes 1769476
  44.1 22.7 %all-to-all-start = ((f32[32,16,128]{2,1,0:T(8,128)}), f32[32,16,128]{2,1,0:T(8,128)S(1)}, u32[]{:S(2)}, u32[]{:S(2)}) async-start(f32[32,16,128]{2,1,0:T(8,128)} %own_residual.1), calls=%async_computation | async-start | bytes 524288 | tf_op jit(solution)/shard_map/all_to_all | solution.py:451
  58.1 8.6 %copy-start.1 = (bf16[576,512]{1,0:T(8,128)(2,1)S(1)}, bf16[576,512]{1,0:T(8,128)(2,1)}, u32[]{:S(2)}) copy-start(bf16[576,512]{1,0:T(8,128)(2,1)} %copy-done) | copy-start | bytes 1769476

commit v6 on v5

--- a/solution.py
+++ b/solution.py
@@ -114,14 +114,13 @@
     to_down[:, 15:16, :] = jnp.zeros((28, 1, 128), F32)
 
 
-def add_quads(quads, sums, x):
-    if (x - 6) % 4 == 3:
-        for at, f in enumerate(sums):
-            f = f + pltpu.roll(f, 15, 0)
-            f = f + pltpu.roll(f, 14, 0)
-            for tile in range(f.shape[1] // 128):
-                start = 64 * (at * (f.shape[1] // 128) + tile) + 16 * ((x - 6) // 4)
-                quads[start : start + 16, :] = f[:, 128 * tile : 128 * tile + 128]
+def sum_quads(quads, q, sums):
+    for at, f in enumerate(sums):
+        f = f + pltpu.roll(f, 15, 0)
+        f = f + pltpu.roll(f, 14, 0)
+        for tile in range(f.shape[1] // 128):
+            start = 64 * (at * (f.shape[1] // 128) + tile) + 16 * q
+            quads[pl.ds(pl.multiple_of(start, 16), 16), :] = f[:, 128 * tile : 128 * tile + 128]
 
 
 def read_quads(quads):
@@ -129,29 +128,37 @@
     return jnp.concatenate([quads[pl.ds(64 * at, 16, stride=4), :] for at in range(count)], axis=1)
 
 
-def pack_z(ext, from_down, from_up, full, to_up, to_down, quads):
+def pack_z(ext, from_down, from_up, full, to_up, to_down, inner, in_y, quads):
     for field in range(3):
         h, a, b = HALO[field], ROWS[field], ROWS[field + 1]
         full[field, :, 0:16, :] = ext[field]
         full[field, :, 16 : 16 + h, :] = from_up[:, a:b, :]
         full[field, :, 16 + h : 32 - h, :] = jnp.zeros((28, 16 - 2 * h, 128), F32)
         full[field, :, 32 - h : 32, :] = from_down[:, a:b, :]
-    in_y = {}
-    sums = [None, None]
-    for x in range(5, 23):
+
+    def bands_y(x, carry):
         k = full[0, x]
         v = full[1, x]
-        in_y[x] = [band(f, 0)[0:16, :] for f in (k, v, k * v)]
-        x = x - 1
-        if x < 6:
-            continue
-        tu = [band((low + high) + 2.0 * f, 1) for low, f, high in zip(in_y.pop(x - 1), in_y[x], in_y[x + 1])]
-        k = full[0, x, 0:16, :]
-        v = full[1, x, 0:16, :]
-        diagonal = 6.0 * k + 0.125 * tu[0]
-        res = full[2, x, 0:16, :] - (v * diagonal + 2.0 * (k * v) - 0.125 * (k * tu[1] + tu[2]))
-        sums = [f if (x - 6) % 4 == 0 else total + f for total, f in zip(sums, (res, k))]
-        add_quads(quads, sums, x)
+        for at, f in enumerate((k, v, k * v)):
+            in_y[at, x] = band(f, 0)[0:16, :]
+        return carry
+
+    lax.fori_loop(5, 23, bands_y, 0, unroll=2)
+
+    def quad(q, carry):
+        sums = [None, None]
+        for j in range(4):
+            x = 6 + 4 * q + j
+            tu = [band((in_y[at, x - 1] + in_y[at, x + 1]) + 2.0 * in_y[at, x], 1) for at in range(3)]
+            k = full[0, x, 0:16, :]
+            v = full[1, x, 0:16, :]
+            diagonal = 6.0 * k + 0.125 * tu[0]
+            res = full[2, x, 0:16, :] - (v * diagonal + 2.0 * (k * v) - 0.125 * (k * tu[1] + tu[2]))
+            sums = [f if j == 0 else total + f for total, f in zip(sums, (res, k))]
+        sum_quads(quads, q, sums)
+        return carry
+
+    lax.fori_loop(0, 4, quad, 0)
     source = iota((256, 128), 0)
     lane = iota((256, 128), 1)
     coarse = (source & 127) >> 2
@@ -159,9 +166,12 @@
     scale = jnp.where(source < 128, F32(0.25), F32(1.0 / 64.0))
     upper = (lane == base + coarse - 16) & (coarse >= 16) & (coarse <= 30)
     lower = (lane == base + coarse) & (coarse >= 1) & (coarse <= 15)
-    place = jnp.concatenate([jnp.where(upper, scale, 0.0), jnp.where(lower, scale, 0.0)], axis=1).astype(BF16)
+    stay = (lane == (source >> 7) * 64 + 16 + coarse) & (coarse >= 1) & (coarse <= 30)
+    place = jnp.concatenate([jnp.where(found, scale, 0.0) for found in (upper, lower, stay)], axis=1).astype(BF16)
     level3 = select_lanes(read_quads(quads), place)
+    inner[...] = level3[:, 256:384]
     lane = iota((32, 128), 1)
+
     for group in range(4):
         up = jnp.zeros((32, 128), F32)
         down = jnp.zeros((32, 128), F32)
@@ -216,42 +226,50 @@
             xy[field, x] = jnp.zeros((32, 128), F32)
 
 
-def own_residual(full, xy, from_down, from_up, chunks, quads):
-    def edge(cells, shift_v, shift_right):
-        k = cells
-        v = pltpu.roll(cells, 512 - shift_v, 1)
-        found = [k, v, pltpu.roll(cells, 512 - shift_right, 1)]
-        for f in (k, v, k * v):
-            f = band(f, 0)
-            f = f + pltpu.roll(f, 16, 1)
-            found.append(f + pltpu.roll(f, 512 - 16, 1))
-        return [f[0:16, :] for f in found]
-
-    below = edge(from_down[...], 5, 9)
-    above = edge(from_up[...], 6, 11)
+def end_cells(lower_k, lower_v, lower_right, upper_k, upper_v, upper_right):
+    position = iota((32, 512), 1) & 15
+    k = jnp.where(position < 6, lower_k, jnp.where(position < 12, upper_k, 0.0))
+    v = jnp.where(position < 6, lower_v, upper_v)
+    right = jnp.where(position < 6, lower_right, upper_right)[0:16, :]
+    tu = []
+    for f in (k, v, k * v):
+        f = band(f, 0)[0:16, :]
+        f = f + pltpu.roll(f, 16, 1)
+        tu.append(band(f + pltpu.roll(f, 512 - 16, 1), 1))
+    k, v = k[0:16, :], v[0:16, :]
+    diagonal = 6.0 * k + 0.125 * tu[0]
+    return right - (v * diagonal + 2.0 * (k * v) - 0.125 * (k * tu[1] + tu[2])), k
+
+
+def own_cells(sent_up, sent_down, from_down, from_up, inner, chunks, quads):
+    def moved(f, shift):
+        return pltpu.roll(f, shift % 512, 1)
+
+    low, first, last, high = from_down[...], sent_down[...], sent_up[...], from_up[...]
+    found = [
+        end_cells(low, moved(low, -5), moved(low, -9), moved(first, 6), first, moved(first, -5)),
+        end_cells(last, moved(last, -5), moved(last, -9), moved(high, 6), high, moved(high, -5)),
+    ]
+    rows = []
+    for f in (found[0][0], found[1][0], found[0][1], found[1][1]):
+        f = f[:, 0:384]
+        f = f + pltpu.roll(f, 15, 0)
+        rows.append(f + pltpu.roll(f, 14, 0))
+    source = iota((384, 128), 0)
+    x = (source >> 4) - 6
+    z = (source & 15) - 2
+    place = (x >= 0) & (x < 16) & (z >= 0) & (z < 8) & (iota((384, 128), 1) == (x >> 2) * 32 + (z >> 2))
+    ends = select_lanes(jnp.concatenate(rows, axis=0), ones_where(place))
+    ends = [0.25 * ends[0:16], 0.25 * ends[16:32], ends[32:48] / 64.0, ends[48:64] / 64.0]
+    for q in range(4):
+        for at in range(4):
+            start = 64 * at + 16 * q
+            quads[start : start + 16, :] = rolled(ends[at], -32 * q)
     lane = iota((16, 128), 1)
-    sums = [None, None]
-    for x in range(6, 22):
-        group, first = 128 * (x // 8), 16 * (x % 8)
-        beyond = []
-        for low, high in zip(below, above):
-            tile = jnp.where(lane >= 122, rolled(low[:, group : group + 128], 122 - first), 0.0)
-            beyond.append(jnp.where(lane < 6, rolled(high[:, group : group + 128], -first), tile))
-        k, v, right = [jnp.concatenate([full[at, x, 0:16, :], beyond[at]], axis=1) for at in range(3)]
-        tu = [band(jnp.concatenate([xy[at, x, 0:16, :], beyond[3 + at]], axis=1), 1) for at in range(3)]
-        diagonal = 6.0 * k + 0.125 * tu[0]
-        res = right - (v * diagonal + 2.0 * (k * v) - 0.125 * (k * tu[1] + tu[2]))
-        sums = [f if (x - 6) % 4 == 0 else total + f for total, f in zip(sums, (res, k))]
-        add_quads(quads, sums, x)
-    source = iota((512, 128), 0)
-    lane = iota((512, 128), 1)
-    cell = source & 255
-    coarse = jnp.where(cell < 132, cell >> 2, -1)
-    used = (cell < 132) | (cell >= 252)
-    scale = jnp.where(source < 256, F32(0.25), F32(1.0 / 64.0))
-    place = jnp.where(used & (lane == (source >> 8) * 64 + 16 + coarse), scale, 0.0).astype(BF16)
-    mine = select_lanes(read_quads(quads), place)
-    lane = iota((16, 128), 1)
+    mine = inner[...]
+    for at, target in enumerate((15, 47, 79, 111)):
+        cells = pltpu.roll(quads[pl.ds(64 * at, 16, stride=4), :], target, 1)
+        mine = jnp.where((lane == target) | (lane == target + 1), cells, mine)
     low = from_down[0:16, 384:512]
     high = from_up[0:16, 384:512]
     mine = jnp.where(lane < 15, pltpu.roll(low, 64, 1), mine)
@@ -263,6 +281,7 @@
 
 def fine_residual(full, xy, from_down, from_up, coef, res, inv, side, sides_kv, product):
     lane = iota((32, 128), 1)
+
     for x in range(28):
         group, first = 128 * (x // 8), 16 * (x % 8)
         up = from_up[:, group : group + 128]
@@ -432,8 +451,11 @@
     ext, to_up, to_down = call(pack_y, [(3, 28, 16, 128), (28, 16, 128), (28, 16, 128)], [fields, from_down, from_up])
     from_down, from_up = swap("gy", to_up, to_down)
     planes = (3, 28, 32, 128)
-    full, to_up, to_down = call(
-        pack_z, [planes, (32, 512), (32, 512)], [ext, from_down, from_up], scratch=[(128, 128)]
+    full, to_up, to_down, inner = call(
+        pack_z,
+        [planes, (32, 512), (32, 512), (16, 128)],
+        [ext, from_down, from_up],
+        scratch=[(3, 28, 16, 128), (128, 128)],
     )
     from_down, from_up = swap("gz", to_up, to_down)
     place = jnp.stack([lax.axis_index("gx"), lax.axis_index("gy")]).astype(jnp.int32)
@@ -447,7 +469,7 @@
     )
     z_sides = [from_down, from_up]
     count = lax.axis_size("gx") * lax.axis_size("gy")
-    (chunks,) = call(own_residual, [(count, 16, 128)], [full, xy, *z_sides], scratch=[(256, 128)])
+    (chunks,) = call(own_cells, [(count, 16, 128)], [to_up, to_down, *z_sides, inner], scratch=[(256, 128)])
     plane = lax.all_to_all(chunks, ("gx", "gy"), 0, 0, tiled=True)
     wide = (28, 32, 256)
     coef, res, inv = call(

time: 69.8 us -> 66.5 us (0.953)
  Pallas kernels: 22.3 us -> 18.9 us
  local copies, waits for them, and re-layouts: 1.81 us -> 1 us
  waiting for transfers between devices: 16.5 us -> 17.3 us
    pallas_call x8, Pallas kernels: 22.3 us -> 18.9 us  [call(): pl.pallas_call(kernel, out_shape=[out if isinstance(out, jax.ShapeDtypeSt...]
    ppermute x6, waiting for transfers between devices: 14 us -> 16.3 us  [swap(): return (lax.ppermute(to_up, axis, up), lax.ppermute(to_down, axis, down))]
    all_to_all x1, waiting for transfers between devices: 2.48 us -> 1.06 us  [on_device(): plane = lax.all_to_all(chunks, ('gx', 'gy'), 0, 0, tiled=True)]
    unnamed x6 -> x2, local copies, waits for them, and re-layouts: 1.81 us -> 1 us
  transfers between devices with their start and end apart: 7 -> 7, of which waited for: 6 -> 7; matrix products, arithmetic and copies ran while one was open for 0% -> 0% of each run, Pallas kernels for 16% -> 16%
where the time goes in v6:
time: 66.5 us; the launch traced here: 66.1 us
  starting transfers between devices  28.6 us (43%)
  Pallas kernels  18.9 us (28%)
  waiting for transfers between devices  17.3 us (26%)
  local copies, waits for them, and re-layouts  1 us (2%)
    pallas_call x8, Pallas kernels, call(): pl.pallas_call(kernel, out_shape=[out if isinstance(out, jax.ShapeDtypeSt...  18.9 us
    ppermute x6, starting transfers between devices, swap(): return (lax.ppermute(to_up, axis, up), lax.ppermute(to_down, axis, down))  17.9 us
    ppermute x6, waiting for transfers between devices, swap(): return (lax.ppermute(to_up, axis, up), lax.ppermute(to_down, axis, down))  16.3 us
    all_to_all x1, starting transfers between devices, on_device(): plane = lax.all_to_all(chunks, ('gx', 'gy'), 0, 0, tiled=True)  10.8 us
  transfers between devices with their start and end apart: 7, of which 7 were waited for; matrix products, arithmetic and copies ran while one was open for 0% of the time, Pallas kernels for 16%

profile of v6, /device:TPU:56, one launch (start us, length us, event | category | flops | bytes accessed | tf_op | source)
XLA Modules:
  0.0 66.1 jit_solution(14657335786524967602)
XLA Ops:
  0.0 1.9 %send_x.1 = (f32[3,16,16,128]{3,2,1,0:T(8,128)}, f32[15,16,128]{2,1,0:T(8,128)}, f32[15,16,128]{2,1,0:T(8,128)}) custom-call(f32[4]{0:T(128)} %table.1, s32[16,16,128]{2,1,0:T(8,128)} %phase.1, f32[16,16,128]{2,1,0:T(8,128)} %iterate.1, f32[16,16,128]{2,1,0:T(8,128)} %right.1), custom_call_target="tpu_custom_call" | custom-call | flops 1000000 | bytes 393232 | tf_op jit(solution)/shard_map/send_x/pallas_call | solution.py:420
  1.9 4.3 %collective-permute-start = (f32[15,16,128]{2,1,0:T(8,128)}, f32[15,16,128]{2,1,0:T(8,128)S(1)}, u32[]{:S(2)}, u32[]{:S(2)}) collective-permute-start(f32[15,16,128]{2,1,0:T(8,128)} %get-tuple-element.21), channel_id=1, source_target_pairs={{0,64},{64,128},{128,192},{192,256},{256,320},{320,384},{384,448},... | collective-permute-start | bytes 368648 | tf_op jit(solution)/shard_map/ppermute | solution.py:436
  6.2 1.3 %collective-permute-start.1 = (f32[15,16,128]{2,1,0:T(8,128)}, f32[15,16,128]{2,1,0:T(8,128)S(1)}, u32[]{:S(2)}, u32[]{:S(2)}) collective-permute-start(f32[15,16,128]{2,1,0:T(8,128)} %get-tuple-element.22), channel_id=1, source_target_pairs={{64,0},{128,64},{192,128},{256,192},{320,256},{384,320},{448,384},... | collective-permute-start | bytes 368648 | tf_op jit(solution)/shard_map/ppermute | solution.py:436
  7.5 1.6 %collective-permute-done.from_down = f32[15,16,128]{2,1,0:T(8,128)S(1)} collective-permute-done((f32[15,16,128]{2,1,0:T(8,128)}, f32[15,16,128]{2,1,0:T(8,128)S(1)}, u32[]{:S(2)}, u32[]{:S(2)}) %collective-permute-start) | collective-permute-done | bytes 122912 | tf_op jit(solution)/shard_map/ppermute | solution.py:436
  9.1 4.6 %collective-permute-done.1.from_up = f32[15,16,128]{2,1,0:T(8,128)S(1)} collective-permute-done((f32[15,16,128]{2,1,0:T(8,128)}, f32[15,16,128]{2,1,0:T(8,128)S(1)}, u32[]{:S(2)}, u32[]{:S(2)}) %collective-permute-start.1) | collective-permute-done | bytes 122912 | tf_op jit(solution)/shard_map/ppermute | solution.py:436
  13.7 0.0 copy-start
  13.7 1.0 %copy-done = f32[3,16,16,128]{3,2,1,0:T(8,128)S(1)} copy-done((f32[3,16,16,128]{3,2,1,0:T(8,128)S(1)}, f32[3,16,16,128]{3,2,1,0:T(8,128)}, u32[]{:S(2)}) %copy-start) | copy-done | bytes 393240
  14.7 0.1 pack_y.1
  14.9 1.9 %collective-permute-start.2 = (f32[28,16,128]{2,1,0:T(8,128)S(1)}, f32[28,16,128]{2,1,0:T(8,128)S(1)}, u32[]{:S(2)}, u32[]{:S(2)}) collective-permute-start(f32[28,16,128]{2,1,0:T(8,128)S(1)} %get-tuple-element.24), channel_id=1, source_target_pairs={{0,16},{16,32},{32,48},{1,17},{17,33},{33,49},{2,18},{18,34},{34,5... | collective-permute-start | bytes 688136 | tf_op jit(solution)/shard_map/ppermute | solution.py:436
  16.8 3.6 %collective-permute-start.3 = (f32[28,16,128]{2,1,0:T(8,128)S(1)}, f32[28,16,128]{2,1,0:T(8,128)S(1)}, u32[]{:S(2)}, u32[]{:S(2)}) collective-permute-start(f32[28,16,128]{2,1,0:T(8,128)S(1)} %get-tuple-element.25), channel_id=1, source_target_pairs={{16,0},{32,16},{48,32},{17,1},{33,17},{49,33},{18,2},{34,18},{50,3... | collective-permute-start | bytes 688136 | tf_op jit(solution)/shard_map/ppermute | solution.py:436
  20.4 1.8 %collective-permute-done.2.from_down = f32[28,16,128]{2,1,0:T(8,128)S(1)} collective-permute-done((f32[28,16,128]{2,1,0:T(8,128)S(1)}, f32[28,16,128]{2,1,0:T(8,128)S(1)}, u32[]{:S(2)}, u32[]{:S(2)}) %collective-permute-start.2) | collective-permute-done | bytes 229408 | tf_op jit(solution)/shard_map/ppermute | solution.py:436
  22.2 1.8 %collective-permute-done.3.from_up = f32[28,16,128]{2,1,0:T(8,128)S(1)} collective-permute-done((f32[28,16,128]{2,1,0:T(8,128)S(1)}, f32[28,16,128]{2,1,0:T(8,128)S(1)}, u32[]{:S(2)}, u32[]{:S(2)}) %collective-permute-start.3) | collective-permute-done | bytes 229408 | tf_op jit(solution)/shard_map/ppermute | solution.py:436
  24.0 1.8 %pack_z.1 = (f32[3,28,32,128]{3,2,1,0:T(8,128)S(1)}, f32[32,512]{1,0:T(8,128)S(1)}, f32[32,512]{1,0:T(8,128)S(1)}, f32[16,128]{1,0:T(8,128)S(1)}) custom-call(f32[3,28,16,128]{3,2,1,0:T(8,128)S(1)} %get-tuple-element.23.ext, f32[28,16,128]{2,1,0:T(8,128)S(1)} %collective-permute-done.2.from_down, f32[28,16,128]{2,1,0:T(8,128)S(1)} %collective-permute-done.3.from_up), custom_call_target="tpu_custom_call" | custom-call | flops 1000000 | bytes 1146880 | tf_op jit(solution)/shard_map/pack_z/pallas_call | solution.py:420
  25.8 3.6 %collective-permute-start.4 = (f32[32,512]{1,0:T(8,128)S(1)}, f32[32,512]{1,0:T(8,128)S(1)}, u32[]{:S(2)}, u32[]{:S(2)}) collective-permute-start(f32[32,512]{1,0:T(8,128)S(1)} %get-tuple-element.28.sent_up), channel_id=1, source_target_pairs={{0,1},{1,2},{2,3},{3,4},{4,5},{5,6},{6,7},{7,8},{8,9},{9,10},{10,1... | collective-permute-start | bytes 196616 | tf_op jit(solution)/shard_map/ppermute | solution.py:436
  29.4 3.1 %collective-permute-start.5 = (f32[32,512]{1,0:T(8,128)S(1)}, f32[32,512]{1,0:T(8,128)S(1)}, u32[]{:S(2)}, u32[]{:S(2)}) collective-permute-start(f32[32,512]{1,0:T(8,128)S(1)} %get-tuple-element.29.sent_down), channel_id=1, source_target_pairs={{1,0},{2,1},{3,2},{4,3},{5,4},{6,5},{7,6},{8,7},{9,8},{10,9},{11,1... | collective-permute-start | bytes 196616 | tf_op jit(solution)/shard_map/ppermute | solution.py:436
  32.5 0.4 collective-permute-done.4.from_down
  32.9 6.2 %collective-permute-done.5.from_up = f32[32,512]{1,0:T(8,128)S(1)} collective-permute-done((f32[32,512]{1,0:T(8,128)S(1)}, f32[32,512]{1,0:T(8,128)S(1)}, u32[]{:S(2)}, u32[]{:S(2)}) %collective-permute-start.5) | collective-permute-done | bytes 65568 | tf_op jit(solution)/shard_map/ppermute | solution.py:436
  39.1 1.6 %own_cells.1 = f32[32,16,128]{2,1,0:T(8,128)} custom-call(f32[32,512]{1,0:T(8,128)S(1)} %get-tuple-element.28.sent_up, f32[32,512]{1,0:T(8,128)S(1)} %get-tuple-element.29.sent_down, f32[32,512]{1,0:T(8,128)S(1)} %collective-permute-done.4.from_down, f32[32,512]{1,0:T(8,128)S(1)} %collective-permute-done.5.from_up, f32[16,128]{1,0:T(8,128)S(1)} %get-tuple-element.30.inner), custom_call_target="tpu_custom_call" | custom-call | flops 1000000 | bytes 270336 | tf_op jit(solution)/shard_map/own_cells/pallas_call | solution.py:420
  40.7 10.8 %all-to-all-start = ((f32[32,16,128]{2,1,0:T(8,128)}), f32[32,16,128]{2,1,0:T(8,128)S(1)}, u32[]{:S(2)}, u32[]{:S(2)}) async-start(f32[32,16,128]{2,1,0:T(8,128)} %own_cells.1), calls=%async_computation | async-start | bytes 524288 | tf_op jit(solution)/shard_map/all_to_all | solution.py:473
  51.4 0.1 pad_add_fusion.place
  51.5 1.3 %bands_xy.1 = (f32[3,28,32,128]{3,2,1,0:T(8,128)S(1)}, bf16[576,512]{1,0:T(8,128)(2,1)S(1)}) custom-call(s32[2]{0:T(128)S(1)} %pad_add_fusion.place, f32[3,28,32,128]{3,2,1,0:T(8,128)S(1)} %get-tuple-element.26.full), custom_call_target="tpu_custom_call" | custom-call | flops 30000000 | bytes 1376264 | tf_op jit(solution)/shard_map/bands_xy/pallas_call | solution.py:420
  52.9 3.3 %fine_residual.1 = (f32[28,32,256]{2,1,0:T(8,128)S(1)}, f32[28,32,256]{2,1,0:T(8,128)S(1)}, f32[28,32,256]{2,1,0:T(8,128)S(1)}) custom-call(f32[3,28,32,128]{3,2,1,0:T(8,128)S(1)} %get-tuple-element.26.full, f32[3,28,32,128]{3,2,1,0:T(8,128)S(1)} %get-tuple-element.31.xy, f32[32,512]{1,0:T(8,128)S(1)} %collective-permute-done.4.from_down, ...), custom_call_target="tpu_custom_call" | custom-call | flops 30000000 | bytes 2883584 | tf_op jit(solution)/shard_map/fine_residual/pallas_call | solution.py:420
  56.2 6.1 %fine_sweeps.1.base = f32[16,16,128]{2,1,0:T(8,128)S(1)} custom-call(f32[3,28,32,128]{3,2,1,0:T(8,128)S(1)} %get-tuple-element.26.full, f32[28,32,256]{2,1,0:T(8,128)S(1)} %get-tuple-element.32.coef, f32[28,32,256]{2,1,0:T(8,128)S(1)} %get-tuple-element.33.res, f32[28,32,256]{2,1,0:T(8,128)S(1)} %get-tuple-element.34.inv), custom_call_target="tpu_custom_call" | custom-call | flops 60000000 | bytes 4128768 | tf_op jit(solution)/shard_map/fine_sweeps/pallas_call | solution.py:420
  62.3 1.1 %all-to-all-done = f32[32,16,128]{2,1,0:T(8,128)S(1)} async-done(((f32[32,16,128]{2,1,0:T(8,128)}), f32[32,16,128]{2,1,0:T(8,128)S(1)}, u32[]{:S(2)}, u32[]{:S(2)}) %all-to-all-start) | async-done | bytes 262176 | tf_op jit(solution)/shard_map/all_to_all | solution.py:473
  63.4 2.7 %coarse_levels.1 = f32[16,16,128]{2,1,0:T(8,128)} custom-call(bf16[576,512]{1,0:T(8,128)(2,1)S(1)} %get-tuple-element.27.patterns, f32[512,128]{1,0:T(8,128)S(1)} %bitcast.3, f32[16,16,128]{2,1,0:T(8,128)S(1)} %fine_sweeps.1.base), custom_call_target="tpu_custom_call" | custom-call | flops 30000000 | bytes 1572864 | tf_op jit(solution)/shard_map/coarse_levels/pallas_call | solution.py:420
Async XLA Ops:
  1.9 7.2 %collective-permute-start = (f32[15,16,128]{2,1,0:T(8,128)}, f32[15,16,128]{2,1,0:T(8,128)S(1)}, u32[]{:S(2)}, u32[]{:S(2)}) collective-permute-start(f32[15,16,128]{2,1,0:T(8,128)} %get-tuple-element.21), channel_id=1, source_target_pairs={{0,64},{64,128},{128,192},{192,256},{256,320},{320,384},{384,448},... | collective-permute-start | bytes 368648 | tf_op jit(solution)/shard_map/ppermute | solution.py:436
  6.2 7.5 %collective-permute-start.1 = (f32[15,16,128]{2,1,0:T(8,128)}, f32[15,16,128]{2,1,0:T(8,128)S(1)}, u32[]{:S(2)}, u32[]{:S(2)}) collective-permute-start(f32[15,16,128]{2,1,0:T(8,128)} %get-tuple-element.22), channel_id=1, source_target_pairs={{64,0},{128,64},{192,128},{256,192},{320,256},{384,320},{448,384},... | collective-permute-start | bytes 368648 | tf_op jit(solution)/shard_map/ppermute | solution.py:436
  13.7 1.0 %copy-start = (f32[3,16,16,128]{3,2,1,0:T(8,128)S(1)}, f32[3,16,16,128]{3,2,1,0:T(8,128)}, u32[]{:S(2)}) copy-start(f32[3,16,16,128]{3,2,1,0:T(8,128)} %get-tuple-element.20.fields) | copy-start | bytes 1179652
  14.9 7.3 %collective-permute-start.2 = (f32[28,16,128]{2,1,0:T(8,128)S(1)}, f32[28,16,128]{2,1,0:T(8,128)S(1)}, u32[]{:S(2)}, u32[]{:S(2)}) collective-permute-start(f32[28,16,128]{2,1,0:T(8,128)S(1)} %get-tuple-element.24), channel_id=1, source_target_pairs={{0,16},{16,32},{32,48},{1,17},{17,33},{33,49},{2,18},{18,34},{34,5... | collective-permute-start | bytes 688136 | tf_op jit(solution)/shard_map/ppermute | solution.py:436
  16.8 7.2 %collective-permute-start.3 = (f32[28,16,128]{2,1,0:T(8,128)S(1)}, f32[28,16,128]{2,1,0:T(8,128)S(1)}, u32[]{:S(2)}, u32[]{:S(2)}) collective-permute-start(f32[28,16,128]{2,1,0:T(8,128)S(1)} %get-tuple-element.25), channel_id=1, source_target_pairs={{16,0},{32,16},{48,32},{17,1},{33,17},{49,33},{18,2},{34,18},{50,3... | collective-permute-start | bytes 688136 | tf_op jit(solution)/shard_map/ppermute | solution.py:436
  25.8 7.1 %collective-permute-start.4 = (f32[32,512]{1,0:T(8,128)S(1)}, f32[32,512]{1,0:T(8,128)S(1)}, u32[]{:S(2)}, u32[]{:S(2)}) collective-permute-start(f32[32,512]{1,0:T(8,128)S(1)} %get-tuple-element.28.sent_up), channel_id=1, source_target_pairs={{0,1},{1,2},{2,3},{3,4},{4,5},{5,6},{6,7},{7,8},{8,9},{9,10},{10,1... | collective-permute-start | bytes 196616 | tf_op jit(solution)/shard_map/ppermute | solution.py:436
  29.4 9.7 %collective-permute-start.5 = (f32[32,512]{1,0:T(8,128)S(1)}, f32[32,512]{1,0:T(8,128)S(1)}, u32[]{:S(2)}, u32[]{:S(2)}) collective-permute-start(f32[32,512]{1,0:T(8,128)S(1)} %get-tuple-element.29.sent_down), channel_id=1, source_target_pairs={{1,0},{2,1},{3,2},{4,3},{5,4},{6,5},{7,6},{8,7},{9,8},{10,9},{11,1... | collective-permute-start | bytes 196616 | tf_op jit(solution)/shard_map/ppermute | solution.py:436
  40.7 22.7 %all-to-all-start = ((f32[32,16,128]{2,1,0:T(8,128)}), f32[32,16,128]{2,1,0:T(8,128)S(1)}, u32[]{:S(2)}, u32[]{:S(2)}) async-start(f32[32,16,128]{2,1,0:T(8,128)} %own_cells.1), calls=%async_computation | async-start | bytes 524288 | tf_op jit(solution)/shard_map/all_to_all | solution.py:473

commit v7 on v6

--- a/solution.py
+++ b/solution.py
@@ -97,6 +97,10 @@
         h, a, b = HALO[field], ROWS[field], ROWS[field + 1]
         to_up[a:b] = fields[field, 16 - h : 16]
         to_down[a:b] = fields[field, 0:h]
+
+
+def hold(fields, held):
+    held[...] = fields[...]
 
 
 def pack_y(fields, from_down, from_up, ext, to_up, to_down):
@@ -448,6 +452,8 @@
         grant=60,
     )
     from_down, from_up = swap("gx", to_up, to_down)
+    (held,) = call(hold, [(3, *block)], [fields], flops=30000000)
+    from_down, from_up, fields = lax.optimization_barrier((from_down, from_up, held))
     ext, to_up, to_down = call(pack_y, [(3, 28, 16, 128), (28, 16, 128), (28, 16, 128)], [fields, from_down, from_up])
     from_down, from_up = swap("gy", to_up, to_down)
     planes = (3, 28, 32, 128)
@@ -467,6 +473,7 @@
         first=SMEM,
         flops=30000000,
     )
+    from_down, from_up, xy, patterns = lax.optimization_barrier((from_down, from_up, xy, patterns))
     z_sides = [from_down, from_up]
     count = lax.axis_size("gx") * lax.axis_size("gy")
     (chunks,) = call(own_cells, [(count, 16, 128)], [to_up, to_down, *z_sides, inner], scratch=[(256, 128)])

time: 66.5 us -> 65.5 us (0.985)
  waiting for transfers between devices: 17.3 us -> 15.5 us
  local copies, waits for them, and re-layouts: 1 us -> 1.8 us
    ppermute x6, waiting for transfers between devices: 16.3 us -> 13 us  [swap(): return (lax.ppermute(to_up, axis, up), lax.ppermute(to_down, axis, down))]
    all_to_all x1, waiting for transfers between devices: 1.06 us -> 2.48 us  [on_device(): plane = lax.all_to_all(chunks, ('gx', 'gy'), 0, 0, tiled=True)]
    unnamed x2 -> x6, local copies, waits for them, and re-layouts: 1 us -> 1.8 us
    pallas_call x8 -> x9, Pallas kernels: 18.9 us -> 19 us  [call(): pl.pallas_call(kernel, out_shape=[out if isinstance(out, jax.ShapeDtypeSt...]
  transfers between devices with their start and end apart: 7 -> 7, of which waited for: 7 -> 6; matrix products, arithmetic and copies ran while one was open for 0% -> 0% of each run, Pallas kernels for 16% -> 17%
where the time goes in v7:
time: 65.5 us; the launch traced here: 65.1 us
  starting transfers between devices  28.6 us (44%)
  Pallas kernels  19 us (29%)
  waiting for transfers between devices  15.5 us (24%)
  local copies, waits for them, and re-layouts  1.8 us (3%)
    pallas_call x9, Pallas kernels, call(): pl.pallas_call(kernel, out_shape=[out if isinstance(out, jax.ShapeDtypeSt...  19 us
    ppermute x6, starting transfers between devices, swap(): return (lax.ppermute(to_up, axis, up), lax.ppermute(to_down, axis, down))  17.9 us
    ppermute x6, waiting for transfers between devices, swap(): return (lax.ppermute(to_up, axis, up), lax.ppermute(to_down, axis, down))  13 us
    all_to_all x1, starting transfers between devices, on_device(): plane = lax.all_to_all(chunks, ('gx', 'gy'), 0, 0, tiled=True)  10.8 us
    all_to_all x1, waiting for transfers between devices, on_device(): plane = lax.all_to_all(chunks, ('gx', 'gy'), 0, 0, tiled=True)  2.48 us
    unnamed x6, local copies, waits for them, and re-layouts  1.8 us
  transfers between devices with their start and end apart: 7, of which 6 were waited for; matrix products, arithmetic and copies ran while one was open for 0% of the time, Pallas kernels for 17%

profile of v7, /device:TPU:56, one launch (start us, length us, event | category | flops | bytes accessed | tf_op | source)
XLA Modules:
  0.0 65.1 jit_solution(3066943558995101791)
XLA Ops:
  0.0 1.9 %send_x.1 = (f32[3,16,16,128]{3,2,1,0:T(8,128)}, f32[15,16,128]{2,1,0:T(8,128)}, f32[15,16,128]{2,1,0:T(8,128)}) custom-call(f32[4]{0:T(128)} %table.1, s32[16,16,128]{2,1,0:T(8,128)} %phase.1, f32[16,16,128]{2,1,0:T(8,128)} %iterate.1, f32[16,16,128]{2,1,0:T(8,128)} %right.1), custom_call_target="tpu_custom_call" | custom-call | flops 1000000 | bytes 393232 | tf_op jit(solution)/shard_map/send_x/pallas_call | solution.py:424
  1.9 4.3 %collective-permute-start = (f32[15,16,128]{2,1,0:T(8,128)}, f32[15,16,128]{2,1,0:T(8,128)S(1)}, u32[]{:S(2)}, u32[]{:S(2)}) collective-permute-start(f32[15,16,128]{2,1,0:T(8,128)} %get-tuple-element.27), channel_id=1, source_target_pairs={{0,64},{64,128},{128,192},{192,256},{256,320},{320,384},{384,448},... | collective-permute-start | bytes 368648 | tf_op jit(solution)/shard_map/ppermute | solution.py:440
  6.2 1.3 %collective-permute-start.1 = (f32[15,16,128]{2,1,0:T(8,128)}, f32[15,16,128]{2,1,0:T(8,128)S(1)}, u32[]{:S(2)}, u32[]{:S(2)}) collective-permute-start(f32[15,16,128]{2,1,0:T(8,128)} %get-tuple-element.28), channel_id=1, source_target_pairs={{64,0},{128,64},{192,128},{256,192},{320,256},{384,320},{448,384},... | collective-permute-start | bytes 368648 | tf_op jit(solution)/shard_map/ppermute | solution.py:440
  7.5 0.0 copy-start.2
  7.5 1.0 %copy-done.2 = f32[3,16,16,128]{3,2,1,0:T(8,128)S(1)} copy-done((f32[3,16,16,128]{3,2,1,0:T(8,128)S(1)}, f32[3,16,16,128]{3,2,1,0:T(8,128)}, u32[]{:S(2)}) %copy-start.2) | copy-done | bytes 393240
  8.5 0.5 collective-permute-done.from_down
  9.1 4.6 %collective-permute-done.1.from_up = f32[15,16,128]{2,1,0:T(8,128)S(1)} collective-permute-done((f32[15,16,128]{2,1,0:T(8,128)}, f32[15,16,128]{2,1,0:T(8,128)S(1)}, u32[]{:S(2)}, u32[]{:S(2)}) %collective-permute-start.1) | collective-permute-done | bytes 122912 | tf_op jit(solution)/shard_map/ppermute | solution.py:440
  13.7 0.1 pack_y.1
  13.9 1.9 %collective-permute-start.2 = (f32[28,16,128]{2,1,0:T(8,128)S(1)}, f32[28,16,128]{2,1,0:T(8,128)S(1)}, u32[]{:S(2)}, u32[]{:S(2)}) collective-permute-start(f32[28,16,128]{2,1,0:T(8,128)S(1)} %get-tuple-element.34), channel_id=1, source_target_pairs={{0,16},{16,32},{32,48},{1,17},{17,33},{33,49},{2,18},{18,34},{34,5... | collective-permute-start | bytes 688136 | tf_op jit(solution)/shard_map/ppermute | solution.py:440
  15.8 3.6 %collective-permute-start.3 = (f32[28,16,128]{2,1,0:T(8,128)S(1)}, f32[28,16,128]{2,1,0:T(8,128)S(1)}, u32[]{:S(2)}, u32[]{:S(2)}) collective-permute-start(f32[28,16,128]{2,1,0:T(8,128)S(1)} %get-tuple-element.35), channel_id=1, source_target_pairs={{16,0},{32,16},{48,32},{17,1},{33,17},{49,33},{18,2},{34,18},{50,3... | collective-permute-start | bytes 688136 | tf_op jit(solution)/shard_map/ppermute | solution.py:440
  19.4 1.8 %collective-permute-done.2.from_down = f32[28,16,128]{2,1,0:T(8,128)S(1)} collective-permute-done((f32[28,16,128]{2,1,0:T(8,128)S(1)}, f32[28,16,128]{2,1,0:T(8,128)S(1)}, u32[]{:S(2)}, u32[]{:S(2)}) %collective-permute-start.2) | collective-permute-done | bytes 229408 | tf_op jit(solution)/shard_map/ppermute | solution.py:440
  21.2 1.8 %collective-permute-done.3.from_up = f32[28,16,128]{2,1,0:T(8,128)S(1)} collective-permute-done((f32[28,16,128]{2,1,0:T(8,128)S(1)}, f32[28,16,128]{2,1,0:T(8,128)S(1)}, u32[]{:S(2)}, u32[]{:S(2)}) %collective-permute-start.3) | collective-permute-done | bytes 229408 | tf_op jit(solution)/shard_map/ppermute | solution.py:440
  23.0 1.8 %pack_z.1 = (f32[3,28,32,128]{3,2,1,0:T(8,128)S(1)}, f32[32,512]{1,0:T(8,128)S(1)}, f32[32,512]{1,0:T(8,128)S(1)}, f32[16,128]{1,0:T(8,128)S(1)}) custom-call(f32[3,28,16,128]{3,2,1,0:T(8,128)S(1)} %get-tuple-element.33.ext, f32[28,16,128]{2,1,0:T(8,128)S(1)} %collective-permute-done.2.from_down, f32[28,16,128]{2,1,0:T(8,128)S(1)} %collective-permute-done.3.from_up), custom_call_target="tpu_custom_call" | custom-call | flops 1000000 | bytes 1146880 | tf_op jit(solution)/shard_map/pack_z/pallas_call | solution.py:424
  24.8 3.6 %collective-permute-start.4 = (f32[32,512]{1,0:T(8,128)S(1)}, f32[32,512]{1,0:T(8,128)S(1)}, u32[]{:S(2)}, u32[]{:S(2)}) collective-permute-start(f32[32,512]{1,0:T(8,128)S(1)} %get-tuple-element.36.sent_up), channel_id=1, source_target_pairs={{0,1},{1,2},{2,3},{3,4},{4,5},{5,6},{6,7},{7,8},{8,9},{9,10},{10,1... | collective-permute-start | bytes 196616 | tf_op jit(solution)/shard_map/ppermute | solution.py:440
  28.4 3.1 %collective-permute-start.5 = (f32[32,512]{1,0:T(8,128)S(1)}, f32[32,512]{1,0:T(8,128)S(1)}, u32[]{:S(2)}, u32[]{:S(2)}) collective-permute-start(f32[32,512]{1,0:T(8,128)S(1)} %get-tuple-element.37.sent_down), channel_id=1, source_target_pairs={{1,0},{2,1},{3,2},{4,3},{5,4},{6,5},{7,6},{8,7},{9,8},{10,9},{11,1... | collective-permute-start | bytes 196616 | tf_op jit(solution)/shard_map/ppermute | solution.py:440
  31.5 0.1 pad_add_fusion.place
  31.6 1.3 %bands_xy.1 = (f32[3,28,32,128]{3,2,1,0:T(8,128)S(1)}, bf16[576,512]{1,0:T(8,128)(2,1)S(1)}) custom-call(s32[2]{0:T(128)S(1)} %pad_add_fusion.place, f32[3,28,32,128]{3,2,1,0:T(8,128)S(1)} %get-tuple-element.38.full), custom_call_target="tpu_custom_call" | custom-call | flops 30000000 | bytes 1376264 | tf_op jit(solution)/shard_map/bands_xy/pallas_call | solution.py:424
  33.0 0.0 copy-start
  33.0 0.8 %copy-done = bf16[576,512]{1,0:T(8,128)(2,1)} copy-done((bf16[576,512]{1,0:T(8,128)(2,1)}, bf16[576,512]{1,0:T(8,128)(2,1)S(1)}, u32[]{:S(2)}) %copy-start) | copy-done | bytes 589848
  33.8 0.0 collective-permute-done.4.from_down
  33.8 4.3 %collective-permute-done.5.from_up = f32[32,512]{1,0:T(8,128)S(1)} collective-permute-done((f32[32,512]{1,0:T(8,128)S(1)}, f32[32,512]{1,0:T(8,128)S(1)}, u32[]{:S(2)}, u32[]{:S(2)}) %collective-permute-start.5) | collective-permute-done | bytes 65568 | tf_op jit(solution)/shard_map/ppermute | solution.py:440
  38.1 1.6 %own_cells.1 = f32[32,16,128]{2,1,0:T(8,128)} custom-call(f32[32,512]{1,0:T(8,128)S(1)} %get-tuple-element.36.sent_up, f32[32,512]{1,0:T(8,128)S(1)} %get-tuple-element.37.sent_down, f32[32,512]{1,0:T(8,128)S(1)} %collective-permute-done.4.from_down, f32[32,512]{1,0:T(8,128)S(1)} %collective-permute-done.5.from_up, f32[16,128]{1,0:T(8,128)S(1)} %get-tuple-element.44.inner), custom_call_target="tpu_custom_call" | custom-call | flops 1000000 | bytes 270336 | tf_op jit(solution)/shard_map/own_cells/pallas_call | solution.py:424
  39.7 10.8 %all-to-all-start = ((f32[32,16,128]{2,1,0:T(8,128)}), f32[32,16,128]{2,1,0:T(8,128)S(1)}, u32[]{:S(2)}, u32[]{:S(2)}) async-start(f32[32,16,128]{2,1,0:T(8,128)} %own_cells.1), calls=%async_computation | async-start | bytes 524288 | tf_op jit(solution)/shard_map/all_to_all | solution.py:480
  50.5 3.3 %fine_residual.1 = (f32[28,32,256]{2,1,0:T(8,128)S(1)}, f32[28,32,256]{2,1,0:T(8,128)S(1)}, f32[28,32,256]{2,1,0:T(8,128)S(1)}) custom-call(f32[3,28,32,128]{3,2,1,0:T(8,128)S(1)} %get-tuple-element.38.full, f32[3,28,32,128]{3,2,1,0:T(8,128)S(1)} %get-tuple-element.45.xy, f32[32,512]{1,0:T(8,128)S(1)} %collective-permute-done.4.from_down, ...), custom_call_target="tpu_custom_call" | custom-call | flops 30000000 | bytes 2883584 | tf_op jit(solution)/shard_map/fine_residual/pallas_call | solution.py:424
  53.8 0.0 copy-start.1
  53.8 6.1 %fine_sweeps.1.base = f32[16,16,128]{2,1,0:T(8,128)S(1)} custom-call(f32[3,28,32,128]{3,2,1,0:T(8,128)S(1)} %get-tuple-element.38.full, f32[28,32,256]{2,1,0:T(8,128)S(1)} %get-tuple-element.46.coef, f32[28,32,256]{2,1,0:T(8,128)S(1)} %get-tuple-element.47.res, f32[28,32,256]{2,1,0:T(8,128)S(1)} %get-tuple-element.48.inv), custom_call_target="tpu_custom_call" | custom-call | flops 60000000 | bytes 4128768 | tf_op jit(solution)/shard_map/fine_sweeps/pallas_call | solution.py:424
  59.9 2.5 %all-to-all-done = f32[32,16,128]{2,1,0:T(8,128)S(1)} async-done(((f32[32,16,128]{2,1,0:T(8,128)}), f32[32,16,128]{2,1,0:T(8,128)S(1)}, u32[]{:S(2)}, u32[]{:S(2)}) %all-to-all-start) | async-done | bytes 262176 | tf_op jit(solution)/shard_map/all_to_all | solution.py:480
  62.4 0.0 copy-done.1
  62.4 2.7 %coarse_levels.1 = f32[16,16,128]{2,1,0:T(8,128)} custom-call(bf16[576,512]{1,0:T(8,128)(2,1)S(1)} %copy-done.1, f32[512,128]{1,0:T(8,128)S(1)} %bitcast.3, f32[16,16,128]{2,1,0:T(8,128)S(1)} %fine_sweeps.1.base), custom_call_target="tpu_custom_call" | custom-call | flops 30000000 | bytes 1572864 | tf_op jit(solution)/shard_map/coarse_levels/pallas_call | solution.py:424
  (1 shorter events, 0.0 us)
Async XLA Ops:
  1.9 7.2 %collective-permute-start = (f32[15,16,128]{2,1,0:T(8,128)}, f32[15,16,128]{2,1,0:T(8,128)S(1)}, u32[]{:S(2)}, u32[]{:S(2)}) collective-permute-start(f32[15,16,128]{2,1,0:T(8,128)} %get-tuple-element.27), channel_id=1, source_target_pairs={{0,64},{64,128},{128,192},{192,256},{256,320},{320,384},{384,448},... | collective-permute-start | bytes 368648 | tf_op jit(solution)/shard_map/ppermute | solution.py:440
  6.2 7.5 %collective-permute-start.1 = (f32[15,16,128]{2,1,0:T(8,128)}, f32[15,16,128]{2,1,0:T(8,128)S(1)}, u32[]{:S(2)}, u32[]{:S(2)}) collective-permute-start(f32[15,16,128]{2,1,0:T(8,128)} %get-tuple-element.28), channel_id=1, source_target_pairs={{64,0},{128,64},{192,128},{256,192},{320,256},{384,320},{448,384},... | collective-permute-start | bytes 368648 | tf_op jit(solution)/shard_map/ppermute | solution.py:440
  7.5 1.0 %copy-start.2 = (f32[3,16,16,128]{3,2,1,0:T(8,128)S(1)}, f32[3,16,16,128]{3,2,1,0:T(8,128)}, u32[]{:S(2)}) copy-start(f32[3,16,16,128]{3,2,1,0:T(8,128)} %get-tuple-element.29.fields) | copy-start | bytes 1179652
  13.9 7.3 %collective-permute-start.2 = (f32[28,16,128]{2,1,0:T(8,128)S(1)}, f32[28,16,128]{2,1,0:T(8,128)S(1)}, u32[]{:S(2)}, u32[]{:S(2)}) collective-permute-start(f32[28,16,128]{2,1,0:T(8,128)S(1)} %get-tuple-element.34), channel_id=1, source_target_pairs={{0,16},{16,32},{32,48},{1,17},{17,33},{33,49},{2,18},{18,34},{34,5... | collective-permute-start | bytes 688136 | tf_op jit(solution)/shard_map/ppermute | solution.py:440
  15.8 7.2 %collective-permute-start.3 = (f32[28,16,128]{2,1,0:T(8,128)S(1)}, f32[28,16,128]{2,1,0:T(8,128)S(1)}, u32[]{:S(2)}, u32[]{:S(2)}) collective-permute-start(f32[28,16,128]{2,1,0:T(8,128)S(1)} %get-tuple-element.35), channel_id=1, source_target_pairs={{16,0},{32,16},{48,32},{17,1},{33,17},{49,33},{18,2},{34,18},{50,3... | collective-permute-start | bytes 688136 | tf_op jit(solution)/shard_map/ppermute | solution.py:440
  24.8 9.0 %collective-permute-start.4 = (f32[32,512]{1,0:T(8,128)S(1)}, f32[32,512]{1,0:T(8,128)S(1)}, u32[]{:S(2)}, u32[]{:S(2)}) collective-permute-start(f32[32,512]{1,0:T(8,128)S(1)} %get-tuple-element.36.sent_up), channel_id=1, source_target_pairs={{0,1},{1,2},{2,3},{3,4},{4,5},{5,6},{6,7},{7,8},{8,9},{9,10},{10,1... | collective-permute-start | bytes 196616 | tf_op jit(solution)/shard_map/ppermute | solution.py:440
  28.4 9.7 %collective-permute-start.5 = (f32[32,512]{1,0:T(8,128)S(1)}, f32[32,512]{1,0:T(8,128)S(1)}, u32[]{:S(2)}, u32[]{:S(2)}) collective-permute-start(f32[32,512]{1,0:T(8,128)S(1)} %get-tuple-element.37.sent_down), channel_id=1, source_target_pairs={{1,0},{2,1},{3,2},{4,3},{5,4},{6,5},{7,6},{8,7},{9,8},{10,9},{11,1... | collective-permute-start | bytes 196616 | tf_op jit(solution)/shard_map/ppermute | solution.py:440
  33.0 0.8 %copy-start = (bf16[576,512]{1,0:T(8,128)(2,1)}, bf16[576,512]{1,0:T(8,128)(2,1)S(1)}, u32[]{:S(2)}) copy-start(bf16[576,512]{1,0:T(8,128)(2,1)S(1)} %get-tuple-element.41.patterns) | copy-start | bytes 1769476
  39.7 22.7 %all-to-all-start = ((f32[32,16,128]{2,1,0:T(8,128)}), f32[32,16,128]{2,1,0:T(8,128)S(1)}, u32[]{:S(2)}, u32[]{:S(2)}) async-start(f32[32,16,128]{2,1,0:T(8,128)} %own_cells.1), calls=%async_computation | async-start | bytes 524288 | tf_op jit(solution)/shard_map/all_to_all | solution.py:480
  53.8 8.6 %copy-start.1 = (bf16[576,512]{1,0:T(8,128)(2,1)S(1)}, bf16[576,512]{1,0:T(8,128)(2,1)}, u32[]{:S(2)}) copy-start(bf16[576,512]{1,0:T(8,128)(2,1)} %copy-done) | copy-start | bytes 1769476

commit v8 on v7

--- a/solution.py
+++ b/solution.py
@@ -20,22 +20,31 @@
     return jnp.where(cond, F32(scale), F32(0.0)).astype(BF16)
 
 
-def split3(x):
+def split(x):
     high = x.astype(BF16)
-    rest = x - high.astype(F32)
-    middle = rest.astype(BF16)
-    low = (rest - middle.astype(F32)).astype(BF16)
-    return high, middle, low
+    return high, (x - high.astype(F32)).astype(BF16)
 
 
 def select_rows(pattern, x):
-    parts = [jnp.dot(pattern, part, preferred_element_type=F32) for part in split3(x)]
-    return parts[0] + (parts[1] + parts[2])
+    high, low = [jnp.dot(pattern, part, preferred_element_type=F32) for part in split(x)]
+    return high + low
 
 
 def select_lanes(x, pattern):
-    parts = [jnp.dot(part, pattern, preferred_element_type=F32) for part in split3(x)]
-    return parts[0] + (parts[1] + parts[2])
+    high, low = [jnp.dot(part, pattern, preferred_element_type=F32) for part in split(x)]
+    return high + low
+
+
+def band_matrix(size):
+    apart = jnp.abs(iota((size, size), 0) - iota((size, size), 1))
+    return jnp.where(apart == 0, 2.0, jnp.where((apart == 1) | (apart == size - 1), 1.0, 0.0)).astype(BF16)
+
+
+def band_z(fields, matrix):
+    shape = fields[0].shape
+    rows = fields[0].size // shape[-1]
+    found = select_lanes(jnp.concatenate([f.reshape(rows, shape[-1]) for f in fields], axis=0), matrix)
+    return [found[rows * at : rows * at + rows].reshape(shape) for at in range(len(fields))]
 
 
 def band(x, axis):
@@ -63,18 +72,13 @@
 
 
 def smooth_small(residual, coef, sweeps):
-    inverse = damped_inverse(coef, 6.0 * coef + 0.125 * band_x(band_yz(coef)))
+    matrix = band_matrix(coef.shape[-1])
+    inverse = damped_inverse(coef, 6.0 * coef + 0.125 * band_z([band_x(band(coef, 1))], matrix)[0])
     corr = inverse * residual
     for _ in range(sweeps - 1):
-        corr = relax(corr, inverse, residual, coef, band_x(band_yz(corr)), band_x(band_yz(coef * corr)))
+        tu = band_z([band_x(band(f, 1)) for f in (corr, coef * corr)], matrix)
+        corr = relax(corr, inverse, residual, coef, *tu)
     return corr
-
-
-def lookup(phase, values):
-    k = jnp.zeros(phase.shape, F32)
-    for index in range(4):
-        k = jnp.where(phase == index, values[index], k)
-    return k
 
 
 def send_x(table, phase, iterate, right, fields, to_up, to_down, values, phases, sems):
@@ -149,11 +153,16 @@
 
     lax.fori_loop(5, 23, bands_y, 0, unroll=2)
 
+    matrix = band_matrix(128)
+
     def quad(q, carry):
         sums = [None, None]
-        for j in range(4):
-            x = 6 + 4 * q + j
-            tu = [band((in_y[at, x - 1] + in_y[at, x + 1]) + 2.0 * in_y[at, x], 1) for at in range(3)]
+        xs = [6 + 4 * q + j for j in range(4)]
+        all_tu = band_z(
+            [(in_y[at, x - 1] + in_y[at, x + 1]) + 2.0 * in_y[at, x] for x in xs for at in range(3)], matrix
+        )
+        for j, x in enumerate(xs):
+            tu = all_tu[3 * j : 3 * j + 3]
             k = full[0, x, 0:16, :]
             v = full[1, x, 0:16, :]
             diagonal = 6.0 * k + 0.125 * tu[0]
@@ -198,7 +207,7 @@
     return pltpu.roll(x, shift, 1) if shift else x
 
 
-def bands_xy(place, full, xy, patterns, bands):
+def bands_xy(place, full, xy, tables, bands):
     row = iota((192, 512), 0)
     cell = iota((192, 512), 1)
     cell_x = (cell >> 6) * 4 + ((cell >> 2) & 3)
@@ -207,7 +216,24 @@
         at_x = place[0] * (4 >> level) - 4 + (row >> 4)
         at_y = place[1] * (4 >> level) - 4 + (row & 15)
         found = ((cell_x >> level) == at_x) & ((cell_y >> level) == at_y)
-        patterns[192 * level : 192 * level + 192, :] = ones_where(found)
+        tables[192 * level : 192 * level + 192, :] = ones_where(found)
+    source = iota((128, 256), 0)
+    lane = iota((128, 256), 1)
+    is_coef = source >> 6
+    for level, start in enumerate((0, 64, 96)):
+        scale = jnp.where(is_coef == 1, F32(0.125**level), F32(0.5**level))
+        found = lane == is_coef * 128 + start + ((source & 63) >> level)
+        at = 576 + 128 * level
+        tables[at : at + 128, 0:256] = jnp.where(found, scale, 0.0).astype(BF16)
+    source = iota((128, 128), 0)
+    lane = iota((128, 128), 1)
+    row = iota((256, 64), 0)
+    found = iota((256, 64), 1)
+    for level, start in enumerate((16, 72, 100)):
+        shift = level + 2
+        tables[960:1088, 128 * level : 128 * level + 128] = ones_where(source == start + (lane >> shift))
+        at = ((row >> 4) >> shift) * 16 + 4 + ((row & 15) >> shift)
+        tables[1088:1344, 64 * level : 64 * level + 64] = ones_where(found == at)
 
     def in_y(x, carry):
         k = full[0, x]
@@ -309,62 +335,83 @@
     def over_x(ref, x):
         return (ref[x - 1] + ref[x + 1]) + 2.0 * ref[x]
 
-    def cells(x, carry):
-        sides = over_x(sides_kv, x)
-        tu_k = band(jnp.concatenate([xy[0, x], sides[:, 0:128]], axis=1), 1)
-        tu_v = band(jnp.concatenate([xy[1, x], sides[:, 128:256]], axis=1), 1)
-        tu_kv = band(jnp.concatenate([xy[2, x], over_x(product, x)], axis=1), 1)
-        k = coef[x]
-        v = jnp.concatenate([full[1, x], side[0, x]], axis=1)
-        diagonal = 6.0 * k + 0.125 * tu_k
-        applied = v * diagonal + 2.0 * (k * v) - 0.125 * (k * tu_v + tu_kv)
-        res[x] = jnp.concatenate([full[2, x], side[1, x]], axis=1) - applied
-        inv[x] = damped_inverse(k, diagonal)
-        return carry
-
-    lax.fori_loop(2, 26, cells, 0, unroll=2)
-
-
-def fine_sweeps(full, coef, res, inv, base, corr, corr_next, yz_c, yz_kc, pairs, narrow, spread):
+    matrix = band_matrix(256)
+
+    def cells(step, carry):
+        xs = [2 + 8 * step + j for j in range(8)]
+        wanted = []
+        for x in xs:
+            sides = over_x(sides_kv, x)
+            wanted += [
+                jnp.concatenate([xy[0, x], sides[:, 0:128]], axis=1),
+                jnp.concatenate([xy[1, x], sides[:, 128:256]], axis=1),
+                jnp.concatenate([xy[2, x], over_x(product, x)], axis=1),
+            ]
+        found = band_z(wanted, matrix)
+        for j, x in enumerate(xs):
+            tu_k, tu_v, tu_kv = found[3 * j : 3 * j + 3]
+            k = coef[x]
+            v = jnp.concatenate([full[1, x], side[0, x]], axis=1)
+            diagonal = 6.0 * k + 0.125 * tu_k
+            applied = v * diagonal + 2.0 * (k * v) - 0.125 * (k * tu_v + tu_kv)
+            res[x] = jnp.concatenate([full[2, x], side[1, x]], axis=1) - applied
+            inv[x] = damped_inverse(k, diagonal)
+        return carry
+
+    lax.fori_loop(0, 3, cells, 0)
+
+
+def fine_sweeps(full, coef, res, inv, base, corr, corr_next, yz_c, yz_kc, pairs, spread):
     def over_x(ref, x):
         return (ref[x - 1] + ref[x + 1]) + 2.0 * ref[x]
 
-    def first_sweep(x, carry):
-        c = inv[x] * res[x]
-        corr[x] = c
-        yz_c[x] = band_yz(c)
-        yz_kc[x] = band_yz(coef[x] * c)
-        return carry
-
-    lax.fori_loop(4, 24, first_sweep, 0, unroll=2)
+    matrix = band_matrix(256)
+
+    def bands_of(xs, ref):
+        wanted = []
+        for x in xs:
+            c = ref[x]
+            wanted += [band(c, 0), band(coef[x] * c, 0)]
+        found = band_z(wanted, matrix)
+        for j, x in enumerate(xs):
+            yz_c[x] = found[2 * j]
+            yz_kc[x] = found[2 * j + 1]
+
+    def first_sweep(step, carry):
+        xs = [4 + 4 * step + j for j in range(4)]
+        for x in xs:
+            corr[x] = inv[x] * res[x]
+        bands_of(xs, corr)
+        return carry
+
+    lax.fori_loop(0, 5, first_sweep, 0)
 
     def second(x, carry):
         corr_next[x] = relax(corr[x], inv[x], res[x], coef[x], over_x(yz_c, x), over_x(yz_kc, x))
         return carry
 
-    lax.fori_loop(5, 23, second, 0, unroll=2)
-
-    def second_bands(x, carry):
-        c = corr_next[x]
-        yz_c[x] = band_yz(c)
-        yz_kc[x] = band_yz(coef[x] * c)
-        return carry
-
-    lax.fori_loop(5, 23, second_bands, 0, unroll=2)
+    lax.fori_loop(5, 23, second, 0, unroll=3)
+
+    def second_bands(step, carry):
+        bands_of([5 + 3 * step + j for j in range(3)], corr_next)
+        return carry
+
+    lax.fori_loop(0, 6, second_bands, 0)
 
     halves = ones_where((iota((256, 128), 0) >> 1) == iota((256, 128), 1))
 
-    def coarse(ref, scale):
-        def pair(x, carry):
-            pairs[pl.ds(pl.multiple_of(32 * x, 32), 32), :] = ref[2 * x] + ref[2 * x + 1]
-            return carry
-
-        lax.fori_loop(0, 14, pair, 0, unroll=2)
-        narrow[...] = select_lanes(pairs[...], halves)
-        summed = narrow[pl.ds(0, 224, stride=2), :] + narrow[pl.ds(1, 224, stride=2), :]
-        return (scale * summed).reshape(14, 16, 128)
-
-    corr_two = smooth_small(coarse(res, 0.5), coarse(coef, 0.125), 3)
+    def pair(x, carry):
+        for at, ref in enumerate((res, coef)):
+            f = ref[2 * x] + ref[2 * x + 1]
+            for tile in range(2):
+                place = pl.ds(pl.multiple_of(448 * at + 32 * x, 32), 32)
+                pairs[tile, place, :] = f[:, 128 * tile : 128 * tile + 128]
+        return carry
+
+    lax.fori_loop(0, 14, pair, 0, unroll=2)
+    sums = [pairs[tile, pl.ds(0, 448, stride=2), :] + pairs[tile, pl.ds(1, 448, stride=2), :] for tile in range(2)]
+    sums = select_lanes(jnp.concatenate(sums, axis=1), halves).reshape(2, 14, 16, 128)
+    corr_two = smooth_small(0.5 * sums[0], 0.125 * sums[1], 3)
     doubled = ones_where(iota((128, 128), 0) == (iota((128, 128), 1) >> 1))
     wide = select_lanes(corr_two[3:11].reshape(128, 128), doubled).reshape(8, 16, 128)
     rows = wide[:, 0:8, :].reshape(64, 128)
@@ -384,34 +431,18 @@
         base[block] = full[1, x, 0:16, :] + (c + spread[pl.ds(pl.multiple_of(16 * (block // 2), 16), 16), :])
         return carry
 
-    lax.fori_loop(6, 22, third, 0, unroll=2)
-
-
-def coarse_levels(patterns, plane, base, out):
-    found = jnp.dot(patterns[...], jnp.concatenate(split3(plane[...]), axis=1), preferred_element_type=F32)
-    found = found[:, 0:128] + (found[:, 128:256] + found[:, 256:384])
+    lax.fori_loop(6, 22, third, 0, unroll=4)
+
+
+def coarse_levels(tables, plane, base, out):
+    found = jnp.dot(tables[0:576, :], jnp.concatenate(split(plane[...]), axis=1), preferred_element_type=F32)
+    found = found[:, 0:128] + found[:, 128:256]
     windows = jnp.concatenate([found[192 * level : 192 * level + 192, :] for level in range(3)], axis=1)
-    source = iota((384, 256), 0)
-    lane = iota((384, 256), 1)
-    level = source >> 7
-    is_coef = (source >> 6) & 1
-    start = jnp.where(level == 0, 0, jnp.where(level == 1, 64, 96))
-    scale = jnp.where(is_coef == 1, jnp.where(level == 0, 1.0, jnp.where(level == 1, 0.125, 0.125**2)), 1.0)
-    scale = jnp.where(is_coef == 0, jnp.where(level == 0, 1.0, jnp.where(level == 1, 0.5, 0.25)), scale)
-    at = is_coef * 128 + start + ((source & 63) >> level)
-    both = select_lanes(windows, jnp.where(lane == at, scale, 0.0).astype(BF16))
+    both = select_lanes(windows, tables[576:960, 0:256])
     corr = smooth_small(both[:, 0:128].reshape(12, 16, 128), both[:, 128:256].reshape(12, 16, 128), 4)
-    source = iota((128, 384), 0)
-    lane = iota((128, 384), 1)
-    level = lane >> 7
-    start = jnp.where(level == 0, 16, jnp.where(level == 1, 72, 100))
-    wide = select_lanes(corr[4:8].reshape(64, 128), ones_where(source == start + ((lane & 127) >> (level + 2))))
+    wide = select_lanes(corr[4:8].reshape(64, 128), tables[960:1088, 0:384])
     wide = jnp.concatenate([wide[:, 128 * level : 128 * level + 128] for level in range(3)], axis=0)
-    row = iota((256, 192), 0)
-    found = iota((256, 192), 1)
-    shift = (found >> 6) + 2
-    at = ((row >> 4) >> shift) * 16 + 4 + ((row & 15) >> shift)
-    out[...] = base[...] + select_rows(ones_where((found & 63) == at), wide).reshape(16, 16, 128)
+    out[...] = base[...] + select_rows(tables[1088:1344, 0:192], wide).reshape(16, 16, 128)
 
 
 VMEM = pl.BlockSpec(memory_space=pltpu.VMEM)
@@ -465,15 +496,15 @@
     )
     from_down, from_up = swap("gz", to_up, to_down)
     place = jnp.stack([lax.axis_index("gx"), lax.axis_index("gy")]).astype(jnp.int32)
-    xy, patterns = call(
+    xy, tables = call(
         bands_xy,
-        [planes, jax.ShapeDtypeStruct((576, 512), BF16)],
+        [planes, jax.ShapeDtypeStruct((1344, 512), BF16)],
         [place, full],
         scratch=[planes],
         first=SMEM,
         flops=30000000,
     )
-    from_down, from_up, xy, patterns = lax.optimization_barrier((from_down, from_up, xy, patterns))
+    from_down, from_up, xy, tables = lax.optimization_barrier((from_down, from_up, xy, tables))
     z_sides = [from_down, from_up]
     count = lax.axis_size("gx") * lax.axis_size("gy")
     (chunks,) = call(own_cells, [(count, 16, 128)], [to_up, to_down, *z_sides, inner], scratch=[(256, 128)])
@@ -490,10 +521,10 @@
         fine_sweeps,
         [block],
         [full, coef, res, inv],
-        scratch=[wide, wide, wide, wide, (448, 256), (448, 128), (128, 128)],
+        scratch=[wide, wide, wide, wide, (2, 896, 128), (128, 128)],
         flops=60000000,
     )
-    (out,) = call(coarse_levels, [block], [patterns, plane.reshape(count * 16, 128), base], flops=30000000)
+    (out,) = call(coarse_levels, [block], [tables, plane.reshape(count * 16, 128), base], flops=30000000)
     return out
 
 

time: 65.5 us -> 65.5 us (level)
  Pallas kernels: 19 us -> 16.2 us
  waiting for transfers between devices: 15.5 us -> 17.9 us
    all_to_all x1, waiting for transfers between devices: 2.48 us -> 5.46 us  [on_device(): plane = lax.all_to_all(chunks, ('gx', 'gy'), 0, 0, tiled=True)]
    pallas_call x9, Pallas kernels: 19 us -> 16.2 us  [call(): pl.pallas_call(kernel, out_shape=[out if isinstance(out, jax.ShapeDtypeSt...]
  transfers between devices with their start and end apart: 7 -> 7, of which waited for: 6 -> 6; matrix products, arithmetic and copies ran while one was open for 0% -> 0% of each run, Pallas kernels for 17% -> 12%
where the time goes in v8:
time: 65.5 us; the launch traced here: 65.1 us
  starting transfers between devices  28.6 us (44%)
  waiting for transfers between devices  17.9 us (27%)
  Pallas kernels  16.2 us (25%)
  local copies, waits for them, and re-layouts  2.09 us (3%)
    ppermute x6, starting transfers between devices, swap(): return (lax.ppermute(to_up, axis, up), lax.ppermute(to_down, axis, down))  17.9 us
    pallas_call x9, Pallas kernels, call(): pl.pallas_call(kernel, out_shape=[out if isinstance(out, jax.ShapeDtypeSt...  16.2 us
    ppermute x6, waiting for transfers between devices, swap(): return (lax.ppermute(to_up, axis, up), lax.ppermute(to_down, axis, down))  12.4 us
    all_to_all x1, starting transfers between devices, on_device(): plane = lax.all_to_all(chunks, ('gx', 'gy'), 0, 0, tiled=True)  10.8 us
    all_to_all x1, waiting for transfers between devices, on_device(): plane = lax.all_to_all(chunks, ('gx', 'gy'), 0, 0, tiled=True)  5.46 us
    unnamed x6, local copies, waits for them, and re-layouts  2.09 us
  transfers between devices with their start and end apart: 7, of which 6 were waited for; matrix products, arithmetic and copies ran while one was open for 0% of the time, Pallas kernels for 12%

profile of v8, /device:TPU:56, one launch (start us, length us, event | category | flops | bytes accessed | tf_op | source)
XLA Modules:
  0.0 65.1 jit_solution(15307487676219655408)
XLA Ops:
  0.0 1.9 %send_x.1 = (f32[3,16,16,128]{3,2,1,0:T(8,128)}, f32[15,16,128]{2,1,0:T(8,128)}, f32[15,16,128]{2,1,0:T(8,128)}) custom-call(f32[4]{0:T(128)} %table.1, s32[16,16,128]{2,1,0:T(8,128)} %phase.1, f32[16,16,128]{2,1,0:T(8,128)} %iterate.1, f32[16,16,128]{2,1,0:T(8,128)} %right.1), custom_call_target="tpu_custom_call" | custom-call | flops 1000000 | bytes 393232 | tf_op jit(solution)/shard_map/send_x/pallas_call | solution.py:455
  1.9 4.3 %collective-permute-start = (f32[15,16,128]{2,1,0:T(8,128)}, f32[15,16,128]{2,1,0:T(8,128)S(1)}, u32[]{:S(2)}, u32[]{:S(2)}) collective-permute-start(f32[15,16,128]{2,1,0:T(8,128)} %get-tuple-element.27), channel_id=1, source_target_pairs={{0,64},{64,128},{128,192},{192,256},{256,320},{320,384},{384,448},... | collective-permute-start | bytes 368648 | tf_op jit(solution)/shard_map/ppermute | solution.py:471
  6.2 1.3 %collective-permute-start.1 = (f32[15,16,128]{2,1,0:T(8,128)}, f32[15,16,128]{2,1,0:T(8,128)S(1)}, u32[]{:S(2)}, u32[]{:S(2)}) collective-permute-start(f32[15,16,128]{2,1,0:T(8,128)} %get-tuple-element.28), channel_id=1, source_target_pairs={{64,0},{128,64},{192,128},{256,192},{320,256},{384,320},{448,384},... | collective-permute-start | bytes 368648 | tf_op jit(solution)/shard_map/ppermute | solution.py:471
  7.5 0.0 copy-start.2
  7.5 1.0 %copy-done.2 = f32[3,16,16,128]{3,2,1,0:T(8,128)S(1)} copy-done((f32[3,16,16,128]{3,2,1,0:T(8,128)S(1)}, f32[3,16,16,128]{3,2,1,0:T(8,128)}, u32[]{:S(2)}) %copy-start.2) | copy-done | bytes 393240
  8.5 0.5 collective-permute-done.from_down
  9.1 4.6 %collective-permute-done.1.from_up = f32[15,16,128]{2,1,0:T(8,128)S(1)} collective-permute-done((f32[15,16,128]{2,1,0:T(8,128)}, f32[15,16,128]{2,1,0:T(8,128)S(1)}, u32[]{:S(2)}, u32[]{:S(2)}) %collective-permute-start.1) | collective-permute-done | bytes 122912 | tf_op jit(solution)/shard_map/ppermute | solution.py:471
  13.7 0.1 pack_y.1
  13.9 1.9 %collective-permute-start.2 = (f32[28,16,128]{2,1,0:T(8,128)S(1)}, f32[28,16,128]{2,1,0:T(8,128)S(1)}, u32[]{:S(2)}, u32[]{:S(2)}) collective-permute-start(f32[28,16,128]{2,1,0:T(8,128)S(1)} %get-tuple-element.34), channel_id=1, source_target_pairs={{0,16},{16,32},{32,48},{1,17},{17,33},{33,49},{2,18},{18,34},{34,5... | collective-permute-start | bytes 688136 | tf_op jit(solution)/shard_map/ppermute | solution.py:471
  15.8 3.6 %collective-permute-start.3 = (f32[28,16,128]{2,1,0:T(8,128)S(1)}, f32[28,16,128]{2,1,0:T(8,128)S(1)}, u32[]{:S(2)}, u32[]{:S(2)}) collective-permute-start(f32[28,16,128]{2,1,0:T(8,128)S(1)} %get-tuple-element.35), channel_id=1, source_target_pairs={{16,0},{32,16},{48,32},{17,1},{33,17},{49,33},{18,2},{34,18},{50,3... | collective-permute-start | bytes 688136 | tf_op jit(solution)/shard_map/ppermute | solution.py:471
  19.4 1.8 %collective-permute-done.2.from_down = f32[28,16,128]{2,1,0:T(8,128)S(1)} collective-permute-done((f32[28,16,128]{2,1,0:T(8,128)S(1)}, f32[28,16,128]{2,1,0:T(8,128)S(1)}, u32[]{:S(2)}, u32[]{:S(2)}) %collective-permute-start.2) | collective-permute-done | bytes 229408 | tf_op jit(solution)/shard_map/ppermute | solution.py:471
  21.2 1.8 %collective-permute-done.3.from_up = f32[28,16,128]{2,1,0:T(8,128)S(1)} collective-permute-done((f32[28,16,128]{2,1,0:T(8,128)S(1)}, f32[28,16,128]{2,1,0:T(8,128)S(1)}, u32[]{:S(2)}, u32[]{:S(2)}) %collective-permute-start.3) | collective-permute-done | bytes 229408 | tf_op jit(solution)/shard_map/ppermute | solution.py:471
  23.0 1.8 %pack_z.1 = (f32[3,28,32,128]{3,2,1,0:T(8,128)S(1)}, f32[32,512]{1,0:T(8,128)S(1)}, f32[32,512]{1,0:T(8,128)S(1)}, f32[16,128]{1,0:T(8,128)S(1)}) custom-call(f32[3,28,16,128]{3,2,1,0:T(8,128)S(1)} %get-tuple-element.33.ext, f32[28,16,128]{2,1,0:T(8,128)S(1)} %collective-permute-done.2.from_down, f32[28,16,128]{2,1,0:T(8,128)S(1)} %collective-permute-done.3.from_up), custom_call_target="tpu_custom_call" | custom-call | flops 1000000 | bytes 1146880 | tf_op jit(solution)/shard_map/pack_z/pallas_call | solution.py:455
  24.8 3.6 %collective-permute-start.4 = (f32[32,512]{1,0:T(8,128)S(1)}, f32[32,512]{1,0:T(8,128)S(1)}, u32[]{:S(2)}, u32[]{:S(2)}) collective-permute-start(f32[32,512]{1,0:T(8,128)S(1)} %get-tuple-element.36.sent_up), channel_id=1, source_target_pairs={{0,1},{1,2},{2,3},{3,4},{4,5},{5,6},{6,7},{7,8},{8,9},{9,10},{10,1... | collective-permute-start | bytes 196616 | tf_op jit(solution)/shard_map/ppermute | solution.py:471
  28.4 3.1 %collective-permute-start.5 = (f32[32,512]{1,0:T(8,128)S(1)}, f32[32,512]{1,0:T(8,128)S(1)}, u32[]{:S(2)}, u32[]{:S(2)}) collective-permute-start(f32[32,512]{1,0:T(8,128)S(1)} %get-tuple-element.37.sent_down), channel_id=1, source_target_pairs={{1,0},{2,1},{3,2},{4,3},{5,4},{6,5},{7,6},{8,7},{9,8},{10,9},{11,1... | collective-permute-start | bytes 196616 | tf_op jit(solution)/shard_map/ppermute | solution.py:471
  31.6 0.1 pad_add_fusion.place
  31.7 1.6 %bands_xy.1 = (f32[3,28,32,128]{3,2,1,0:T(8,128)S(1)}, bf16[1344,512]{1,0:T(8,128)(2,1)S(1)}) custom-call(s32[2]{0:T(128)S(1)} %pad_add_fusion.place, f32[3,28,32,128]{3,2,1,0:T(8,128)S(1)} %get-tuple-element.38.full), custom_call_target="tpu_custom_call" | custom-call | flops 30000000 | bytes 1376264 | tf_op jit(solution)/shard_map/bands_xy/pallas_call | solution.py:455
  33.2 0.0 copy-start
  33.3 1.1 %copy-done = bf16[1344,512]{1,0:T(8,128)(2,1)} copy-done((bf16[1344,512]{1,0:T(8,128)(2,1)}, bf16[1344,512]{1,0:T(8,128)(2,1)S(1)}, u32[]{:S(2)}) %copy-start) | copy-done | bytes 1376280
  34.4 0.0 collective-permute-done.4.from_down
  34.4 3.7 %collective-permute-done.5.from_up = f32[32,512]{1,0:T(8,128)S(1)} collective-permute-done((f32[32,512]{1,0:T(8,128)S(1)}, f32[32,512]{1,0:T(8,128)S(1)}, u32[]{:S(2)}, u32[]{:S(2)}) %collective-permute-start.5) | collective-permute-done | bytes 65568 | tf_op jit(solution)/shard_map/ppermute | solution.py:471
  38.1 1.6 %own_cells.1 = f32[32,16,128]{2,1,0:T(8,128)} custom-call(f32[32,512]{1,0:T(8,128)S(1)} %get-tuple-element.36.sent_up, f32[32,512]{1,0:T(8,128)S(1)} %get-tuple-element.37.sent_down, f32[32,512]{1,0:T(8,128)S(1)} %collective-permute-done.4.from_down, f32[32,512]{1,0:T(8,128)S(1)} %collective-permute-done.5.from_up, f32[16,128]{1,0:T(8,128)S(1)} %get-tuple-element.44.inner), custom_call_target="tpu_custom_call" | custom-call | flops 1000000 | bytes 270336 | tf_op jit(solution)/shard_map/own_cells/pallas_call | solution.py:455
  39.7 10.8 %all-to-all-start = ((f32[32,16,128]{2,1,0:T(8,128)}), f32[32,16,128]{2,1,0:T(8,128)S(1)}, u32[]{:S(2)}, u32[]{:S(2)}) async-start(f32[32,16,128]{2,1,0:T(8,128)} %own_cells.1), calls=%async_computation | async-start | bytes 524288 | tf_op jit(solution)/shard_map/all_to_all | solution.py:511
  50.5 2.0 %fine_residual.1 = (f32[28,32,256]{2,1,0:T(8,128)S(1)}, f32[28,32,256]{2,1,0:T(8,128)S(1)}, f32[28,32,256]{2,1,0:T(8,128)S(1)}) custom-call(f32[3,28,32,128]{3,2,1,0:T(8,128)S(1)} %get-tuple-element.38.full, f32[3,28,32,128]{3,2,1,0:T(8,128)S(1)} %get-tuple-element.45.xy, f32[32,512]{1,0:T(8,128)S(1)} %collective-permute-done.4.from_down, ...), custom_call_target="tpu_custom_call" | custom-call | flops 30000000 | bytes 2883584 | tf_op jit(solution)/shard_map/fine_residual/pallas_call | solution.py:455
  52.5 0.0 copy-start.1
  52.5 4.5 %fine_sweeps.1.base = f32[16,16,128]{2,1,0:T(8,128)S(1)} custom-call(f32[3,28,32,128]{3,2,1,0:T(8,128)S(1)} %get-tuple-element.38.full, f32[28,32,256]{2,1,0:T(8,128)S(1)} %get-tuple-element.46.coef, f32[28,32,256]{2,1,0:T(8,128)S(1)} %get-tuple-element.47.res, f32[28,32,256]{2,1,0:T(8,128)S(1)} %get-tuple-element.48.inv), custom_call_target="tpu_custom_call" | custom-call | flops 60000000 | bytes 4128768 | tf_op jit(solution)/shard_map/fine_sweeps/pallas_call | solution.py:455
  56.9 5.5 %all-to-all-done = f32[32,16,128]{2,1,0:T(8,128)S(1)} async-done(((f32[32,16,128]{2,1,0:T(8,128)}), f32[32,16,128]{2,1,0:T(8,128)S(1)}, u32[]{:S(2)}, u32[]{:S(2)}) %all-to-all-start) | async-done | bytes 262176 | tf_op jit(solution)/shard_map/all_to_all | solution.py:511
  62.4 0.0 copy-done.1
  62.4 2.7 %coarse_levels.1 = f32[16,16,128]{2,1,0:T(8,128)} custom-call(bf16[1344,512]{1,0:T(8,128)(2,1)S(1)} %copy-done.1, f32[512,128]{1,0:T(8,128)S(1)} %bitcast.3, f32[16,16,128]{2,1,0:T(8,128)S(1)} %fine_sweeps.1.base), custom_call_target="tpu_custom_call" | custom-call | flops 30000000 | bytes 3145728 | tf_op jit(solution)/shard_map/coarse_levels/pallas_call | solution.py:455
  (1 shorter events, 0.0 us)
Async XLA Ops:
  1.9 7.2 %collective-permute-start = (f32[15,16,128]{2,1,0:T(8,128)}, f32[15,16,128]{2,1,0:T(8,128)S(1)}, u32[]{:S(2)}, u32[]{:S(2)}) collective-permute-start(f32[15,16,128]{2,1,0:T(8,128)} %get-tuple-element.27), channel_id=1, source_target_pairs={{0,64},{64,128},{128,192},{192,256},{256,320},{320,384},{384,448},... | collective-permute-start | bytes 368648 | tf_op jit(solution)/shard_map/ppermute | solution.py:471
  6.2 7.5 %collective-permute-start.1 = (f32[15,16,128]{2,1,0:T(8,128)}, f32[15,16,128]{2,1,0:T(8,128)S(1)}, u32[]{:S(2)}, u32[]{:S(2)}) collective-permute-start(f32[15,16,128]{2,1,0:T(8,128)} %get-tuple-element.28), channel_id=1, source_target_pairs={{64,0},{128,64},{192,128},{256,192},{320,256},{384,320},{448,384},... | collective-permute-start | bytes 368648 | tf_op jit(solution)/shard_map/ppermute | solution.py:471
  7.5 1.0 %copy-start.2 = (f32[3,16,16,128]{3,2,1,0:T(8,128)S(1)}, f32[3,16,16,128]{3,2,1,0:T(8,128)}, u32[]{:S(2)}) copy-start(f32[3,16,16,128]{3,2,1,0:T(8,128)} %get-tuple-element.29.fields) | copy-start | bytes 1179652
  13.9 7.3 %collective-permute-start.2 = (f32[28,16,128]{2,1,0:T(8,128)S(1)}, f32[28,16,128]{2,1,0:T(8,128)S(1)}, u32[]{:S(2)}, u32[]{:S(2)}) collective-permute-start(f32[28,16,128]{2,1,0:T(8,128)S(1)} %get-tuple-element.34), channel_id=1, source_target_pairs={{0,16},{16,32},{32,48},{1,17},{17,33},{33,49},{2,18},{18,34},{34,5... | collective-permute-start | bytes 688136 | tf_op jit(solution)/shard_map/ppermute | solution.py:471
  15.8 7.2 %collective-permute-start.3 = (f32[28,16,128]{2,1,0:T(8,128)S(1)}, f32[28,16,128]{2,1,0:T(8,128)S(1)}, u32[]{:S(2)}, u32[]{:S(2)}) collective-permute-start(f32[28,16,128]{2,1,0:T(8,128)S(1)} %get-tuple-element.35), channel_id=1, source_target_pairs={{16,0},{32,16},{48,32},{17,1},{33,17},{49,33},{18,2},{34,18},{50,3... | collective-permute-start | bytes 688136 | tf_op jit(solution)/shard_map/ppermute | solution.py:471
  24.8 9.5 %collective-permute-start.4 = (f32[32,512]{1,0:T(8,128)S(1)}, f32[32,512]{1,0:T(8,128)S(1)}, u32[]{:S(2)}, u32[]{:S(2)}) collective-permute-start(f32[32,512]{1,0:T(8,128)S(1)} %get-tuple-element.36.sent_up), channel_id=1, source_target_pairs={{0,1},{1,2},{2,3},{3,4},{4,5},{5,6},{6,7},{7,8},{8,9},{9,10},{10,1... | collective-permute-start | bytes 196616 | tf_op jit(solution)/shard_map/ppermute | solution.py:471
  28.4 9.7 %collective-permute-start.5 = (f32[32,512]{1,0:T(8,128)S(1)}, f32[32,512]{1,0:T(8,128)S(1)}, u32[]{:S(2)}, u32[]{:S(2)}) collective-permute-start(f32[32,512]{1,0:T(8,128)S(1)} %get-tuple-element.37.sent_down), channel_id=1, source_target_pairs={{1,0},{2,1},{3,2},{4,3},{5,4},{6,5},{7,6},{8,7},{9,8},{10,9},{11,1... | collective-permute-start | bytes 196616 | tf_op jit(solution)/shard_map/ppermute | solution.py:471
  33.2 1.1 %copy-start = (bf16[1344,512]{1,0:T(8,128)(2,1)}, bf16[1344,512]{1,0:T(8,128)(2,1)S(1)}, u32[]{:S(2)}) copy-start(bf16[1344,512]{1,0:T(8,128)(2,1)S(1)} %get-tuple-element.41.tables) | copy-start | bytes 4128772
  39.7 22.7 %all-to-all-start = ((f32[32,16,128]{2,1,0:T(8,128)}), f32[32,16,128]{2,1,0:T(8,128)S(1)}, u32[]{:S(2)}, u32[]{:S(2)}) async-start(f32[32,16,128]{2,1,0:T(8,128)} %own_cells.1), calls=%async_computation | async-start | bytes 524288 | tf_op jit(solution)/shard_map/all_to_all | solution.py:511
  52.5 9.9 %copy-start.1 = (bf16[1344,512]{1,0:T(8,128)(2,1)S(1)}, bf16[1344,512]{1,0:T(8,128)(2,1)}, u32[]{:S(2)}) copy-start(bf16[1344,512]{1,0:T(8,128)(2,1)} %copy-done) | copy-start | bytes 4128772

commit v9 on v8

--- a/solution.py
+++ b/solution.py
@@ -22,17 +22,19 @@
 
 def split(x):
     high = x.astype(BF16)
-    return high, (x - high.astype(F32)).astype(BF16)
+    rest = x - high.astype(F32)
+    middle = rest.astype(BF16)
+    return high, middle, (rest - middle.astype(F32)).astype(BF16)
 
 
 def select_rows(pattern, x):
-    high, low = [jnp.dot(pattern, part, preferred_element_type=F32) for part in split(x)]
-    return high + low
+    high, middle, low = [jnp.dot(pattern, part, preferred_element_type=F32) for part in split(x)]
+    return high + (middle + low)
 
 
 def select_lanes(x, pattern):
-    high, low = [jnp.dot(part, pattern, preferred_element_type=F32) for part in split(x)]
-    return high + low
+    high, middle, low = [jnp.dot(part, pattern, preferred_element_type=F32) for part in split(x)]
+    return high + (middle + low)
 
 
 def band_matrix(size):
@@ -48,12 +50,7 @@
 
 
 def band(x, axis):
-    x = x + pltpu.roll(x, 1, axis)
-    return x + pltpu.roll(x, x.shape[axis] - 1, axis)
-
-
-def band_yz(x):
-    return band(band(x, x.ndim - 1), x.ndim - 2)
+    return (pltpu.roll(x, 1, axis) + pltpu.roll(x, x.shape[axis] - 1, axis)) + 2.0 * x
 
 
 def band_x(x):
@@ -71,12 +68,11 @@
     return corr * (1.0 / 3.0) + inverse * (residual - 2.0 * (coef * corr) + 0.125 * (coef * tu_corr + tu_product))
 
 
-def smooth_small(residual, coef, sweeps):
-    matrix = band_matrix(coef.shape[-1])
-    inverse = damped_inverse(coef, 6.0 * coef + 0.125 * band_z([band_x(band(coef, 1))], matrix)[0])
+def smooth_small(residual, coef, sweeps, bands_z):
+    inverse = damped_inverse(coef, 6.0 * coef + 0.125 * bands_z([band_x(band(coef, 1))])[0])
     corr = inverse * residual
     for _ in range(sweeps - 1):
-        tu = band_z([band_x(band(f, 1)) for f in (corr, coef * corr)], matrix)
+        tu = bands_z([band_x(band(f, 1)) for f in (corr, coef * corr)])
         corr = relax(corr, inverse, residual, coef, *tu)
     return corr
 
@@ -411,7 +407,8 @@
     lax.fori_loop(0, 14, pair, 0, unroll=2)
     sums = [pairs[tile, pl.ds(0, 448, stride=2), :] + pairs[tile, pl.ds(1, 448, stride=2), :] for tile in range(2)]
     sums = select_lanes(jnp.concatenate(sums, axis=1), halves).reshape(2, 14, 16, 128)
-    corr_two = smooth_small(0.5 * sums[0], 0.125 * sums[1], 3)
+    small = band_matrix(128)
+    corr_two = smooth_small(0.5 * sums[0], 0.125 * sums[1], 3, lambda fields: band_z(fields, small))
     doubled = ones_where(iota((128, 128), 0) == (iota((128, 128), 1) >> 1))
     wide = select_lanes(corr_two[3:11].reshape(128, 128), doubled).reshape(8, 16, 128)
     rows = wide[:, 0:8, :].reshape(64, 128)
@@ -434,12 +431,16 @@
     lax.fori_loop(6, 22, third, 0, unroll=4)
 
 
+def rolled_bands(fields):
+    return [band(f, 2) for f in fields]
+
+
 def coarse_levels(tables, plane, base, out):
     found = jnp.dot(tables[0:576, :], jnp.concatenate(split(plane[...]), axis=1), preferred_element_type=F32)
-    found = found[:, 0:128] + found[:, 128:256]
+    found = found[:, 0:128] + (found[:, 128:256] + found[:, 256:384])
     windows = jnp.concatenate([found[192 * level : 192 * level + 192, :] for level in range(3)], axis=1)
     both = select_lanes(windows, tables[576:960, 0:256])
-    corr = smooth_small(both[:, 0:128].reshape(12, 16, 128), both[:, 128:256].reshape(12, 16, 128), 4)
+    corr = smooth_small(both[:, 0:128].reshape(12, 16, 128), both[:, 128:256].reshape(12, 16, 128), 4, rolled_bands)
     wide = select_lanes(corr[4:8].reshape(64, 128), tables[960:1088, 0:384])
     wide = jnp.concatenate([wide[:, 128 * level : 128 * level + 128] for level in range(3)], axis=0)
     out[...] = base[...] + select_rows(tables[1088:1344, 0:192], wide).reshape(16, 16, 128)

time: 65.5 us -> 65.2 us (level)
  waiting for transfers between devices: 17.9 us -> 16.7 us
  Pallas kernels: 16.2 us -> 17.2 us
    all_to_all x1, waiting for transfers between devices: 5.46 us -> 4.32 us  [on_device(): plane = lax.all_to_all(chunks, ('gx', 'gy'), 0, 0, tiled=True)]
    pallas_call x9, Pallas kernels: 16.2 us -> 17.2 us  [call(): pl.pallas_call(kernel, out_shape=[out if isinstance(out, jax.ShapeDtypeSt...]
  transfers between devices with their start and end apart: 7 -> 7, of which waited for: 6 -> 6; matrix products, arithmetic and copies ran while one was open for 0% -> 0% of each run, Pallas kernels for 12% -> 14%
where the time goes in v9:
time: 65.2 us; the launch traced here: 64.9 us
  starting transfers between devices  28.6 us (44%)
  Pallas kernels  17.2 us (26%)
  waiting for transfers between devices  16.7 us (26%)
  local copies, waits for them, and re-layouts  2.09 us (3%)
    ppermute x6, starting transfers between devices, swap(): return (lax.ppermute(to_up, axis, up), lax.ppermute(to_down, axis, down))  17.9 us
    pallas_call x9, Pallas kernels, call(): pl.pallas_call(kernel, out_shape=[out if isinstance(out, jax.ShapeDtypeSt...  17.2 us
    ppermute x6, waiting for transfers between devices, swap(): return (lax.ppermute(to_up, axis, up), lax.ppermute(to_down, axis, down))  12.4 us
    all_to_all x1, starting transfers between devices, on_device(): plane = lax.all_to_all(chunks, ('gx', 'gy'), 0, 0, tiled=True)  10.8 us
    all_to_all x1, waiting for transfers between devices, on_device(): plane = lax.all_to_all(chunks, ('gx', 'gy'), 0, 0, tiled=True)  4.32 us
    unnamed x6, local copies, waits for them, and re-layouts  2.09 us
  transfers between devices with their start and end apart: 7, of which 6 were waited for; matrix products, arithmetic and copies ran while one was open for 0% of the time, Pallas kernels for 14%

profile of v9, /device:TPU:56, one launch (start us, length us, event | category | flops | bytes accessed | tf_op | source)
XLA Modules:
  0.0 64.9 jit_solution(3513257397753891147)
XLA Ops:
  0.0 1.9 %send_x.1 = (f32[3,16,16,128]{3,2,1,0:T(8,128)}, f32[15,16,128]{2,1,0:T(8,128)}, f32[15,16,128]{2,1,0:T(8,128)}) custom-call(f32[4]{0:T(128)} %table.1, s32[16,16,128]{2,1,0:T(8,128)} %phase.1, f32[16,16,128]{2,1,0:T(8,128)} %iterate.1, f32[16,16,128]{2,1,0:T(8,128)} %right.1), custom_call_target="tpu_custom_call" | custom-call | flops 1000000 | bytes 393232 | tf_op jit(solution)/shard_map/send_x/pallas_call | solution.py:456
  1.9 4.3 %collective-permute-start = (f32[15,16,128]{2,1,0:T(8,128)}, f32[15,16,128]{2,1,0:T(8,128)S(1)}, u32[]{:S(2)}, u32[]{:S(2)}) collective-permute-start(f32[15,16,128]{2,1,0:T(8,128)} %get-tuple-element.27), channel_id=1, source_target_pairs={{0,64},{64,128},{128,192},{192,256},{256,320},{320,384},{384,448},... | collective-permute-start | bytes 368648 | tf_op jit(solution)/shard_map/ppermute | solution.py:472
  6.2 1.3 %collective-permute-start.1 = (f32[15,16,128]{2,1,0:T(8,128)}, f32[15,16,128]{2,1,0:T(8,128)S(1)}, u32[]{:S(2)}, u32[]{:S(2)}) collective-permute-start(f32[15,16,128]{2,1,0:T(8,128)} %get-tuple-element.28), channel_id=1, source_target_pairs={{64,0},{128,64},{192,128},{256,192},{320,256},{384,320},{448,384},... | collective-permute-start | bytes 368648 | tf_op jit(solution)/shard_map/ppermute | solution.py:472
  7.5 0.0 copy-start.2
  7.5 1.0 %copy-done.2 = f32[3,16,16,128]{3,2,1,0:T(8,128)S(1)} copy-done((f32[3,16,16,128]{3,2,1,0:T(8,128)S(1)}, f32[3,16,16,128]{3,2,1,0:T(8,128)}, u32[]{:S(2)}) %copy-start.2) | copy-done | bytes 393240
  8.5 0.5 collective-permute-done.from_down
  9.1 4.6 %collective-permute-done.1.from_up = f32[15,16,128]{2,1,0:T(8,128)S(1)} collective-permute-done((f32[15,16,128]{2,1,0:T(8,128)}, f32[15,16,128]{2,1,0:T(8,128)S(1)}, u32[]{:S(2)}, u32[]{:S(2)}) %collective-permute-start.1) | collective-permute-done | bytes 122912 | tf_op jit(solution)/shard_map/ppermute | solution.py:472
  13.7 0.1 pack_y.1
  13.9 1.9 %collective-permute-start.2 = (f32[28,16,128]{2,1,0:T(8,128)S(1)}, f32[28,16,128]{2,1,0:T(8,128)S(1)}, u32[]{:S(2)}, u32[]{:S(2)}) collective-permute-start(f32[28,16,128]{2,1,0:T(8,128)S(1)} %get-tuple-element.34), channel_id=1, source_target_pairs={{0,16},{16,32},{32,48},{1,17},{17,33},{33,49},{2,18},{18,34},{34,5... | collective-permute-start | bytes 688136 | tf_op jit(solution)/shard_map/ppermute | solution.py:472
  15.8 3.6 %collective-permute-start.3 = (f32[28,16,128]{2,1,0:T(8,128)S(1)}, f32[28,16,128]{2,1,0:T(8,128)S(1)}, u32[]{:S(2)}, u32[]{:S(2)}) collective-permute-start(f32[28,16,128]{2,1,0:T(8,128)S(1)} %get-tuple-element.35), channel_id=1, source_target_pairs={{16,0},{32,16},{48,32},{17,1},{33,17},{49,33},{18,2},{34,18},{50,3... | collective-permute-start | bytes 688136 | tf_op jit(solution)/shard_map/ppermute | solution.py:472
  19.4 1.8 %collective-permute-done.2.from_down = f32[28,16,128]{2,1,0:T(8,128)S(1)} collective-permute-done((f32[28,16,128]{2,1,0:T(8,128)S(1)}, f32[28,16,128]{2,1,0:T(8,128)S(1)}, u32[]{:S(2)}, u32[]{:S(2)}) %collective-permute-start.2) | collective-permute-done | bytes 229408 | tf_op jit(solution)/shard_map/ppermute | solution.py:472
  21.2 1.8 %collective-permute-done.3.from_up = f32[28,16,128]{2,1,0:T(8,128)S(1)} collective-permute-done((f32[28,16,128]{2,1,0:T(8,128)S(1)}, f32[28,16,128]{2,1,0:T(8,128)S(1)}, u32[]{:S(2)}, u32[]{:S(2)}) %collective-permute-start.3) | collective-permute-done | bytes 229408 | tf_op jit(solution)/shard_map/ppermute | solution.py:472
  23.0 1.9 %pack_z.1 = (f32[3,28,32,128]{3,2,1,0:T(8,128)S(1)}, f32[32,512]{1,0:T(8,128)S(1)}, f32[32,512]{1,0:T(8,128)S(1)}, f32[16,128]{1,0:T(8,128)S(1)}) custom-call(f32[3,28,16,128]{3,2,1,0:T(8,128)S(1)} %get-tuple-element.33.ext, f32[28,16,128]{2,1,0:T(8,128)S(1)} %collective-permute-done.2.from_down, f32[28,16,128]{2,1,0:T(8,128)S(1)} %collective-permute-done.3.from_up), custom_call_target="tpu_custom_call" | custom-call | flops 1000000 | bytes 1146880 | tf_op jit(solution)/shard_map/pack_z/pallas_call | solution.py:456
  24.9 3.6 %collective-permute-start.4 = (f32[32,512]{1,0:T(8,128)S(1)}, f32[32,512]{1,0:T(8,128)S(1)}, u32[]{:S(2)}, u32[]{:S(2)}) collective-permute-start(f32[32,512]{1,0:T(8,128)S(1)} %get-tuple-element.36.sent_up), channel_id=1, source_target_pairs={{0,1},{1,2},{2,3},{3,4},{4,5},{5,6},{6,7},{7,8},{8,9},{9,10},{10,1... | collective-permute-start | bytes 196616 | tf_op jit(solution)/shard_map/ppermute | solution.py:472
  28.5 3.1 %collective-permute-start.5 = (f32[32,512]{1,0:T(8,128)S(1)}, f32[32,512]{1,0:T(8,128)S(1)}, u32[]{:S(2)}, u32[]{:S(2)}) collective-permute-start(f32[32,512]{1,0:T(8,128)S(1)} %get-tuple-element.37.sent_down), channel_id=1, source_target_pairs={{1,0},{2,1},{3,2},{4,3},{5,4},{6,5},{7,6},{8,7},{9,8},{10,9},{11,1... | collective-permute-start | bytes 196616 | tf_op jit(solution)/shard_map/ppermute | solution.py:472
  31.6 0.1 pad_add_fusion.place
  31.7 1.6 %bands_xy.1 = (f32[3,28,32,128]{3,2,1,0:T(8,128)S(1)}, bf16[1344,512]{1,0:T(8,128)(2,1)S(1)}) custom-call(s32[2]{0:T(128)S(1)} %pad_add_fusion.place, f32[3,28,32,128]{3,2,1,0:T(8,128)S(1)} %get-tuple-element.38.full), custom_call_target="tpu_custom_call" | custom-call | flops 30000000 | bytes 1376264 | tf_op jit(solution)/shard_map/bands_xy/pallas_call | solution.py:456
  33.3 0.0 copy-start
  33.4 1.1 %copy-done = bf16[1344,512]{1,0:T(8,128)(2,1)} copy-done((bf16[1344,512]{1,0:T(8,128)(2,1)}, bf16[1344,512]{1,0:T(8,128)(2,1)S(1)}, u32[]{:S(2)}) %copy-start) | copy-done | bytes 1376280
  34.4 0.0 collective-permute-done.4.from_down
  34.5 3.7 %collective-permute-done.5.from_up = f32[32,512]{1,0:T(8,128)S(1)} collective-permute-done((f32[32,512]{1,0:T(8,128)S(1)}, f32[32,512]{1,0:T(8,128)S(1)}, u32[]{:S(2)}, u32[]{:S(2)}) %collective-permute-start.5) | collective-permute-done | bytes 65568 | tf_op jit(solution)/shard_map/ppermute | solution.py:472
  38.2 1.6 %own_cells.1 = f32[32,16,128]{2,1,0:T(8,128)} custom-call(f32[32,512]{1,0:T(8,128)S(1)} %get-tuple-element.36.sent_up, f32[32,512]{1,0:T(8,128)S(1)} %get-tuple-element.37.sent_down, f32[32,512]{1,0:T(8,128)S(1)} %collective-permute-done.4.from_down, f32[32,512]{1,0:T(8,128)S(1)} %collective-permute-done.5.from_up, f32[16,128]{1,0:T(8,128)S(1)} %get-tuple-element.44.inner), custom_call_target="tpu_custom_call" | custom-call | flops 1000000 | bytes 270336 | tf_op jit(solution)/shard_map/own_cells/pallas_call | solution.py:456
  39.7 10.8 %all-to-all-start = ((f32[32,16,128]{2,1,0:T(8,128)}), f32[32,16,128]{2,1,0:T(8,128)S(1)}, u32[]{:S(2)}, u32[]{:S(2)}) async-start(f32[32,16,128]{2,1,0:T(8,128)} %own_cells.1), calls=%async_computation | async-start | bytes 524288 | tf_op jit(solution)/shard_map/all_to_all | solution.py:512
  50.5 2.3 %fine_residual.1 = (f32[28,32,256]{2,1,0:T(8,128)S(1)}, f32[28,32,256]{2,1,0:T(8,128)S(1)}, f32[28,32,256]{2,1,0:T(8,128)S(1)}) custom-call(f32[3,28,32,128]{3,2,1,0:T(8,128)S(1)} %get-tuple-element.38.full, f32[3,28,32,128]{3,2,1,0:T(8,128)S(1)} %get-tuple-element.45.xy, f32[32,512]{1,0:T(8,128)S(1)} %collective-permute-done.4.from_down, ...), custom_call_target="tpu_custom_call" | custom-call | flops 30000000 | bytes 2883584 | tf_op jit(solution)/shard_map/fine_residual/pallas_call | solution.py:456
  52.8 0.0 copy-start.1
  52.8 5.3 %fine_sweeps.1.base = f32[16,16,128]{2,1,0:T(8,128)S(1)} custom-call(f32[3,28,32,128]{3,2,1,0:T(8,128)S(1)} %get-tuple-element.38.full, f32[28,32,256]{2,1,0:T(8,128)S(1)} %get-tuple-element.46.coef, f32[28,32,256]{2,1,0:T(8,128)S(1)} %get-tuple-element.47.res, f32[28,32,256]{2,1,0:T(8,128)S(1)} %get-tuple-element.48.inv), custom_call_target="tpu_custom_call" | custom-call | flops 60000000 | bytes 4128768 | tf_op jit(solution)/shard_map/fine_sweeps/pallas_call | solution.py:456
  58.1 4.3 %all-to-all-done = f32[32,16,128]{2,1,0:T(8,128)S(1)} async-done(((f32[32,16,128]{2,1,0:T(8,128)}), f32[32,16,128]{2,1,0:T(8,128)S(1)}, u32[]{:S(2)}, u32[]{:S(2)}) %all-to-all-start) | async-done | bytes 262176 | tf_op jit(solution)/shard_map/all_to_all | solution.py:512
  62.5 0.0 copy-done.1
  62.5 2.4 %coarse_levels.1 = f32[16,16,128]{2,1,0:T(8,128)} custom-call(bf16[1344,512]{1,0:T(8,128)(2,1)S(1)} %copy-done.1, f32[512,128]{1,0:T(8,128)S(1)} %bitcast.3, f32[16,16,128]{2,1,0:T(8,128)S(1)} %fine_sweeps.1.base), custom_call_target="tpu_custom_call" | custom-call | flops 30000000 | bytes 3145728 | tf_op jit(solution)/shard_map/coarse_levels/pallas_call | solution.py:456
  (1 shorter events, 0.0 us)
Async XLA Ops:
  1.9 7.2 %collective-permute-start = (f32[15,16,128]{2,1,0:T(8,128)}, f32[15,16,128]{2,1,0:T(8,128)S(1)}, u32[]{:S(2)}, u32[]{:S(2)}) collective-permute-start(f32[15,16,128]{2,1,0:T(8,128)} %get-tuple-element.27), channel_id=1, source_target_pairs={{0,64},{64,128},{128,192},{192,256},{256,320},{320,384},{384,448},... | collective-permute-start | bytes 368648 | tf_op jit(solution)/shard_map/ppermute | solution.py:472
  6.2 7.5 %collective-permute-start.1 = (f32[15,16,128]{2,1,0:T(8,128)}, f32[15,16,128]{2,1,0:T(8,128)S(1)}, u32[]{:S(2)}, u32[]{:S(2)}) collective-permute-start(f32[15,16,128]{2,1,0:T(8,128)} %get-tuple-element.28), channel_id=1, source_target_pairs={{64,0},{128,64},{192,128},{256,192},{320,256},{384,320},{448,384},... | collective-permute-start | bytes 368648 | tf_op jit(solution)/shard_map/ppermute | solution.py:472
  7.5 1.0 %copy-start.2 = (f32[3,16,16,128]{3,2,1,0:T(8,128)S(1)}, f32[3,16,16,128]{3,2,1,0:T(8,128)}, u32[]{:S(2)}) copy-start(f32[3,16,16,128]{3,2,1,0:T(8,128)} %get-tuple-element.29.fields) | copy-start | bytes 1179652
  13.9 7.3 %collective-permute-start.2 = (f32[28,16,128]{2,1,0:T(8,128)S(1)}, f32[28,16,128]{2,1,0:T(8,128)S(1)}, u32[]{:S(2)}, u32[]{:S(2)}) collective-permute-start(f32[28,16,128]{2,1,0:T(8,128)S(1)} %get-tuple-element.34), channel_id=1, source_target_pairs={{0,16},{16,32},{32,48},{1,17},{17,33},{33,49},{2,18},{18,34},{34,5... | collective-permute-start | bytes 688136 | tf_op jit(solution)/shard_map/ppermute | solution.py:472
  15.8 7.2 %collective-permute-start.3 = (f32[28,16,128]{2,1,0:T(8,128)S(1)}, f32[28,16,128]{2,1,0:T(8,128)S(1)}, u32[]{:S(2)}, u32[]{:S(2)}) collective-permute-start(f32[28,16,128]{2,1,0:T(8,128)S(1)} %get-tuple-element.35), channel_id=1, source_target_pairs={{16,0},{32,16},{48,32},{17,1},{33,17},{49,33},{18,2},{34,18},{50,3... | collective-permute-start | bytes 688136 | tf_op jit(solution)/shard_map/ppermute | solution.py:472
  24.9 9.6 %collective-permute-start.4 = (f32[32,512]{1,0:T(8,128)S(1)}, f32[32,512]{1,0:T(8,128)S(1)}, u32[]{:S(2)}, u32[]{:S(2)}) collective-permute-start(f32[32,512]{1,0:T(8,128)S(1)} %get-tuple-element.36.sent_up), channel_id=1, source_target_pairs={{0,1},{1,2},{2,3},{3,4},{4,5},{5,6},{6,7},{7,8},{8,9},{9,10},{10,1... | collective-permute-start | bytes 196616 | tf_op jit(solution)/shard_map/ppermute | solution.py:472
  28.5 9.7 %collective-permute-start.5 = (f32[32,512]{1,0:T(8,128)S(1)}, f32[32,512]{1,0:T(8,128)S(1)}, u32[]{:S(2)}, u32[]{:S(2)}) collective-permute-start(f32[32,512]{1,0:T(8,128)S(1)} %get-tuple-element.37.sent_down), channel_id=1, source_target_pairs={{1,0},{2,1},{3,2},{4,3},{5,4},{6,5},{7,6},{8,7},{9,8},{10,9},{11,1... | collective-permute-start | bytes 196616 | tf_op jit(solution)/shard_map/ppermute | solution.py:472
  33.3 1.1 %copy-start = (bf16[1344,512]{1,0:T(8,128)(2,1)}, bf16[1344,512]{1,0:T(8,128)(2,1)S(1)}, u32[]{:S(2)}) copy-start(bf16[1344,512]{1,0:T(8,128)(2,1)S(1)} %get-tuple-element.41.tables) | copy-start | bytes 4128772
  39.7 22.7 %all-to-all-start = ((f32[32,16,128]{2,1,0:T(8,128)}), f32[32,16,128]{2,1,0:T(8,128)S(1)}, u32[]{:S(2)}, u32[]{:S(2)}) async-start(f32[32,16,128]{2,1,0:T(8,128)} %own_cells.1), calls=%async_computation | async-start | bytes 524288 | tf_op jit(solution)/shard_map/all_to_all | solution.py:512
  52.8 9.6 %copy-start.1 = (bf16[1344,512]{1,0:T(8,128)(2,1)S(1)}, bf16[1344,512]{1,0:T(8,128)(2,1)}, u32[]{:S(2)}) copy-start(bf16[1344,512]{1,0:T(8,128)(2,1)} %copy-done) | copy-start | bytes 4128772

commit v10 on v9

--- a/solution.py
+++ b/solution.py
@@ -132,37 +132,73 @@
     return jnp.concatenate([quads[pl.ds(64 * at, 16, stride=4), :] for at in range(count)], axis=1)
 
 
-def pack_z(ext, from_down, from_up, full, to_up, to_down, inner, in_y, quads):
+def pack_lanes(cells_of, rows, to_up, to_down, at):
+    lane = iota((rows, 128), 1)
+    for group in range(4):
+        up = jnp.zeros((rows, 128), F32)
+        down = jnp.zeros((rows, 128), F32)
+        for x in range(8 * group, min(8 * group + 8, 28)):
+            first = 16 * (x - 8 * group)
+            for field in range(3):
+                h, a, b = HALO[field], ROWS[field], ROWS[field + 1]
+                cells = cells_of(field, x)
+                mine = (lane >= first + a) & (lane < first + b)
+                up = jnp.where(mine, pltpu.roll(cells, (first + a + h) % 128, 1), up)
+                down = jnp.where(mine, rolled(cells, first + a), down)
+        to_up[at : at + rows, 128 * group : 128 * group + 128] = up
+        to_down[at : at + rows, 128 * group : 128 * group + 128] = down
+
+
+def own_rows(ext, up, down, xz):
+    pack_lanes(lambda field, x: ext[field, x], 16, up, down, 0)
+    matrix = band_matrix(128)
+
+    def bands(step, carry):
+        xs = [6 + 4 * step + j for j in range(4)]
+        wanted = []
+        for x in xs:
+            around = [(ext[0, x + d], ext[1, x + d]) for d in (-1, 0, 1)]
+            for low, here, high in zip(*[(k, v, k * v) for k, v in around]):
+                wanted.append((low + high) + 2.0 * here)
+        for at, f in enumerate(band_z(wanted, matrix)):
+            xz[at % 3, xs[at // 3] - 6] = f
+        return carry
+
+    lax.fori_loop(0, 4, bands, 0)
+
+
+def pack_z(ext, from_down, from_up, up_rows, down_rows, xz, full, to_up, to_down, inner, edges, quads):
     for field in range(3):
         h, a, b = HALO[field], ROWS[field], ROWS[field + 1]
         full[field, :, 0:16, :] = ext[field]
         full[field, :, 16 : 16 + h, :] = from_up[:, a:b, :]
         full[field, :, 16 + h : 32 - h, :] = jnp.zeros((28, 16 - 2 * h, 128), F32)
         full[field, :, 32 - h : 32, :] = from_down[:, a:b, :]
-
-    def bands_y(x, carry):
-        k = full[0, x]
-        v = full[1, x]
-        for at, f in enumerate((k, v, k * v)):
-            in_y[at, x] = band(f, 0)[0:16, :]
-        return carry
-
-    lax.fori_loop(5, 23, bands_y, 0, unroll=2)
-
+    edges[:, 24:32, :] = jnp.zeros((6, 8, 128), F32)
+    for at, (source, row_k, row_v) in enumerate(((from_down, 5, 10), (from_up, 0, 6))):
+        k = source[:, row_k, :]
+        v = source[:, row_v, :]
+        for place, f in enumerate((k, v, k * v)):
+            edges[3 * at + place, 0:28, :] = f
     matrix = band_matrix(128)
+    for at, f in enumerate(band_z([band(edges[at], 0) for at in range(6)], matrix)):
+        edges[at] = f
+    row = iota((16, 128), 0)
 
     def quad(q, carry):
         sums = [None, None]
-        xs = [6 + 4 * q + j for j in range(4)]
-        all_tu = band_z(
-            [(in_y[at, x - 1] + in_y[at, x + 1]) + 2.0 * in_y[at, x] for x in xs for at in range(3)], matrix
-        )
-        for j, x in enumerate(xs):
-            tu = all_tu[3 * j : 3 * j + 3]
-            k = full[0, x, 0:16, :]
-            v = full[1, x, 0:16, :]
+        for j in range(4):
+            x = 6 + 4 * q + j
+            tu = []
+            for at in range(3):
+                f = xz[at, 4 * q + j]
+                below = jnp.where(row == 0, edges[at, pl.ds(x, 1), :], pltpu.roll(f, 1, 0))
+                above = jnp.where(row == 15, edges[3 + at, pl.ds(x, 1), :], pltpu.roll(f, 15, 0))
+                tu.append((below + above) + 2.0 * f)
+            k = ext[0, x]
+            v = ext[1, x]
             diagonal = 6.0 * k + 0.125 * tu[0]
-            res = full[2, x, 0:16, :] - (v * diagonal + 2.0 * (k * v) - 0.125 * (k * tu[1] + tu[2]))
+            res = ext[2, x] - (v * diagonal + 2.0 * (k * v) - 0.125 * (k * tu[1] + tu[2]))
             sums = [f if j == 0 else total + f for total, f in zip(sums, (res, k))]
         sum_quads(quads, q, sums)
         return carry
@@ -179,21 +215,9 @@
     place = jnp.concatenate([jnp.where(found, scale, 0.0) for found in (upper, lower, stay)], axis=1).astype(BF16)
     level3 = select_lanes(read_quads(quads), place)
     inner[...] = level3[:, 256:384]
-    lane = iota((32, 128), 1)
-
-    for group in range(4):
-        up = jnp.zeros((32, 128), F32)
-        down = jnp.zeros((32, 128), F32)
-        for x in range(8 * group, min(8 * group + 8, 28)):
-            first = 16 * (x - 8 * group)
-            for field in range(3):
-                h, a, b = HALO[field], ROWS[field], ROWS[field + 1]
-                cells = full[field, x]
-                mine = (lane >= first + a) & (lane < first + b)
-                up = jnp.where(mine, pltpu.roll(cells, (first + a + h) % 128, 1), up)
-                down = jnp.where(mine, rolled(cells, first + a), down)
-        to_up[:, 128 * group : 128 * group + 128] = up
-        to_down[:, 128 * group : 128 * group + 128] = down
+    to_up[0:16, :] = up_rows[...]
+    to_down[0:16, :] = down_rows[...]
+    pack_lanes(lambda field, x: full[field, x, 16:32, :], 16, to_up, to_down, 16)
     to_up[0:16, 384:512] += level3[:, 0:128]
     to_down[0:16, 384:512] += level3[:, 128:256]
 
@@ -223,13 +247,9 @@
         tables[at : at + 128, 0:256] = jnp.where(found, scale, 0.0).astype(BF16)
     source = iota((128, 128), 0)
     lane = iota((128, 128), 1)
-    row = iota((256, 64), 0)
-    found = iota((256, 64), 1)
     for level, start in enumerate((16, 72, 100)):
-        shift = level + 2
-        tables[960:1088, 128 * level : 128 * level + 128] = ones_where(source == start + (lane >> shift))
-        at = ((row >> 4) >> shift) * 16 + 4 + ((row & 15) >> shift)
-        tables[1088:1344, 64 * level : 64 * level + 64] = ones_where(found == at)
+        found = source == start + (lane >> (level + 2))
+        tables[960:1088, 128 * level : 128 * level + 128] = ones_where(found)
 
     def in_y(x, carry):
         k = full[0, x]
@@ -435,15 +455,22 @@
     return [band(f, 2) for f in fields]
 
 
-def coarse_levels(tables, plane, base, out):
+def coarse_levels(tables, plane, base, out, spread):
     found = jnp.dot(tables[0:576, :], jnp.concatenate(split(plane[...]), axis=1), preferred_element_type=F32)
     found = found[:, 0:128] + (found[:, 128:256] + found[:, 256:384])
     windows = jnp.concatenate([found[192 * level : 192 * level + 192, :] for level in range(3)], axis=1)
     both = select_lanes(windows, tables[576:960, 0:256])
     corr = smooth_small(both[:, 0:128].reshape(12, 16, 128), both[:, 128:256].reshape(12, 16, 128), 4, rolled_bands)
     wide = select_lanes(corr[4:8].reshape(64, 128), tables[960:1088, 0:384])
-    wide = jnp.concatenate([wide[:, 128 * level : 128 * level + 128] for level in range(3)], axis=0)
-    out[...] = base[...] + select_rows(tables[1088:1344, 0:192], wide).reshape(16, 16, 128)
+    for x in range(4):
+        level4 = wide[16 * (x // 2) : 16 * (x // 2) + 16, 128:256]
+        level4 = jnp.concatenate([jnp.broadcast_to(level4[y : y + 1], (2, 128)) for y in (4, 5)], axis=0)
+        rows = wide[16 * x + 4 : 16 * x + 8, 0:128] + (level4 + wide[4:5, 256:384])
+        for y in range(4):
+            spread[pl.ds(16 * x + y, 4, stride=4), :] = rows
+    for x in range(16):
+        start = 16 * (x // 4)
+        out[x] = base[x] + spread[start : start + 16, :]
 
 
 VMEM = pl.BlockSpec(memory_space=pltpu.VMEM)
@@ -489,17 +516,19 @@
     ext, to_up, to_down = call(pack_y, [(3, 28, 16, 128), (28, 16, 128), (28, 16, 128)], [fields, from_down, from_up])
     from_down, from_up = swap("gy", to_up, to_down)
     planes = (3, 28, 32, 128)
+    mine = call(own_rows, [(16, 512), (16, 512), (3, *block)], [ext], flops=30000000)
+    from_down, from_up, *mine = lax.optimization_barrier((from_down, from_up, *mine))
     full, to_up, to_down, inner = call(
         pack_z,
         [planes, (32, 512), (32, 512), (16, 128)],
-        [ext, from_down, from_up],
-        scratch=[(3, 28, 16, 128), (128, 128)],
+        [ext, from_down, from_up, *mine],
+        scratch=[(6, 32, 128), (128, 128)],
     )
     from_down, from_up = swap("gz", to_up, to_down)
     place = jnp.stack([lax.axis_index("gx"), lax.axis_index("gy")]).astype(jnp.int32)
     xy, tables = call(
         bands_xy,
-        [planes, jax.ShapeDtypeStruct((1344, 512), BF16)],
+        [planes, jax.ShapeDtypeStruct((1088, 512), BF16)],
         [place, full],
         scratch=[planes],
         first=SMEM,
@@ -525,7 +554,7 @@
         scratch=[wide, wide, wide, wide, (2, 896, 128), (128, 128)],
         flops=60000000,
     )
-    (out,) = call(coarse_levels, [block], [tables, plane.reshape(count * 16, 128), base], flops=30000000)
+    (out,) = call(coarse_levels, [block], [tables, plane.reshape(count * 16, 128), base], scratch=[(64, 128)])
     return out
 
 

time: 65.2 us -> 64.2 us (0.985)
  waiting for transfers between devices: 16.7 us -> 15.8 us
    ppermute x6, waiting for transfers between devices: 12.4 us -> 11.5 us  [swap(): return (lax.ppermute(to_up, axis, up), lax.ppermute(to_down, axis, down))]
    pallas_call x9 -> x10, Pallas kernels: 17.2 us -> 17.1 us  [call(): pl.pallas_call(kernel, out_shape=[out if isinstance(out, jax.ShapeDtypeSt...]
  transfers between devices with their start and end apart: 7 -> 7, of which waited for: 6 -> 6; matrix products, arithmetic and copies ran while one was open for 0% -> 0% of each run, Pallas kernels for 14% -> 16%
where the time goes in v10:
time: 64.2 us; the launch traced here: 63.8 us
  starting transfers between devices  28.6 us (45%)
  Pallas kernels  17.1 us (27%)
  waiting for transfers between devices  15.8 us (25%)
  local copies, waits for them, and re-layouts  2 us (3%)
    ppermute x6, starting transfers between devices, swap(): return (lax.ppermute(to_up, axis, up), lax.ppermute(to_down, axis, down))  17.9 us
    pallas_call x10, Pallas kernels, call(): pl.pallas_call(kernel, out_shape=[out if isinstance(out, jax.ShapeDtypeSt...  17.1 us
    ppermute x6, waiting for transfers between devices, swap(): return (lax.ppermute(to_up, axis, up), lax.ppermute(to_down, axis, down))  11.5 us
    all_to_all x1, starting transfers between devices, on_device(): plane = lax.all_to_all(chunks, ('gx', 'gy'), 0, 0, tiled=True)  10.8 us
    all_to_all x1, waiting for transfers between devices, on_device(): plane = lax.all_to_all(chunks, ('gx', 'gy'), 0, 0, tiled=True)  4.31 us
    unnamed x6, local copies, waits for them, and re-layouts  2 us
  transfers between devices with their start and end apart: 7, of which 6 were waited for; matrix products, arithmetic and copies ran while one was open for 0% of the time, Pallas kernels for 16%

profile of v10, /device:TPU:56, one launch (start us, length us, event | category | flops | bytes accessed | tf_op | source)
XLA Modules:
  0.0 63.8 jit_solution(3691444135847262215)
XLA Ops:
  0.0 1.9 %send_x.1 = (f32[3,16,16,128]{3,2,1,0:T(8,128)}, f32[15,16,128]{2,1,0:T(8,128)}, f32[15,16,128]{2,1,0:T(8,128)}) custom-call(f32[4]{0:T(128)} %table.1, s32[16,16,128]{2,1,0:T(8,128)} %phase.1, f32[16,16,128]{2,1,0:T(8,128)} %iterate.1, f32[16,16,128]{2,1,0:T(8,128)} %right.1), custom_call_target="tpu_custom_call" | custom-call | flops 1000000 | bytes 393232 | tf_op jit(solution)/shard_map/send_x/pallas_call | solution.py:483
  1.9 4.3 %collective-permute-start = (f32[15,16,128]{2,1,0:T(8,128)}, f32[15,16,128]{2,1,0:T(8,128)S(1)}, u32[]{:S(2)}, u32[]{:S(2)}) collective-permute-start(f32[15,16,128]{2,1,0:T(8,128)} %get-tuple-element.35), channel_id=1, source_target_pairs={{0,64},{64,128},{128,192},{192,256},{256,320},{320,384},{384,448},... | collective-permute-start | bytes 368648 | tf_op jit(solution)/shard_map/ppermute | solution.py:499
  6.2 1.3 %collective-permute-start.1 = (f32[15,16,128]{2,1,0:T(8,128)}, f32[15,16,128]{2,1,0:T(8,128)S(1)}, u32[]{:S(2)}, u32[]{:S(2)}) collective-permute-start(f32[15,16,128]{2,1,0:T(8,128)} %get-tuple-element.36), channel_id=1, source_target_pairs={{64,0},{128,64},{192,128},{256,192},{320,256},{384,320},{448,384},... | collective-permute-start | bytes 368648 | tf_op jit(solution)/shard_map/ppermute | solution.py:499
  7.5 0.0 copy-start.2
  7.5 1.0 %copy-done.2 = f32[3,16,16,128]{3,2,1,0:T(8,128)S(1)} copy-done((f32[3,16,16,128]{3,2,1,0:T(8,128)S(1)}, f32[3,16,16,128]{3,2,1,0:T(8,128)}, u32[]{:S(2)}) %copy-start.2) | copy-done | bytes 393240
  8.6 0.5 collective-permute-done.from_down
  9.1 4.6 %collective-permute-done.1.from_up = f32[15,16,128]{2,1,0:T(8,128)S(1)} collective-permute-done((f32[15,16,128]{2,1,0:T(8,128)}, f32[15,16,128]{2,1,0:T(8,128)S(1)}, u32[]{:S(2)}, u32[]{:S(2)}) %collective-permute-start.1) | collective-permute-done | bytes 122912 | tf_op jit(solution)/shard_map/ppermute | solution.py:499
  13.7 0.1 pack_y.1
  13.9 1.9 %collective-permute-start.2 = (f32[28,16,128]{2,1,0:T(8,128)S(1)}, f32[28,16,128]{2,1,0:T(8,128)S(1)}, u32[]{:S(2)}, u32[]{:S(2)}) collective-permute-start(f32[28,16,128]{2,1,0:T(8,128)S(1)} %get-tuple-element.42), channel_id=1, source_target_pairs={{0,16},{16,32},{32,48},{1,17},{17,33},{33,49},{2,18},{18,34},{34,5... | collective-permute-start | bytes 688136 | tf_op jit(solution)/shard_map/ppermute | solution.py:499
  15.8 3.6 %collective-permute-start.3 = (f32[28,16,128]{2,1,0:T(8,128)S(1)}, f32[28,16,128]{2,1,0:T(8,128)S(1)}, u32[]{:S(2)}, u32[]{:S(2)}) collective-permute-start(f32[28,16,128]{2,1,0:T(8,128)S(1)} %get-tuple-element.43), channel_id=1, source_target_pairs={{16,0},{32,16},{48,32},{17,1},{33,17},{49,33},{18,2},{34,18},{50,3... | collective-permute-start | bytes 688136 | tf_op jit(solution)/shard_map/ppermute | solution.py:499
  19.5 1.1 %own_rows.1 = (f32[16,512]{1,0:T(8,128)S(1)}, f32[16,512]{1,0:T(8,128)S(1)}, f32[3,16,16,128]{3,2,1,0:T(8,128)S(1)}) custom-call(f32[3,28,16,128]{3,2,1,0:T(8,128)S(1)} %get-tuple-element.41.ext), custom_call_target="tpu_custom_call" | custom-call | flops 30000000 | bytes 688128 | tf_op jit(solution)/shard_map/own_rows/pallas_call | solution.py:483
  20.6 0.6 collective-permute-done.2.from_down
  21.2 1.8 %collective-permute-done.3.from_up = f32[28,16,128]{2,1,0:T(8,128)S(1)} collective-permute-done((f32[28,16,128]{2,1,0:T(8,128)S(1)}, f32[28,16,128]{2,1,0:T(8,128)S(1)}, u32[]{:S(2)}, u32[]{:S(2)}) %collective-permute-start.3) | collective-permute-done | bytes 229408 | tf_op jit(solution)/shard_map/ppermute | solution.py:499
  23.0 1.1 %pack_z.1 = (f32[3,28,32,128]{3,2,1,0:T(8,128)S(1)}, f32[32,512]{1,0:T(8,128)S(1)}, f32[32,512]{1,0:T(8,128)S(1)}, f32[16,128]{1,0:T(8,128)S(1)}) custom-call(f32[3,28,16,128]{3,2,1,0:T(8,128)S(1)} %get-tuple-element.41.ext, f32[28,16,128]{2,1,0:T(8,128)S(1)} %collective-permute-done.2.from_down, f32[28,16,128]{2,1,0:T(8,128)S(1)} %collective-permute-done.3.from_up, ...), custom_call_target="tpu_custom_call" | custom-call | flops 1000000 | bytes 1605632 | tf_op jit(solution)/shard_map/pack_z/pallas_call | solution.py:483
  24.0 3.6 %collective-permute-start.4 = (f32[32,512]{1,0:T(8,128)S(1)}, f32[32,512]{1,0:T(8,128)S(1)}, u32[]{:S(2)}, u32[]{:S(2)}) collective-permute-start(f32[32,512]{1,0:T(8,128)S(1)} %get-tuple-element.52.sent_up), channel_id=1, source_target_pairs={{0,1},{1,2},{2,3},{3,4},{4,5},{5,6},{6,7},{7,8},{8,9},{9,10},{10,1... | collective-permute-start | bytes 196616 | tf_op jit(solution)/shard_map/ppermute | solution.py:499
  27.7 3.1 %collective-permute-start.5 = (f32[32,512]{1,0:T(8,128)S(1)}, f32[32,512]{1,0:T(8,128)S(1)}, u32[]{:S(2)}, u32[]{:S(2)}) collective-permute-start(f32[32,512]{1,0:T(8,128)S(1)} %get-tuple-element.53.sent_down), channel_id=1, source_target_pairs={{1,0},{2,1},{3,2},{4,3},{5,4},{6,5},{7,6},{8,7},{9,8},{10,9},{11,1... | collective-permute-start | bytes 196616 | tf_op jit(solution)/shard_map/ppermute | solution.py:499
  30.8 0.1 pad_add_fusion.place
  30.9 1.5 %bands_xy.1 = (f32[3,28,32,128]{3,2,1,0:T(8,128)S(1)}, bf16[1088,512]{1,0:T(8,128)(2,1)S(1)}) custom-call(s32[2]{0:T(128)S(1)} %pad_add_fusion.place, f32[3,28,32,128]{3,2,1,0:T(8,128)S(1)} %get-tuple-element.54.full), custom_call_target="tpu_custom_call" | custom-call | flops 30000000 | bytes 1376264 | tf_op jit(solution)/shard_map/bands_xy/pallas_call | solution.py:483
  32.4 0.0 copy-start
  32.4 1.0 %copy-done = bf16[1088,512]{1,0:T(8,128)(2,1)} copy-done((bf16[1088,512]{1,0:T(8,128)(2,1)}, bf16[1088,512]{1,0:T(8,128)(2,1)S(1)}, u32[]{:S(2)}) %copy-start) | copy-done | bytes 1114136
  33.4 0.0 collective-permute-done.4.from_down
  33.4 4.0 %collective-permute-done.5.from_up = f32[32,512]{1,0:T(8,128)S(1)} collective-permute-done((f32[32,512]{1,0:T(8,128)S(1)}, f32[32,512]{1,0:T(8,128)S(1)}, u32[]{:S(2)}, u32[]{:S(2)}) %collective-permute-start.5) | collective-permute-done | bytes 65568 | tf_op jit(solution)/shard_map/ppermute | solution.py:499
  37.3 1.6 %own_cells.1 = f32[32,16,128]{2,1,0:T(8,128)} custom-call(f32[32,512]{1,0:T(8,128)S(1)} %get-tuple-element.52.sent_up, f32[32,512]{1,0:T(8,128)S(1)} %get-tuple-element.53.sent_down, f32[32,512]{1,0:T(8,128)S(1)} %collective-permute-done.4.from_down, f32[32,512]{1,0:T(8,128)S(1)} %collective-permute-done.5.from_up, f32[16,128]{1,0:T(8,128)S(1)} %get-tuple-element.60.inner), custom_call_target="tpu_custom_call" | custom-call | flops 1000000 | bytes 270336 | tf_op jit(solution)/shard_map/own_cells/pallas_call | solution.py:483
  38.9 10.8 %all-to-all-start = ((f32[32,16,128]{2,1,0:T(8,128)}), f32[32,16,128]{2,1,0:T(8,128)S(1)}, u32[]{:S(2)}, u32[]{:S(2)}) async-start(f32[32,16,128]{2,1,0:T(8,128)} %own_cells.1), calls=%async_computation | async-start | bytes 524288 | tf_op jit(solution)/shard_map/all_to_all | solution.py:541
  49.7 2.3 %fine_residual.1 = (f32[28,32,256]{2,1,0:T(8,128)S(1)}, f32[28,32,256]{2,1,0:T(8,128)S(1)}, f32[28,32,256]{2,1,0:T(8,128)S(1)}) custom-call(f32[3,28,32,128]{3,2,1,0:T(8,128)S(1)} %get-tuple-element.54.full, f32[3,28,32,128]{3,2,1,0:T(8,128)S(1)} %get-tuple-element.61.xy, f32[32,512]{1,0:T(8,128)S(1)} %collective-permute-done.4.from_down, ...), custom_call_target="tpu_custom_call" | custom-call | flops 30000000 | bytes 2883584 | tf_op jit(solution)/shard_map/fine_residual/pallas_call | solution.py:483
  52.0 0.0 copy-start.1
  52.0 5.3 %fine_sweeps.1.base = f32[16,16,128]{2,1,0:T(8,128)S(1)} custom-call(f32[3,28,32,128]{3,2,1,0:T(8,128)S(1)} %get-tuple-element.54.full, f32[28,32,256]{2,1,0:T(8,128)S(1)} %get-tuple-element.62.coef, f32[28,32,256]{2,1,0:T(8,128)S(1)} %get-tuple-element.63.res, f32[28,32,256]{2,1,0:T(8,128)S(1)} %get-tuple-element.64.inv), custom_call_target="tpu_custom_call" | custom-call | flops 60000000 | bytes 4128768 | tf_op jit(solution)/shard_map/fine_sweeps/pallas_call | solution.py:483
  57.3 4.3 %all-to-all-done = f32[32,16,128]{2,1,0:T(8,128)S(1)} async-done(((f32[32,16,128]{2,1,0:T(8,128)}), f32[32,16,128]{2,1,0:T(8,128)S(1)}, u32[]{:S(2)}, u32[]{:S(2)}) %all-to-all-start) | async-done | bytes 262176 | tf_op jit(solution)/shard_map/all_to_all | solution.py:541
  61.6 0.0 copy-done.1
  61.6 2.2 %coarse_levels.1 = f32[16,16,128]{2,1,0:T(8,128)} custom-call(bf16[1088,512]{1,0:T(8,128)(2,1)S(1)} %copy-done.1, f32[512,128]{1,0:T(8,128)S(1)} %bitcast.3, f32[16,16,128]{2,1,0:T(8,128)S(1)} %fine_sweeps.1.base), custom_call_target="tpu_custom_call" | custom-call | flops 1000000 | bytes 2621440 | tf_op jit(solution)/shard_map/coarse_levels/pallas_call | solution.py:483
  (1 shorter events, 0.0 us)
Async XLA Ops:
  1.9 7.2 %collective-permute-start = (f32[15,16,128]{2,1,0:T(8,128)}, f32[15,16,128]{2,1,0:T(8,128)S(1)}, u32[]{:S(2)}, u32[]{:S(2)}) collective-permute-start(f32[15,16,128]{2,1,0:T(8,128)} %get-tuple-element.35), channel_id=1, source_target_pairs={{0,64},{64,128},{128,192},{192,256},{256,320},{320,384},{384,448},... | collective-permute-start | bytes 368648 | tf_op jit(solution)/shard_map/ppermute | solution.py:499
  6.2 7.5 %collective-permute-start.1 = (f32[15,16,128]{2,1,0:T(8,128)}, f32[15,16,128]{2,1,0:T(8,128)S(1)}, u32[]{:S(2)}, u32[]{:S(2)}) collective-permute-start(f32[15,16,128]{2,1,0:T(8,128)} %get-tuple-element.36), channel_id=1, source_target_pairs={{64,0},{128,64},{192,128},{256,192},{320,256},{384,320},{448,384},... | collective-permute-start | bytes 368648 | tf_op jit(solution)/shard_map/ppermute | solution.py:499
  7.5 1.0 %copy-start.2 = (f32[3,16,16,128]{3,2,1,0:T(8,128)S(1)}, f32[3,16,16,128]{3,2,1,0:T(8,128)}, u32[]{:S(2)}) copy-start(f32[3,16,16,128]{3,2,1,0:T(8,128)} %get-tuple-element.37.fields) | copy-start | bytes 1179652
  13.9 7.3 %collective-permute-start.2 = (f32[28,16,128]{2,1,0:T(8,128)S(1)}, f32[28,16,128]{2,1,0:T(8,128)S(1)}, u32[]{:S(2)}, u32[]{:S(2)}) collective-permute-start(f32[28,16,128]{2,1,0:T(8,128)S(1)} %get-tuple-element.42), channel_id=1, source_target_pairs={{0,16},{16,32},{32,48},{1,17},{17,33},{33,49},{2,18},{18,34},{34,5... | collective-permute-start | bytes 688136 | tf_op jit(solution)/shard_map/ppermute | solution.py:499
  15.8 7.2 %collective-permute-start.3 = (f32[28,16,128]{2,1,0:T(8,128)S(1)}, f32[28,16,128]{2,1,0:T(8,128)S(1)}, u32[]{:S(2)}, u32[]{:S(2)}) collective-permute-start(f32[28,16,128]{2,1,0:T(8,128)S(1)} %get-tuple-element.43), channel_id=1, source_target_pairs={{16,0},{32,16},{48,32},{17,1},{33,17},{49,33},{18,2},{34,18},{50,3... | collective-permute-start | bytes 688136 | tf_op jit(solution)/shard_map/ppermute | solution.py:499
  24.0 9.3 %collective-permute-start.4 = (f32[32,512]{1,0:T(8,128)S(1)}, f32[32,512]{1,0:T(8,128)S(1)}, u32[]{:S(2)}, u32[]{:S(2)}) collective-permute-start(f32[32,512]{1,0:T(8,128)S(1)} %get-tuple-element.52.sent_up), channel_id=1, source_target_pairs={{0,1},{1,2},{2,3},{3,4},{4,5},{5,6},{6,7},{7,8},{8,9},{9,10},{10,1... | collective-permute-start | bytes 196616 | tf_op jit(solution)/shard_map/ppermute | solution.py:499
  27.7 9.7 %collective-permute-start.5 = (f32[32,512]{1,0:T(8,128)S(1)}, f32[32,512]{1,0:T(8,128)S(1)}, u32[]{:S(2)}, u32[]{:S(2)}) collective-permute-start(f32[32,512]{1,0:T(8,128)S(1)} %get-tuple-element.53.sent_down), channel_id=1, source_target_pairs={{1,0},{2,1},{3,2},{4,3},{5,4},{6,5},{7,6},{8,7},{9,8},{10,9},{11,1... | collective-permute-start | bytes 196616 | tf_op jit(solution)/shard_map/ppermute | solution.py:499
  32.4 1.0 %copy-start = (bf16[1088,512]{1,0:T(8,128)(2,1)}, bf16[1088,512]{1,0:T(8,128)(2,1)S(1)}, u32[]{:S(2)}) copy-start(bf16[1088,512]{1,0:T(8,128)(2,1)S(1)} %get-tuple-element.57.tables) | copy-start | bytes 3342340
  38.9 22.7 %all-to-all-start = ((f32[32,16,128]{2,1,0:T(8,128)}), f32[32,16,128]{2,1,0:T(8,128)S(1)}, u32[]{:S(2)}, u32[]{:S(2)}) async-start(f32[32,16,128]{2,1,0:T(8,128)} %own_cells.1), calls=%async_computation | async-start | bytes 524288 | tf_op jit(solution)/shard_map/all_to_all | solution.py:541
  52.0 9.6 %copy-start.1 = (bf16[1088,512]{1,0:T(8,128)(2,1)S(1)}, bf16[1088,512]{1,0:T(8,128)(2,1)}, u32[]{:S(2)}) copy-start(bf16[1088,512]{1,0:T(8,128)(2,1)} %copy-done) | copy-start | bytes 3342340

commit v11 on v10

--- a/solution.py
+++ b/solution.py
@@ -103,7 +103,19 @@
     held[...] = fields[...]
 
 
-def pack_y(fields, from_down, from_up, ext, to_up, to_down):
+def by_parity(place, body, first, second):
+    odd = (place[1] & 1) == 1
+
+    @pl.when(odd)
+    def _():
+        body(second, first)
+
+    @pl.when(jnp.logical_not(odd))
+    def _():
+        body(first, second)
+
+
+def pack_y(place, fields, from_down, from_up, ext, to_first, to_second):
     for field in range(3):
         h, a, b = HALO[field], ROWS[field], ROWS[field + 1]
         if h < 6:
@@ -112,10 +124,16 @@
         ext[field, 6 - h : 6] = from_down[a:b]
         ext[field, 6:22] = fields[field]
         ext[field, 22 : 22 + h] = from_up[a:b]
-        to_up[:, a:b, :] = ext[field, :, 16 - h : 16, :]
-        to_down[:, a:b, :] = ext[field, :, 0:h, :]
-    to_up[:, 15:16, :] = jnp.zeros((28, 1, 128), F32)
-    to_down[:, 15:16, :] = jnp.zeros((28, 1, 128), F32)
+
+    def rows(to_down, to_up):
+        for field in range(3):
+            h, a, b = HALO[field], ROWS[field], ROWS[field + 1]
+            to_up[:, a:b, :] = ext[field, :, 16 - h : 16, :]
+            to_down[:, a:b, :] = ext[field, :, 0:h, :]
+
+    by_parity(place, rows, to_first, to_second)
+    to_first[:, 15:16, :] = jnp.zeros((28, 1, 128), F32)
+    to_second[:, 15:16, :] = jnp.zeros((28, 1, 128), F32)
 
 
 def sum_quads(quads, q, sums):
@@ -167,19 +185,25 @@
     lax.fori_loop(0, 4, bands, 0)
 
 
-def pack_z(ext, from_down, from_up, up_rows, down_rows, xz, full, to_up, to_down, inner, edges, quads):
+def pack_z(place, ext, from_first, from_second, up_rows, down_rows, xz, full, to_up, to_down, inner, edges, quads):
+    edges[:, 24:32, :] = jnp.zeros((6, 8, 128), F32)
     for field in range(3):
-        h, a, b = HALO[field], ROWS[field], ROWS[field + 1]
+        h = HALO[field]
         full[field, :, 0:16, :] = ext[field]
-        full[field, :, 16 : 16 + h, :] = from_up[:, a:b, :]
         full[field, :, 16 + h : 32 - h, :] = jnp.zeros((28, 16 - 2 * h, 128), F32)
-        full[field, :, 32 - h : 32, :] = from_down[:, a:b, :]
-    edges[:, 24:32, :] = jnp.zeros((6, 8, 128), F32)
-    for at, (source, row_k, row_v) in enumerate(((from_down, 5, 10), (from_up, 0, 6))):
-        k = source[:, row_k, :]
-        v = source[:, row_v, :]
-        for place, f in enumerate((k, v, k * v)):
-            edges[3 * at + place, 0:28, :] = f
+
+    def rows(from_down, from_up):
+        for field in range(3):
+            h, a, b = HALO[field], ROWS[field], ROWS[field + 1]
+            full[field, :, 16 : 16 + h, :] = from_up[:, a:b, :]
+            full[field, :, 32 - h : 32, :] = from_down[:, a:b, :]
+        for at, (source, row_k, row_v) in enumerate(((from_down, 5, 10), (from_up, 0, 6))):
+            k = source[:, row_k, :]
+            v = source[:, row_v, :]
+            for number, f in enumerate((k, v, k * v)):
+                edges[3 * at + number, 0:28, :] = f
+
+    by_parity(place, rows, from_first, from_second)
     matrix = band_matrix(128)
     for at, f in enumerate(band_z([band(edges[at], 0) for at in range(6)], matrix)):
         edges[at] = f
@@ -492,6 +516,12 @@
     )(*ins)
 
 
+def neighbour_pairs(count):
+    for start in (1, 0):
+        lower = range(start, count - 1, 2)
+        yield [(i, i + 1) for i in lower] + [(i + 1, i) for i in lower]
+
+
 def swap(axis, to_up, to_down):
     count = lax.axis_size(axis)
     up = [(i, i + 1) for i in range(count - 1)]
@@ -501,6 +531,7 @@
 
 def on_device(right, iterate, phase, table):
     block = (16, 16, 128)
+    place = jnp.stack([lax.axis_index("gx"), lax.axis_index("gy")]).astype(jnp.int32)
     fields, to_up, to_down = call(
         send_x,
         [(3, *block), (15, 16, 128), (15, 16, 128)],
@@ -512,20 +543,25 @@
     )
     from_down, from_up = swap("gx", to_up, to_down)
     (held,) = call(hold, [(3, *block)], [fields], flops=30000000)
-    from_down, from_up, fields = lax.optimization_barrier((from_down, from_up, held))
-    ext, to_up, to_down = call(pack_y, [(3, 28, 16, 128), (28, 16, 128), (28, 16, 128)], [fields, from_down, from_up])
-    from_down, from_up = swap("gy", to_up, to_down)
+    from_down, from_up, fields, place = lax.optimization_barrier((from_down, from_up, held, place))
+    ext, *sent = call(
+        pack_y,
+        [(3, 28, 16, 128), (28, 16, 128), (28, 16, 128)],
+        [place, fields, from_down, from_up],
+        first=SMEM,
+    )
+    found = [lax.ppermute(rows, "gy", pairs) for rows, pairs in zip(sent, neighbour_pairs(lax.axis_size("gy")))]
     planes = (3, 28, 32, 128)
     mine = call(own_rows, [(16, 512), (16, 512), (3, *block)], [ext], flops=30000000)
-    from_down, from_up, *mine = lax.optimization_barrier((from_down, from_up, *mine))
+    *found, up_rows, down_rows, xz = lax.optimization_barrier((*found, *mine))
     full, to_up, to_down, inner = call(
         pack_z,
         [planes, (32, 512), (32, 512), (16, 128)],
-        [ext, from_down, from_up, *mine],
+        [place, ext, *found, up_rows, down_rows, xz],
         scratch=[(6, 32, 128), (128, 128)],
+        first=SMEM,
     )
     from_down, from_up = swap("gz", to_up, to_down)
-    place = jnp.stack([lax.axis_index("gx"), lax.axis_index("gy")]).astype(jnp.int32)
     xy, tables = call(
         bands_xy,
         [planes, jax.ShapeDtypeStruct((1088, 512), BF16)],

time: 64.2 us -> 63.4 us (0.988)
  starting transfers between devices: 28.6 us -> 26.9 us
  Pallas kernels: 17.1 us -> 18.2 us
    ppermute x6 -> x4, starting transfers between devices: 17.9 us -> 12.3 us  [swap(): return (lax.ppermute(to_up, axis, up), lax.ppermute(to_down, axis, down))]
    ppermute x0 -> x2, starting transfers between devices: none -> 3.84 us  [on_device(): lax.ppermute(rows, 'gy', pairs)]
    ppermute x6 -> x4, waiting for transfers between devices: 11.5 us -> 8.66 us  [swap(): return (lax.ppermute(to_up, axis, up), lax.ppermute(to_down, axis, down))]
    ppermute x0 -> x2, waiting for transfers between devices: none -> 2.33 us  [on_device(): lax.ppermute(rows, 'gy', pairs)]
    pallas_call x10, Pallas kernels: 17.1 us -> 18.2 us  [call(): pl.pallas_call(kernel, out_shape=[out if isinstance(out, jax.ShapeDtypeSt...]
  transfers between devices with their start and end apart: 7 -> 7, of which waited for: 6 -> 5; matrix products, arithmetic and copies ran while one was open for 0% -> 0% of each run, Pallas kernels for 16% -> 16%
where the time goes in v11:
time: 63.4 us; the launch traced here: 62.7 us
  starting transfers between devices  26.9 us (42%)
  Pallas kernels  18.2 us (29%)
  waiting for transfers between devices  15.3 us (24%)
  local copies, waits for them, and re-layouts  2 us (3%)
    pallas_call x10, Pallas kernels, call(): pl.pallas_call(kernel, out_shape=[out if isinstance(out, jax.ShapeDtypeSt...  18.2 us
    ppermute x4, starting transfers between devices, swap(): return (lax.ppermute(to_up, axis, up), lax.ppermute(to_down, axis, down))  12.3 us
    all_to_all x1, starting transfers between devices, on_device(): plane = lax.all_to_all(chunks, ('gx', 'gy'), 0, 0, tiled=True)  10.8 us
    ppermute x4, waiting for transfers between devices, swap(): return (lax.ppermute(to_up, axis, up), lax.ppermute(to_down, axis, down))  8.66 us
    all_to_all x1, waiting for transfers between devices, on_device(): plane = lax.all_to_all(chunks, ('gx', 'gy'), 0, 0, tiled=True)  4.32 us
    ppermute x2, starting transfers between devices, on_device(): lax.ppermute(rows, 'gy', pairs)  3.84 us
    ppermute x2, waiting for transfers between devices, on_device(): lax.ppermute(rows, 'gy', pairs)  2.33 us
    unnamed x6, local copies, waits for them, and re-layouts  2 us
  transfers between devices with their start and end apart: 7, of which 5 were waited for; matrix products, arithmetic and copies ran while one was open for 0% of the time, Pallas kernels for 16%

profile of v11, /device:TPU:56, one launch (start us, length us, event | category | flops | bytes accessed | tf_op | source)
XLA Modules:
  0.0 62.7 jit_solution(10477864303045239631)
XLA Ops:
  0.0 1.9 %send_x.1 = (f32[3,16,16,128]{3,2,1,0:T(8,128)}, f32[15,16,128]{2,1,0:T(8,128)}, f32[15,16,128]{2,1,0:T(8,128)}) custom-call(f32[4]{0:T(128)} %table.1, s32[16,16,128]{2,1,0:T(8,128)} %phase.1, f32[16,16,128]{2,1,0:T(8,128)} %iterate.1, f32[16,16,128]{2,1,0:T(8,128)} %right.1), custom_call_target="tpu_custom_call" | custom-call | flops 1000000 | bytes 393232 | tf_op jit(solution)/shard_map/send_x/pallas_call | solution.py:507
  1.9 4.3 %collective-permute-start = (f32[15,16,128]{2,1,0:T(8,128)}, f32[15,16,128]{2,1,0:T(8,128)S(1)}, u32[]{:S(2)}, u32[]{:S(2)}) collective-permute-start(f32[15,16,128]{2,1,0:T(8,128)} %get-tuple-element.36), channel_id=1, source_target_pairs={{0,64},{64,128},{128,192},{192,256},{256,320},{320,384},{384,448},... | collective-permute-start | bytes 368648 | tf_op jit(solution)/shard_map/ppermute | solution.py:529
  6.2 1.3 %collective-permute-start.1 = (f32[15,16,128]{2,1,0:T(8,128)}, f32[15,16,128]{2,1,0:T(8,128)S(1)}, u32[]{:S(2)}, u32[]{:S(2)}) collective-permute-start(f32[15,16,128]{2,1,0:T(8,128)} %get-tuple-element.37), channel_id=1, source_target_pairs={{64,0},{128,64},{192,128},{256,192},{320,256},{384,320},{448,384},... | collective-permute-start | bytes 368648 | tf_op jit(solution)/shard_map/ppermute | solution.py:529
  7.5 0.0 copy-start.2
  7.5 1.0 %copy-done.2 = f32[3,16,16,128]{3,2,1,0:T(8,128)S(1)} copy-done((f32[3,16,16,128]{3,2,1,0:T(8,128)S(1)}, f32[3,16,16,128]{3,2,1,0:T(8,128)}, u32[]{:S(2)}) %copy-start.2) | copy-done | bytes 393240
  8.6 0.1 pad_add_fusion.place
  8.6 0.5 collective-permute-done.from_down
  9.1 4.6 %collective-permute-done.1.from_up = f32[15,16,128]{2,1,0:T(8,128)S(1)} collective-permute-done((f32[15,16,128]{2,1,0:T(8,128)}, f32[15,16,128]{2,1,0:T(8,128)S(1)}, u32[]{:S(2)}, u32[]{:S(2)}) %collective-permute-start.1) | collective-permute-done | bytes 122912 | tf_op jit(solution)/shard_map/ppermute | solution.py:529
  13.7 0.7 %pack_y.1 = (f32[3,28,16,128]{3,2,1,0:T(8,128)S(1)}, f32[28,16,128]{2,1,0:T(8,128)S(1)}, f32[28,16,128]{2,1,0:T(8,128)S(1)}) custom-call(s32[2]{0:T(128)S(1)} %pad_add_fusion.place, f32[3,16,16,128]{3,2,1,0:T(8,128)S(1)} %hold.1.fields, f32[15,16,128]{2,1,0:T(8,128)S(1)} %collective-permute-done.from_down, f32[15,16,128]{2,1,0:T(8,128)S(1)} %collective-permute-done.1.from_up), custom_call_target="tpu_custom_call" | custom-call | flops 1000000 | bytes 638984 | tf_op jit(solution)/shard_map/pack_y/pallas_call | solution.py:507
  14.4 1.9 %collective-permute-start.2 = (f32[28,16,128]{2,1,0:T(8,128)S(1)}, f32[28,16,128]{2,1,0:T(8,128)S(1)}, u32[]{:S(2)}, u32[]{:S(2)}) collective-permute-start(f32[28,16,128]{2,1,0:T(8,128)S(1)} %get-tuple-element.44), channel_id=1, source_target_pairs={{16,32},{32,16},{17,33},{33,17},{18,34},{34,18},{19,35},{35,19},{2... | collective-permute-start | bytes 688136 | tf_op jit(solution)/shard_map/ppermute | solution.py:553
  16.3 1.9 %collective-permute-start.3 = (f32[28,16,128]{2,1,0:T(8,128)S(1)}, f32[28,16,128]{2,1,0:T(8,128)S(1)}, u32[]{:S(2)}, u32[]{:S(2)}) collective-permute-start(f32[28,16,128]{2,1,0:T(8,128)S(1)} %get-tuple-element.45), channel_id=1, source_target_pairs={{0,16},{32,48},{16,0},{48,32},{1,17},{33,49},{17,1},{49,33},{2,18}... | collective-permute-start | bytes 688136 | tf_op jit(solution)/shard_map/ppermute | solution.py:553
  18.3 1.1 %own_rows.1 = (f32[16,512]{1,0:T(8,128)S(1)}, f32[16,512]{1,0:T(8,128)S(1)}, f32[3,16,16,128]{3,2,1,0:T(8,128)S(1)}) custom-call(f32[3,28,16,128]{3,2,1,0:T(8,128)S(1)} %get-tuple-element.43.ext), custom_call_target="tpu_custom_call" | custom-call | flops 30000000 | bytes 688128 | tf_op jit(solution)/shard_map/own_rows/pallas_call | solution.py:507
  19.4 2.3 %collective-permute-done.2.from_first = f32[28,16,128]{2,1,0:T(8,128)S(1)} collective-permute-done((f32[28,16,128]{2,1,0:T(8,128)S(1)}, f32[28,16,128]{2,1,0:T(8,128)S(1)}, u32[]{:S(2)}, u32[]{:S(2)}) %collective-permute-start.2) | collective-permute-done | bytes 229408 | tf_op jit(solution)/shard_map/ppermute | solution.py:553
  21.8 0.0 collective-permute-done.3.from_second
  21.8 1.6 %pack_z.1 = (f32[3,28,32,128]{3,2,1,0:T(8,128)S(1)}, f32[32,512]{1,0:T(8,128)S(1)}, f32[32,512]{1,0:T(8,128)S(1)}, f32[16,128]{1,0:T(8,128)S(1)}) custom-call(s32[2]{0:T(128)S(1)} %pad_add_fusion.place, f32[3,28,16,128]{3,2,1,0:T(8,128)S(1)} %get-tuple-element.43.ext, f32[28,16,128]{2,1,0:T(8,128)S(1)} %collective-permute-done.2.from_first, ...), custom_call_target="tpu_custom_call" | custom-call | flops 1000000 | bytes 1605640 | tf_op jit(solution)/shard_map/pack_z/pallas_call | solution.py:507
  23.4 3.6 %collective-permute-start.4 = (f32[32,512]{1,0:T(8,128)S(1)}, f32[32,512]{1,0:T(8,128)S(1)}, u32[]{:S(2)}, u32[]{:S(2)}) collective-permute-start(f32[32,512]{1,0:T(8,128)S(1)} %get-tuple-element.54.sent_up), channel_id=1, source_target_pairs={{0,1},{1,2},{2,3},{3,4},{4,5},{5,6},{6,7},{7,8},{8,9},{9,10},{10,1... | collective-permute-start | bytes 196616 | tf_op jit(solution)/shard_map/ppermute | solution.py:529
  27.0 3.1 %collective-permute-start.5 = (f32[32,512]{1,0:T(8,128)S(1)}, f32[32,512]{1,0:T(8,128)S(1)}, u32[]{:S(2)}, u32[]{:S(2)}) collective-permute-start(f32[32,512]{1,0:T(8,128)S(1)} %get-tuple-element.55.sent_down), channel_id=1, source_target_pairs={{1,0},{2,1},{3,2},{4,3},{5,4},{6,5},{7,6},{8,7},{9,8},{10,9},{11,1... | collective-permute-start | bytes 196616 | tf_op jit(solution)/shard_map/ppermute | solution.py:529
  30.2 1.5 %bands_xy.1 = (f32[3,28,32,128]{3,2,1,0:T(8,128)S(1)}, bf16[1088,512]{1,0:T(8,128)(2,1)S(1)}) custom-call(s32[2]{0:T(128)S(1)} %pad_add_fusion.place, f32[3,28,32,128]{3,2,1,0:T(8,128)S(1)} %get-tuple-element.56.full), custom_call_target="tpu_custom_call" | custom-call | flops 30000000 | bytes 1376264 | tf_op jit(solution)/shard_map/bands_xy/pallas_call | solution.py:507
  31.6 0.0 copy-start
  31.6 1.0 %copy-done = bf16[1088,512]{1,0:T(8,128)(2,1)} copy-done((bf16[1088,512]{1,0:T(8,128)(2,1)}, bf16[1088,512]{1,0:T(8,128)(2,1)S(1)}, u32[]{:S(2)}) %copy-start) | copy-done | bytes 1114136
  32.6 0.0 collective-permute-done.4.from_down
  32.6 3.5 %collective-permute-done.5.from_up = f32[32,512]{1,0:T(8,128)S(1)} collective-permute-done((f32[32,512]{1,0:T(8,128)S(1)}, f32[32,512]{1,0:T(8,128)S(1)}, u32[]{:S(2)}, u32[]{:S(2)}) %collective-permute-start.5) | collective-permute-done | bytes 65568 | tf_op jit(solution)/shard_map/ppermute | solution.py:529
  36.2 1.6 %own_cells.1 = f32[32,16,128]{2,1,0:T(8,128)} custom-call(f32[32,512]{1,0:T(8,128)S(1)} %get-tuple-element.54.sent_up, f32[32,512]{1,0:T(8,128)S(1)} %get-tuple-element.55.sent_down, f32[32,512]{1,0:T(8,128)S(1)} %collective-permute-done.4.from_down, f32[32,512]{1,0:T(8,128)S(1)} %collective-permute-done.5.from_up, f32[16,128]{1,0:T(8,128)S(1)} %get-tuple-element.62.inner), custom_call_target="tpu_custom_call" | custom-call | flops 1000000 | bytes 270336 | tf_op jit(solution)/shard_map/own_cells/pallas_call | solution.py:507
  37.8 10.8 %all-to-all-start = ((f32[32,16,128]{2,1,0:T(8,128)}), f32[32,16,128]{2,1,0:T(8,128)S(1)}, u32[]{:S(2)}, u32[]{:S(2)}) async-start(f32[32,16,128]{2,1,0:T(8,128)} %own_cells.1), calls=%async_computation | async-start | bytes 524288 | tf_op jit(solution)/shard_map/all_to_all | solution.py:577
  48.5 2.3 %fine_residual.1 = (f32[28,32,256]{2,1,0:T(8,128)S(1)}, f32[28,32,256]{2,1,0:T(8,128)S(1)}, f32[28,32,256]{2,1,0:T(8,128)S(1)}) custom-call(f32[3,28,32,128]{3,2,1,0:T(8,128)S(1)} %get-tuple-element.56.full, f32[3,28,32,128]{3,2,1,0:T(8,128)S(1)} %get-tuple-element.63.xy, f32[32,512]{1,0:T(8,128)S(1)} %collective-permute-done.4.from_down, ...), custom_call_target="tpu_custom_call" | custom-call | flops 30000000 | bytes 2883584 | tf_op jit(solution)/shard_map/fine_residual/pallas_call | solution.py:507
  50.8 0.0 copy-start.1
  50.9 5.3 %fine_sweeps.1.base = f32[16,16,128]{2,1,0:T(8,128)S(1)} custom-call(f32[3,28,32,128]{3,2,1,0:T(8,128)S(1)} %get-tuple-element.56.full, f32[28,32,256]{2,1,0:T(8,128)S(1)} %get-tuple-element.64.coef, f32[28,32,256]{2,1,0:T(8,128)S(1)} %get-tuple-element.65.res, f32[28,32,256]{2,1,0:T(8,128)S(1)} %get-tuple-element.66.inv), custom_call_target="tpu_custom_call" | custom-call | flops 60000000 | bytes 4128768 | tf_op jit(solution)/shard_map/fine_sweeps/pallas_call | solution.py:507
  56.2 4.3 %all-to-all-done = f32[32,16,128]{2,1,0:T(8,128)S(1)} async-done(((f32[32,16,128]{2,1,0:T(8,128)}), f32[32,16,128]{2,1,0:T(8,128)S(1)}, u32[]{:S(2)}, u32[]{:S(2)}) %all-to-all-start) | async-done | bytes 262176 | tf_op jit(solution)/shard_map/all_to_all | solution.py:577
  60.5 0.0 copy-done.1
  60.5 2.2 %coarse_levels.1 = f32[16,16,128]{2,1,0:T(8,128)} custom-call(bf16[1088,512]{1,0:T(8,128)(2,1)S(1)} %copy-done.1, f32[512,128]{1,0:T(8,128)S(1)} %bitcast.3, f32[16,16,128]{2,1,0:T(8,128)S(1)} %fine_sweeps.1.base), custom_call_target="tpu_custom_call" | custom-call | flops 1000000 | bytes 2621440 | tf_op jit(solution)/shard_map/coarse_levels/pallas_call | solution.py:507
  (1 shorter events, 0.0 us)
Async XLA Ops:
  1.9 7.2 %collective-permute-start = (f32[15,16,128]{2,1,0:T(8,128)}, f32[15,16,128]{2,1,0:T(8,128)S(1)}, u32[]{:S(2)}, u32[]{:S(2)}) collective-permute-start(f32[15,16,128]{2,1,0:T(8,128)} %get-tuple-element.36), channel_id=1, source_target_pairs={{0,64},{64,128},{128,192},{192,256},{256,320},{320,384},{384,448},... | collective-permute-start | bytes 368648 | tf_op jit(solution)/shard_map/ppermute | solution.py:529
  6.2 7.5 %collective-permute-start.1 = (f32[15,16,128]{2,1,0:T(8,128)}, f32[15,16,128]{2,1,0:T(8,128)S(1)}, u32[]{:S(2)}, u32[]{:S(2)}) collective-permute-start(f32[15,16,128]{2,1,0:T(8,128)} %get-tuple-element.37), channel_id=1, source_target_pairs={{64,0},{128,64},{192,128},{256,192},{320,256},{384,320},{448,384},... | collective-permute-start | bytes 368648 | tf_op jit(solution)/shard_map/ppermute | solution.py:529
  7.5 1.0 %copy-start.2 = (f32[3,16,16,128]{3,2,1,0:T(8,128)S(1)}, f32[3,16,16,128]{3,2,1,0:T(8,128)}, u32[]{:S(2)}) copy-start(f32[3,16,16,128]{3,2,1,0:T(8,128)} %get-tuple-element.38.fields) | copy-start | bytes 1179652
  14.4 7.3 %collective-permute-start.2 = (f32[28,16,128]{2,1,0:T(8,128)S(1)}, f32[28,16,128]{2,1,0:T(8,128)S(1)}, u32[]{:S(2)}, u32[]{:S(2)}) collective-permute-start(f32[28,16,128]{2,1,0:T(8,128)S(1)} %get-tuple-element.44), channel_id=1, source_target_pairs={{16,32},{32,16},{17,33},{33,17},{18,34},{34,18},{19,35},{35,19},{2... | collective-permute-start | bytes 688136 | tf_op jit(solution)/shard_map/ppermute | solution.py:553
  16.3 5.4 %collective-permute-start.3 = (f32[28,16,128]{2,1,0:T(8,128)S(1)}, f32[28,16,128]{2,1,0:T(8,128)S(1)}, u32[]{:S(2)}, u32[]{:S(2)}) collective-permute-start(f32[28,16,128]{2,1,0:T(8,128)S(1)} %get-tuple-element.45), channel_id=1, source_target_pairs={{0,16},{32,48},{16,0},{48,32},{1,17},{33,49},{17,1},{49,33},{2,18}... | collective-permute-start | bytes 688136 | tf_op jit(solution)/shard_map/ppermute | solution.py:553
  23.4 9.2 %collective-permute-start.4 = (f32[32,512]{1,0:T(8,128)S(1)}, f32[32,512]{1,0:T(8,128)S(1)}, u32[]{:S(2)}, u32[]{:S(2)}) collective-permute-start(f32[32,512]{1,0:T(8,128)S(1)} %get-tuple-element.54.sent_up), channel_id=1, source_target_pairs={{0,1},{1,2},{2,3},{3,4},{4,5},{5,6},{6,7},{7,8},{8,9},{9,10},{10,1... | collective-permute-start | bytes 196616 | tf_op jit(solution)/shard_map/ppermute | solution.py:529
  27.0 9.2 %collective-permute-start.5 = (f32[32,512]{1,0:T(8,128)S(1)}, f32[32,512]{1,0:T(8,128)S(1)}, u32[]{:S(2)}, u32[]{:S(2)}) collective-permute-start(f32[32,512]{1,0:T(8,128)S(1)} %get-tuple-element.55.sent_down), channel_id=1, source_target_pairs={{1,0},{2,1},{3,2},{4,3},{5,4},{6,5},{7,6},{8,7},{9,8},{10,9},{11,1... | collective-permute-start | bytes 196616 | tf_op jit(solution)/shard_map/ppermute | solution.py:529
  31.6 1.0 %copy-start = (bf16[1088,512]{1,0:T(8,128)(2,1)}, bf16[1088,512]{1,0:T(8,128)(2,1)S(1)}, u32[]{:S(2)}) copy-start(bf16[1088,512]{1,0:T(8,128)(2,1)S(1)} %get-tuple-element.59.tables) | copy-start | bytes 3342340
  37.8 22.7 %all-to-all-start = ((f32[32,16,128]{2,1,0:T(8,128)}), f32[32,16,128]{2,1,0:T(8,128)S(1)}, u32[]{:S(2)}, u32[]{:S(2)}) async-start(f32[32,16,128]{2,1,0:T(8,128)} %own_cells.1), calls=%async_computation | async-start | bytes 524288 | tf_op jit(solution)/shard_map/all_to_all | solution.py:577
  50.8 9.6 %copy-start.1 = (bf16[1088,512]{1,0:T(8,128)(2,1)S(1)}, bf16[1088,512]{1,0:T(8,128)(2,1)}, u32[]{:S(2)}) copy-start(bf16[1088,512]{1,0:T(8,128)(2,1)} %copy-done) | copy-start | bytes 3342340

commit v12 on v11

--- a/solution.py
+++ b/solution.py
@@ -103,8 +103,8 @@
     held[...] = fields[...]
 
 
-def by_parity(place, body, first, second):
-    odd = (place[1] & 1) == 1
+def by_parity(body, first, second):
+    odd = (lax.axis_index("gy") & 1) == 1
 
     @pl.when(odd)
     def _():
@@ -115,7 +115,7 @@
         body(first, second)
 
 
-def pack_y(place, fields, from_down, from_up, ext, to_first, to_second):
+def pack_y(fields, from_down, from_up, ext, to_first, to_second):
     for field in range(3):
         h, a, b = HALO[field], ROWS[field], ROWS[field + 1]
         if h < 6:
@@ -131,7 +131,7 @@
             to_up[:, a:b, :] = ext[field, :, 16 - h : 16, :]
             to_down[:, a:b, :] = ext[field, :, 0:h, :]
 
-    by_parity(place, rows, to_first, to_second)
+    by_parity(rows, to_first, to_second)
     to_first[:, 15:16, :] = jnp.zeros((28, 1, 128), F32)
     to_second[:, 15:16, :] = jnp.zeros((28, 1, 128), F32)
 
@@ -185,7 +185,7 @@
     lax.fori_loop(0, 4, bands, 0)
 
 
-def pack_z(place, ext, from_first, from_second, up_rows, down_rows, xz, full, to_up, to_down, inner, edges, quads):
+def pack_z(ext, from_first, from_second, up_rows, down_rows, xz, full, to_up, to_down, inner, edges, quads):
     edges[:, 24:32, :] = jnp.zeros((6, 8, 128), F32)
     for field in range(3):
         h = HALO[field]
@@ -203,7 +203,7 @@
             for number, f in enumerate((k, v, k * v)):
                 edges[3 * at + number, 0:28, :] = f
 
-    by_parity(place, rows, from_first, from_second)
+    by_parity(rows, from_first, from_second)
     matrix = band_matrix(128)
     for at, f in enumerate(band_z([band(edges[at], 0) for at in range(6)], matrix)):
         edges[at] = f
@@ -251,14 +251,14 @@
     return pltpu.roll(x, shift, 1) if shift else x
 
 
-def bands_xy(place, full, xy, tables, bands):
+def bands_xy(full, xy, tables, bands):
     row = iota((192, 512), 0)
     cell = iota((192, 512), 1)
     cell_x = (cell >> 6) * 4 + ((cell >> 2) & 3)
     cell_y = ((cell >> 4) & 3) * 4 + (cell & 3)
     for level in range(3):
-        at_x = place[0] * (4 >> level) - 4 + (row >> 4)
-        at_y = place[1] * (4 >> level) - 4 + (row & 15)
+        at_x = lax.axis_index("gx") * (4 >> level) - 4 + (row >> 4)
+        at_y = lax.axis_index("gy") * (4 >> level) - 4 + (row & 15)
         found = ((cell_x >> level) == at_x) & ((cell_y >> level) == at_y)
         tables[192 * level : 192 * level + 192, :] = ones_where(found)
     source = iota((128, 256), 0)
@@ -498,7 +498,6 @@
 
 
 VMEM = pl.BlockSpec(memory_space=pltpu.VMEM)
-SMEM = pl.BlockSpec(memory_space=pltpu.SMEM)
 HBM = pl.BlockSpec(memory_space=pltpu.HBM)
 
 
@@ -531,7 +530,6 @@
 
 def on_device(right, iterate, phase, table):
     block = (16, 16, 128)
-    place = jnp.stack([lax.axis_index("gx"), lax.axis_index("gy")]).astype(jnp.int32)
     fields, to_up, to_down = call(
         send_x,
         [(3, *block), (15, 16, 128), (15, 16, 128)],
@@ -543,12 +541,11 @@
     )
     from_down, from_up = swap("gx", to_up, to_down)
     (held,) = call(hold, [(3, *block)], [fields], flops=30000000)
-    from_down, from_up, fields, place = lax.optimization_barrier((from_down, from_up, held, place))
+    from_down, from_up, fields = lax.optimization_barrier((from_down, from_up, held))
     ext, *sent = call(
         pack_y,
         [(3, 28, 16, 128), (28, 16, 128), (28, 16, 128)],
-        [place, fields, from_down, from_up],
-        first=SMEM,
+        [fields, from_down, from_up],
     )
     found = [lax.ppermute(rows, "gy", pairs) for rows, pairs in zip(sent, neighbour_pairs(lax.axis_size("gy")))]
     planes = (3, 28, 32, 128)
@@ -557,17 +554,15 @@
     full, to_up, to_down, inner = call(
         pack_z,
         [planes, (32, 512), (32, 512), (16, 128)],
-        [place, ext, *found, up_rows, down_rows, xz],
+        [ext, *found, up_rows, down_rows, xz],
         scratch=[(6, 32, 128), (128, 128)],
-        first=SMEM,
     )
     from_down, from_up = swap("gz", to_up, to_down)
     xy, tables = call(
         bands_xy,
         [planes, jax.ShapeDtypeStruct((1088, 512), BF16)],
-        [place, full],
+        [full],
         scratch=[planes],
-        first=SMEM,
         flops=30000000,
     )
     from_down, from_up, xy, tables = lax.optimization_barrier((from_down, from_up, xy, tables))

time: 63.4 us -> 62.3 us (0.983)
  Pallas kernels: 18.2 us -> 16.6 us
    pallas_call x10, Pallas kernels: 18.2 us -> 16.6 us  [call(): pl.pallas_call(kernel, out_shape=[out if isinstance(out, jax.ShapeDtypeSt...]
where the time goes in v12:
time: 62.3 us; the launch traced here: 61.6 us
  starting transfers between devices  26.9 us (43%)
  Pallas kernels  16.6 us (27%)
  waiting for transfers between devices  15.9 us (26%)
  local copies, waits for them, and re-layouts  2 us (3%)
    pallas_call x10, Pallas kernels, call(): pl.pallas_call(kernel, out_shape=[out if isinstance(out, jax.ShapeDtypeSt...  16.6 us
    ppermute x4, starting transfers between devices, swap(): return (lax.ppermute(to_up, axis, up), lax.ppermute(to_down, axis, down))  12.3 us
    all_to_all x1, starting transfers between devices, on_device(): plane = lax.all_to_all(chunks, ('gx', 'gy'), 0, 0, tiled=True)  10.8 us
    ppermute x4, waiting for transfers between devices, swap(): return (lax.ppermute(to_up, axis, up), lax.ppermute(to_down, axis, down))  9.28 us
    all_to_all x1, waiting for transfers between devices, on_device(): plane = lax.all_to_all(chunks, ('gx', 'gy'), 0, 0, tiled=True)  4.31 us
    ppermute x2, starting transfers between devices, on_device(): lax.ppermute(rows, 'gy', pairs)  3.84 us
    ppermute x2, waiting for transfers between devices, on_device(): lax.ppermute(rows, 'gy', pairs)  2.34 us
    unnamed x6, local copies, waits for them, and re-layouts  2 us
  transfers between devices with their start and end apart: 7, of which 5 were waited for; matrix products, arithmetic and copies ran while one was open for 0% of the time, Pallas kernels for 16%

profile of v12, /device:TPU:56, one launch (start us, length us, event | category | flops | bytes accessed | tf_op | source)
XLA Modules:
  0.0 61.6 jit_solution(17762601445442330869)
XLA Ops:
  0.0 1.9 %send_x.1 = (f32[3,16,16,128]{3,2,1,0:T(8,128)}, f32[15,16,128]{2,1,0:T(8,128)}, f32[15,16,128]{2,1,0:T(8,128)}) custom-call(f32[4]{0:T(128)} %table.1, s32[16,16,128]{2,1,0:T(8,128)} %phase.1, f32[16,16,128]{2,1,0:T(8,128)} %iterate.1, f32[16,16,128]{2,1,0:T(8,128)} %right.1), custom_call_target="tpu_custom_call" | custom-call | flops 1000000 | bytes 393232 | tf_op jit(solution)/shard_map/send_x/pallas_call | solution.py:506
  1.9 4.3 %collective-permute-start = (f32[15,16,128]{2,1,0:T(8,128)}, f32[15,16,128]{2,1,0:T(8,128)S(1)}, u32[]{:S(2)}, u32[]{:S(2)}) collective-permute-start(f32[15,16,128]{2,1,0:T(8,128)} %get-tuple-element.35), channel_id=1, source_target_pairs={{0,64},{64,128},{128,192},{192,256},{256,320},{320,384},{384,448},... | collective-permute-start | bytes 368648 | tf_op jit(solution)/shard_map/ppermute | solution.py:528
  6.2 1.3 %collective-permute-start.1 = (f32[15,16,128]{2,1,0:T(8,128)}, f32[15,16,128]{2,1,0:T(8,128)S(1)}, u32[]{:S(2)}, u32[]{:S(2)}) collective-permute-start(f32[15,16,128]{2,1,0:T(8,128)} %get-tuple-element.36), channel_id=1, source_target_pairs={{64,0},{128,64},{192,128},{256,192},{320,256},{384,320},{448,384},... | collective-permute-start | bytes 368648 | tf_op jit(solution)/shard_map/ppermute | solution.py:528
  7.5 0.0 copy-start.2
  7.5 1.0 %copy-done.2 = f32[3,16,16,128]{3,2,1,0:T(8,128)S(1)} copy-done((f32[3,16,16,128]{3,2,1,0:T(8,128)S(1)}, f32[3,16,16,128]{3,2,1,0:T(8,128)}, u32[]{:S(2)}) %copy-start.2) | copy-done | bytes 393240
  8.6 0.5 collective-permute-done.from_down
  9.1 4.6 %collective-permute-done.1.from_up = f32[15,16,128]{2,1,0:T(8,128)S(1)} collective-permute-done((f32[15,16,128]{2,1,0:T(8,128)}, f32[15,16,128]{2,1,0:T(8,128)S(1)}, u32[]{:S(2)}, u32[]{:S(2)}) %collective-permute-start.1) | collective-permute-done | bytes 122912 | tf_op jit(solution)/shard_map/ppermute | solution.py:528
  13.7 0.1 pack_y.1
  13.9 1.9 %collective-permute-start.2 = (f32[28,16,128]{2,1,0:T(8,128)S(1)}, f32[28,16,128]{2,1,0:T(8,128)S(1)}, u32[]{:S(2)}, u32[]{:S(2)}) collective-permute-start(f32[28,16,128]{2,1,0:T(8,128)S(1)} %get-tuple-element.42), channel_id=1, source_target_pairs={{16,32},{32,16},{17,33},{33,17},{18,34},{34,18},{19,35},{35,19},{2... | collective-permute-start | bytes 688136 | tf_op jit(solution)/shard_map/ppermute | solution.py:550
  15.8 1.9 %collective-permute-start.3 = (f32[28,16,128]{2,1,0:T(8,128)S(1)}, f32[28,16,128]{2,1,0:T(8,128)S(1)}, u32[]{:S(2)}, u32[]{:S(2)}) collective-permute-start(f32[28,16,128]{2,1,0:T(8,128)S(1)} %get-tuple-element.43), channel_id=1, source_target_pairs={{0,16},{32,48},{16,0},{48,32},{1,17},{33,49},{17,1},{49,33},{2,18}... | collective-permute-start | bytes 688136 | tf_op jit(solution)/shard_map/ppermute | solution.py:550
  17.7 1.1 %own_rows.1 = (f32[16,512]{1,0:T(8,128)S(1)}, f32[16,512]{1,0:T(8,128)S(1)}, f32[3,16,16,128]{3,2,1,0:T(8,128)S(1)}) custom-call(f32[3,28,16,128]{3,2,1,0:T(8,128)S(1)} %get-tuple-element.41.ext), custom_call_target="tpu_custom_call" | custom-call | flops 30000000 | bytes 688128 | tf_op jit(solution)/shard_map/own_rows/pallas_call | solution.py:506
  18.9 2.3 %collective-permute-done.2.from_first = f32[28,16,128]{2,1,0:T(8,128)S(1)} collective-permute-done((f32[28,16,128]{2,1,0:T(8,128)S(1)}, f32[28,16,128]{2,1,0:T(8,128)S(1)}, u32[]{:S(2)}, u32[]{:S(2)}) %collective-permute-start.2) | collective-permute-done | bytes 229408 | tf_op jit(solution)/shard_map/ppermute | solution.py:550
  21.2 0.0 collective-permute-done.3.from_second
  21.2 1.1 %pack_z.1 = (f32[3,28,32,128]{3,2,1,0:T(8,128)S(1)}, f32[32,512]{1,0:T(8,128)S(1)}, f32[32,512]{1,0:T(8,128)S(1)}, f32[16,128]{1,0:T(8,128)S(1)}) custom-call(f32[3,28,16,128]{3,2,1,0:T(8,128)S(1)} %get-tuple-element.41.ext, f32[28,16,128]{2,1,0:T(8,128)S(1)} %collective-permute-done.2.from_first, f32[28,16,128]{2,1,0:T(8,128)S(1)} %collective-permute-done.3.from_second, ...), custom_call_target="tpu_custom_call" | custom-call | flops 1000000 | bytes 1605632 | tf_op jit(solution)/shard_map/pack_z/pallas_call | solution.py:506
  22.3 3.6 %collective-permute-start.4 = (f32[32,512]{1,0:T(8,128)S(1)}, f32[32,512]{1,0:T(8,128)S(1)}, u32[]{:S(2)}, u32[]{:S(2)}) collective-permute-start(f32[32,512]{1,0:T(8,128)S(1)} %get-tuple-element.52.sent_up), channel_id=1, source_target_pairs={{0,1},{1,2},{2,3},{3,4},{4,5},{5,6},{6,7},{7,8},{8,9},{9,10},{10,1... | collective-permute-start | bytes 196616 | tf_op jit(solution)/shard_map/ppermute | solution.py:528
  25.9 3.1 %collective-permute-start.5 = (f32[32,512]{1,0:T(8,128)S(1)}, f32[32,512]{1,0:T(8,128)S(1)}, u32[]{:S(2)}, u32[]{:S(2)}) collective-permute-start(f32[32,512]{1,0:T(8,128)S(1)} %get-tuple-element.53.sent_down), channel_id=1, source_target_pairs={{1,0},{2,1},{3,2},{4,3},{5,4},{6,5},{7,6},{8,7},{9,8},{10,9},{11,1... | collective-permute-start | bytes 196616 | tf_op jit(solution)/shard_map/ppermute | solution.py:528
  29.1 0.9 %bands_xy.1 = (f32[3,28,32,128]{3,2,1,0:T(8,128)S(1)}, bf16[1088,512]{1,0:T(8,128)(2,1)S(1)}) custom-call(f32[3,28,32,128]{3,2,1,0:T(8,128)S(1)} %get-tuple-element.54.full), custom_call_target="tpu_custom_call" | custom-call | flops 30000000 | bytes 1376256 | tf_op jit(solution)/shard_map/bands_xy/pallas_call | solution.py:506
  30.0 0.0 copy-start
  30.0 1.0 %copy-done = bf16[1088,512]{1,0:T(8,128)(2,1)} copy-done((bf16[1088,512]{1,0:T(8,128)(2,1)}, bf16[1088,512]{1,0:T(8,128)(2,1)S(1)}, u32[]{:S(2)}) %copy-start) | copy-done | bytes 1114136
  31.0 0.0 collective-permute-done.4.from_down
  31.0 4.1 %collective-permute-done.5.from_up = f32[32,512]{1,0:T(8,128)S(1)} collective-permute-done((f32[32,512]{1,0:T(8,128)S(1)}, f32[32,512]{1,0:T(8,128)S(1)}, u32[]{:S(2)}, u32[]{:S(2)}) %collective-permute-start.5) | collective-permute-done | bytes 65568 | tf_op jit(solution)/shard_map/ppermute | solution.py:528
  35.1 1.6 %own_cells.1 = f32[32,16,128]{2,1,0:T(8,128)} custom-call(f32[32,512]{1,0:T(8,128)S(1)} %get-tuple-element.52.sent_up, f32[32,512]{1,0:T(8,128)S(1)} %get-tuple-element.53.sent_down, f32[32,512]{1,0:T(8,128)S(1)} %collective-permute-done.4.from_down, f32[32,512]{1,0:T(8,128)S(1)} %collective-permute-done.5.from_up, f32[16,128]{1,0:T(8,128)S(1)} %get-tuple-element.60.inner), custom_call_target="tpu_custom_call" | custom-call | flops 1000000 | bytes 270336 | tf_op jit(solution)/shard_map/own_cells/pallas_call | solution.py:506
  36.7 10.8 %all-to-all-start = ((f32[32,16,128]{2,1,0:T(8,128)}), f32[32,16,128]{2,1,0:T(8,128)S(1)}, u32[]{:S(2)}, u32[]{:S(2)}) async-start(f32[32,16,128]{2,1,0:T(8,128)} %own_cells.1), calls=%async_computation | async-start | bytes 524288 | tf_op jit(solution)/shard_map/all_to_all | solution.py:572
  47.5 2.3 %fine_residual.1 = (f32[28,32,256]{2,1,0:T(8,128)S(1)}, f32[28,32,256]{2,1,0:T(8,128)S(1)}, f32[28,32,256]{2,1,0:T(8,128)S(1)}) custom-call(f32[3,28,32,128]{3,2,1,0:T(8,128)S(1)} %get-tuple-element.54.full, f32[3,28,32,128]{3,2,1,0:T(8,128)S(1)} %get-tuple-element.61.xy, f32[32,512]{1,0:T(8,128)S(1)} %collective-permute-done.4.from_down, ...), custom_call_target="tpu_custom_call" | custom-call | flops 30000000 | bytes 2883584 | tf_op jit(solution)/shard_map/fine_residual/pallas_call | solution.py:506
  49.8 0.0 copy-start.1
  49.8 5.3 %fine_sweeps.1.base = f32[16,16,128]{2,1,0:T(8,128)S(1)} custom-call(f32[3,28,32,128]{3,2,1,0:T(8,128)S(1)} %get-tuple-element.54.full, f32[28,32,256]{2,1,0:T(8,128)S(1)} %get-tuple-element.62.coef, f32[28,32,256]{2,1,0:T(8,128)S(1)} %get-tuple-element.63.res, f32[28,32,256]{2,1,0:T(8,128)S(1)} %get-tuple-element.64.inv), custom_call_target="tpu_custom_call" | custom-call | flops 60000000 | bytes 4128768 | tf_op jit(solution)/shard_map/fine_sweeps/pallas_call | solution.py:506
  55.1 4.3 %all-to-all-done = f32[32,16,128]{2,1,0:T(8,128)S(1)} async-done(((f32[32,16,128]{2,1,0:T(8,128)}), f32[32,16,128]{2,1,0:T(8,128)S(1)}, u32[]{:S(2)}, u32[]{:S(2)}) %all-to-all-start) | async-done | bytes 262176 | tf_op jit(solution)/shard_map/all_to_all | solution.py:572
  59.4 0.0 copy-done.1
  59.4 2.2 %coarse_levels.1 = f32[16,16,128]{2,1,0:T(8,128)} custom-call(bf16[1088,512]{1,0:T(8,128)(2,1)S(1)} %copy-done.1, f32[512,128]{1,0:T(8,128)S(1)} %bitcast.1, f32[16,16,128]{2,1,0:T(8,128)S(1)} %fine_sweeps.1.base), custom_call_target="tpu_custom_call" | custom-call | flops 1000000 | bytes 2621440 | tf_op jit(solution)/shard_map/coarse_levels/pallas_call | solution.py:506
  (1 shorter events, 0.0 us)
Async XLA Ops:
  1.9 7.2 %collective-permute-start = (f32[15,16,128]{2,1,0:T(8,128)}, f32[15,16,128]{2,1,0:T(8,128)S(1)}, u32[]{:S(2)}, u32[]{:S(2)}) collective-permute-start(f32[15,16,128]{2,1,0:T(8,128)} %get-tuple-element.35), channel_id=1, source_target_pairs={{0,64},{64,128},{128,192},{192,256},{256,320},{320,384},{384,448},... | collective-permute-start | bytes 368648 | tf_op jit(solution)/shard_map/ppermute | solution.py:528
  6.2 7.5 %collective-permute-start.1 = (f32[15,16,128]{2,1,0:T(8,128)}, f32[15,16,128]{2,1,0:T(8,128)S(1)}, u32[]{:S(2)}, u32[]{:S(2)}) collective-permute-start(f32[15,16,128]{2,1,0:T(8,128)} %get-tuple-element.36), channel_id=1, source_target_pairs={{64,0},{128,64},{192,128},{256,192},{320,256},{384,320},{448,384},... | collective-permute-start | bytes 368648 | tf_op jit(solution)/shard_map/ppermute | solution.py:528
  7.5 1.0 %copy-start.2 = (f32[3,16,16,128]{3,2,1,0:T(8,128)S(1)}, f32[3,16,16,128]{3,2,1,0:T(8,128)}, u32[]{:S(2)}) copy-start(f32[3,16,16,128]{3,2,1,0:T(8,128)} %get-tuple-element.37.fields) | copy-start | bytes 1179652
  13.9 7.3 %collective-permute-start.2 = (f32[28,16,128]{2,1,0:T(8,128)S(1)}, f32[28,16,128]{2,1,0:T(8,128)S(1)}, u32[]{:S(2)}, u32[]{:S(2)}) collective-permute-start(f32[28,16,128]{2,1,0:T(8,128)S(1)} %get-tuple-element.42), channel_id=1, source_target_pairs={{16,32},{32,16},{17,33},{33,17},{18,34},{34,18},{19,35},{35,19},{2... | collective-permute-start | bytes 688136 | tf_op jit(solution)/shard_map/ppermute | solution.py:550
  15.8 5.4 %collective-permute-start.3 = (f32[28,16,128]{2,1,0:T(8,128)S(1)}, f32[28,16,128]{2,1,0:T(8,128)S(1)}, u32[]{:S(2)}, u32[]{:S(2)}) collective-permute-start(f32[28,16,128]{2,1,0:T(8,128)S(1)} %get-tuple-element.43), channel_id=1, source_target_pairs={{0,16},{32,48},{16,0},{48,32},{1,17},{33,49},{17,1},{49,33},{2,18}... | collective-permute-start | bytes 688136 | tf_op jit(solution)/shard_map/ppermute | solution.py:550
  22.3 8.7 %collective-permute-start.4 = (f32[32,512]{1,0:T(8,128)S(1)}, f32[32,512]{1,0:T(8,128)S(1)}, u32[]{:S(2)}, u32[]{:S(2)}) collective-permute-start(f32[32,512]{1,0:T(8,128)S(1)} %get-tuple-element.52.sent_up), channel_id=1, source_target_pairs={{0,1},{1,2},{2,3},{3,4},{4,5},{5,6},{6,7},{7,8},{8,9},{9,10},{10,1... | collective-permute-start | bytes 196616 | tf_op jit(solution)/shard_map/ppermute | solution.py:528
  25.9 9.2 %collective-permute-start.5 = (f32[32,512]{1,0:T(8,128)S(1)}, f32[32,512]{1,0:T(8,128)S(1)}, u32[]{:S(2)}, u32[]{:S(2)}) collective-permute-start(f32[32,512]{1,0:T(8,128)S(1)} %get-tuple-element.53.sent_down), channel_id=1, source_target_pairs={{1,0},{2,1},{3,2},{4,3},{5,4},{6,5},{7,6},{8,7},{9,8},{10,9},{11,1... | collective-permute-start | bytes 196616 | tf_op jit(solution)/shard_map/ppermute | solution.py:528
  30.0 1.0 %copy-start = (bf16[1088,512]{1,0:T(8,128)(2,1)}, bf16[1088,512]{1,0:T(8,128)(2,1)S(1)}, u32[]{:S(2)}) copy-start(bf16[1088,512]{1,0:T(8,128)(2,1)S(1)} %get-tuple-element.57.tables) | copy-start | bytes 3342340
  36.7 22.7 %all-to-all-start = ((f32[32,16,128]{2,1,0:T(8,128)}), f32[32,16,128]{2,1,0:T(8,128)S(1)}, u32[]{:S(2)}, u32[]{:S(2)}) async-start(f32[32,16,128]{2,1,0:T(8,128)} %own_cells.1), calls=%async_computation | async-start | bytes 524288 | tf_op jit(solution)/shard_map/all_to_all | solution.py:572
  49.8 9.6 %copy-start.1 = (bf16[1088,512]{1,0:T(8,128)(2,1)S(1)}, bf16[1088,512]{1,0:T(8,128)(2,1)}, u32[]{:S(2)}) copy-start(bf16[1088,512]{1,0:T(8,128)(2,1)} %copy-done) | copy-start | bytes 3342340

commit v13 on v12

--- a/solution.py
+++ b/solution.py
@@ -68,11 +68,11 @@
     return corr * (1.0 / 3.0) + inverse * (residual - 2.0 * (coef * corr) + 0.125 * (coef * tu_corr + tu_product))
 
 
-def smooth_small(residual, coef, sweeps, bands_z):
-    inverse = damped_inverse(coef, 6.0 * coef + 0.125 * bands_z([band_x(band(coef, 1))])[0])
+def smooth_small(residual, coef, sweeps):
+    inverse = damped_inverse(coef, 6.0 * coef + 0.125 * band(band_x(band(coef, 1)), 2))
     corr = inverse * residual
     for _ in range(sweeps - 1):
-        tu = bands_z([band_x(band(f, 1)) for f in (corr, coef * corr)])
+        tu = [band(band_x(band(f, 1)), 2) for f in (corr, coef * corr)]
         corr = relax(corr, inverse, residual, coef, *tu)
     return corr
 
@@ -167,7 +167,7 @@
         to_down[at : at + rows, 128 * group : 128 * group + 128] = down
 
 
-def own_rows(ext, up, down, xz):
+def own_rows(ext, up, down, xz, level3_lanes):
     pack_lanes(lambda field, x: ext[field, x], 16, up, down, 0)
     matrix = band_matrix(128)
 
@@ -183,9 +183,19 @@
         return carry
 
     lax.fori_loop(0, 4, bands, 0)
-
-
-def pack_z(ext, from_first, from_second, up_rows, down_rows, xz, full, to_up, to_down, inner, edges, quads):
+    source = iota((256, 128), 0)
+    lane = iota((256, 128), 1)
+    coarse = (source & 127) >> 2
+    base = 64 + (source >> 7) * 16
+    scale = jnp.where(source < 128, F32(0.25), F32(1.0 / 64.0))
+    upper = (lane == base + coarse - 16) & (coarse >= 16) & (coarse <= 30)
+    lower = (lane == base + coarse) & (coarse >= 1) & (coarse <= 15)
+    stay = (lane == (source >> 7) * 64 + 16 + coarse) & (coarse >= 1) & (coarse <= 30)
+    for at, found in enumerate((upper, lower, stay)):
+        level3_lanes[:, 128 * at : 128 * at + 128] = jnp.where(found, scale, 0.0).astype(BF16)
+
+
+def pack_z(ext, from_first, from_second, up_rows, down_rows, xz, level3_lanes, full, to_up, to_down, inner, edges, quads):
     edges[:, 24:32, :] = jnp.zeros((6, 8, 128), F32)
     for field in range(3):
         h = HALO[field]
@@ -204,9 +214,8 @@
                 edges[3 * at + number, 0:28, :] = f
 
     by_parity(rows, from_first, from_second)
-    matrix = band_matrix(128)
-    for at, f in enumerate(band_z([band(edges[at], 0) for at in range(6)], matrix)):
-        edges[at] = f
+    for at in range(6):
+        edges[at] = band(band(edges[at], 0), 1)
     row = iota((16, 128), 0)
 
     def quad(q, carry):
@@ -228,16 +237,7 @@
         return carry
 
     lax.fori_loop(0, 4, quad, 0)
-    source = iota((256, 128), 0)
-    lane = iota((256, 128), 1)
-    coarse = (source & 127) >> 2
-    base = 64 + (source >> 7) * 16
-    scale = jnp.where(source < 128, F32(0.25), F32(1.0 / 64.0))
-    upper = (lane == base + coarse - 16) & (coarse >= 16) & (coarse <= 30)
-    lower = (lane == base + coarse) & (coarse >= 1) & (coarse <= 15)
-    stay = (lane == (source >> 7) * 64 + 16 + coarse) & (coarse >= 1) & (coarse <= 30)
-    place = jnp.concatenate([jnp.where(found, scale, 0.0) for found in (upper, lower, stay)], axis=1).astype(BF16)
-    level3 = select_lanes(read_quads(quads), place)
+    level3 = select_lanes(read_quads(quads), level3_lanes[...])
     inner[...] = level3[:, 256:384]
     to_up[0:16, :] = up_rows[...]
     to_down[0:16, :] = down_rows[...]
@@ -251,7 +251,7 @@
     return pltpu.roll(x, shift, 1) if shift else x
 
 
-def bands_xy(full, xy, tables, bands):
+def bands_xy(full, xy, tables, end_lanes, bands):
     row = iota((192, 512), 0)
     cell = iota((192, 512), 1)
     cell_x = (cell >> 6) * 4 + ((cell >> 2) & 3)
@@ -275,6 +275,12 @@
         found = source == start + (lane >> (level + 2))
         tables[960:1088, 128 * level : 128 * level + 128] = ones_where(found)
 
+    source = iota((384, 128), 0)
+    x = (source >> 4) - 6
+    z = (source & 15) - 2
+    place = (x >= 0) & (x < 16) & (z >= 0) & (z < 8) & (iota((384, 128), 1) == (x >> 2) * 32 + (z >> 2))
+    end_lanes[...] = ones_where(place)
+
     def in_y(x, carry):
         k = full[0, x]
         v = full[1, x]
@@ -287,13 +293,10 @@
 
     def in_x(x, carry):
         for field in range(3):
-            xy[field, x] = (bands[field, x - 1] + bands[field, x + 1]) + 2.0 * bands[field, x]
-        return carry
-
-    lax.fori_loop(1, 27, in_x, 0, unroll=2)
-    for field in range(3):
-        for x in (0, 27):
-            xy[field, x] = jnp.zeros((32, 128), F32)
+            xy[field, x - 2] = (bands[field, x - 1] + bands[field, x + 1]) + 2.0 * bands[field, x]
+        return carry
+
+    lax.fori_loop(2, 26, in_x, 0, unroll=2)
 
 
 def end_cells(lower_k, lower_v, lower_right, upper_k, upper_v, upper_right):
@@ -311,7 +314,7 @@
     return right - (v * diagonal + 2.0 * (k * v) - 0.125 * (k * tu[1] + tu[2])), k
 
 
-def own_cells(sent_up, sent_down, from_down, from_up, inner, chunks, quads):
+def own_cells(sent_up, sent_down, from_down, from_up, inner, end_lanes, chunks, quads):
     def moved(f, shift):
         return pltpu.roll(f, shift % 512, 1)
 
@@ -325,11 +328,7 @@
         f = f[:, 0:384]
         f = f + pltpu.roll(f, 15, 0)
         rows.append(f + pltpu.roll(f, 14, 0))
-    source = iota((384, 128), 0)
-    x = (source >> 4) - 6
-    z = (source & 15) - 2
-    place = (x >= 0) & (x < 16) & (z >= 0) & (z < 8) & (iota((384, 128), 1) == (x >> 2) * 32 + (z >> 2))
-    ends = select_lanes(jnp.concatenate(rows, axis=0), ones_where(place))
+    ends = select_lanes(jnp.concatenate(rows, axis=0), end_lanes[...])
     ends = [0.25 * ends[0:16], 0.25 * ends[16:32], ends[32:48] / 64.0, ends[48:64] / 64.0]
     for q in range(4):
         for at in range(4):
@@ -383,9 +382,9 @@
         for x in xs:
             sides = over_x(sides_kv, x)
             wanted += [
-                jnp.concatenate([xy[0, x], sides[:, 0:128]], axis=1),
-                jnp.concatenate([xy[1, x], sides[:, 128:256]], axis=1),
-                jnp.concatenate([xy[2, x], over_x(product, x)], axis=1),
+                jnp.concatenate([xy[0, x - 2], sides[:, 0:128]], axis=1),
+                jnp.concatenate([xy[1, x - 2], sides[:, 128:256]], axis=1),
+                jnp.concatenate([xy[2, x - 2], over_x(product, x)], axis=1),
             ]
         found = band_z(wanted, matrix)
         for j, x in enumerate(xs):
@@ -405,14 +404,12 @@
     def over_x(ref, x):
         return (ref[x - 1] + ref[x + 1]) + 2.0 * ref[x]
 
-    matrix = band_matrix(256)
-
     def bands_of(xs, ref):
         wanted = []
         for x in xs:
             c = ref[x]
             wanted += [band(c, 0), band(coef[x] * c, 0)]
-        found = band_z(wanted, matrix)
+        found = [band(f, 1) for f in wanted]
         for j, x in enumerate(xs):
             yz_c[x] = found[2 * j]
             yz_kc[x] = found[2 * j + 1]
@@ -451,8 +448,7 @@
     lax.fori_loop(0, 14, pair, 0, unroll=2)
     sums = [pairs[tile, pl.ds(0, 448, stride=2), :] + pairs[tile, pl.ds(1, 448, stride=2), :] for tile in range(2)]
     sums = select_lanes(jnp.concatenate(sums, axis=1), halves).reshape(2, 14, 16, 128)
-    small = band_matrix(128)
-    corr_two = smooth_small(0.5 * sums[0], 0.125 * sums[1], 3, lambda fields: band_z(fields, small))
+    corr_two = smooth_small(0.5 * sums[0], 0.125 * sums[1], 3)
     doubled = ones_where(iota((128, 128), 0) == (iota((128, 128), 1) >> 1))
     wide = select_lanes(corr_two[3:11].reshape(128, 128), doubled).reshape(8, 16, 128)
     rows = wide[:, 0:8, :].reshape(64, 128)
@@ -475,16 +471,12 @@
     lax.fori_loop(6, 22, third, 0, unroll=4)
 
 
-def rolled_bands(fields):
-    return [band(f, 2) for f in fields]
-
-
 def coarse_levels(tables, plane, base, out, spread):
     found = jnp.dot(tables[0:576, :], jnp.concatenate(split(plane[...]), axis=1), preferred_element_type=F32)
     found = found[:, 0:128] + (found[:, 128:256] + found[:, 256:384])
     windows = jnp.concatenate([found[192 * level : 192 * level + 192, :] for level in range(3)], axis=1)
     both = select_lanes(windows, tables[576:960, 0:256])
-    corr = smooth_small(both[:, 0:128].reshape(12, 16, 128), both[:, 128:256].reshape(12, 16, 128), 4, rolled_bands)
+    corr = smooth_small(both[:, 0:128].reshape(12, 16, 128), both[:, 128:256].reshape(12, 16, 128), 4)
     wide = select_lanes(corr[4:8].reshape(64, 128), tables[960:1088, 0:384])
     for x in range(4):
         level4 = wide[16 * (x // 2) : 16 * (x // 2) + 16, 128:256]
@@ -549,26 +541,31 @@
     )
     found = [lax.ppermute(rows, "gy", pairs) for rows, pairs in zip(sent, neighbour_pairs(lax.axis_size("gy")))]
     planes = (3, 28, 32, 128)
-    mine = call(own_rows, [(16, 512), (16, 512), (3, *block)], [ext], flops=30000000)
-    *found, up_rows, down_rows, xz = lax.optimization_barrier((*found, *mine))
+    mine = call(
+        own_rows,
+        [(16, 512), (16, 512), (3, *block), jax.ShapeDtypeStruct((256, 384), BF16)],
+        [ext],
+        flops=30000000,
+    )
+    *found, up_rows, down_rows, xz, level3_lanes = lax.optimization_barrier((*found, *mine))
     full, to_up, to_down, inner = call(
         pack_z,
         [planes, (32, 512), (32, 512), (16, 128)],
-        [ext, *found, up_rows, down_rows, xz],
+        [ext, *found, up_rows, down_rows, xz, level3_lanes],
         scratch=[(6, 32, 128), (128, 128)],
     )
     from_down, from_up = swap("gz", to_up, to_down)
-    xy, tables = call(
+    xy, tables, end_lanes = call(
         bands_xy,
-        [planes, jax.ShapeDtypeStruct((1088, 512), BF16)],
+        [(3, 24, 32, 128), jax.ShapeDtypeStruct((1088, 512), BF16), jax.ShapeDtypeStruct((384, 128), BF16)],
         [full],
         scratch=[planes],
         flops=30000000,
     )
-    from_down, from_up, xy, tables = lax.optimization_barrier((from_down, from_up, xy, tables))
+    from_down, from_up, xy, tables, end_lanes = lax.optimization_barrier((from_down, from_up, xy, tables, end_lanes))
     z_sides = [from_down, from_up]
     count = lax.axis_size("gx") * lax.axis_size("gy")
-    (chunks,) = call(own_cells, [(count, 16, 128)], [to_up, to_down, *z_sides, inner], scratch=[(256, 128)])
+    (chunks,) = call(own_cells, [(count, 16, 128)], [to_up, to_down, *z_sides, inner, end_lanes], scratch=[(256, 128)])
     plane = lax.all_to_all(chunks, ("gx", "gy"), 0, 0, tiled=True)
     wide = (28, 32, 256)
     coef, res, inv = call(

time: 62.3 us -> 62.1 us (level)
  Pallas kernels: 16.6 us -> 15 us
  waiting for transfers between devices: 15.9 us -> 17.4 us
    all_to_all x1, waiting for transfers between devices: 4.31 us -> 6.04 us  [on_device(): plane = lax.all_to_all(chunks, ('gx', 'gy'), 0, 0, tiled=True)]
    pallas_call x10, Pallas kernels: 16.6 us -> 15 us  [call(): pl.pallas_call(kernel, out_shape=[out if isinstance(out, jax.ShapeDtypeSt...]
  transfers between devices with their start and end apart: 7 -> 7, of which waited for: 5 -> 5; matrix products, arithmetic and copies ran while one was open for 0% -> 0% of each run, Pallas kernels for 16% -> 13%
where the time goes in v13:
time: 62.1 us; the launch traced here: 61.4 us
  starting transfers between devices  26.9 us (43%)
  waiting for transfers between devices  17.4 us (28%)
  Pallas kernels  15 us (24%)
  local copies, waits for them, and re-layouts  2 us (3%)
    pallas_call x10, Pallas kernels, call(): pl.pallas_call(kernel, out_shape=[out if isinstance(out, jax.ShapeDtypeSt...  15 us
    ppermute x4, starting transfers between devices, swap(): return (lax.ppermute(to_up, axis, up), lax.ppermute(to_down, axis, down))  12.3 us
    all_to_all x1, starting transfers between devices, on_device(): plane = lax.all_to_all(chunks, ('gx', 'gy'), 0, 0, tiled=True)  10.8 us
    ppermute x4, waiting for transfers between devices, swap(): return (lax.ppermute(to_up, axis, up), lax.ppermute(to_down, axis, down))  9.17 us
    all_to_all x1, waiting for transfers between devices, on_device(): plane = lax.all_to_all(chunks, ('gx', 'gy'), 0, 0, tiled=True)  6.04 us
    ppermute x2, starting transfers between devices, on_device(): lax.ppermute(rows, 'gy', pairs)  3.84 us
    ppermute x2, waiting for transfers between devices, on_device(): lax.ppermute(rows, 'gy', pairs)  2.2 us
    unnamed x6, local copies, waits for them, and re-layouts  2 us
  transfers between devices with their start and end apart: 7, of which 5 were waited for; matrix products, arithmetic and copies ran while one was open for 0% of the time, Pallas kernels for 13%

profile of v13, /device:TPU:56, one launch (start us, length us, event | category | flops | bytes accessed | tf_op | source)
XLA Modules:
  0.0 61.4 jit_solution(5736679480256709057)
XLA Ops:
  0.0 1.9 %send_x.1 = (f32[3,16,16,128]{3,2,1,0:T(8,128)}, f32[15,16,128]{2,1,0:T(8,128)}, f32[15,16,128]{2,1,0:T(8,128)}) custom-call(f32[4]{0:T(128)} %table.1, s32[16,16,128]{2,1,0:T(8,128)} %phase.1, f32[16,16,128]{2,1,0:T(8,128)} %iterate.1, f32[16,16,128]{2,1,0:T(8,128)} %right.1), custom_call_target="tpu_custom_call" | custom-call | flops 1000000 | bytes 393232 | tf_op jit(solution)/shard_map/send_x/pallas_call | solution.py:498
  1.9 4.3 %collective-permute-start = (f32[15,16,128]{2,1,0:T(8,128)}, f32[15,16,128]{2,1,0:T(8,128)S(1)}, u32[]{:S(2)}, u32[]{:S(2)}) collective-permute-start(f32[15,16,128]{2,1,0:T(8,128)} %get-tuple-element.39), channel_id=1, source_target_pairs={{0,64},{64,128},{128,192},{192,256},{256,320},{320,384},{384,448},... | collective-permute-start | bytes 368648 | tf_op jit(solution)/shard_map/ppermute | solution.py:520
  6.2 1.3 %collective-permute-start.1 = (f32[15,16,128]{2,1,0:T(8,128)}, f32[15,16,128]{2,1,0:T(8,128)S(1)}, u32[]{:S(2)}, u32[]{:S(2)}) collective-permute-start(f32[15,16,128]{2,1,0:T(8,128)} %get-tuple-element.40), channel_id=1, source_target_pairs={{64,0},{128,64},{192,128},{256,192},{320,256},{384,320},{448,384},... | collective-permute-start | bytes 368648 | tf_op jit(solution)/shard_map/ppermute | solution.py:520
  7.5 0.0 copy-start.2
  7.5 1.0 %copy-done.2 = f32[3,16,16,128]{3,2,1,0:T(8,128)S(1)} copy-done((f32[3,16,16,128]{3,2,1,0:T(8,128)S(1)}, f32[3,16,16,128]{3,2,1,0:T(8,128)}, u32[]{:S(2)}) %copy-start.2) | copy-done | bytes 393240
  8.6 0.5 collective-permute-done.from_down
  9.1 4.6 %collective-permute-done.1.from_up = f32[15,16,128]{2,1,0:T(8,128)S(1)} collective-permute-done((f32[15,16,128]{2,1,0:T(8,128)}, f32[15,16,128]{2,1,0:T(8,128)S(1)}, u32[]{:S(2)}, u32[]{:S(2)}) %collective-permute-start.1) | collective-permute-done | bytes 122912 | tf_op jit(solution)/shard_map/ppermute | solution.py:520
  13.7 0.1 pack_y.1
  13.9 1.9 %collective-permute-start.2 = (f32[28,16,128]{2,1,0:T(8,128)S(1)}, f32[28,16,128]{2,1,0:T(8,128)S(1)}, u32[]{:S(2)}, u32[]{:S(2)}) collective-permute-start(f32[28,16,128]{2,1,0:T(8,128)S(1)} %get-tuple-element.46), channel_id=1, source_target_pairs={{16,32},{32,16},{17,33},{33,17},{18,34},{34,18},{19,35},{35,19},{2... | collective-permute-start | bytes 688136 | tf_op jit(solution)/shard_map/ppermute | solution.py:542
  15.8 1.9 %collective-permute-start.3 = (f32[28,16,128]{2,1,0:T(8,128)S(1)}, f32[28,16,128]{2,1,0:T(8,128)S(1)}, u32[]{:S(2)}, u32[]{:S(2)}) collective-permute-start(f32[28,16,128]{2,1,0:T(8,128)S(1)} %get-tuple-element.47), channel_id=1, source_target_pairs={{0,16},{32,48},{16,0},{48,32},{1,17},{33,49},{17,1},{49,33},{2,18}... | collective-permute-start | bytes 688136 | tf_op jit(solution)/shard_map/ppermute | solution.py:542
  17.7 1.3 %own_rows.1 = (f32[16,512]{1,0:T(8,128)S(1)}, f32[16,512]{1,0:T(8,128)S(1)}, f32[3,16,16,128]{3,2,1,0:T(8,128)S(1)}, bf16[256,384]{1,0:T(8,128)(2,1)S(1)}) custom-call(f32[3,28,16,128]{3,2,1,0:T(8,128)S(1)} %get-tuple-element.45.ext), custom_call_target="tpu_custom_call" | custom-call | flops 30000000 | bytes 688128 | tf_op jit(solution)/shard_map/own_rows/pallas_call | solution.py:498
  19.0 2.2 %collective-permute-done.2.from_first = f32[28,16,128]{2,1,0:T(8,128)S(1)} collective-permute-done((f32[28,16,128]{2,1,0:T(8,128)S(1)}, f32[28,16,128]{2,1,0:T(8,128)S(1)}, u32[]{:S(2)}, u32[]{:S(2)}) %collective-permute-start.2) | collective-permute-done | bytes 229408 | tf_op jit(solution)/shard_map/ppermute | solution.py:542
  21.2 0.0 collective-permute-done.3.from_second
  21.2 1.0 %pack_z.1 = (f32[3,28,32,128]{3,2,1,0:T(8,128)S(1)}, f32[32,512]{1,0:T(8,128)S(1)}, f32[32,512]{1,0:T(8,128)S(1)}, f32[16,128]{1,0:T(8,128)S(1)}) custom-call(f32[3,28,16,128]{3,2,1,0:T(8,128)S(1)} %get-tuple-element.45.ext, f32[28,16,128]{2,1,0:T(8,128)S(1)} %collective-permute-done.2.from_first, f32[28,16,128]{2,1,0:T(8,128)S(1)} %collective-permute-done.3.from_second, ...), custom_call_target="tpu_custom_call" | custom-call | flops 1000000 | bytes 1998848 | tf_op jit(solution)/shard_map/pack_z/pallas_call | solution.py:498
  22.2 3.6 %collective-permute-start.4 = (f32[32,512]{1,0:T(8,128)S(1)}, f32[32,512]{1,0:T(8,128)S(1)}, u32[]{:S(2)}, u32[]{:S(2)}) collective-permute-start(f32[32,512]{1,0:T(8,128)S(1)} %get-tuple-element.58.sent_up), channel_id=1, source_target_pairs={{0,1},{1,2},{2,3},{3,4},{4,5},{5,6},{6,7},{7,8},{8,9},{9,10},{10,1... | collective-permute-start | bytes 196616 | tf_op jit(solution)/shard_map/ppermute | solution.py:520
  25.8 3.1 %collective-permute-start.5 = (f32[32,512]{1,0:T(8,128)S(1)}, f32[32,512]{1,0:T(8,128)S(1)}, u32[]{:S(2)}, u32[]{:S(2)}) collective-permute-start(f32[32,512]{1,0:T(8,128)S(1)} %get-tuple-element.59.sent_down), channel_id=1, source_target_pairs={{1,0},{2,1},{3,2},{4,3},{5,4},{6,5},{7,6},{8,7},{9,8},{10,9},{11,1... | collective-permute-start | bytes 196616 | tf_op jit(solution)/shard_map/ppermute | solution.py:520
  29.0 1.0 %bands_xy.1 = (f32[3,24,32,128]{3,2,1,0:T(8,128)S(1)}, bf16[1088,512]{1,0:T(8,128)(2,1)S(1)}, bf16[384,128]{1,0:T(8,128)(2,1)S(1)}) custom-call(f32[3,28,32,128]{3,2,1,0:T(8,128)S(1)} %get-tuple-element.60.full), custom_call_target="tpu_custom_call" | custom-call | flops 30000000 | bytes 1376256 | tf_op jit(solution)/shard_map/bands_xy/pallas_call | solution.py:498
  30.0 0.0 copy-start
  30.0 1.0 %copy-done = bf16[1088,512]{1,0:T(8,128)(2,1)} copy-done((bf16[1088,512]{1,0:T(8,128)(2,1)}, bf16[1088,512]{1,0:T(8,128)(2,1)S(1)}, u32[]{:S(2)}) %copy-start) | copy-done | bytes 1114136
  31.0 0.0 collective-permute-done.4.from_down
  31.0 4.0 %collective-permute-done.5.from_up = f32[32,512]{1,0:T(8,128)S(1)} collective-permute-done((f32[32,512]{1,0:T(8,128)S(1)}, f32[32,512]{1,0:T(8,128)S(1)}, u32[]{:S(2)}, u32[]{:S(2)}) %collective-permute-start.5) | collective-permute-done | bytes 65568 | tf_op jit(solution)/shard_map/ppermute | solution.py:520
  35.0 1.5 %own_cells.1 = f32[32,16,128]{2,1,0:T(8,128)} custom-call(f32[32,512]{1,0:T(8,128)S(1)} %get-tuple-element.58.sent_up, f32[32,512]{1,0:T(8,128)S(1)} %get-tuple-element.59.sent_down, f32[32,512]{1,0:T(8,128)S(1)} %collective-permute-done.4.from_down, f32[32,512]{1,0:T(8,128)S(1)} %collective-permute-done.5.from_up, f32[16,128]{1,0:T(8,128)S(1)} %get-tuple-element.67.inner, ...), custom_call_target="tpu_custom_call" | custom-call | flops 1000000 | bytes 466944 | tf_op jit(solution)/shard_map/own_cells/pallas_call | solution.py:498
  36.5 10.8 %all-to-all-start = ((f32[32,16,128]{2,1,0:T(8,128)}), f32[32,16,128]{2,1,0:T(8,128)S(1)}, u32[]{:S(2)}, u32[]{:S(2)}) async-start(f32[32,16,128]{2,1,0:T(8,128)} %own_cells.1), calls=%async_computation | async-start | bytes 524288 | tf_op jit(solution)/shard_map/all_to_all | solution.py:569
  47.3 2.3 %fine_residual.1 = (f32[28,32,256]{2,1,0:T(8,128)S(1)}, f32[28,32,256]{2,1,0:T(8,128)S(1)}, f32[28,32,256]{2,1,0:T(8,128)S(1)}) custom-call(f32[3,28,32,128]{3,2,1,0:T(8,128)S(1)} %get-tuple-element.60.full, f32[3,24,32,128]{3,2,1,0:T(8,128)S(1)} %get-tuple-element.69.xy, f32[32,512]{1,0:T(8,128)S(1)} %collective-permute-done.4.from_down, ...), custom_call_target="tpu_custom_call" | custom-call | flops 30000000 | bytes 2686976 | tf_op jit(solution)/shard_map/fine_residual/pallas_call | solution.py:498
  49.6 0.0 copy-start.1
  49.6 3.6 %fine_sweeps.1.base = f32[16,16,128]{2,1,0:T(8,128)S(1)} custom-call(f32[3,28,32,128]{3,2,1,0:T(8,128)S(1)} %get-tuple-element.60.full, f32[28,32,256]{2,1,0:T(8,128)S(1)} %get-tuple-element.70.coef, f32[28,32,256]{2,1,0:T(8,128)S(1)} %get-tuple-element.71.res, f32[28,32,256]{2,1,0:T(8,128)S(1)} %get-tuple-element.72.inv), custom_call_target="tpu_custom_call" | custom-call | flops 60000000 | bytes 4128768 | tf_op jit(solution)/shard_map/fine_sweeps/pallas_call | solution.py:498
  53.2 6.0 %all-to-all-done = f32[32,16,128]{2,1,0:T(8,128)S(1)} async-done(((f32[32,16,128]{2,1,0:T(8,128)}), f32[32,16,128]{2,1,0:T(8,128)S(1)}, u32[]{:S(2)}, u32[]{:S(2)}) %all-to-all-start) | async-done | bytes 262176 | tf_op jit(solution)/shard_map/all_to_all | solution.py:569
  59.2 0.0 copy-done.1
  59.2 2.2 %coarse_levels.1 = f32[16,16,128]{2,1,0:T(8,128)} custom-call(bf16[1088,512]{1,0:T(8,128)(2,1)S(1)} %copy-done.1, f32[512,128]{1,0:T(8,128)S(1)} %bitcast.1, f32[16,16,128]{2,1,0:T(8,128)S(1)} %fine_sweeps.1.base), custom_call_target="tpu_custom_call" | custom-call | flops 1000000 | bytes 2621440 | tf_op jit(solution)/shard_map/coarse_levels/pallas_call | solution.py:498
  (1 shorter events, 0.0 us)
Async XLA Ops:
  1.9 7.2 %collective-permute-start = (f32[15,16,128]{2,1,0:T(8,128)}, f32[15,16,128]{2,1,0:T(8,128)S(1)}, u32[]{:S(2)}, u32[]{:S(2)}) collective-permute-start(f32[15,16,128]{2,1,0:T(8,128)} %get-tuple-element.39), channel_id=1, source_target_pairs={{0,64},{64,128},{128,192},{192,256},{256,320},{320,384},{384,448},... | collective-permute-start | bytes 368648 | tf_op jit(solution)/shard_map/ppermute | solution.py:520
  6.2 7.5 %collective-permute-start.1 = (f32[15,16,128]{2,1,0:T(8,128)}, f32[15,16,128]{2,1,0:T(8,128)S(1)}, u32[]{:S(2)}, u32[]{:S(2)}) collective-permute-start(f32[15,16,128]{2,1,0:T(8,128)} %get-tuple-element.40), channel_id=1, source_target_pairs={{64,0},{128,64},{192,128},{256,192},{320,256},{384,320},{448,384},... | collective-permute-start | bytes 368648 | tf_op jit(solution)/shard_map/ppermute | solution.py:520
  7.5 1.0 %copy-start.2 = (f32[3,16,16,128]{3,2,1,0:T(8,128)S(1)}, f32[3,16,16,128]{3,2,1,0:T(8,128)}, u32[]{:S(2)}) copy-start(f32[3,16,16,128]{3,2,1,0:T(8,128)} %get-tuple-element.41.fields) | copy-start | bytes 1179652
  13.9 7.3 %collective-permute-start.2 = (f32[28,16,128]{2,1,0:T(8,128)S(1)}, f32[28,16,128]{2,1,0:T(8,128)S(1)}, u32[]{:S(2)}, u32[]{:S(2)}) collective-permute-start(f32[28,16,128]{2,1,0:T(8,128)S(1)} %get-tuple-element.46), channel_id=1, source_target_pairs={{16,32},{32,16},{17,33},{33,17},{18,34},{34,18},{19,35},{35,19},{2... | collective-permute-start | bytes 688136 | tf_op jit(solution)/shard_map/ppermute | solution.py:542
  15.8 5.4 %collective-permute-start.3 = (f32[28,16,128]{2,1,0:T(8,128)S(1)}, f32[28,16,128]{2,1,0:T(8,128)S(1)}, u32[]{:S(2)}, u32[]{:S(2)}) collective-permute-start(f32[28,16,128]{2,1,0:T(8,128)S(1)} %get-tuple-element.47), channel_id=1, source_target_pairs={{0,16},{32,48},{16,0},{48,32},{1,17},{33,49},{17,1},{49,33},{2,18}... | collective-permute-start | bytes 688136 | tf_op jit(solution)/shard_map/ppermute | solution.py:542
  22.2 8.8 %collective-permute-start.4 = (f32[32,512]{1,0:T(8,128)S(1)}, f32[32,512]{1,0:T(8,128)S(1)}, u32[]{:S(2)}, u32[]{:S(2)}) collective-permute-start(f32[32,512]{1,0:T(8,128)S(1)} %get-tuple-element.58.sent_up), channel_id=1, source_target_pairs={{0,1},{1,2},{2,3},{3,4},{4,5},{5,6},{6,7},{7,8},{8,9},{9,10},{10,1... | collective-permute-start | bytes 196616 | tf_op jit(solution)/shard_map/ppermute | solution.py:520
  25.8 9.2 %collective-permute-start.5 = (f32[32,512]{1,0:T(8,128)S(1)}, f32[32,512]{1,0:T(8,128)S(1)}, u32[]{:S(2)}, u32[]{:S(2)}) collective-permute-start(f32[32,512]{1,0:T(8,128)S(1)} %get-tuple-element.59.sent_down), channel_id=1, source_target_pairs={{1,0},{2,1},{3,2},{4,3},{5,4},{6,5},{7,6},{8,7},{9,8},{10,9},{11,1... | collective-permute-start | bytes 196616 | tf_op jit(solution)/shard_map/ppermute | solution.py:520
  30.0 1.0 %copy-start = (bf16[1088,512]{1,0:T(8,128)(2,1)}, bf16[1088,512]{1,0:T(8,128)(2,1)S(1)}, u32[]{:S(2)}) copy-start(bf16[1088,512]{1,0:T(8,128)(2,1)S(1)} %get-tuple-element.64.tables) | copy-start | bytes 3342340
  36.5 22.7 %all-to-all-start = ((f32[32,16,128]{2,1,0:T(8,128)}), f32[32,16,128]{2,1,0:T(8,128)S(1)}, u32[]{:S(2)}, u32[]{:S(2)}) async-start(f32[32,16,128]{2,1,0:T(8,128)} %own_cells.1), calls=%async_computation | async-start | bytes 524288 | tf_op jit(solution)/shard_map/all_to_all | solution.py:569
  49.6 9.6 %copy-start.1 = (bf16[1088,512]{1,0:T(8,128)(2,1)S(1)}, bf16[1088,512]{1,0:T(8,128)(2,1)}, u32[]{:S(2)}) copy-start(bf16[1088,512]{1,0:T(8,128)(2,1)} %copy-done) | copy-start | bytes 3342340

commit v14 on v13

--- a/solution.py
+++ b/solution.py
@@ -186,13 +186,17 @@
     source = iota((256, 128), 0)
     lane = iota((256, 128), 1)
     coarse = (source & 127) >> 2
-    base = 64 + (source >> 7) * 16
+    is_coef = source >> 7
     scale = jnp.where(source < 128, F32(0.25), F32(1.0 / 64.0))
-    upper = (lane == base + coarse - 16) & (coarse >= 16) & (coarse <= 30)
-    lower = (lane == base + coarse) & (coarse >= 1) & (coarse <= 15)
-    stay = (lane == (source >> 7) * 64 + 16 + coarse) & (coarse >= 1) & (coarse <= 30)
-    for at, found in enumerate((upper, lower, stay)):
-        level3_lanes[:, 128 * at : 128 * at + 128] = jnp.where(found, scale, 0.0).astype(BF16)
+    upper = jnp.where(coarse >= 28, coarse - 28, jnp.where(coarse >= 24, (coarse >> 1) - 9, (coarse >> 2) + 1))
+    lower = jnp.where(coarse <= 3, coarse - 1, jnp.where(coarse <= 7, (coarse >> 1) + 1, (coarse >> 2) + 3))
+    found = (
+        (lane == 64 + 16 * is_coef + upper) & (coarse >= 16) & (coarse <= 30),
+        (lane == 64 + 16 * is_coef + lower) & (coarse >= 1) & (coarse <= 15),
+        (lane == 40 * is_coef + 4 + coarse) & (coarse >= 1) & (coarse <= 30),
+    )
+    for at, here in enumerate(found):
+        level3_lanes[:, 128 * at : 128 * at + 128] = jnp.where(here, scale, 0.0).astype(BF16)
 
 
 def pack_z(ext, from_first, from_second, up_rows, down_rows, xz, level3_lanes, full, to_up, to_down, inner, edges, quads):
@@ -263,10 +267,21 @@
         tables[192 * level : 192 * level + 192, :] = ones_where(found)
     source = iota((128, 256), 0)
     lane = iota((128, 256), 1)
-    is_coef = source >> 6
-    for level, start in enumerate((0, 64, 96)):
+    is_coef = jnp.where(source < 80, jnp.where(source >= 40, 1, 0), jnp.where(source >= 88, 1, 0))
+    cell = jnp.where(source < 80, source - 40 * is_coef - 4, source - 80 - 8 * is_coef)
+    inner = source < 80
+    pairs = (source >= 80) & (source < 96) & (cell < 4)
+    fours = (source >= 80) & (source < 96) & (cell >= 4)
+    pair = jnp.where(cell < 2, cell - 4, cell + 16)
+    four = jnp.where(cell < 6, cell - 8, cell + 4)
+    targets = (
+        jnp.where(inner, cell + 16, -1),
+        jnp.where(inner, 64 + 8 + (cell >> 1), jnp.where(pairs, 64 + 8 + pair, -1)),
+        jnp.where(inner, 96 + 4 + (cell >> 2), jnp.where(pairs, 96 + 4 + (pair >> 1), jnp.where(fours, 96 + 4 + four, -1))),
+    )
+    for level, target in enumerate(targets):
         scale = jnp.where(is_coef == 1, F32(0.125**level), F32(0.5**level))
-        found = lane == is_coef * 128 + start + ((source & 63) >> level)
+        found = (target >= 0) & (lane == is_coef * 128 + target)
         at = 576 + 128 * level
         tables[at : at + 128, 0:256] = jnp.where(found, scale, 0.0).astype(BF16)
     source = iota((128, 128), 0)
@@ -336,16 +351,22 @@
             quads[start : start + 16, :] = rolled(ends[at], -32 * q)
     lane = iota((16, 128), 1)
     mine = inner[...]
-    for at, target in enumerate((15, 47, 79, 111)):
+    for at, target in enumerate((3, 35, 43, 75)):
         cells = pltpu.roll(quads[pl.ds(64 * at, 16, stride=4), :], target, 1)
         mine = jnp.where((lane == target) | (lane == target + 1), cells, mine)
     low = from_down[0:16, 384:512]
     high = from_up[0:16, 384:512]
-    mine = jnp.where(lane < 15, pltpu.roll(low, 64, 1), mine)
-    mine = jnp.where((lane >= 64) & (lane < 79), pltpu.roll(low, 112, 1), mine)
-    mine = jnp.where((lane >= 49) & (lane < 64), pltpu.roll(high, 112, 1), mine)
-    mine = jnp.where(lane >= 113, pltpu.roll(high, 32, 1), mine)
-    chunks[...] = jnp.broadcast_to(mine[None], chunks.shape)
+    for cells, moves in (
+        (low, ((64, 0, 3), (67, 80, 2), (69, 84, 2), (80, 40, 3), (83, 88, 2), (85, 92, 2))),
+        (high, ((64, 37, 3), (67, 82, 2), (69, 86, 2), (80, 77, 3), (83, 90, 2), (85, 94, 2))),
+    ):
+        for at, target, count in moves:
+            mine = jnp.where((lane >= target) & (lane < target + count), rolled(cells, target - at), mine)
+    lane = iota((4, 128), 1)
+    for part in range(3):
+        rest = rolled(mine, 96 - 32 * part)[12:16]
+        tile = jnp.where(lane < 96, mine[4 * part : 4 * part + 4], rest)
+        chunks[:, part] = jnp.broadcast_to(tile[None], (chunks.shape[0], 4, 128))
 
 
 def fine_residual(full, xy, from_down, from_up, coef, res, inv, side, sides_kv, product):
@@ -471,8 +492,15 @@
     lax.fori_loop(6, 22, third, 0, unroll=4)
 
 
-def coarse_levels(tables, plane, base, out, spread):
-    found = jnp.dot(tables[0:576, :], jnp.concatenate(split(plane[...]), axis=1), preferred_element_type=F32)
+def coarse_levels(tables, plane, base, out, columns, spread):
+    lane = iota((plane.shape[0], 4, 128), 2)
+    parts = [plane[:, part] for part in range(3)]
+    for part in range(3):
+        columns[:, 4 * part : 4 * part + 4, :] = parts[part]
+    rest = [pltpu.roll(parts[part], 32 + 32 * part, 2) for part in range(3)]
+    columns[:, 12:16, :] = jnp.where(lane < 32, rest[0], jnp.where(lane < 64, rest[1], rest[2]))
+    columns = columns[...].reshape(plane.shape[0] * 16, 128)
+    found = jnp.dot(tables[0:576, :], jnp.concatenate(split(columns), axis=1), preferred_element_type=F32)
     found = found[:, 0:128] + (found[:, 128:256] + found[:, 256:384])
     windows = jnp.concatenate([found[192 * level : 192 * level + 192, :] for level in range(3)], axis=1)
     both = select_lanes(windows, tables[576:960, 0:256])
@@ -565,7 +593,7 @@
     from_down, from_up, xy, tables, end_lanes = lax.optimization_barrier((from_down, from_up, xy, tables, end_lanes))
     z_sides = [from_down, from_up]
     count = lax.axis_size("gx") * lax.axis_size("gy")
-    (chunks,) = call(own_cells, [(count, 16, 128)], [to_up, to_down, *z_sides, inner, end_lanes], scratch=[(256, 128)])
+    (chunks,) = call(own_cells, [(count, 3, 4, 128)], [to_up, to_down, *z_sides, inner, end_lanes], scratch=[(256, 128)])
     plane = lax.all_to_all(chunks, ("gx", "gy"), 0, 0, tiled=True)
     wide = (28, 32, 256)
     coef, res, inv = call(
@@ -582,7 +610,7 @@
         scratch=[wide, wide, wide, wide, (2, 896, 128), (128, 128)],
         flops=60000000,
     )
-    (out,) = call(coarse_levels, [block], [tables, plane.reshape(count * 16, 128), base], scratch=[(64, 128)])
+    (out,) = call(coarse_levels, [block], [tables, plane, base], scratch=[(count, 16, 128), (64, 128)])
     return out
 
 

time: 62.1 us -> 61 us (0.982)
  waiting for transfers between devices: 17.4 us -> 16 us
    all_to_all x1, waiting for transfers between devices: 6.04 us -> 4.69 us  [on_device(): plane = lax.all_to_all(chunks, ('gx', 'gy'), 0, 0, tiled=True)]
  transfers between devices with their start and end apart: 7 -> 7, of which waited for: 5 -> 5; matrix products, arithmetic and copies ran while one was open for 0% -> 0% of each run, Pallas kernels for 13% -> 14%
where the time goes in v14:
time: 61 us; the launch traced here: 60.3 us
  starting transfers between devices  26.9 us (44%)
  waiting for transfers between devices  16 us (26%)
  Pallas kernels  15.2 us (25%)
  local copies, waits for them, and re-layouts  2 us (3%)
    pallas_call x10, Pallas kernels, call(): pl.pallas_call(kernel, out_shape=[out if isinstance(out, jax.ShapeDtypeSt...  15.2 us
    ppermute x4, starting transfers between devices, swap(): return (lax.ppermute(to_up, axis, up), lax.ppermute(to_down, axis, down))  12.3 us
    all_to_all x1, starting transfers between devices, on_device(): plane = lax.all_to_all(chunks, ('gx', 'gy'), 0, 0, tiled=True)  10.8 us
    ppermute x4, waiting for transfers between devices, swap(): return (lax.ppermute(to_up, axis, up), lax.ppermute(to_down, axis, down))  9.19 us
    all_to_all x1, waiting for transfers between devices, on_device(): plane = lax.all_to_all(chunks, ('gx', 'gy'), 0, 0, tiled=True)  4.69 us
    ppermute x2, starting transfers between devices, on_device(): lax.ppermute(rows, 'gy', pairs)  3.84 us
    ppermute x2, waiting for transfers between devices, on_device(): lax.ppermute(rows, 'gy', pairs)  2.12 us
    unnamed x6, local copies, waits for them, and re-layouts  2 us
  transfers between devices with their start and end apart: 7, of which 5 were waited for; matrix products, arithmetic and copies ran while one was open for 0% of the time, Pallas kernels for 14%

profile of v14, /device:TPU:56, one launch (start us, length us, event | category | flops | bytes accessed | tf_op | source)
XLA Modules:
  0.0 60.3 jit_solution(68921214429480494)
XLA Ops:
  0.0 1.9 %send_x.1 = (f32[3,16,16,128]{3,2,1,0:T(8,128)}, f32[15,16,128]{2,1,0:T(8,128)}, f32[15,16,128]{2,1,0:T(8,128)}) custom-call(f32[4]{0:T(128)} %table.1, s32[16,16,128]{2,1,0:T(8,128)} %phase.1, f32[16,16,128]{2,1,0:T(8,128)} %iterate.1, f32[16,16,128]{2,1,0:T(8,128)} %right.1), custom_call_target="tpu_custom_call" | custom-call | flops 1000000 | bytes 393232 | tf_op jit(solution)/shard_map/send_x/pallas_call | solution.py:526
  1.9 4.3 %collective-permute-start = (f32[15,16,128]{2,1,0:T(8,128)}, f32[15,16,128]{2,1,0:T(8,128)S(1)}, u32[]{:S(2)}, u32[]{:S(2)}) collective-permute-start(f32[15,16,128]{2,1,0:T(8,128)} %get-tuple-element.39), channel_id=1, source_target_pairs={{0,64},{64,128},{128,192},{192,256},{256,320},{320,384},{384,448},... | collective-permute-start | bytes 368648 | tf_op jit(solution)/shard_map/ppermute | solution.py:548
  6.2 1.3 %collective-permute-start.1 = (f32[15,16,128]{2,1,0:T(8,128)}, f32[15,16,128]{2,1,0:T(8,128)S(1)}, u32[]{:S(2)}, u32[]{:S(2)}) collective-permute-start(f32[15,16,128]{2,1,0:T(8,128)} %get-tuple-element.40), channel_id=1, source_target_pairs={{64,0},{128,64},{192,128},{256,192},{320,256},{384,320},{448,384},... | collective-permute-start | bytes 368648 | tf_op jit(solution)/shard_map/ppermute | solution.py:548
  7.5 0.0 copy-start.2
  7.5 1.0 %copy-done.2 = f32[3,16,16,128]{3,2,1,0:T(8,128)S(1)} copy-done((f32[3,16,16,128]{3,2,1,0:T(8,128)S(1)}, f32[3,16,16,128]{3,2,1,0:T(8,128)}, u32[]{:S(2)}) %copy-start.2) | copy-done | bytes 393240
  8.6 0.5 collective-permute-done.from_down
  9.1 4.6 %collective-permute-done.1.from_up = f32[15,16,128]{2,1,0:T(8,128)S(1)} collective-permute-done((f32[15,16,128]{2,1,0:T(8,128)}, f32[15,16,128]{2,1,0:T(8,128)S(1)}, u32[]{:S(2)}, u32[]{:S(2)}) %collective-permute-start.1) | collective-permute-done | bytes 122912 | tf_op jit(solution)/shard_map/ppermute | solution.py:548
  13.7 0.1 pack_y.1
  13.9 1.9 %collective-permute-start.2 = (f32[28,16,128]{2,1,0:T(8,128)S(1)}, f32[28,16,128]{2,1,0:T(8,128)S(1)}, u32[]{:S(2)}, u32[]{:S(2)}) collective-permute-start(f32[28,16,128]{2,1,0:T(8,128)S(1)} %get-tuple-element.46), channel_id=1, source_target_pairs={{16,32},{32,16},{17,33},{33,17},{18,34},{34,18},{19,35},{35,19},{2... | collective-permute-start | bytes 688136 | tf_op jit(solution)/shard_map/ppermute | solution.py:570
  15.8 1.9 %collective-permute-start.3 = (f32[28,16,128]{2,1,0:T(8,128)S(1)}, f32[28,16,128]{2,1,0:T(8,128)S(1)}, u32[]{:S(2)}, u32[]{:S(2)}) collective-permute-start(f32[28,16,128]{2,1,0:T(8,128)S(1)} %get-tuple-element.47), channel_id=1, source_target_pairs={{0,16},{32,48},{16,0},{48,32},{1,17},{33,49},{17,1},{49,33},{2,18}... | collective-permute-start | bytes 688136 | tf_op jit(solution)/shard_map/ppermute | solution.py:570
  17.7 1.4 %own_rows.1 = (f32[16,512]{1,0:T(8,128)S(1)}, f32[16,512]{1,0:T(8,128)S(1)}, f32[3,16,16,128]{3,2,1,0:T(8,128)S(1)}, bf16[256,384]{1,0:T(8,128)(2,1)S(1)}) custom-call(f32[3,28,16,128]{3,2,1,0:T(8,128)S(1)} %get-tuple-element.45.ext), custom_call_target="tpu_custom_call" | custom-call | flops 30000000 | bytes 688128 | tf_op jit(solution)/shard_map/own_rows/pallas_call | solution.py:526
  19.1 2.1 %collective-permute-done.2.from_first = f32[28,16,128]{2,1,0:T(8,128)S(1)} collective-permute-done((f32[28,16,128]{2,1,0:T(8,128)S(1)}, f32[28,16,128]{2,1,0:T(8,128)S(1)}, u32[]{:S(2)}, u32[]{:S(2)}) %collective-permute-start.2) | collective-permute-done | bytes 229408 | tf_op jit(solution)/shard_map/ppermute | solution.py:570
  21.2 0.0 collective-permute-done.3.from_second
  21.2 1.0 %pack_z.1 = (f32[3,28,32,128]{3,2,1,0:T(8,128)S(1)}, f32[32,512]{1,0:T(8,128)S(1)}, f32[32,512]{1,0:T(8,128)S(1)}, f32[16,128]{1,0:T(8,128)S(1)}) custom-call(f32[3,28,16,128]{3,2,1,0:T(8,128)S(1)} %get-tuple-element.45.ext, f32[28,16,128]{2,1,0:T(8,128)S(1)} %collective-permute-done.2.from_first, f32[28,16,128]{2,1,0:T(8,128)S(1)} %collective-permute-done.3.from_second, ...), custom_call_target="tpu_custom_call" | custom-call | flops 1000000 | bytes 1998848 | tf_op jit(solution)/shard_map/pack_z/pallas_call | solution.py:526
  22.2 3.6 %collective-permute-start.4 = (f32[32,512]{1,0:T(8,128)S(1)}, f32[32,512]{1,0:T(8,128)S(1)}, u32[]{:S(2)}, u32[]{:S(2)}) collective-permute-start(f32[32,512]{1,0:T(8,128)S(1)} %get-tuple-element.58.sent_up), channel_id=1, source_target_pairs={{0,1},{1,2},{2,3},{3,4},{4,5},{5,6},{6,7},{7,8},{8,9},{9,10},{10,1... | collective-permute-start | bytes 196616 | tf_op jit(solution)/shard_map/ppermute | solution.py:548
  25.8 3.1 %collective-permute-start.5 = (f32[32,512]{1,0:T(8,128)S(1)}, f32[32,512]{1,0:T(8,128)S(1)}, u32[]{:S(2)}, u32[]{:S(2)}) collective-permute-start(f32[32,512]{1,0:T(8,128)S(1)} %get-tuple-element.59.sent_down), channel_id=1, source_target_pairs={{1,0},{2,1},{3,2},{4,3},{5,4},{6,5},{7,6},{8,7},{9,8},{10,9},{11,1... | collective-permute-start | bytes 196616 | tf_op jit(solution)/shard_map/ppermute | solution.py:548
  29.0 1.0 %bands_xy.1 = (f32[3,24,32,128]{3,2,1,0:T(8,128)S(1)}, bf16[1088,512]{1,0:T(8,128)(2,1)S(1)}, bf16[384,128]{1,0:T(8,128)(2,1)S(1)}) custom-call(f32[3,28,32,128]{3,2,1,0:T(8,128)S(1)} %get-tuple-element.60.full), custom_call_target="tpu_custom_call" | custom-call | flops 30000000 | bytes 1376256 | tf_op jit(solution)/shard_map/bands_xy/pallas_call | solution.py:526
  30.0 0.0 copy-start
  30.0 1.0 %copy-done = bf16[1088,512]{1,0:T(8,128)(2,1)} copy-done((bf16[1088,512]{1,0:T(8,128)(2,1)}, bf16[1088,512]{1,0:T(8,128)(2,1)S(1)}, u32[]{:S(2)}) %copy-start) | copy-done | bytes 1114136
  31.0 0.0 collective-permute-done.4.from_down
  31.0 4.0 %collective-permute-done.5.from_up = f32[32,512]{1,0:T(8,128)S(1)} collective-permute-done((f32[32,512]{1,0:T(8,128)S(1)}, f32[32,512]{1,0:T(8,128)S(1)}, u32[]{:S(2)}, u32[]{:S(2)}) %collective-permute-start.5) | collective-permute-done | bytes 65568 | tf_op jit(solution)/shard_map/ppermute | solution.py:548
  35.0 1.6 %own_cells.1 = f32[32,3,4,128]{3,2,1,0:T(4,128)} custom-call(f32[32,512]{1,0:T(8,128)S(1)} %get-tuple-element.58.sent_up, f32[32,512]{1,0:T(8,128)S(1)} %get-tuple-element.59.sent_down, f32[32,512]{1,0:T(8,128)S(1)} %collective-permute-done.4.from_down, f32[32,512]{1,0:T(8,128)S(1)} %collective-permute-done.5.from_up, ...), custom_call_target="tpu_custom_call" | custom-call | flops 1000000 | bytes 466944 | tf_op jit(solution)/shard_map/own_cells/pallas_call | solution.py:526
  36.6 10.8 %all-to-all-start = ((f32[32,3,4,128]{3,2,1,0:T(4,128)}), f32[32,3,4,128]{3,2,1,0:T(4,128)S(1)}, u32[]{:S(2)}, u32[]{:S(2)}) async-start(f32[32,3,4,128]{3,2,1,0:T(4,128)} %own_cells.1), calls=%async_computation | async-start | bytes 393216 | tf_op jit(solution)/shard_map/all_to_all | solution.py:597
  47.3 2.3 %fine_residual.1 = (f32[28,32,256]{2,1,0:T(8,128)S(1)}, f32[28,32,256]{2,1,0:T(8,128)S(1)}, f32[28,32,256]{2,1,0:T(8,128)S(1)}) custom-call(f32[3,28,32,128]{3,2,1,0:T(8,128)S(1)} %get-tuple-element.60.full, f32[3,24,32,128]{3,2,1,0:T(8,128)S(1)} %get-tuple-element.69.xy, f32[32,512]{1,0:T(8,128)S(1)} %collective-permute-done.4.from_down, ...), custom_call_target="tpu_custom_call" | custom-call | flops 30000000 | bytes 2686976 | tf_op jit(solution)/shard_map/fine_residual/pallas_call | solution.py:526
  49.7 0.0 copy-start.1
  49.7 3.6 %fine_sweeps.1.base = f32[16,16,128]{2,1,0:T(8,128)S(1)} custom-call(f32[3,28,32,128]{3,2,1,0:T(8,128)S(1)} %get-tuple-element.60.full, f32[28,32,256]{2,1,0:T(8,128)S(1)} %get-tuple-element.70.coef, f32[28,32,256]{2,1,0:T(8,128)S(1)} %get-tuple-element.71.res, f32[28,32,256]{2,1,0:T(8,128)S(1)} %get-tuple-element.72.inv), custom_call_target="tpu_custom_call" | custom-call | flops 60000000 | bytes 4128768 | tf_op jit(solution)/shard_map/fine_sweeps/pallas_call | solution.py:526
  53.3 4.7 %all-to-all-done.plane = f32[32,3,4,128]{3,2,1,0:T(4,128)S(1)} async-done(((f32[32,3,4,128]{3,2,1,0:T(4,128)}), f32[32,3,4,128]{3,2,1,0:T(4,128)S(1)}, u32[]{:S(2)}, u32[]{:S(2)}) %all-to-all-start) | async-done | bytes 196640 | tf_op jit(solution)/shard_map/all_to_all | solution.py:597
  58.0 0.0 copy-done.1
  58.0 2.3 %coarse_levels.1 = f32[16,16,128]{2,1,0:T(8,128)} custom-call(bf16[1088,512]{1,0:T(8,128)(2,1)S(1)} %copy-done.1, f32[32,3,4,128]{3,2,1,0:T(4,128)S(1)} %all-to-all-done.plane, f32[16,16,128]{2,1,0:T(8,128)S(1)} %fine_sweeps.1.base), custom_call_target="tpu_custom_call" | custom-call | flops 1000000 | bytes 2555904 | tf_op jit(solution)/shard_map/coarse_levels/pallas_call | solution.py:526
  (1 shorter events, 0.0 us)
Async XLA Ops:
  1.9 7.2 %collective-permute-start = (f32[15,16,128]{2,1,0:T(8,128)}, f32[15,16,128]{2,1,0:T(8,128)S(1)}, u32[]{:S(2)}, u32[]{:S(2)}) collective-permute-start(f32[15,16,128]{2,1,0:T(8,128)} %get-tuple-element.39), channel_id=1, source_target_pairs={{0,64},{64,128},{128,192},{192,256},{256,320},{320,384},{384,448},... | collective-permute-start | bytes 368648 | tf_op jit(solution)/shard_map/ppermute | solution.py:548
  6.2 7.5 %collective-permute-start.1 = (f32[15,16,128]{2,1,0:T(8,128)}, f32[15,16,128]{2,1,0:T(8,128)S(1)}, u32[]{:S(2)}, u32[]{:S(2)}) collective-permute-start(f32[15,16,128]{2,1,0:T(8,128)} %get-tuple-element.40), channel_id=1, source_target_pairs={{64,0},{128,64},{192,128},{256,192},{320,256},{384,320},{448,384},... | collective-permute-start | bytes 368648 | tf_op jit(solution)/shard_map/ppermute | solution.py:548
  7.5 1.0 %copy-start.2 = (f32[3,16,16,128]{3,2,1,0:T(8,128)S(1)}, f32[3,16,16,128]{3,2,1,0:T(8,128)}, u32[]{:S(2)}) copy-start(f32[3,16,16,128]{3,2,1,0:T(8,128)} %get-tuple-element.41.fields) | copy-start | bytes 1179652
  13.9 7.3 %collective-permute-start.2 = (f32[28,16,128]{2,1,0:T(8,128)S(1)}, f32[28,16,128]{2,1,0:T(8,128)S(1)}, u32[]{:S(2)}, u32[]{:S(2)}) collective-permute-start(f32[28,16,128]{2,1,0:T(8,128)S(1)} %get-tuple-element.46), channel_id=1, source_target_pairs={{16,32},{32,16},{17,33},{33,17},{18,34},{34,18},{19,35},{35,19},{2... | collective-permute-start | bytes 688136 | tf_op jit(solution)/shard_map/ppermute | solution.py:570
  15.8 5.4 %collective-permute-start.3 = (f32[28,16,128]{2,1,0:T(8,128)S(1)}, f32[28,16,128]{2,1,0:T(8,128)S(1)}, u32[]{:S(2)}, u32[]{:S(2)}) collective-permute-start(f32[28,16,128]{2,1,0:T(8,128)S(1)} %get-tuple-element.47), channel_id=1, source_target_pairs={{0,16},{32,48},{16,0},{48,32},{1,17},{33,49},{17,1},{49,33},{2,18}... | collective-permute-start | bytes 688136 | tf_op jit(solution)/shard_map/ppermute | solution.py:570
  22.2 8.8 %collective-permute-start.4 = (f32[32,512]{1,0:T(8,128)S(1)}, f32[32,512]{1,0:T(8,128)S(1)}, u32[]{:S(2)}, u32[]{:S(2)}) collective-permute-start(f32[32,512]{1,0:T(8,128)S(1)} %get-tuple-element.58.sent_up), channel_id=1, source_target_pairs={{0,1},{1,2},{2,3},{3,4},{4,5},{5,6},{6,7},{7,8},{8,9},{9,10},{10,1... | collective-permute-start | bytes 196616 | tf_op jit(solution)/shard_map/ppermute | solution.py:548
  25.8 9.2 %collective-permute-start.5 = (f32[32,512]{1,0:T(8,128)S(1)}, f32[32,512]{1,0:T(8,128)S(1)}, u32[]{:S(2)}, u32[]{:S(2)}) collective-permute-start(f32[32,512]{1,0:T(8,128)S(1)} %get-tuple-element.59.sent_down), channel_id=1, source_target_pairs={{1,0},{2,1},{3,2},{4,3},{5,4},{6,5},{7,6},{8,7},{9,8},{10,9},{11,1... | collective-permute-start | bytes 196616 | tf_op jit(solution)/shard_map/ppermute | solution.py:548
  30.0 1.0 %copy-start = (bf16[1088,512]{1,0:T(8,128)(2,1)}, bf16[1088,512]{1,0:T(8,128)(2,1)S(1)}, u32[]{:S(2)}) copy-start(bf16[1088,512]{1,0:T(8,128)(2,1)S(1)} %get-tuple-element.64.tables) | copy-start | bytes 3342340
  36.6 21.4 %all-to-all-start = ((f32[32,3,4,128]{3,2,1,0:T(4,128)}), f32[32,3,4,128]{3,2,1,0:T(4,128)S(1)}, u32[]{:S(2)}, u32[]{:S(2)}) async-start(f32[32,3,4,128]{3,2,1,0:T(4,128)} %own_cells.1), calls=%async_computation | async-start | bytes 393216 | tf_op jit(solution)/shard_map/all_to_all | solution.py:597
  49.7 8.3 %copy-start.1 = (bf16[1088,512]{1,0:T(8,128)(2,1)S(1)}, bf16[1088,512]{1,0:T(8,128)(2,1)}, u32[]{:S(2)}) copy-start(bf16[1088,512]{1,0:T(8,128)(2,1)} %copy-done) | copy-start | bytes 3342340

commit v15 on v14

--- a/solution.py
+++ b/solution.py
@@ -159,6 +159,8 @@
             first = 16 * (x - 8 * group)
             for field in range(3):
                 h, a, b = HALO[field], ROWS[field], ROWS[field + 1]
+                if not 6 - h <= x < 22 + h:
+                    continue
                 cells = cells_of(field, x)
                 mine = (lane >= first + a) & (lane < first + b)
                 up = jnp.where(mine, pltpu.roll(cells, (first + a + h) % 128, 1), up)
@@ -199,18 +201,17 @@
         level3_lanes[:, 128 * at : 128 * at + 128] = jnp.where(here, scale, 0.0).astype(BF16)
 
 
-def pack_z(ext, from_first, from_second, up_rows, down_rows, xz, level3_lanes, full, to_up, to_down, inner, edges, quads):
+def pack_z(ext, from_first, from_second, up_rows, down_rows, xz, level3_lanes, beyond, to_up, to_down, inner, edges, quads):
     edges[:, 24:32, :] = jnp.zeros((6, 8, 128), F32)
     for field in range(3):
         h = HALO[field]
-        full[field, :, 0:16, :] = ext[field]
-        full[field, :, 16 + h : 32 - h, :] = jnp.zeros((28, 16 - 2 * h, 128), F32)
+        beyond[field, :, h : 16 - h, :] = jnp.zeros((28, 16 - 2 * h, 128), F32)
 
     def rows(from_down, from_up):
         for field in range(3):
             h, a, b = HALO[field], ROWS[field], ROWS[field + 1]
-            full[field, :, 16 : 16 + h, :] = from_up[:, a:b, :]
-            full[field, :, 32 - h : 32, :] = from_down[:, a:b, :]
+            beyond[field, :, 0:h, :] = from_up[:, a:b, :]
+            beyond[field, :, 16 - h : 16, :] = from_down[:, a:b, :]
         for at, (source, row_k, row_v) in enumerate(((from_down, 5, 10), (from_up, 0, 6))):
             k = source[:, row_k, :]
             v = source[:, row_v, :]
@@ -245,7 +246,7 @@
     inner[...] = level3[:, 256:384]
     to_up[0:16, :] = up_rows[...]
     to_down[0:16, :] = down_rows[...]
-    pack_lanes(lambda field, x: full[field, x, 16:32, :], 16, to_up, to_down, 16)
+    pack_lanes(lambda field, x: beyond[field, x], 16, to_up, to_down, 16)
     to_up[0:16, 384:512] += level3[:, 0:128]
     to_down[0:16, 384:512] += level3[:, 128:256]
 
@@ -255,7 +256,11 @@
     return pltpu.roll(x, shift, 1) if shift else x
 
 
-def bands_xy(full, xy, tables, end_lanes, bands):
+def all_rows(ext, beyond, field, x):
+    return jnp.concatenate([ext[field, x], beyond[field, x]], axis=0)
+
+
+def bands_xy(ext, beyond, xy, tables, end_lanes, bands):
     row = iota((192, 512), 0)
     cell = iota((192, 512), 1)
     cell_x = (cell >> 6) * 4 + ((cell >> 2) & 3)
@@ -297,8 +302,7 @@
     end_lanes[...] = ones_where(place)
 
     def in_y(x, carry):
-        k = full[0, x]
-        v = full[1, x]
+        k, v = [all_rows(ext, beyond, field, x) for field in range(2)]
         bands[0, x] = band(k, 0)
         bands[1, x] = band(v, 0)
         bands[2, x] = band(k * v, 0)
@@ -315,7 +319,7 @@
 
 
 def end_cells(lower_k, lower_v, lower_right, upper_k, upper_v, upper_right):
-    position = iota((32, 512), 1) & 15
+    position = iota((32, 384), 1) & 15
     k = jnp.where(position < 6, lower_k, jnp.where(position < 12, upper_k, 0.0))
     v = jnp.where(position < 6, lower_v, upper_v)
     right = jnp.where(position < 6, lower_right, upper_right)[0:16, :]
@@ -323,7 +327,7 @@
     for f in (k, v, k * v):
         f = band(f, 0)[0:16, :]
         f = f + pltpu.roll(f, 16, 1)
-        tu.append(band(f + pltpu.roll(f, 512 - 16, 1), 1))
+        tu.append(band(f + pltpu.roll(f, 384 - 16, 1), 1))
     k, v = k[0:16, :], v[0:16, :]
     diagonal = 6.0 * k + 0.125 * tu[0]
     return right - (v * diagonal + 2.0 * (k * v) - 0.125 * (k * tu[1] + tu[2])), k
@@ -331,16 +335,15 @@
 
 def own_cells(sent_up, sent_down, from_down, from_up, inner, end_lanes, chunks, quads):
     def moved(f, shift):
-        return pltpu.roll(f, shift % 512, 1)
-
-    low, first, last, high = from_down[...], sent_down[...], sent_up[...], from_up[...]
+        return pltpu.roll(f, shift % 384, 1)
+
+    low, first, last, high = [ref[:, 0:384] for ref in (from_down, sent_down, sent_up, from_up)]
     found = [
         end_cells(low, moved(low, -5), moved(low, -9), moved(first, 6), first, moved(first, -5)),
         end_cells(last, moved(last, -5), moved(last, -9), moved(high, 6), high, moved(high, -5)),
     ]
     rows = []
     for f in (found[0][0], found[1][0], found[0][1], found[1][1]):
-        f = f[:, 0:384]
         f = f + pltpu.roll(f, 15, 0)
         rows.append(f + pltpu.roll(f, 14, 0))
     ends = select_lanes(jnp.concatenate(rows, axis=0), end_lanes[...])
@@ -369,7 +372,7 @@
         chunks[:, part] = jnp.broadcast_to(tile[None], (chunks.shape[0], 4, 128))
 
 
-def fine_residual(full, xy, from_down, from_up, coef, res, inv, side, sides_kv, product):
+def fine_residual(ext, beyond, xy, from_down, from_up, coef, res, inv, side, sides_kv, product):
     lane = iota((32, 128), 1)
 
     for x in range(28):
@@ -381,7 +384,7 @@
             h, a = HALO[field], ROWS[field]
             tile = jnp.where(lane >= 128 - h, rolled(down, 128 - h - first - a), 0.0)
             tiles.append(jnp.where(lane < h, rolled(up, -first - a), tile))
-        coef[x, :, 0:128] = full[0, x]
+        coef[x, :, 0:128] = all_rows(ext, beyond, 0, x)
         coef[x, :, 128:256] = tiles[0]
         side[0, x] = tiles[1]
         side[1, x] = tiles[2]
@@ -411,17 +414,17 @@
         for j, x in enumerate(xs):
             tu_k, tu_v, tu_kv = found[3 * j : 3 * j + 3]
             k = coef[x]
-            v = jnp.concatenate([full[1, x], side[0, x]], axis=1)
+            v = jnp.concatenate([all_rows(ext, beyond, 1, x), side[0, x]], axis=1)
             diagonal = 6.0 * k + 0.125 * tu_k
             applied = v * diagonal + 2.0 * (k * v) - 0.125 * (k * tu_v + tu_kv)
-            res[x] = jnp.concatenate([full[2, x], side[1, x]], axis=1) - applied
+            res[x] = jnp.concatenate([all_rows(ext, beyond, 2, x), side[1, x]], axis=1) - applied
             inv[x] = damped_inverse(k, diagonal)
         return carry
 
     lax.fori_loop(0, 3, cells, 0)
 
 
-def fine_sweeps(full, coef, res, inv, base, corr, corr_next, yz_c, yz_kc, pairs, spread):
+def fine_sweeps(ext, coef, res, inv, base, corr, corr_next, yz_c, yz_kc, pairs, spread):
     def over_x(ref, x):
         return (ref[x - 1] + ref[x + 1]) + 2.0 * ref[x]
 
@@ -486,7 +489,7 @@
             (yz_kc[x - 1, 0:16, 0:128] + yz_kc[x + 1, 0:16, 0:128]) + 2.0 * yz_kc[x, 0:16, 0:128],
         )
         block = x - 6
-        base[block] = full[1, x, 0:16, :] + (c + spread[pl.ds(pl.multiple_of(16 * (block // 2), 16), 16), :])
+        base[block] = ext[1, x] + (c + spread[pl.ds(pl.multiple_of(16 * (block // 2), 16), 16), :])
         return carry
 
     lax.fori_loop(6, 22, third, 0, unroll=4)
@@ -576,9 +579,9 @@
         flops=30000000,
     )
     *found, up_rows, down_rows, xz, level3_lanes = lax.optimization_barrier((*found, *mine))
-    full, to_up, to_down, inner = call(
+    beyond, to_up, to_down, inner = call(
         pack_z,
-        [planes, (32, 512), (32, 512), (16, 128)],
+        [(3, 28, 16, 128), (32, 512), (32, 512), (16, 128)],
         [ext, *found, up_rows, down_rows, xz, level3_lanes],
         scratch=[(6, 32, 128), (128, 128)],
     )
@@ -586,7 +589,7 @@
     xy, tables, end_lanes = call(
         bands_xy,
         [(3, 24, 32, 128), jax.ShapeDtypeStruct((1088, 512), BF16), jax.ShapeDtypeStruct((384, 128), BF16)],
-        [full],
+        [ext, beyond],
         scratch=[planes],
         flops=30000000,
     )
@@ -599,14 +602,14 @@
     coef, res, inv = call(
         fine_residual,
         [wide] * 3,
-        [full, xy, *z_sides],
+        [ext, beyond, xy, *z_sides],
         scratch=[(2, 28, 32, 128), wide, (28, 32, 128)],
         flops=30000000,
     )
     (base,) = call(
         fine_sweeps,
         [block],
-        [full, coef, res, inv],
+        [ext, coef, res, inv],
         scratch=[wide, wide, wide, wide, (2, 896, 128), (128, 128)],
         flops=60000000,
     )

time: 61 us -> 60.8 us (level)
  no operation moved by 1% of the time
where the time goes in v15:
time: 60.8 us; the launch traced here: 60.1 us
  starting transfers between devices  26.9 us (44%)
  waiting for transfers between devices  16 us (26%)
  Pallas kernels  15 us (25%)
  local copies, waits for them, and re-layouts  2 us (3%)
    pallas_call x10, Pallas kernels, call(): pl.pallas_call(kernel, out_shape=[out if isinstance(out, jax.ShapeDtypeSt...  15 us
    ppermute x4, starting transfers between devices, swap(): return (lax.ppermute(to_up, axis, up), lax.ppermute(to_down, axis, down))  12.3 us
    all_to_all x1, starting transfers between devices, on_device(): plane = lax.all_to_all(chunks, ('gx', 'gy'), 0, 0, tiled=True)  10.8 us
    ppermute x4, waiting for transfers between devices, swap(): return (lax.ppermute(to_up, axis, up), lax.ppermute(to_down, axis, down))  9.19 us
    all_to_all x1, waiting for transfers between devices, on_device(): plane = lax.all_to_all(chunks, ('gx', 'gy'), 0, 0, tiled=True)  4.69 us
    ppermute x2, starting transfers between devices, on_device(): lax.ppermute(rows, 'gy', pairs)  3.84 us
    ppermute x2, waiting for transfers between devices, on_device(): lax.ppermute(rows, 'gy', pairs)  2.15 us
    unnamed x6, local copies, waits for them, and re-layouts  2 us
  transfers between devices with their start and end apart: 7, of which 5 were waited for; matrix products, arithmetic and copies ran while one was open for 0% of the time, Pallas kernels for 14%

profile of v15, /device:TPU:56, one launch (start us, length us, event | category | flops | bytes accessed | tf_op | source)
XLA Modules:
  0.0 60.1 jit_solution(8839631085055571057)
XLA Ops:
  0.0 1.9 %send_x.1 = (f32[3,16,16,128]{3,2,1,0:T(8,128)}, f32[15,16,128]{2,1,0:T(8,128)}, f32[15,16,128]{2,1,0:T(8,128)}) custom-call(f32[4]{0:T(128)} %table.1, s32[16,16,128]{2,1,0:T(8,128)} %phase.1, f32[16,16,128]{2,1,0:T(8,128)} %iterate.1, f32[16,16,128]{2,1,0:T(8,128)} %right.1), custom_call_target="tpu_custom_call" | custom-call | flops 1000000 | bytes 393232 | tf_op jit(solution)/shard_map/send_x/pallas_call | solution.py:529
  1.9 4.3 %collective-permute-start = (f32[15,16,128]{2,1,0:T(8,128)}, f32[15,16,128]{2,1,0:T(8,128)S(1)}, u32[]{:S(2)}, u32[]{:S(2)}) collective-permute-start(f32[15,16,128]{2,1,0:T(8,128)} %get-tuple-element.39), channel_id=1, source_target_pairs={{0,64},{64,128},{128,192},{192,256},{256,320},{320,384},{384,448},... | collective-permute-start | bytes 368648 | tf_op jit(solution)/shard_map/ppermute | solution.py:551
  6.2 1.3 %collective-permute-start.1 = (f32[15,16,128]{2,1,0:T(8,128)}, f32[15,16,128]{2,1,0:T(8,128)S(1)}, u32[]{:S(2)}, u32[]{:S(2)}) collective-permute-start(f32[15,16,128]{2,1,0:T(8,128)} %get-tuple-element.40), channel_id=1, source_target_pairs={{64,0},{128,64},{192,128},{256,192},{320,256},{384,320},{448,384},... | collective-permute-start | bytes 368648 | tf_op jit(solution)/shard_map/ppermute | solution.py:551
  7.5 0.0 copy-start.2
  7.5 1.0 %copy-done.2 = f32[3,16,16,128]{3,2,1,0:T(8,128)S(1)} copy-done((f32[3,16,16,128]{3,2,1,0:T(8,128)S(1)}, f32[3,16,16,128]{3,2,1,0:T(8,128)}, u32[]{:S(2)}) %copy-start.2) | copy-done | bytes 393240
  8.6 0.5 collective-permute-done.from_down
  9.1 4.6 %collective-permute-done.1.from_up = f32[15,16,128]{2,1,0:T(8,128)S(1)} collective-permute-done((f32[15,16,128]{2,1,0:T(8,128)}, f32[15,16,128]{2,1,0:T(8,128)S(1)}, u32[]{:S(2)}, u32[]{:S(2)}) %collective-permute-start.1) | collective-permute-done | bytes 122912 | tf_op jit(solution)/shard_map/ppermute | solution.py:551
  13.7 0.1 pack_y.1
  13.9 1.9 %collective-permute-start.2 = (f32[28,16,128]{2,1,0:T(8,128)S(1)}, f32[28,16,128]{2,1,0:T(8,128)S(1)}, u32[]{:S(2)}, u32[]{:S(2)}) collective-permute-start(f32[28,16,128]{2,1,0:T(8,128)S(1)} %get-tuple-element.46), channel_id=1, source_target_pairs={{16,32},{32,16},{17,33},{33,17},{18,34},{34,18},{19,35},{35,19},{2... | collective-permute-start | bytes 688136 | tf_op jit(solution)/shard_map/ppermute | solution.py:573
  15.8 1.9 %collective-permute-start.3 = (f32[28,16,128]{2,1,0:T(8,128)S(1)}, f32[28,16,128]{2,1,0:T(8,128)S(1)}, u32[]{:S(2)}, u32[]{:S(2)}) collective-permute-start(f32[28,16,128]{2,1,0:T(8,128)S(1)} %get-tuple-element.47), channel_id=1, source_target_pairs={{0,16},{32,48},{16,0},{48,32},{1,17},{33,49},{17,1},{49,33},{2,18}... | collective-permute-start | bytes 688136 | tf_op jit(solution)/shard_map/ppermute | solution.py:573
  17.7 1.3 %own_rows.1 = (f32[16,512]{1,0:T(8,128)S(1)}, f32[16,512]{1,0:T(8,128)S(1)}, f32[3,16,16,128]{3,2,1,0:T(8,128)S(1)}, bf16[256,384]{1,0:T(8,128)(2,1)S(1)}) custom-call(f32[3,28,16,128]{3,2,1,0:T(8,128)S(1)} %get-tuple-element.45.ext), custom_call_target="tpu_custom_call" | custom-call | flops 30000000 | bytes 688128 | tf_op jit(solution)/shard_map/own_rows/pallas_call | solution.py:529
  19.1 2.1 %collective-permute-done.2.from_first = f32[28,16,128]{2,1,0:T(8,128)S(1)} collective-permute-done((f32[28,16,128]{2,1,0:T(8,128)S(1)}, f32[28,16,128]{2,1,0:T(8,128)S(1)}, u32[]{:S(2)}, u32[]{:S(2)}) %collective-permute-start.2) | collective-permute-done | bytes 229408 | tf_op jit(solution)/shard_map/ppermute | solution.py:573
  21.2 0.0 collective-permute-done.3.from_second
  21.2 0.8 %pack_z.1 = (f32[3,28,16,128]{3,2,1,0:T(8,128)S(1)}, f32[32,512]{1,0:T(8,128)S(1)}, f32[32,512]{1,0:T(8,128)S(1)}, f32[16,128]{1,0:T(8,128)S(1)}) custom-call(f32[3,28,16,128]{3,2,1,0:T(8,128)S(1)} %get-tuple-element.45.ext, f32[28,16,128]{2,1,0:T(8,128)S(1)} %collective-permute-done.2.from_first, f32[28,16,128]{2,1,0:T(8,128)S(1)} %collective-permute-done.3.from_second, ...), custom_call_target="tpu_custom_call" | custom-call | flops 1000000 | bytes 1998848 | tf_op jit(solution)/shard_map/pack_z/pallas_call | solution.py:529
  22.1 3.6 %collective-permute-start.4 = (f32[32,512]{1,0:T(8,128)S(1)}, f32[32,512]{1,0:T(8,128)S(1)}, u32[]{:S(2)}, u32[]{:S(2)}) collective-permute-start(f32[32,512]{1,0:T(8,128)S(1)} %get-tuple-element.58.sent_up), channel_id=1, source_target_pairs={{0,1},{1,2},{2,3},{3,4},{4,5},{5,6},{6,7},{7,8},{8,9},{9,10},{10,1... | collective-permute-start | bytes 196616 | tf_op jit(solution)/shard_map/ppermute | solution.py:551
  25.7 3.1 %collective-permute-start.5 = (f32[32,512]{1,0:T(8,128)S(1)}, f32[32,512]{1,0:T(8,128)S(1)}, u32[]{:S(2)}, u32[]{:S(2)}) collective-permute-start(f32[32,512]{1,0:T(8,128)S(1)} %get-tuple-element.59.sent_down), channel_id=1, source_target_pairs={{1,0},{2,1},{3,2},{4,3},{5,4},{6,5},{7,6},{8,7},{9,8},{10,9},{11,1... | collective-permute-start | bytes 196616 | tf_op jit(solution)/shard_map/ppermute | solution.py:551
  28.8 1.0 %bands_xy.1 = (f32[3,24,32,128]{3,2,1,0:T(8,128)S(1)}, bf16[1088,512]{1,0:T(8,128)(2,1)S(1)}, bf16[384,128]{1,0:T(8,128)(2,1)S(1)}) custom-call(f32[3,28,16,128]{3,2,1,0:T(8,128)S(1)} %get-tuple-element.45.ext, f32[3,28,16,128]{3,2,1,0:T(8,128)S(1)} %get-tuple-element.60.beyond), custom_call_target="tpu_custom_call" | custom-call | flops 30000000 | bytes 1376256 | tf_op jit(solution)/shard_map/bands_xy/pallas_call | solution.py:529
  29.8 0.0 copy-start
  29.9 1.0 %copy-done = bf16[1088,512]{1,0:T(8,128)(2,1)} copy-done((bf16[1088,512]{1,0:T(8,128)(2,1)}, bf16[1088,512]{1,0:T(8,128)(2,1)S(1)}, u32[]{:S(2)}) %copy-start) | copy-done | bytes 1114136
  30.9 0.0 collective-permute-done.4.from_down
  30.9 4.0 %collective-permute-done.5.from_up = f32[32,512]{1,0:T(8,128)S(1)} collective-permute-done((f32[32,512]{1,0:T(8,128)S(1)}, f32[32,512]{1,0:T(8,128)S(1)}, u32[]{:S(2)}, u32[]{:S(2)}) %collective-permute-start.5) | collective-permute-done | bytes 65568 | tf_op jit(solution)/shard_map/ppermute | solution.py:551
  34.9 1.6 %own_cells.1 = f32[32,3,4,128]{3,2,1,0:T(4,128)} custom-call(f32[32,512]{1,0:T(8,128)S(1)} %get-tuple-element.58.sent_up, f32[32,512]{1,0:T(8,128)S(1)} %get-tuple-element.59.sent_down, f32[32,512]{1,0:T(8,128)S(1)} %collective-permute-done.4.from_down, f32[32,512]{1,0:T(8,128)S(1)} %collective-permute-done.5.from_up, ...), custom_call_target="tpu_custom_call" | custom-call | flops 1000000 | bytes 466944 | tf_op jit(solution)/shard_map/own_cells/pallas_call | solution.py:529
  36.4 10.8 %all-to-all-start = ((f32[32,3,4,128]{3,2,1,0:T(4,128)}), f32[32,3,4,128]{3,2,1,0:T(4,128)S(1)}, u32[]{:S(2)}, u32[]{:S(2)}) async-start(f32[32,3,4,128]{3,2,1,0:T(4,128)} %own_cells.1), calls=%async_computation | async-start | bytes 393216 | tf_op jit(solution)/shard_map/all_to_all | solution.py:600
  47.2 2.3 %fine_residual.1 = (f32[28,32,256]{2,1,0:T(8,128)S(1)}, f32[28,32,256]{2,1,0:T(8,128)S(1)}, f32[28,32,256]{2,1,0:T(8,128)S(1)}) custom-call(f32[3,28,16,128]{3,2,1,0:T(8,128)S(1)} %get-tuple-element.45.ext, f32[3,28,16,128]{3,2,1,0:T(8,128)S(1)} %get-tuple-element.60.beyond, f32[3,24,32,128]{3,2,1,0:T(8,128)S(1)} %get-tuple-element.69.xy, ...), custom_call_target="tpu_custom_call" | custom-call | flops 30000000 | bytes 2686976 | tf_op jit(solution)/shard_map/fine_residual/pallas_call | solution.py:529
  49.5 0.0 copy-start.1
  49.5 3.6 %fine_sweeps.1.base = f32[16,16,128]{2,1,0:T(8,128)S(1)} custom-call(f32[3,28,16,128]{3,2,1,0:T(8,128)S(1)} %get-tuple-element.45.ext, f32[28,32,256]{2,1,0:T(8,128)S(1)} %get-tuple-element.70.coef, f32[28,32,256]{2,1,0:T(8,128)S(1)} %get-tuple-element.71.res, f32[28,32,256]{2,1,0:T(8,128)S(1)} %get-tuple-element.72.inv), custom_call_target="tpu_custom_call" | custom-call | flops 60000000 | bytes 3440640 | tf_op jit(solution)/shard_map/fine_sweeps/pallas_call | solution.py:529
  53.1 4.7 %all-to-all-done.plane = f32[32,3,4,128]{3,2,1,0:T(4,128)S(1)} async-done(((f32[32,3,4,128]{3,2,1,0:T(4,128)}), f32[32,3,4,128]{3,2,1,0:T(4,128)S(1)}, u32[]{:S(2)}, u32[]{:S(2)}) %all-to-all-start) | async-done | bytes 196640 | tf_op jit(solution)/shard_map/all_to_all | solution.py:600
  57.8 0.0 copy-done.1
  57.8 2.3 %coarse_levels.1 = f32[16,16,128]{2,1,0:T(8,128)} custom-call(bf16[1088,512]{1,0:T(8,128)(2,1)S(1)} %copy-done.1, f32[32,3,4,128]{3,2,1,0:T(4,128)S(1)} %all-to-all-done.plane, f32[16,16,128]{2,1,0:T(8,128)S(1)} %fine_sweeps.1.base), custom_call_target="tpu_custom_call" | custom-call | flops 1000000 | bytes 2555904 | tf_op jit(solution)/shard_map/coarse_levels/pallas_call | solution.py:529
  (1 shorter events, 0.0 us)
Async XLA Ops:
  1.9 7.2 %collective-permute-start = (f32[15,16,128]{2,1,0:T(8,128)}, f32[15,16,128]{2,1,0:T(8,128)S(1)}, u32[]{:S(2)}, u32[]{:S(2)}) collective-permute-start(f32[15,16,128]{2,1,0:T(8,128)} %get-tuple-element.39), channel_id=1, source_target_pairs={{0,64},{64,128},{128,192},{192,256},{256,320},{320,384},{384,448},... | collective-permute-start | bytes 368648 | tf_op jit(solution)/shard_map/ppermute | solution.py:551
  6.2 7.5 %collective-permute-start.1 = (f32[15,16,128]{2,1,0:T(8,128)}, f32[15,16,128]{2,1,0:T(8,128)S(1)}, u32[]{:S(2)}, u32[]{:S(2)}) collective-permute-start(f32[15,16,128]{2,1,0:T(8,128)} %get-tuple-element.40), channel_id=1, source_target_pairs={{64,0},{128,64},{192,128},{256,192},{320,256},{384,320},{448,384},... | collective-permute-start | bytes 368648 | tf_op jit(solution)/shard_map/ppermute | solution.py:551
  7.5 1.0 %copy-start.2 = (f32[3,16,16,128]{3,2,1,0:T(8,128)S(1)}, f32[3,16,16,128]{3,2,1,0:T(8,128)}, u32[]{:S(2)}) copy-start(f32[3,16,16,128]{3,2,1,0:T(8,128)} %get-tuple-element.41.fields) | copy-start | bytes 1179652
  13.9 7.3 %collective-permute-start.2 = (f32[28,16,128]{2,1,0:T(8,128)S(1)}, f32[28,16,128]{2,1,0:T(8,128)S(1)}, u32[]{:S(2)}, u32[]{:S(2)}) collective-permute-start(f32[28,16,128]{2,1,0:T(8,128)S(1)} %get-tuple-element.46), channel_id=1, source_target_pairs={{16,32},{32,16},{17,33},{33,17},{18,34},{34,18},{19,35},{35,19},{2... | collective-permute-start | bytes 688136 | tf_op jit(solution)/shard_map/ppermute | solution.py:573
  15.8 5.4 %collective-permute-start.3 = (f32[28,16,128]{2,1,0:T(8,128)S(1)}, f32[28,16,128]{2,1,0:T(8,128)S(1)}, u32[]{:S(2)}, u32[]{:S(2)}) collective-permute-start(f32[28,16,128]{2,1,0:T(8,128)S(1)} %get-tuple-element.47), channel_id=1, source_target_pairs={{0,16},{32,48},{16,0},{48,32},{1,17},{33,49},{17,1},{49,33},{2,18}... | collective-permute-start | bytes 688136 | tf_op jit(solution)/shard_map/ppermute | solution.py:573
  22.1 8.8 %collective-permute-start.4 = (f32[32,512]{1,0:T(8,128)S(1)}, f32[32,512]{1,0:T(8,128)S(1)}, u32[]{:S(2)}, u32[]{:S(2)}) collective-permute-start(f32[32,512]{1,0:T(8,128)S(1)} %get-tuple-element.58.sent_up), channel_id=1, source_target_pairs={{0,1},{1,2},{2,3},{3,4},{4,5},{5,6},{6,7},{7,8},{8,9},{9,10},{10,1... | collective-permute-start | bytes 196616 | tf_op jit(solution)/shard_map/ppermute | solution.py:551
  25.7 9.2 %collective-permute-start.5 = (f32[32,512]{1,0:T(8,128)S(1)}, f32[32,512]{1,0:T(8,128)S(1)}, u32[]{:S(2)}, u32[]{:S(2)}) collective-permute-start(f32[32,512]{1,0:T(8,128)S(1)} %get-tuple-element.59.sent_down), channel_id=1, source_target_pairs={{1,0},{2,1},{3,2},{4,3},{5,4},{6,5},{7,6},{8,7},{9,8},{10,9},{11,1... | collective-permute-start | bytes 196616 | tf_op jit(solution)/shard_map/ppermute | solution.py:551
  29.8 1.0 %copy-start = (bf16[1088,512]{1,0:T(8,128)(2,1)}, bf16[1088,512]{1,0:T(8,128)(2,1)S(1)}, u32[]{:S(2)}) copy-start(bf16[1088,512]{1,0:T(8,128)(2,1)S(1)} %get-tuple-element.64.tables) | copy-start | bytes 3342340
  36.4 21.4 %all-to-all-start = ((f32[32,3,4,128]{3,2,1,0:T(4,128)}), f32[32,3,4,128]{3,2,1,0:T(4,128)S(1)}, u32[]{:S(2)}, u32[]{:S(2)}) async-start(f32[32,3,4,128]{3,2,1,0:T(4,128)} %own_cells.1), calls=%async_computation | async-start | bytes 393216 | tf_op jit(solution)/shard_map/all_to_all | solution.py:600
  49.5 8.3 %copy-start.1 = (bf16[1088,512]{1,0:T(8,128)(2,1)S(1)}, bf16[1088,512]{1,0:T(8,128)(2,1)}, u32[]{:S(2)}) copy-start(bf16[1088,512]{1,0:T(8,128)(2,1)} %copy-done) | copy-start | bytes 3342340

commit v16 on v15

--- a/solution.py
+++ b/solution.py
@@ -53,12 +53,6 @@
     return (pltpu.roll(x, 1, axis) + pltpu.roll(x, x.shape[axis] - 1, axis)) + 2.0 * x
 
 
-def band_x(x):
-    up = jnp.concatenate([x[1:], x[:1]], axis=0)
-    down = jnp.concatenate([x[-1:], x[:-1]], axis=0)
-    return (up + down) + 2.0 * x
-
-
 def damped_inverse(coef, diagonal):
     inside = coef > 0.0
     return jnp.where(inside, OMEGA / jnp.where(inside, diagonal, 1.0), 0.0)
@@ -68,11 +62,20 @@
     return corr * (1.0 / 3.0) + inverse * (residual - 2.0 * (coef * corr) + 0.125 * (coef * tu_corr + tu_product))
 
 
-def smooth_small(residual, coef, sweeps):
-    inverse = damped_inverse(coef, 6.0 * coef + 0.125 * band(band_x(band(coef, 1)), 2))
+def sum_x(x):
+    return (x[:-2] + x[2:]) + 2.0 * x[1:-1]
+
+
+def smooth_small(residual, coef, sweeps, first, last):
+    low, high = first - sweeps + 1, last + sweeps - 1
+    tu = band(band(sum_x(coef[low - 1 : high + 1]), 1), 2)
+    coef = coef[low:high]
+    residual = residual[low:high]
+    inverse = damped_inverse(coef, 6.0 * coef + 0.125 * tu)
     corr = inverse * residual
     for _ in range(sweeps - 1):
-        tu = [band(band_x(band(f, 1)), 2) for f in (corr, coef * corr)]
+        tu = [band(band(sum_x(f), 1), 2) for f in (corr, coef * corr)]
+        corr, inverse, residual, coef = [f[1:-1] for f in (corr, inverse, residual, coef)]
         corr = relax(corr, inverse, residual, coef, *tu)
     return corr
 
@@ -472,9 +475,9 @@
     lax.fori_loop(0, 14, pair, 0, unroll=2)
     sums = [pairs[tile, pl.ds(0, 448, stride=2), :] + pairs[tile, pl.ds(1, 448, stride=2), :] for tile in range(2)]
     sums = select_lanes(jnp.concatenate(sums, axis=1), halves).reshape(2, 14, 16, 128)
-    corr_two = smooth_small(0.5 * sums[0], 0.125 * sums[1], 3)
+    corr_two = smooth_small(0.5 * sums[0], 0.125 * sums[1], 3, 3, 11)
     doubled = ones_where(iota((128, 128), 0) == (iota((128, 128), 1) >> 1))
-    wide = select_lanes(corr_two[3:11].reshape(128, 128), doubled).reshape(8, 16, 128)
+    wide = select_lanes(corr_two.reshape(128, 128), doubled).reshape(8, 16, 128)
     rows = wide[:, 0:8, :].reshape(64, 128)
     spread[pl.ds(0, 64, stride=2), :] = rows
     spread[pl.ds(1, 64, stride=2), :] = rows
@@ -507,8 +510,8 @@
     found = found[:, 0:128] + (found[:, 128:256] + found[:, 256:384])
     windows = jnp.concatenate([found[192 * level : 192 * level + 192, :] for level in range(3)], axis=1)
     both = select_lanes(windows, tables[576:960, 0:256])
-    corr = smooth_small(both[:, 0:128].reshape(12, 16, 128), both[:, 128:256].reshape(12, 16, 128), 4)
-    wide = select_lanes(corr[4:8].reshape(64, 128), tables[960:1088, 0:384])
+    corr = smooth_small(both[:, 0:128].reshape(12, 16, 128), both[:, 128:256].reshape(12, 16, 128), 4, 4, 8)
+    wide = select_lanes(corr.reshape(64, 128), tables[960:1088, 0:384])
     for x in range(4):
         level4 = wide[16 * (x // 2) : 16 * (x // 2) + 16, 128:256]
         level4 = jnp.concatenate([jnp.broadcast_to(level4[y : y + 1], (2, 128)) for y in (4, 5)], axis=0)

time: 60.8 us -> 60.8 us (level)
  no operation moved by 1% of the time
where the time goes in v16:
time: 60.8 us; the launch traced here: 60.1 us
  starting transfers between devices  26.9 us (44%)
  waiting for transfers between devices  16 us (26%)
  Pallas kernels  15 us (25%)
  local copies, waits for them, and re-layouts  2 us (3%)
    pallas_call x10, Pallas kernels, call(): pl.pallas_call(kernel, out_shape=[out if isinstance(out, jax.ShapeDtypeSt...  15 us
    ppermute x4, starting transfers between devices, swap(): return (lax.ppermute(to_up, axis, up), lax.ppermute(to_down, axis, down))  12.3 us
    all_to_all x1, starting transfers between devices, on_device(): plane = lax.all_to_all(chunks, ('gx', 'gy'), 0, 0, tiled=True)  10.8 us
    ppermute x4, waiting for transfers between devices, swap(): return (lax.ppermute(to_up, axis, up), lax.ppermute(to_down, axis, down))  9.19 us
    all_to_all x1, waiting for transfers between devices, on_device(): plane = lax.all_to_all(chunks, ('gx', 'gy'), 0, 0, tiled=True)  4.7 us
    ppermute x2, starting transfers between devices, on_device(): lax.ppermute(rows, 'gy', pairs)  3.84 us
    ppermute x2, waiting for transfers between devices, on_device(): lax.ppermute(rows, 'gy', pairs)  2.15 us
    unnamed x6, local copies, waits for them, and re-layouts  2 us
  transfers between devices with their start and end apart: 7, of which 5 were waited for; matrix products, arithmetic and copies ran while one was open for 0% of the time, Pallas kernels for 14%

profile of v16, /device:TPU:56, one launch (start us, length us, event | category | flops | bytes accessed | tf_op | source)
XLA Modules:
  0.0 60.1 jit_solution(11886670407475832515)
XLA Ops:
  0.0 1.9 %send_x.1 = (f32[3,16,16,128]{3,2,1,0:T(8,128)}, f32[15,16,128]{2,1,0:T(8,128)}, f32[15,16,128]{2,1,0:T(8,128)}) custom-call(f32[4]{0:T(128)} %table.1, s32[16,16,128]{2,1,0:T(8,128)} %phase.1, f32[16,16,128]{2,1,0:T(8,128)} %iterate.1, f32[16,16,128]{2,1,0:T(8,128)} %right.1), custom_call_target="tpu_custom_call" | custom-call | flops 1000000 | bytes 393232 | tf_op jit(solution)/shard_map/send_x/pallas_call | solution.py:532
  1.9 4.3 %collective-permute-start = (f32[15,16,128]{2,1,0:T(8,128)}, f32[15,16,128]{2,1,0:T(8,128)S(1)}, u32[]{:S(2)}, u32[]{:S(2)}) collective-permute-start(f32[15,16,128]{2,1,0:T(8,128)} %get-tuple-element.39), channel_id=1, source_target_pairs={{0,64},{64,128},{128,192},{192,256},{256,320},{320,384},{384,448},... | collective-permute-start | bytes 368648 | tf_op jit(solution)/shard_map/ppermute | solution.py:554
  6.2 1.3 %collective-permute-start.1 = (f32[15,16,128]{2,1,0:T(8,128)}, f32[15,16,128]{2,1,0:T(8,128)S(1)}, u32[]{:S(2)}, u32[]{:S(2)}) collective-permute-start(f32[15,16,128]{2,1,0:T(8,128)} %get-tuple-element.40), channel_id=1, source_target_pairs={{64,0},{128,64},{192,128},{256,192},{320,256},{384,320},{448,384},... | collective-permute-start | bytes 368648 | tf_op jit(solution)/shard_map/ppermute | solution.py:554
  7.5 0.0 copy-start.2
  7.5 1.0 %copy-done.2 = f32[3,16,16,128]{3,2,1,0:T(8,128)S(1)} copy-done((f32[3,16,16,128]{3,2,1,0:T(8,128)S(1)}, f32[3,16,16,128]{3,2,1,0:T(8,128)}, u32[]{:S(2)}) %copy-start.2) | copy-done | bytes 393240
  8.6 0.5 collective-permute-done.from_down
  9.1 4.6 %collective-permute-done.1.from_up = f32[15,16,128]{2,1,0:T(8,128)S(1)} collective-permute-done((f32[15,16,128]{2,1,0:T(8,128)}, f32[15,16,128]{2,1,0:T(8,128)S(1)}, u32[]{:S(2)}, u32[]{:S(2)}) %collective-permute-start.1) | collective-permute-done | bytes 122912 | tf_op jit(solution)/shard_map/ppermute | solution.py:554
  13.7 0.1 pack_y.1
  13.9 1.9 %collective-permute-start.2 = (f32[28,16,128]{2,1,0:T(8,128)S(1)}, f32[28,16,128]{2,1,0:T(8,128)S(1)}, u32[]{:S(2)}, u32[]{:S(2)}) collective-permute-start(f32[28,16,128]{2,1,0:T(8,128)S(1)} %get-tuple-element.46), channel_id=1, source_target_pairs={{16,32},{32,16},{17,33},{33,17},{18,34},{34,18},{19,35},{35,19},{2... | collective-permute-start | bytes 688136 | tf_op jit(solution)/shard_map/ppermute | solution.py:576
  15.8 1.9 %collective-permute-start.3 = (f32[28,16,128]{2,1,0:T(8,128)S(1)}, f32[28,16,128]{2,1,0:T(8,128)S(1)}, u32[]{:S(2)}, u32[]{:S(2)}) collective-permute-start(f32[28,16,128]{2,1,0:T(8,128)S(1)} %get-tuple-element.47), channel_id=1, source_target_pairs={{0,16},{32,48},{16,0},{48,32},{1,17},{33,49},{17,1},{49,33},{2,18}... | collective-permute-start | bytes 688136 | tf_op jit(solution)/shard_map/ppermute | solution.py:576
  17.7 1.3 %own_rows.1 = (f32[16,512]{1,0:T(8,128)S(1)}, f32[16,512]{1,0:T(8,128)S(1)}, f32[3,16,16,128]{3,2,1,0:T(8,128)S(1)}, bf16[256,384]{1,0:T(8,128)(2,1)S(1)}) custom-call(f32[3,28,16,128]{3,2,1,0:T(8,128)S(1)} %get-tuple-element.45.ext), custom_call_target="tpu_custom_call" | custom-call | flops 30000000 | bytes 688128 | tf_op jit(solution)/shard_map/own_rows/pallas_call | solution.py:532
  19.1 2.1 %collective-permute-done.2.from_first = f32[28,16,128]{2,1,0:T(8,128)S(1)} collective-permute-done((f32[28,16,128]{2,1,0:T(8,128)S(1)}, f32[28,16,128]{2,1,0:T(8,128)S(1)}, u32[]{:S(2)}, u32[]{:S(2)}) %collective-permute-start.2) | collective-permute-done | bytes 229408 | tf_op jit(solution)/shard_map/ppermute | solution.py:576
  21.2 0.0 collective-permute-done.3.from_second
  21.2 0.8 %pack_z.1 = (f32[3,28,16,128]{3,2,1,0:T(8,128)S(1)}, f32[32,512]{1,0:T(8,128)S(1)}, f32[32,512]{1,0:T(8,128)S(1)}, f32[16,128]{1,0:T(8,128)S(1)}) custom-call(f32[3,28,16,128]{3,2,1,0:T(8,128)S(1)} %get-tuple-element.45.ext, f32[28,16,128]{2,1,0:T(8,128)S(1)} %collective-permute-done.2.from_first, f32[28,16,128]{2,1,0:T(8,128)S(1)} %collective-permute-done.3.from_second, ...), custom_call_target="tpu_custom_call" | custom-call | flops 1000000 | bytes 1998848 | tf_op jit(solution)/shard_map/pack_z/pallas_call | solution.py:532
  22.1 3.6 %collective-permute-start.4 = (f32[32,512]{1,0:T(8,128)S(1)}, f32[32,512]{1,0:T(8,128)S(1)}, u32[]{:S(2)}, u32[]{:S(2)}) collective-permute-start(f32[32,512]{1,0:T(8,128)S(1)} %get-tuple-element.58.sent_up), channel_id=1, source_target_pairs={{0,1},{1,2},{2,3},{3,4},{4,5},{5,6},{6,7},{7,8},{8,9},{9,10},{10,1... | collective-permute-start | bytes 196616 | tf_op jit(solution)/shard_map/ppermute | solution.py:554
  25.7 3.1 %collective-permute-start.5 = (f32[32,512]{1,0:T(8,128)S(1)}, f32[32,512]{1,0:T(8,128)S(1)}, u32[]{:S(2)}, u32[]{:S(2)}) collective-permute-start(f32[32,512]{1,0:T(8,128)S(1)} %get-tuple-element.59.sent_down), channel_id=1, source_target_pairs={{1,0},{2,1},{3,2},{4,3},{5,4},{6,5},{7,6},{8,7},{9,8},{10,9},{11,1... | collective-permute-start | bytes 196616 | tf_op jit(solution)/shard_map/ppermute | solution.py:554
  28.8 1.0 %bands_xy.1 = (f32[3,24,32,128]{3,2,1,0:T(8,128)S(1)}, bf16[1088,512]{1,0:T(8,128)(2,1)S(1)}, bf16[384,128]{1,0:T(8,128)(2,1)S(1)}) custom-call(f32[3,28,16,128]{3,2,1,0:T(8,128)S(1)} %get-tuple-element.45.ext, f32[3,28,16,128]{3,2,1,0:T(8,128)S(1)} %get-tuple-element.60.beyond), custom_call_target="tpu_custom_call" | custom-call | flops 30000000 | bytes 1376256 | tf_op jit(solution)/shard_map/bands_xy/pallas_call | solution.py:532
  29.8 0.0 copy-start
  29.9 1.0 %copy-done = bf16[1088,512]{1,0:T(8,128)(2,1)} copy-done((bf16[1088,512]{1,0:T(8,128)(2,1)}, bf16[1088,512]{1,0:T(8,128)(2,1)S(1)}, u32[]{:S(2)}) %copy-start) | copy-done | bytes 1114136
  30.9 0.0 collective-permute-done.4.from_down
  30.9 4.0 %collective-permute-done.5.from_up = f32[32,512]{1,0:T(8,128)S(1)} collective-permute-done((f32[32,512]{1,0:T(8,128)S(1)}, f32[32,512]{1,0:T(8,128)S(1)}, u32[]{:S(2)}, u32[]{:S(2)}) %collective-permute-start.5) | collective-permute-done | bytes 65568 | tf_op jit(solution)/shard_map/ppermute | solution.py:554
  34.9 1.6 %own_cells.1 = f32[32,3,4,128]{3,2,1,0:T(4,128)} custom-call(f32[32,512]{1,0:T(8,128)S(1)} %get-tuple-element.58.sent_up, f32[32,512]{1,0:T(8,128)S(1)} %get-tuple-element.59.sent_down, f32[32,512]{1,0:T(8,128)S(1)} %collective-permute-done.4.from_down, f32[32,512]{1,0:T(8,128)S(1)} %collective-permute-done.5.from_up, ...), custom_call_target="tpu_custom_call" | custom-call | flops 1000000 | bytes 466944 | tf_op jit(solution)/shard_map/own_cells/pallas_call | solution.py:532
  36.4 10.8 %all-to-all-start = ((f32[32,3,4,128]{3,2,1,0:T(4,128)}), f32[32,3,4,128]{3,2,1,0:T(4,128)S(1)}, u32[]{:S(2)}, u32[]{:S(2)}) async-start(f32[32,3,4,128]{3,2,1,0:T(4,128)} %own_cells.1), calls=%async_computation | async-start | bytes 393216 | tf_op jit(solution)/shard_map/all_to_all | solution.py:603
  47.2 2.3 %fine_residual.1 = (f32[28,32,256]{2,1,0:T(8,128)S(1)}, f32[28,32,256]{2,1,0:T(8,128)S(1)}, f32[28,32,256]{2,1,0:T(8,128)S(1)}) custom-call(f32[3,28,16,128]{3,2,1,0:T(8,128)S(1)} %get-tuple-element.45.ext, f32[3,28,16,128]{3,2,1,0:T(8,128)S(1)} %get-tuple-element.60.beyond, f32[3,24,32,128]{3,2,1,0:T(8,128)S(1)} %get-tuple-element.69.xy, ...), custom_call_target="tpu_custom_call" | custom-call | flops 30000000 | bytes 2686976 | tf_op jit(solution)/shard_map/fine_residual/pallas_call | solution.py:532
  49.5 0.0 copy-start.1
  49.5 3.6 %fine_sweeps.1.base = f32[16,16,128]{2,1,0:T(8,128)S(1)} custom-call(f32[3,28,16,128]{3,2,1,0:T(8,128)S(1)} %get-tuple-element.45.ext, f32[28,32,256]{2,1,0:T(8,128)S(1)} %get-tuple-element.70.coef, f32[28,32,256]{2,1,0:T(8,128)S(1)} %get-tuple-element.71.res, f32[28,32,256]{2,1,0:T(8,128)S(1)} %get-tuple-element.72.inv), custom_call_target="tpu_custom_call" | custom-call | flops 60000000 | bytes 3440640 | tf_op jit(solution)/shard_map/fine_sweeps/pallas_call | solution.py:532
  53.1 4.7 %all-to-all-done.plane = f32[32,3,4,128]{3,2,1,0:T(4,128)S(1)} async-done(((f32[32,3,4,128]{3,2,1,0:T(4,128)}), f32[32,3,4,128]{3,2,1,0:T(4,128)S(1)}, u32[]{:S(2)}, u32[]{:S(2)}) %all-to-all-start) | async-done | bytes 196640 | tf_op jit(solution)/shard_map/all_to_all | solution.py:603
  57.8 0.0 copy-done.1
  57.8 2.3 %coarse_levels.1 = f32[16,16,128]{2,1,0:T(8,128)} custom-call(bf16[1088,512]{1,0:T(8,128)(2,1)S(1)} %copy-done.1, f32[32,3,4,128]{3,2,1,0:T(4,128)S(1)} %all-to-all-done.plane, f32[16,16,128]{2,1,0:T(8,128)S(1)} %fine_sweeps.1.base), custom_call_target="tpu_custom_call" | custom-call | flops 1000000 | bytes 2555904 | tf_op jit(solution)/shard_map/coarse_levels/pallas_call | solution.py:532
  (1 shorter events, 0.0 us)
Async XLA Ops:
  1.9 7.2 %collective-permute-start = (f32[15,16,128]{2,1,0:T(8,128)}, f32[15,16,128]{2,1,0:T(8,128)S(1)}, u32[]{:S(2)}, u32[]{:S(2)}) collective-permute-start(f32[15,16,128]{2,1,0:T(8,128)} %get-tuple-element.39), channel_id=1, source_target_pairs={{0,64},{64,128},{128,192},{192,256},{256,320},{320,384},{384,448},... | collective-permute-start | bytes 368648 | tf_op jit(solution)/shard_map/ppermute | solution.py:554
  6.2 7.5 %collective-permute-start.1 = (f32[15,16,128]{2,1,0:T(8,128)}, f32[15,16,128]{2,1,0:T(8,128)S(1)}, u32[]{:S(2)}, u32[]{:S(2)}) collective-permute-start(f32[15,16,128]{2,1,0:T(8,128)} %get-tuple-element.40), channel_id=1, source_target_pairs={{64,0},{128,64},{192,128},{256,192},{320,256},{384,320},{448,384},... | collective-permute-start | bytes 368648 | tf_op jit(solution)/shard_map/ppermute | solution.py:554
  7.5 1.0 %copy-start.2 = (f32[3,16,16,128]{3,2,1,0:T(8,128)S(1)}, f32[3,16,16,128]{3,2,1,0:T(8,128)}, u32[]{:S(2)}) copy-start(f32[3,16,16,128]{3,2,1,0:T(8,128)} %get-tuple-element.41.fields) | copy-start | bytes 1179652
  13.9 7.3 %collective-permute-start.2 = (f32[28,16,128]{2,1,0:T(8,128)S(1)}, f32[28,16,128]{2,1,0:T(8,128)S(1)}, u32[]{:S(2)}, u32[]{:S(2)}) collective-permute-start(f32[28,16,128]{2,1,0:T(8,128)S(1)} %get-tuple-element.46), channel_id=1, source_target_pairs={{16,32},{32,16},{17,33},{33,17},{18,34},{34,18},{19,35},{35,19},{2... | collective-permute-start | bytes 688136 | tf_op jit(solution)/shard_map/ppermute | solution.py:576
  15.8 5.4 %collective-permute-start.3 = (f32[28,16,128]{2,1,0:T(8,128)S(1)}, f32[28,16,128]{2,1,0:T(8,128)S(1)}, u32[]{:S(2)}, u32[]{:S(2)}) collective-permute-start(f32[28,16,128]{2,1,0:T(8,128)S(1)} %get-tuple-element.47), channel_id=1, source_target_pairs={{0,16},{32,48},{16,0},{48,32},{1,17},{33,49},{17,1},{49,33},{2,18}... | collective-permute-start | bytes 688136 | tf_op jit(solution)/shard_map/ppermute | solution.py:576
  22.1 8.8 %collective-permute-start.4 = (f32[32,512]{1,0:T(8,128)S(1)}, f32[32,512]{1,0:T(8,128)S(1)}, u32[]{:S(2)}, u32[]{:S(2)}) collective-permute-start(f32[32,512]{1,0:T(8,128)S(1)} %get-tuple-element.58.sent_up), channel_id=1, source_target_pairs={{0,1},{1,2},{2,3},{3,4},{4,5},{5,6},{6,7},{7,8},{8,9},{9,10},{10,1... | collective-permute-start | bytes 196616 | tf_op jit(solution)/shard_map/ppermute | solution.py:554
  25.7 9.2 %collective-permute-start.5 = (f32[32,512]{1,0:T(8,128)S(1)}, f32[32,512]{1,0:T(8,128)S(1)}, u32[]{:S(2)}, u32[]{:S(2)}) collective-permute-start(f32[32,512]{1,0:T(8,128)S(1)} %get-tuple-element.59.sent_down), channel_id=1, source_target_pairs={{1,0},{2,1},{3,2},{4,3},{5,4},{6,5},{7,6},{8,7},{9,8},{10,9},{11,1... | collective-permute-start | bytes 196616 | tf_op jit(solution)/shard_map/ppermute | solution.py:554
  29.8 1.0 %copy-start = (bf16[1088,512]{1,0:T(8,128)(2,1)}, bf16[1088,512]{1,0:T(8,128)(2,1)S(1)}, u32[]{:S(2)}) copy-start(bf16[1088,512]{1,0:T(8,128)(2,1)S(1)} %get-tuple-element.64.tables) | copy-start | bytes 3342340
  36.4 21.4 %all-to-all-start = ((f32[32,3,4,128]{3,2,1,0:T(4,128)}), f32[32,3,4,128]{3,2,1,0:T(4,128)S(1)}, u32[]{:S(2)}, u32[]{:S(2)}) async-start(f32[32,3,4,128]{3,2,1,0:T(4,128)} %own_cells.1), calls=%async_computation | async-start | bytes 393216 | tf_op jit(solution)/shard_map/all_to_all | solution.py:603
  49.5 8.3 %copy-start.1 = (bf16[1088,512]{1,0:T(8,128)(2,1)S(1)}, bf16[1088,512]{1,0:T(8,128)(2,1)}, u32[]{:S(2)}) copy-start(bf16[1088,512]{1,0:T(8,128)(2,1)} %copy-done) | copy-start | bytes 3342340

commit v17 on v16

--- a/solution.py
+++ b/solution.py
@@ -80,30 +80,41 @@
     return corr
 
 
-def send_x(table, phase, iterate, right, fields, to_up, to_down, values, phases, sems):
-    copies = [
-        pltpu.make_async_copy(table, values, sems.at[0]),
-        pltpu.make_async_copy(phase, phases, sems.at[1]),
-        pltpu.make_async_copy(iterate, fields.at[1], sems.at[2]),
-        pltpu.make_async_copy(right, fields.at[2], sems.at[3]),
-    ]
+def lookup(phase, values):
+    k = jnp.zeros(phase.shape, F32)
+    for index in range(4):
+        k = jnp.where(phase == index, values[index], k)
+    return k
+
+
+def fetch(pairs, sems):
+    copies = [pltpu.make_async_copy(source, target, sems.at[at]) for at, (source, target) in enumerate(pairs)]
     for copy in copies:
         copy.start()
     for copy in copies:
         copy.wait()
-    p = phases[...]
-    k = jnp.zeros(p.shape, F32)
-    for index in range(4):
-        k = jnp.where(p == index, values[index], k)
-    fields[0] = k
-    for field in range(3):
-        h, a, b = HALO[field], ROWS[field], ROWS[field + 1]
-        to_up[a:b] = fields[field, 16 - h : 16]
-        to_down[a:b] = fields[field, 0:h]
-
-
-def hold(fields, held):
-    held[...] = fields[...]
+
+
+def send_x(table, phase, iterate, right, to_up, to_down, values, upper, lower, sems):
+    fetch(
+        [
+            (table, values),
+            (phase.at[10:16], upper),
+            (phase.at[0:6], lower),
+            (iterate.at[11:16], to_up.at[6:11]),
+            (iterate.at[0:5], to_down.at[6:11]),
+            (right.at[12:16], to_up.at[11:15]),
+            (right.at[0:4], to_down.at[11:15]),
+        ],
+        sems,
+    )
+    to_up[0:6] = lookup(upper[...], values)
+    to_down[0:6] = lookup(lower[...], values)
+
+
+def hold(table, phase, iterate, right, fields, values, phases, sems):
+    fetch([(table, values), (phase, phases), (iterate, fields.at[1]), (right, fields.at[2])], sems)
+    fields[0] = lookup(phases[...], values)
 
 
 def by_parity(body, first, second):
@@ -556,17 +567,29 @@
 
 def on_device(right, iterate, phase, table):
     block = (16, 16, 128)
-    fields, to_up, to_down = call(
+    inputs = [table, phase, iterate, right]
+    values = pltpu.SMEM((4,), F32)
+    edge = pltpu.VMEM((6, 16, 128), jnp.int32)
+    to_up, to_down = call(
         send_x,
-        [(3, *block), (15, 16, 128), (15, 16, 128)],
-        [table, phase, iterate, right],
-        scratch=[pltpu.SMEM((4,), F32), pltpu.VMEM(block, jnp.int32), pltpu.SemaphoreType.DMA((4,))],
+        [(15, 16, 128), (15, 16, 128)],
+        inputs,
+        scratch=[values, edge, edge, pltpu.SemaphoreType.DMA((7,))],
         first=HBM,
         rest=HBM,
         grant=60,
     )
     from_down, from_up = swap("gx", to_up, to_down)
-    (held,) = call(hold, [(3, *block)], [fields], flops=30000000)
+    (held,) = call(
+        hold,
+        [(3, *block)],
+        inputs,
+        scratch=[values, pltpu.VMEM(block, jnp.int32), pltpu.SemaphoreType.DMA((4,))],
+        first=HBM,
+        rest=HBM,
+        flops=30000000,
+        grant=60,
+    )
     from_down, from_up, fields = lax.optimization_barrier((from_down, from_up, held))
     ext, *sent = call(
         pack_y,

time: 60.8 us -> 61.6 us (1.013)
  Pallas kernels: 15 us -> 16.5 us
  waiting for transfers between devices: 16 us -> 15.2 us
    pallas_call x10, Pallas kernels: 15 us -> 16.5 us  [call(): pl.pallas_call(kernel, out_shape=[out if isinstance(out, jax.ShapeDtypeSt...]
    ppermute x4, waiting for transfers between devices: 9.19 us -> 8.33 us  [swap(): return (lax.ppermute(to_up, axis, up), lax.ppermute(to_down, axis, down))]
  transfers between devices with their start and end apart: 7 -> 7, of which waited for: 5 -> 4; matrix products, arithmetic and copies ran while one was open for 0% -> 0% of each run, Pallas kernels for 14% -> 17%
where the time goes in v17:
time: 61.6 us; the launch traced here: 60.8 us
  starting transfers between devices  26.9 us (44%)
  Pallas kernels  16.5 us (27%)
  waiting for transfers between devices  15.2 us (25%)
  local copies, waits for them, and re-layouts  2 us (3%)
    pallas_call x10, Pallas kernels, call(): pl.pallas_call(kernel, out_shape=[out if isinstance(out, jax.ShapeDtypeSt...  16.5 us
    ppermute x4, starting transfers between devices, swap(): return (lax.ppermute(to_up, axis, up), lax.ppermute(to_down, axis, down))  12.3 us
    all_to_all x1, starting transfers between devices, on_device(): plane = lax.all_to_all(chunks, ('gx', 'gy'), 0, 0, tiled=True)  10.8 us
    ppermute x4, waiting for transfers between devices, swap(): return (lax.ppermute(to_up, axis, up), lax.ppermute(to_down, axis, down))  8.33 us
    all_to_all x1, waiting for transfers between devices, on_device(): plane = lax.all_to_all(chunks, ('gx', 'gy'), 0, 0, tiled=True)  4.7 us
    ppermute x2, starting transfers between devices, on_device(): lax.ppermute(rows, 'gy', pairs)  3.84 us
    ppermute x2, waiting for transfers between devices, on_device(): lax.ppermute(rows, 'gy', pairs)  2.14 us
    unnamed x6, local copies, waits for them, and re-layouts  2 us
  transfers between devices with their start and end apart: 7, of which 4 were waited for; matrix products, arithmetic and copies ran while one was open for 0% of the time, Pallas kernels for 17%

profile of v17, /device:TPU:56, one launch (start us, length us, event | category | flops | bytes accessed | tf_op | source)
XLA Modules:
  0.0 60.8 jit_solution(14291390273710448575)
XLA Ops:
  0.0 1.6 %send_x.1 = (f32[15,16,128]{2,1,0:T(8,128)}, f32[15,16,128]{2,1,0:T(8,128)}) custom-call(f32[4]{0:T(128)} %table.3, s32[16,16,128]{2,1,0:T(8,128)} %phase.3, f32[16,16,128]{2,1,0:T(8,128)} %iterate.3, f32[16,16,128]{2,1,0:T(8,128)} %right.3), custom_call_target="tpu_custom_call" | custom-call | flops 1000000 | bytes 393232 | tf_op jit(solution)/shard_map/send_x/pallas_call | solution.py:543
  1.6 4.3 %collective-permute-start = (f32[15,16,128]{2,1,0:T(8,128)}, f32[15,16,128]{2,1,0:T(8,128)S(1)}, u32[]{:S(2)}, u32[]{:S(2)}) collective-permute-start(f32[15,16,128]{2,1,0:T(8,128)} %get-tuple-element.38), channel_id=1, source_target_pairs={{0,64},{64,128},{128,192},{192,256},{256,320},{320,384},{384,448},... | collective-permute-start | bytes 368648 | tf_op jit(solution)/shard_map/ppermute | solution.py:565
  5.9 1.3 %collective-permute-start.1 = (f32[15,16,128]{2,1,0:T(8,128)}, f32[15,16,128]{2,1,0:T(8,128)S(1)}, u32[]{:S(2)}, u32[]{:S(2)}) collective-permute-start(f32[15,16,128]{2,1,0:T(8,128)} %get-tuple-element.39), channel_id=1, source_target_pairs={{64,0},{128,64},{192,128},{256,192},{320,256},{384,320},{448,384},... | collective-permute-start | bytes 368648 | tf_op jit(solution)/shard_map/ppermute | solution.py:565
  7.2 1.9 %hold.1.fields = f32[3,16,16,128]{3,2,1,0:T(8,128)} custom-call(f32[4]{0:T(128)} %table.3, s32[16,16,128]{2,1,0:T(8,128)} %phase.3, f32[16,16,128]{2,1,0:T(8,128)} %iterate.3, f32[16,16,128]{2,1,0:T(8,128)} %right.3), custom_call_target="tpu_custom_call" | custom-call | flops 30000000 | bytes 393232 | tf_op jit(solution)/shard_map/hold/pallas_call | solution.py:543
  9.1 0.0 collective-permute-done.from_down
  9.1 4.3 %collective-permute-done.1.from_up = f32[15,16,128]{2,1,0:T(8,128)S(1)} collective-permute-done((f32[15,16,128]{2,1,0:T(8,128)}, f32[15,16,128]{2,1,0:T(8,128)S(1)}, u32[]{:S(2)}, u32[]{:S(2)}) %collective-permute-start.1) | collective-permute-done | bytes 122912 | tf_op jit(solution)/shard_map/ppermute | solution.py:565
  13.4 0.0 copy-start
  13.4 1.0 %copy-done = f32[3,16,16,128]{3,2,1,0:T(8,128)S(1)} copy-done((f32[3,16,16,128]{3,2,1,0:T(8,128)S(1)}, f32[3,16,16,128]{3,2,1,0:T(8,128)}, u32[]{:S(2)}) %copy-start) | copy-done | bytes 393240
  14.4 0.1 pack_y.1
  14.6 1.9 %collective-permute-start.2 = (f32[28,16,128]{2,1,0:T(8,128)S(1)}, f32[28,16,128]{2,1,0:T(8,128)S(1)}, u32[]{:S(2)}, u32[]{:S(2)}) collective-permute-start(f32[28,16,128]{2,1,0:T(8,128)S(1)} %get-tuple-element.44), channel_id=1, source_target_pairs={{16,32},{32,16},{17,33},{33,17},{18,34},{34,18},{19,35},{35,19},{2... | collective-permute-start | bytes 688136 | tf_op jit(solution)/shard_map/ppermute | solution.py:599
  16.5 1.9 %collective-permute-start.3 = (f32[28,16,128]{2,1,0:T(8,128)S(1)}, f32[28,16,128]{2,1,0:T(8,128)S(1)}, u32[]{:S(2)}, u32[]{:S(2)}) collective-permute-start(f32[28,16,128]{2,1,0:T(8,128)S(1)} %get-tuple-element.45), channel_id=1, source_target_pairs={{0,16},{32,48},{16,0},{48,32},{1,17},{33,49},{17,1},{49,33},{2,18}... | collective-permute-start | bytes 688136 | tf_op jit(solution)/shard_map/ppermute | solution.py:599
  18.4 1.3 %own_rows.1 = (f32[16,512]{1,0:T(8,128)S(1)}, f32[16,512]{1,0:T(8,128)S(1)}, f32[3,16,16,128]{3,2,1,0:T(8,128)S(1)}, bf16[256,384]{1,0:T(8,128)(2,1)S(1)}) custom-call(f32[3,28,16,128]{3,2,1,0:T(8,128)S(1)} %get-tuple-element.43.ext), custom_call_target="tpu_custom_call" | custom-call | flops 30000000 | bytes 688128 | tf_op jit(solution)/shard_map/own_rows/pallas_call | solution.py:543
  19.8 2.1 %collective-permute-done.2.from_first = f32[28,16,128]{2,1,0:T(8,128)S(1)} collective-permute-done((f32[28,16,128]{2,1,0:T(8,128)S(1)}, f32[28,16,128]{2,1,0:T(8,128)S(1)}, u32[]{:S(2)}, u32[]{:S(2)}) %collective-permute-start.2) | collective-permute-done | bytes 229408 | tf_op jit(solution)/shard_map/ppermute | solution.py:599
  21.9 0.0 collective-permute-done.3.from_second
  21.9 0.8 %pack_z.1 = (f32[3,28,16,128]{3,2,1,0:T(8,128)S(1)}, f32[32,512]{1,0:T(8,128)S(1)}, f32[32,512]{1,0:T(8,128)S(1)}, f32[16,128]{1,0:T(8,128)S(1)}) custom-call(f32[3,28,16,128]{3,2,1,0:T(8,128)S(1)} %get-tuple-element.43.ext, f32[28,16,128]{2,1,0:T(8,128)S(1)} %collective-permute-done.2.from_first, f32[28,16,128]{2,1,0:T(8,128)S(1)} %collective-permute-done.3.from_second, ...), custom_call_target="tpu_custom_call" | custom-call | flops 1000000 | bytes 1998848 | tf_op jit(solution)/shard_map/pack_z/pallas_call | solution.py:543
  22.8 3.6 %collective-permute-start.4 = (f32[32,512]{1,0:T(8,128)S(1)}, f32[32,512]{1,0:T(8,128)S(1)}, u32[]{:S(2)}, u32[]{:S(2)}) collective-permute-start(f32[32,512]{1,0:T(8,128)S(1)} %get-tuple-element.56.sent_up), channel_id=1, source_target_pairs={{0,1},{1,2},{2,3},{3,4},{4,5},{5,6},{6,7},{7,8},{8,9},{9,10},{10,1... | collective-permute-start | bytes 196616 | tf_op jit(solution)/shard_map/ppermute | solution.py:565
  26.4 3.1 %collective-permute-start.5 = (f32[32,512]{1,0:T(8,128)S(1)}, f32[32,512]{1,0:T(8,128)S(1)}, u32[]{:S(2)}, u32[]{:S(2)}) collective-permute-start(f32[32,512]{1,0:T(8,128)S(1)} %get-tuple-element.57.sent_down), channel_id=1, source_target_pairs={{1,0},{2,1},{3,2},{4,3},{5,4},{6,5},{7,6},{8,7},{9,8},{10,9},{11,1... | collective-permute-start | bytes 196616 | tf_op jit(solution)/shard_map/ppermute | solution.py:565
  29.5 1.0 %bands_xy.1 = (f32[3,24,32,128]{3,2,1,0:T(8,128)S(1)}, bf16[1088,512]{1,0:T(8,128)(2,1)S(1)}, bf16[384,128]{1,0:T(8,128)(2,1)S(1)}) custom-call(f32[3,28,16,128]{3,2,1,0:T(8,128)S(1)} %get-tuple-element.43.ext, f32[3,28,16,128]{3,2,1,0:T(8,128)S(1)} %get-tuple-element.58.beyond), custom_call_target="tpu_custom_call" | custom-call | flops 30000000 | bytes 1376256 | tf_op jit(solution)/shard_map/bands_xy/pallas_call | solution.py:543
  30.5 0.0 copy-start.1
  30.6 1.0 %copy-done.1 = bf16[1088,512]{1,0:T(8,128)(2,1)} copy-done((bf16[1088,512]{1,0:T(8,128)(2,1)}, bf16[1088,512]{1,0:T(8,128)(2,1)S(1)}, u32[]{:S(2)}) %copy-start.1) | copy-done | bytes 1114136
  31.6 0.0 collective-permute-done.4.from_down
  31.6 4.0 %collective-permute-done.5.from_up = f32[32,512]{1,0:T(8,128)S(1)} collective-permute-done((f32[32,512]{1,0:T(8,128)S(1)}, f32[32,512]{1,0:T(8,128)S(1)}, u32[]{:S(2)}, u32[]{:S(2)}) %collective-permute-start.5) | collective-permute-done | bytes 65568 | tf_op jit(solution)/shard_map/ppermute | solution.py:565
  35.5 1.6 %own_cells.1 = f32[32,3,4,128]{3,2,1,0:T(4,128)} custom-call(f32[32,512]{1,0:T(8,128)S(1)} %get-tuple-element.56.sent_up, f32[32,512]{1,0:T(8,128)S(1)} %get-tuple-element.57.sent_down, f32[32,512]{1,0:T(8,128)S(1)} %collective-permute-done.4.from_down, f32[32,512]{1,0:T(8,128)S(1)} %collective-permute-done.5.from_up, ...), custom_call_target="tpu_custom_call" | custom-call | flops 1000000 | bytes 466944 | tf_op jit(solution)/shard_map/own_cells/pallas_call | solution.py:543
  37.1 10.8 %all-to-all-start = ((f32[32,3,4,128]{3,2,1,0:T(4,128)}), f32[32,3,4,128]{3,2,1,0:T(4,128)S(1)}, u32[]{:S(2)}, u32[]{:S(2)}) async-start(f32[32,3,4,128]{3,2,1,0:T(4,128)} %own_cells.1), calls=%async_computation | async-start | bytes 393216 | tf_op jit(solution)/shard_map/all_to_all | solution.py:626
  47.9 2.3 %fine_residual.1 = (f32[28,32,256]{2,1,0:T(8,128)S(1)}, f32[28,32,256]{2,1,0:T(8,128)S(1)}, f32[28,32,256]{2,1,0:T(8,128)S(1)}) custom-call(f32[3,28,16,128]{3,2,1,0:T(8,128)S(1)} %get-tuple-element.43.ext, f32[3,28,16,128]{3,2,1,0:T(8,128)S(1)} %get-tuple-element.58.beyond, f32[3,24,32,128]{3,2,1,0:T(8,128)S(1)} %get-tuple-element.67.xy, ...), custom_call_target="tpu_custom_call" | custom-call | flops 30000000 | bytes 2686976 | tf_op jit(solution)/shard_map/fine_residual/pallas_call | solution.py:543
  50.2 0.0 copy-start.2
  50.2 3.6 %fine_sweeps.1.base = f32[16,16,128]{2,1,0:T(8,128)S(1)} custom-call(f32[3,28,16,128]{3,2,1,0:T(8,128)S(1)} %get-tuple-element.43.ext, f32[28,32,256]{2,1,0:T(8,128)S(1)} %get-tuple-element.68.coef, f32[28,32,256]{2,1,0:T(8,128)S(1)} %get-tuple-element.69.res, f32[28,32,256]{2,1,0:T(8,128)S(1)} %get-tuple-element.70.inv), custom_call_target="tpu_custom_call" | custom-call | flops 60000000 | bytes 3440640 | tf_op jit(solution)/shard_map/fine_sweeps/pallas_call | solution.py:543
  53.8 4.7 %all-to-all-done.plane = f32[32,3,4,128]{3,2,1,0:T(4,128)S(1)} async-done(((f32[32,3,4,128]{3,2,1,0:T(4,128)}), f32[32,3,4,128]{3,2,1,0:T(4,128)S(1)}, u32[]{:S(2)}, u32[]{:S(2)}) %all-to-all-start) | async-done | bytes 196640 | tf_op jit(solution)/shard_map/all_to_all | solution.py:626
  58.5 0.0 copy-done.2
  58.5 2.3 %coarse_levels.1 = f32[16,16,128]{2,1,0:T(8,128)} custom-call(bf16[1088,512]{1,0:T(8,128)(2,1)S(1)} %copy-done.2, f32[32,3,4,128]{3,2,1,0:T(4,128)S(1)} %all-to-all-done.plane, f32[16,16,128]{2,1,0:T(8,128)S(1)} %fine_sweeps.1.base), custom_call_target="tpu_custom_call" | custom-call | flops 1000000 | bytes 2555904 | tf_op jit(solution)/shard_map/coarse_levels/pallas_call | solution.py:543
Async XLA Ops:
  1.6 7.5 %collective-permute-start = (f32[15,16,128]{2,1,0:T(8,128)}, f32[15,16,128]{2,1,0:T(8,128)S(1)}, u32[]{:S(2)}, u32[]{:S(2)}) collective-permute-start(f32[15,16,128]{2,1,0:T(8,128)} %get-tuple-element.38), channel_id=1, source_target_pairs={{0,64},{64,128},{128,192},{192,256},{256,320},{320,384},{384,448},... | collective-permute-start | bytes 368648 | tf_op jit(solution)/shard_map/ppermute | solution.py:565
  5.9 7.5 %collective-permute-start.1 = (f32[15,16,128]{2,1,0:T(8,128)}, f32[15,16,128]{2,1,0:T(8,128)S(1)}, u32[]{:S(2)}, u32[]{:S(2)}) collective-permute-start(f32[15,16,128]{2,1,0:T(8,128)} %get-tuple-element.39), channel_id=1, source_target_pairs={{64,0},{128,64},{192,128},{256,192},{320,256},{384,320},{448,384},... | collective-permute-start | bytes 368648 | tf_op jit(solution)/shard_map/ppermute | solution.py:565
  13.4 1.0 %copy-start = (f32[3,16,16,128]{3,2,1,0:T(8,128)S(1)}, f32[3,16,16,128]{3,2,1,0:T(8,128)}, u32[]{:S(2)}) copy-start(f32[3,16,16,128]{3,2,1,0:T(8,128)} %hold.1.fields) | copy-start | bytes 1179652
  14.6 7.3 %collective-permute-start.2 = (f32[28,16,128]{2,1,0:T(8,128)S(1)}, f32[28,16,128]{2,1,0:T(8,128)S(1)}, u32[]{:S(2)}, u32[]{:S(2)}) collective-permute-start(f32[28,16,128]{2,1,0:T(8,128)S(1)} %get-tuple-element.44), channel_id=1, source_target_pairs={{16,32},{32,16},{17,33},{33,17},{18,34},{34,18},{19,35},{35,19},{2... | collective-permute-start | bytes 688136 | tf_op jit(solution)/shard_map/ppermute | solution.py:599
  16.5 5.4 %collective-permute-start.3 = (f32[28,16,128]{2,1,0:T(8,128)S(1)}, f32[28,16,128]{2,1,0:T(8,128)S(1)}, u32[]{:S(2)}, u32[]{:S(2)}) collective-permute-start(f32[28,16,128]{2,1,0:T(8,128)S(1)} %get-tuple-element.45), channel_id=1, source_target_pairs={{0,16},{32,48},{16,0},{48,32},{1,17},{33,49},{17,1},{49,33},{2,18}... | collective-permute-start | bytes 688136 | tf_op jit(solution)/shard_map/ppermute | solution.py:599
  22.8 8.8 %collective-permute-start.4 = (f32[32,512]{1,0:T(8,128)S(1)}, f32[32,512]{1,0:T(8,128)S(1)}, u32[]{:S(2)}, u32[]{:S(2)}) collective-permute-start(f32[32,512]{1,0:T(8,128)S(1)} %get-tuple-element.56.sent_up), channel_id=1, source_target_pairs={{0,1},{1,2},{2,3},{3,4},{4,5},{5,6},{6,7},{7,8},{8,9},{9,10},{10,1... | collective-permute-start | bytes 196616 | tf_op jit(solution)/shard_map/ppermute | solution.py:565
  26.4 9.2 %collective-permute-start.5 = (f32[32,512]{1,0:T(8,128)S(1)}, f32[32,512]{1,0:T(8,128)S(1)}, u32[]{:S(2)}, u32[]{:S(2)}) collective-permute-start(f32[32,512]{1,0:T(8,128)S(1)} %get-tuple-element.57.sent_down), channel_id=1, source_target_pairs={{1,0},{2,1},{3,2},{4,3},{5,4},{6,5},{7,6},{8,7},{9,8},{10,9},{11,1... | collective-permute-start | bytes 196616 | tf_op jit(solution)/shard_map/ppermute | solution.py:565
  30.5 1.0 %copy-start.1 = (bf16[1088,512]{1,0:T(8,128)(2,1)}, bf16[1088,512]{1,0:T(8,128)(2,1)S(1)}, u32[]{:S(2)}) copy-start(bf16[1088,512]{1,0:T(8,128)(2,1)S(1)} %get-tuple-element.62.tables) | copy-start | bytes 3342340
  37.1 21.4 %all-to-all-start = ((f32[32,3,4,128]{3,2,1,0:T(4,128)}), f32[32,3,4,128]{3,2,1,0:T(4,128)S(1)}, u32[]{:S(2)}, u32[]{:S(2)}) async-start(f32[32,3,4,128]{3,2,1,0:T(4,128)} %own_cells.1), calls=%async_computation | async-start | bytes 393216 | tf_op jit(solution)/shard_map/all_to_all | solution.py:626
  50.2 8.3 %copy-start.2 = (bf16[1088,512]{1,0:T(8,128)(2,1)S(1)}, bf16[1088,512]{1,0:T(8,128)(2,1)}, u32[]{:S(2)}) copy-start(bf16[1088,512]{1,0:T(8,128)(2,1)} %copy-done.1) | copy-start | bytes 3342340

commit v18 on v17

--- a/solution.py
+++ b/solution.py
@@ -115,6 +115,10 @@
 def hold(table, phase, iterate, right, fields, values, phases, sems):
     fetch([(table, values), (phase, phases), (iterate, fields.at[1]), (right, fields.at[2])], sems)
     fields[0] = lookup(phases[...], values)
+
+
+def near(fields, held):
+    held[...] = fields[...]
 
 
 def by_parity(body, first, second):
@@ -590,6 +594,7 @@
         flops=30000000,
         grant=60,
     )
+    (held,) = call(near, [(3, *block)], [held], flops=30000000)
     from_down, from_up, fields = lax.optimization_barrier((from_down, from_up, held))
     ext, *sent = call(
         pack_y,

time: 61.6 us -> 60.6 us (0.984)
  waiting for transfers between devices: 15.2 us -> 14.1 us
    ppermute x4, waiting for transfers between devices: 8.33 us -> 7.31 us  [swap(): return (lax.ppermute(to_up, axis, up), lax.ppermute(to_down, axis, down))]
    pallas_call x10 -> x11, Pallas kernels: 16.5 us -> 16.6 us  [call(): pl.pallas_call(kernel, out_shape=[out if isinstance(out, jax.ShapeDtypeSt...]
where the time goes in v18:
time: 60.6 us; the launch traced here: 59.8 us
  starting transfers between devices  26.9 us (44%)
  Pallas kernels  16.6 us (27%)
  waiting for transfers between devices  14.1 us (23%)
  local copies, waits for them, and re-layouts  2 us (3%)
    pallas_call x11, Pallas kernels, call(): pl.pallas_call(kernel, out_shape=[out if isinstance(out, jax.ShapeDtypeSt...  16.6 us
    ppermute x4, starting transfers between devices, swap(): return (lax.ppermute(to_up, axis, up), lax.ppermute(to_down, axis, down))  12.3 us
    all_to_all x1, starting transfers between devices, on_device(): plane = lax.all_to_all(chunks, ('gx', 'gy'), 0, 0, tiled=True)  10.8 us
    ppermute x4, waiting for transfers between devices, swap(): return (lax.ppermute(to_up, axis, up), lax.ppermute(to_down, axis, down))  7.31 us
    all_to_all x1, waiting for transfers between devices, on_device(): plane = lax.all_to_all(chunks, ('gx', 'gy'), 0, 0, tiled=True)  4.69 us
    ppermute x2, starting transfers between devices, on_device(): lax.ppermute(rows, 'gy', pairs)  3.84 us
    ppermute x2, waiting for transfers between devices, on_device(): lax.ppermute(rows, 'gy', pairs)  2.14 us
    unnamed x6, local copies, waits for them, and re-layouts  2 us
  transfers between devices with their start and end apart: 7, of which 4 were waited for; matrix products, arithmetic and copies ran while one was open for 0% of the time, Pallas kernels for 17%

profile of v18, /device:TPU:56, one launch (start us, length us, event | category | flops | bytes accessed | tf_op | source)
XLA Modules:
  0.0 59.8 jit_solution(18003806287894121751)
XLA Ops:
  0.0 1.6 %send_x.1 = (f32[15,16,128]{2,1,0:T(8,128)}, f32[15,16,128]{2,1,0:T(8,128)}) custom-call(f32[4]{0:T(128)} %table.3, s32[16,16,128]{2,1,0:T(8,128)} %phase.3, f32[16,16,128]{2,1,0:T(8,128)} %iterate.3, f32[16,16,128]{2,1,0:T(8,128)} %right.3), custom_call_target="tpu_custom_call" | custom-call | flops 1000000 | bytes 393232 | tf_op jit(solution)/shard_map/send_x/pallas_call | solution.py:547
  1.6 4.3 %collective-permute-start = (f32[15,16,128]{2,1,0:T(8,128)}, f32[15,16,128]{2,1,0:T(8,128)S(1)}, u32[]{:S(2)}, u32[]{:S(2)}) collective-permute-start(f32[15,16,128]{2,1,0:T(8,128)} %get-tuple-element.38), channel_id=1, source_target_pairs={{0,64},{64,128},{128,192},{192,256},{256,320},{320,384},{384,448},... | collective-permute-start | bytes 368648 | tf_op jit(solution)/shard_map/ppermute | solution.py:569
  5.9 1.3 %collective-permute-start.1 = (f32[15,16,128]{2,1,0:T(8,128)}, f32[15,16,128]{2,1,0:T(8,128)S(1)}, u32[]{:S(2)}, u32[]{:S(2)}) collective-permute-start(f32[15,16,128]{2,1,0:T(8,128)} %get-tuple-element.39), channel_id=1, source_target_pairs={{64,0},{128,64},{192,128},{256,192},{320,256},{384,320},{448,384},... | collective-permute-start | bytes 368648 | tf_op jit(solution)/shard_map/ppermute | solution.py:569
  7.2 1.9 %hold.1.fields = f32[3,16,16,128]{3,2,1,0:T(8,128)} custom-call(f32[4]{0:T(128)} %table.3, s32[16,16,128]{2,1,0:T(8,128)} %phase.3, f32[16,16,128]{2,1,0:T(8,128)} %iterate.3, f32[16,16,128]{2,1,0:T(8,128)} %right.3), custom_call_target="tpu_custom_call" | custom-call | flops 30000000 | bytes 393232 | tf_op jit(solution)/shard_map/hold/pallas_call | solution.py:547
  9.1 0.0 copy-start
  9.1 1.0 %copy-done = f32[3,16,16,128]{3,2,1,0:T(8,128)S(1)} copy-done((f32[3,16,16,128]{3,2,1,0:T(8,128)S(1)}, f32[3,16,16,128]{3,2,1,0:T(8,128)}, u32[]{:S(2)}) %copy-start) | copy-done | bytes 393240
  10.1 0.0 collective-permute-done.from_down
  10.1 3.3 %collective-permute-done.1.from_up = f32[15,16,128]{2,1,0:T(8,128)S(1)} collective-permute-done((f32[15,16,128]{2,1,0:T(8,128)}, f32[15,16,128]{2,1,0:T(8,128)S(1)}, u32[]{:S(2)}, u32[]{:S(2)}) %collective-permute-start.1) | collective-permute-done | bytes 122912 | tf_op jit(solution)/shard_map/ppermute | solution.py:569
  13.4 0.1 pack_y.1
  13.6 1.9 %collective-permute-start.2 = (f32[28,16,128]{2,1,0:T(8,128)S(1)}, f32[28,16,128]{2,1,0:T(8,128)S(1)}, u32[]{:S(2)}, u32[]{:S(2)}) collective-permute-start(f32[28,16,128]{2,1,0:T(8,128)S(1)} %get-tuple-element.44), channel_id=1, source_target_pairs={{16,32},{32,16},{17,33},{33,17},{18,34},{34,18},{19,35},{35,19},{2... | collective-permute-start | bytes 688136 | tf_op jit(solution)/shard_map/ppermute | solution.py:604
  15.5 1.9 %collective-permute-start.3 = (f32[28,16,128]{2,1,0:T(8,128)S(1)}, f32[28,16,128]{2,1,0:T(8,128)S(1)}, u32[]{:S(2)}, u32[]{:S(2)}) collective-permute-start(f32[28,16,128]{2,1,0:T(8,128)S(1)} %get-tuple-element.45), channel_id=1, source_target_pairs={{0,16},{32,48},{16,0},{48,32},{1,17},{33,49},{17,1},{49,33},{2,18}... | collective-permute-start | bytes 688136 | tf_op jit(solution)/shard_map/ppermute | solution.py:604
  17.4 1.3 %own_rows.1 = (f32[16,512]{1,0:T(8,128)S(1)}, f32[16,512]{1,0:T(8,128)S(1)}, f32[3,16,16,128]{3,2,1,0:T(8,128)S(1)}, bf16[256,384]{1,0:T(8,128)(2,1)S(1)}) custom-call(f32[3,28,16,128]{3,2,1,0:T(8,128)S(1)} %get-tuple-element.43.ext), custom_call_target="tpu_custom_call" | custom-call | flops 30000000 | bytes 688128 | tf_op jit(solution)/shard_map/own_rows/pallas_call | solution.py:547
  18.8 2.1 %collective-permute-done.2.from_first = f32[28,16,128]{2,1,0:T(8,128)S(1)} collective-permute-done((f32[28,16,128]{2,1,0:T(8,128)S(1)}, f32[28,16,128]{2,1,0:T(8,128)S(1)}, u32[]{:S(2)}, u32[]{:S(2)}) %collective-permute-start.2) | collective-permute-done | bytes 229408 | tf_op jit(solution)/shard_map/ppermute | solution.py:604
  20.9 0.0 collective-permute-done.3.from_second
  20.9 0.8 %pack_z.1 = (f32[3,28,16,128]{3,2,1,0:T(8,128)S(1)}, f32[32,512]{1,0:T(8,128)S(1)}, f32[32,512]{1,0:T(8,128)S(1)}, f32[16,128]{1,0:T(8,128)S(1)}) custom-call(f32[3,28,16,128]{3,2,1,0:T(8,128)S(1)} %get-tuple-element.43.ext, f32[28,16,128]{2,1,0:T(8,128)S(1)} %collective-permute-done.2.from_first, f32[28,16,128]{2,1,0:T(8,128)S(1)} %collective-permute-done.3.from_second, ...), custom_call_target="tpu_custom_call" | custom-call | flops 1000000 | bytes 1998848 | tf_op jit(solution)/shard_map/pack_z/pallas_call | solution.py:547
  21.8 3.6 %collective-permute-start.4 = (f32[32,512]{1,0:T(8,128)S(1)}, f32[32,512]{1,0:T(8,128)S(1)}, u32[]{:S(2)}, u32[]{:S(2)}) collective-permute-start(f32[32,512]{1,0:T(8,128)S(1)} %get-tuple-element.56.sent_up), channel_id=1, source_target_pairs={{0,1},{1,2},{2,3},{3,4},{4,5},{5,6},{6,7},{7,8},{8,9},{9,10},{10,1... | collective-permute-start | bytes 196616 | tf_op jit(solution)/shard_map/ppermute | solution.py:569
  25.4 3.1 %collective-permute-start.5 = (f32[32,512]{1,0:T(8,128)S(1)}, f32[32,512]{1,0:T(8,128)S(1)}, u32[]{:S(2)}, u32[]{:S(2)}) collective-permute-start(f32[32,512]{1,0:T(8,128)S(1)} %get-tuple-element.57.sent_down), channel_id=1, source_target_pairs={{1,0},{2,1},{3,2},{4,3},{5,4},{6,5},{7,6},{8,7},{9,8},{10,9},{11,1... | collective-permute-start | bytes 196616 | tf_op jit(solution)/shard_map/ppermute | solution.py:569
  28.5 1.0 %bands_xy.1 = (f32[3,24,32,128]{3,2,1,0:T(8,128)S(1)}, bf16[1088,512]{1,0:T(8,128)(2,1)S(1)}, bf16[384,128]{1,0:T(8,128)(2,1)S(1)}) custom-call(f32[3,28,16,128]{3,2,1,0:T(8,128)S(1)} %get-tuple-element.43.ext, f32[3,28,16,128]{3,2,1,0:T(8,128)S(1)} %get-tuple-element.58.beyond), custom_call_target="tpu_custom_call" | custom-call | flops 30000000 | bytes 1376256 | tf_op jit(solution)/shard_map/bands_xy/pallas_call | solution.py:547
  29.5 0.0 copy-start.1
  29.6 1.0 %copy-done.1 = bf16[1088,512]{1,0:T(8,128)(2,1)} copy-done((bf16[1088,512]{1,0:T(8,128)(2,1)}, bf16[1088,512]{1,0:T(8,128)(2,1)S(1)}, u32[]{:S(2)}) %copy-start.1) | copy-done | bytes 1114136
  30.6 0.0 collective-permute-done.4.from_down
  30.6 4.0 %collective-permute-done.5.from_up = f32[32,512]{1,0:T(8,128)S(1)} collective-permute-done((f32[32,512]{1,0:T(8,128)S(1)}, f32[32,512]{1,0:T(8,128)S(1)}, u32[]{:S(2)}, u32[]{:S(2)}) %collective-permute-start.5) | collective-permute-done | bytes 65568 | tf_op jit(solution)/shard_map/ppermute | solution.py:569
  34.5 1.6 %own_cells.1 = f32[32,3,4,128]{3,2,1,0:T(4,128)} custom-call(f32[32,512]{1,0:T(8,128)S(1)} %get-tuple-element.56.sent_up, f32[32,512]{1,0:T(8,128)S(1)} %get-tuple-element.57.sent_down, f32[32,512]{1,0:T(8,128)S(1)} %collective-permute-done.4.from_down, f32[32,512]{1,0:T(8,128)S(1)} %collective-permute-done.5.from_up, ...), custom_call_target="tpu_custom_call" | custom-call | flops 1000000 | bytes 466944 | tf_op jit(solution)/shard_map/own_cells/pallas_call | solution.py:547
  36.1 10.8 %all-to-all-start = ((f32[32,3,4,128]{3,2,1,0:T(4,128)}), f32[32,3,4,128]{3,2,1,0:T(4,128)S(1)}, u32[]{:S(2)}, u32[]{:S(2)}) async-start(f32[32,3,4,128]{3,2,1,0:T(4,128)} %own_cells.1), calls=%async_computation | async-start | bytes 393216 | tf_op jit(solution)/shard_map/all_to_all | solution.py:631
  46.9 2.3 %fine_residual.1 = (f32[28,32,256]{2,1,0:T(8,128)S(1)}, f32[28,32,256]{2,1,0:T(8,128)S(1)}, f32[28,32,256]{2,1,0:T(8,128)S(1)}) custom-call(f32[3,28,16,128]{3,2,1,0:T(8,128)S(1)} %get-tuple-element.43.ext, f32[3,28,16,128]{3,2,1,0:T(8,128)S(1)} %get-tuple-element.58.beyond, f32[3,24,32,128]{3,2,1,0:T(8,128)S(1)} %get-tuple-element.67.xy, ...), custom_call_target="tpu_custom_call" | custom-call | flops 30000000 | bytes 2686976 | tf_op jit(solution)/shard_map/fine_residual/pallas_call | solution.py:547
  49.2 0.0 copy-start.2
  49.2 3.6 %fine_sweeps.1.base = f32[16,16,128]{2,1,0:T(8,128)S(1)} custom-call(f32[3,28,16,128]{3,2,1,0:T(8,128)S(1)} %get-tuple-element.43.ext, f32[28,32,256]{2,1,0:T(8,128)S(1)} %get-tuple-element.68.coef, f32[28,32,256]{2,1,0:T(8,128)S(1)} %get-tuple-element.69.res, f32[28,32,256]{2,1,0:T(8,128)S(1)} %get-tuple-element.70.inv), custom_call_target="tpu_custom_call" | custom-call | flops 60000000 | bytes 3440640 | tf_op jit(solution)/shard_map/fine_sweeps/pallas_call | solution.py:547
  52.8 4.7 %all-to-all-done.plane = f32[32,3,4,128]{3,2,1,0:T(4,128)S(1)} async-done(((f32[32,3,4,128]{3,2,1,0:T(4,128)}), f32[32,3,4,128]{3,2,1,0:T(4,128)S(1)}, u32[]{:S(2)}, u32[]{:S(2)}) %all-to-all-start) | async-done | bytes 196640 | tf_op jit(solution)/shard_map/all_to_all | solution.py:631
  57.5 0.0 copy-done.2
  57.5 2.3 %coarse_levels.1 = f32[16,16,128]{2,1,0:T(8,128)} custom-call(bf16[1088,512]{1,0:T(8,128)(2,1)S(1)} %copy-done.2, f32[32,3,4,128]{3,2,1,0:T(4,128)S(1)} %all-to-all-done.plane, f32[16,16,128]{2,1,0:T(8,128)S(1)} %fine_sweeps.1.base), custom_call_target="tpu_custom_call" | custom-call | flops 1000000 | bytes 2555904 | tf_op jit(solution)/shard_map/coarse_levels/pallas_call | solution.py:547
  (1 shorter events, 0.0 us)
Async XLA Ops:
  1.6 8.5 %collective-permute-start = (f32[15,16,128]{2,1,0:T(8,128)}, f32[15,16,128]{2,1,0:T(8,128)S(1)}, u32[]{:S(2)}, u32[]{:S(2)}) collective-permute-start(f32[15,16,128]{2,1,0:T(8,128)} %get-tuple-element.38), channel_id=1, source_target_pairs={{0,64},{64,128},{128,192},{192,256},{256,320},{320,384},{384,448},... | collective-permute-start | bytes 368648 | tf_op jit(solution)/shard_map/ppermute | solution.py:569
  5.9 7.5 %collective-permute-start.1 = (f32[15,16,128]{2,1,0:T(8,128)}, f32[15,16,128]{2,1,0:T(8,128)S(1)}, u32[]{:S(2)}, u32[]{:S(2)}) collective-permute-start(f32[15,16,128]{2,1,0:T(8,128)} %get-tuple-element.39), channel_id=1, source_target_pairs={{64,0},{128,64},{192,128},{256,192},{320,256},{384,320},{448,384},... | collective-permute-start | bytes 368648 | tf_op jit(solution)/shard_map/ppermute | solution.py:569
  9.1 1.0 %copy-start = (f32[3,16,16,128]{3,2,1,0:T(8,128)S(1)}, f32[3,16,16,128]{3,2,1,0:T(8,128)}, u32[]{:S(2)}) copy-start(f32[3,16,16,128]{3,2,1,0:T(8,128)} %hold.1.fields) | copy-start | bytes 1179652
  13.6 7.3 %collective-permute-start.2 = (f32[28,16,128]{2,1,0:T(8,128)S(1)}, f32[28,16,128]{2,1,0:T(8,128)S(1)}, u32[]{:S(2)}, u32[]{:S(2)}) collective-permute-start(f32[28,16,128]{2,1,0:T(8,128)S(1)} %get-tuple-element.44), channel_id=1, source_target_pairs={{16,32},{32,16},{17,33},{33,17},{18,34},{34,18},{19,35},{35,19},{2... | collective-permute-start | bytes 688136 | tf_op jit(solution)/shard_map/ppermute | solution.py:604
  15.5 5.4 %collective-permute-start.3 = (f32[28,16,128]{2,1,0:T(8,128)S(1)}, f32[28,16,128]{2,1,0:T(8,128)S(1)}, u32[]{:S(2)}, u32[]{:S(2)}) collective-permute-start(f32[28,16,128]{2,1,0:T(8,128)S(1)} %get-tuple-element.45), channel_id=1, source_target_pairs={{0,16},{32,48},{16,0},{48,32},{1,17},{33,49},{17,1},{49,33},{2,18}... | collective-permute-start | bytes 688136 | tf_op jit(solution)/shard_map/ppermute | solution.py:604
  21.8 8.8 %collective-permute-start.4 = (f32[32,512]{1,0:T(8,128)S(1)}, f32[32,512]{1,0:T(8,128)S(1)}, u32[]{:S(2)}, u32[]{:S(2)}) collective-permute-start(f32[32,512]{1,0:T(8,128)S(1)} %get-tuple-element.56.sent_up), channel_id=1, source_target_pairs={{0,1},{1,2},{2,3},{3,4},{4,5},{5,6},{6,7},{7,8},{8,9},{9,10},{10,1... | collective-permute-start | bytes 196616 | tf_op jit(solution)/shard_map/ppermute | solution.py:569
  25.4 9.2 %collective-permute-start.5 = (f32[32,512]{1,0:T(8,128)S(1)}, f32[32,512]{1,0:T(8,128)S(1)}, u32[]{:S(2)}, u32[]{:S(2)}) collective-permute-start(f32[32,512]{1,0:T(8,128)S(1)} %get-tuple-element.57.sent_down), channel_id=1, source_target_pairs={{1,0},{2,1},{3,2},{4,3},{5,4},{6,5},{7,6},{8,7},{9,8},{10,9},{11,1... | collective-permute-start | bytes 196616 | tf_op jit(solution)/shard_map/ppermute | solution.py:569
  29.5 1.0 %copy-start.1 = (bf16[1088,512]{1,0:T(8,128)(2,1)}, bf16[1088,512]{1,0:T(8,128)(2,1)S(1)}, u32[]{:S(2)}) copy-start(bf16[1088,512]{1,0:T(8,128)(2,1)S(1)} %get-tuple-element.62.tables) | copy-start | bytes 3342340
  36.1 21.4 %all-to-all-start = ((f32[32,3,4,128]{3,2,1,0:T(4,128)}), f32[32,3,4,128]{3,2,1,0:T(4,128)S(1)}, u32[]{:S(2)}, u32[]{:S(2)}) async-start(f32[32,3,4,128]{3,2,1,0:T(4,128)} %own_cells.1), calls=%async_computation | async-start | bytes 393216 | tf_op jit(solution)/shard_map/all_to_all | solution.py:631
  49.2 8.3 %copy-start.2 = (bf16[1088,512]{1,0:T(8,128)(2,1)S(1)}, bf16[1088,512]{1,0:T(8,128)(2,1)}, u32[]{:S(2)}) copy-start(bf16[1088,512]{1,0:T(8,128)(2,1)} %copy-done.1) | copy-start | bytes 3342340
